TPU v7x, 32 devices: a whole 2x2x4 slice. The times are simulated.
32 devices in a mesh: groups: 2 (over x), fsdp: 16 (over z, y, core).
Axes of the slice: x: 2, y: 2, z: 4, core: 2. Of those that a mesh axis runs over, the one named last changes fastest.
Arguments:
- queries: bfloat16 [2048, 8192], P(('groups', 'fsdp')), parts along dimension 0, may hold values from -68 to 68
- out_grad: bfloat16 [2048, 8192], P(('groups', 'fsdp')), parts along dimension 0, may hold values from -6 to 6
- neighbours: bfloat16 [4096, 2, 8192], P(('groups', 'fsdp')), parts along dimension 0, may hold values from -6 to 6
- neighbour_ids: int32 [64], P('groups'), parts along dimension 0, may hold values from 0 to 15, as said below
Outputs:
- attn_out: bfloat16 [2048, 8192], P(('groups', 'fsdp')), parts along dimension 0
- query_grad: bfloat16 [2048, 8192], P(('groups', 'fsdp')), parts along dimension 0
- neighbour_grad: bfloat16 [4096, 2, 8192], P(('groups', 'fsdp')), parts along dimension 0
There are 2 independent parts, one for each index of `groups`. A program takes and returns all parts, laid end to end along the dimension named above; each array names one. Nothing has to cross between parts.
Inputs may be any that keep to these rules, and one draw needn't show every extreme that they name: `neighbour_ids`: every row of 0 to 15 appears exactly twice, and the two rows of a span differ.
All inputs are finite; a program needn't handle non-finite values.
Results may differ from a plain program's by a relative error of at most 0.009.
Values may be sent and summed in bfloat16 or wider, within the bound.
No kernel may reach another device: no remote copies, remote signals or barrier semaphores. Data moves between devices by JAX's collectives and lax.ppermute only.
A program may use at most 128 MiB of HBM per device.

v0:
```python
import math

import jax
import jax.numpy as jnp
from jax import lax
from jax.sharding import PartitionSpec as P

HD = 128
SPAN = 64
NTOK = 128


def shift_in(tokens):
    padding = jnp.zeros((SPAN - 1,) + tokens.shape[1:], tokens.dtype)
    moved = jnp.concatenate([tokens[SPAN - 1 :], padding], 0)
    return moved.reshape((-1, SPAN) + tokens.shape[1:])


def shift_out(spans):
    flattened = spans.reshape((-1,) + spans.shape[2:])
    padding = jnp.zeros((SPAN - 1,) + flattened.shape[1:], flattened.dtype)
    return jnp.concatenate([padding, flattened[: flattened.shape[0] - (SPAN - 1)]], 0)


def span_keys(key_table, value_table, chosen_rows):
    per_block = chosen_rows.shape[0]
    local_heads = key_table.shape[2]
    key_block = key_table[chosen_rows].reshape(per_block, 2 * NTOK, local_heads, HD)
    value_block = value_table[chosen_rows].reshape(per_block, 2 * NTOK, local_heads, HD)
    return (key_block, value_block)


def forward_block(query_block, key_block, value_block):
    score_scale = 1.0 / math.sqrt(HD)
    scores = (
        jnp.einsum("gqhd,gkhd->ghqk", query_block, key_block, preferred_element_type=jnp.float32)
        * score_scale
    )
    row_max = jnp.max(scores, -1, keepdims=True)
    exponent = jnp.exp(scores - row_max)
    softmax = exponent / jnp.sum(exponent, -1, keepdims=True)
    weights = softmax.astype(jnp.bfloat16)
    attended = jnp.einsum(
        "ghqk,gkhd->gqhd", weights, value_block, preferred_element_type=jnp.float32
    )
    return (softmax, attended)


def backward_block(query_block, grad_block, key_block, value_block, softmax, attended):
    score_scale = 1.0 / math.sqrt(HD)
    per_block = query_block.shape[0]
    weights = softmax.astype(jnp.bfloat16)
    value_grad = jnp.einsum(
        "ghqk,gqhd->gkhd", weights, grad_block, preferred_element_type=jnp.float32
    )
    prob_grad = jnp.einsum(
        "gqhd,gkhd->ghqk", grad_block, value_block, preferred_element_type=jnp.float32
    )
    row_delta = jnp.sum(grad_block.astype(jnp.float32) * attended, -1)
    row_delta = jnp.transpose(row_delta, (0, 2, 1))[..., None]
    score_grad = (softmax * (prob_grad - row_delta)).astype(jnp.bfloat16)
    span_grad = (
        jnp.einsum("ghqk,gkhd->gqhd", score_grad, key_block, preferred_element_type=jnp.float32)
        * score_scale
    )
    key_grad = (
        jnp.einsum("ghqk,gqhd->gkhd", score_grad, query_block, preferred_element_type=jnp.float32)
        * score_scale
    )
    key_grad = key_grad.reshape(per_block * 2, NTOK, -1)
    value_grad = value_grad.reshape(per_block * 2, NTOK, -1)
    return (span_grad.astype(jnp.bfloat16), key_grad, value_grad)


def body(queries, out_grad, neighbours, neighbour_ids):
    devices = lax.axis_size("fsdp")
    head_width = queries.shape[1] // devices
    local_heads = head_width // HD
    query_all = lax.all_to_all(queries, "fsdp", split_axis=1, concat_axis=0, tiled=True)
    neighbour_all = lax.all_to_all(neighbours, "fsdp", split_axis=2, concat_axis=0, tiled=True)
    row_count = neighbour_all.shape[0] // NTOK
    key_table = neighbour_all[:, 0].reshape(row_count, NTOK, local_heads, HD)
    value_table = neighbour_all[:, 1].reshape(row_count, NTOK, local_heads, HD)
    span_count = neighbour_ids.shape[0] // 2
    per_block = math.gcd(span_count, max(1, 512 // SPAN))
    blocks = span_count // per_block
    id_blocks = neighbour_ids.reshape(blocks, per_block, 2)
    query_blocks = shift_in(query_all).reshape(blocks, per_block, SPAN, local_heads, HD)

    def forward_one(element):
        query_block, chosen_rows = element
        key_block, value_block = span_keys(key_table, value_table, chosen_rows)
        return forward_block(query_block, key_block, value_block)

    softmax_all, attended_all = lax.map(forward_one, (query_blocks, id_blocks))
    out_heads = shift_out(attended_all.astype(jnp.bfloat16).reshape(span_count, SPAN, head_width))
    attn_out = lax.all_to_all(out_heads, "fsdp", split_axis=0, concat_axis=1, tiled=True)
    grad_all = lax.all_to_all(out_grad, "fsdp", split_axis=1, concat_axis=0, tiled=True)
    grad_blocks = shift_in(grad_all).reshape(blocks, per_block, SPAN, local_heads, HD)

    def backward_step(element):
        query_block, grad_block, chosen_rows, softmax, attended = element
        key_block, value_block = span_keys(key_table, value_table, chosen_rows)
        return backward_block(query_block, grad_block, key_block, value_block, softmax, attended)

    span_grads, key_grads, value_grads = lax.map(
        backward_step, (query_blocks, grad_blocks, id_blocks, softmax_all, attended_all)
    )
    qgrad_heads = shift_out(span_grads.reshape(span_count, SPAN, head_width))
    key_slots = key_grads.reshape(2 * span_count, NTOK, head_width)
    value_slots = value_grads.reshape(2 * span_count, NTOK, head_width)
    slot_order = jnp.argsort(neighbour_ids, stable=True).reshape(row_count, 2)
    first_slot = slot_order[:, 0]
    second_slot = slot_order[:, 1]
    key_rows = (key_slots[first_slot] + key_slots[second_slot]).astype(jnp.bfloat16)
    value_rows = (value_slots[first_slot] + value_slots[second_slot]).astype(jnp.bfloat16)
    row_grads = jnp.stack([key_rows, value_rows], 2).reshape(row_count * NTOK, 2, head_width)
    query_grad = lax.all_to_all(qgrad_heads, "fsdp", split_axis=0, concat_axis=1, tiled=True)
    neighbour_grad = lax.all_to_all(row_grads, "fsdp", split_axis=0, concat_axis=2, tiled=True)
    return (attn_out, query_grad, neighbour_grad)


def solution(mesh):
    in_specs = (
        P(("groups", "fsdp"), None),
        P(("groups", "fsdp"), None),
        P(("groups", "fsdp"), None, None),
        P("groups"),
    )
    out_specs = (
        P(("groups", "fsdp"), None),
        P(("groups", "fsdp"), None),
        P(("groups", "fsdp"), None, None),
    )
    return jax.shard_map(body, mesh=mesh, in_specs=in_specs, out_specs=out_specs, check_vma=False)
```

profile of v0, /device:TPU:15, one launch (start us, length us, event | category | flops | bytes accessed | tf_op | source)
XLA Modules:
  0.0 563.7 jit_solution(12174597941378949861)
XLA Ops:
  3.0 6.6 %all-to-all-start = ((bf16[64,16,512]{2,0,1:T(8,128)(2,1)}), bf16[64,16,512]{2,0,1:T(8,128)(2,1)S(1)}, u32[]{:S(2)}, u32[]{:S(2)}) async-start(bf16[64,16,512]{2,0,1:T(8,128)(2,1)} %bitcast.108), calls=%async_computation | async-start | bytes 2097152 | tf_op jit(solution)/shard_map/all_to_all | solution.py:79
  10.7 23.8 %all-to-all-done = bf16[64,16,512]{2,0,1:T(8,128)(2,1)S(1)} async-done(((bf16[64,16,512]{2,0,1:T(8,128)(2,1)}), bf16[64,16,512]{2,0,1:T(8,128)(2,1)S(1)}, u32[]{:S(2)}, u32[]{:S(2)}) %all-to-all-start) | async-done | bytes 1048608 | tf_op jit(solution)/shard_map/all_to_all | solution.py:79
  39.4 14.8 %copy.148 = bf16[128,2,8192]{0,1,2:T(2,128)(2,1)} copy(bf16[128,2,8192]{2,1,0:T(2,128)(2,1)} %param.10) | data formatting | bytes 8388608 | tf_op args[2]
  54.2 10.1 %all-to-all-done.3 = bf16[64,16,512]{2,0,1:T(8,128)(2,1)S(1)} async-done(((bf16[64,16,512]{2,0,1:T(8,128)(2,1)}), bf16[64,16,512]{2,0,1:T(8,128)(2,1)S(1)}, u32[]{:S(2)}, u32[]{:S(2)}) %all-to-all-start.3) | async-done | bytes 1048608 | tf_op jit(solution)/shard_map/all_to_all | solution.py:98
  76.0 86.7 %all-to-all-done.1 = bf16[128,2,8192]{0,1,2:T(2,128)(2,1)} async-done(((bf16[128,2,8192]{0,1,2:T(2,128)(2,1)}), bf16[128,2,8192]{0,1,2:T(2,128)(2,1)}, u32[]{:S(2)}, u32[]{:S(2)}) %all-to-all-start.1) | async-done | bytes 4194336 | tf_op jit(solution)/shard_map/all_to_all | solution.py:80
  167.4 6.2 %copy.150 = bf16[16,128,2,512]{3,1,0,2:T(8,128)(2,1)} copy(bf16[16,128,2,512]{1,3,0,2:T(8,128)(2,1)} %bitcast.161) | data formatting | bytes 8388608 | tf_op jit(solution)/shard_map/all_to_all | solution.py:80
  184.6 53.4 %while.26 = (s32[]{:T(128)}, f32[2,8,4,64,256]{4,3,2,1,0:T(8,128)}, f32[2,8,64,4,128]{4,2,3,1,0:T(8,128)}, bf16[2,8,64,4,128]{4,2,3,1,0:T(8,128)(2,1)S(1)}, s32[...) while((s32[]{:T(128)}, f32[2,8,4,64,256]{4,3,2,1,0:T(8,128)}, ...), condition=%wide.region_3.4_spmd, body=%wide.region_0.3_spmd.sunk | while | flops 406851136 | bytes 27292336 | solution.py:95
  204.4 6.9 %fusion.92 = f32[2,8,64,4,128]{4,2,3,1,0:T(8,128)} fusion(f32[2,8,64,4,128]{4,2,3,1,0:T(8,128)} %get-tuple-element.422, s32[]{:T(128)S(6)} %copy.263, bf16[8,256,4,128]{3,2,1,0:T(4,128)(2,1)} %bitcast.158, f32[8,4,64]{2,1,0:T(4,128)S(1)} %get-tuple-element.398, f32[8,4,64,256]{3,2,1,0:T(8,128)} %fusion.91), kind=kOutput, calls=%fused_computation.18.clone.1 | convolution fusion | flops 136317184 | bytes 5251076 | tf_op jit(solution)/shard_map/while/body/eval_jaxpr/ghqk,gkhd->gqhd/dot_general | solution.py:43
  231.1 6.9 %fusion.92 = f32[2,8,64,4,128]{4,2,3,1,0:T(8,128)} fusion(f32[2,8,64,4,128]{4,2,3,1,0:T(8,128)} %get-tuple-element.422, s32[]{:T(128)S(6)} %copy.263, bf16[8,256,4,128]{3,2,1,0:T(4,128)(2,1)} %bitcast.158, f32[8,4,64]{2,1,0:T(4,128)S(1)} %get-tuple-element.398, f32[8,4,64,256]{3,2,1,0:T(8,128)} %fusion.91), kind=kOutput, calls=%fused_computation.18.clone.1 | convolution fusion | flops 136317184 | bytes 5251076 | tf_op jit(solution)/shard_map/while/body/eval_jaxpr/ghqk,gkhd->gqhd/dot_general | solution.py:43
  247.0 115.0 %while.27 = (s32[]{:T(128)}, bf16[2,8,64,4,128]{4,3,2,1,0:T(4,128)(2,1)}, f32[2,16,128,512]{3,2,1,0:T(8,128)}, f32[2,16,128,512]{3,2,1,0:T(8,128)}, s32[2,8,2]{1...) while((s32[]{:T(128)}, ...), condition=%wide.region_6.7_spmd, body=%wide.region_4.6_spmd.sunk | while | flops 540802112 | bytes 112743296 | solution.py:106
  296.2 8.3 %constant_dynamic-update-slice_fusion.3 = (f32[2,16,128,512]{3,2,1,0:T(8,128)}, f32[2,16,128,512]{3,2,1,0:T(8,128)}) fusion(f32[2,16,128,512]{3,2,1,0:T(8,128)} %get-tuple-element.451, f32[1,16,128,512]{3,2,1,0:T(8,128)} %reshape.258, s32[]{:T(128)S(6)} %copy.273, f32[2,16,128,512]{3,2,1,0:T(8,128)} %get-tuple-element.450, ...), kind=kLoop, calls=%fused_computation.51.clone.1 | loop fusion | bytes 16777220 | tf_op jit(solution)/shard_map/while/body/jit(dynamic_update_index_in_dim)/dynamic_update_slice | solution.py:106
  353.7 8.4 %constant_dynamic-update-slice_fusion.3 = (f32[2,16,128,512]{3,2,1,0:T(8,128)}, f32[2,16,128,512]{3,2,1,0:T(8,128)}) fusion(f32[2,16,128,512]{3,2,1,0:T(8,128)} %get-tuple-element.451, f32[1,16,128,512]{3,2,1,0:T(8,128)} %reshape.258, s32[]{:T(128)S(6)} %copy.273, f32[2,16,128,512]{3,2,1,0:T(8,128)} %get-tuple-element.450, ...), kind=kLoop, calls=%fused_computation.51.clone.1 | loop fusion | bytes 16777220 | tf_op jit(solution)/shard_map/while/body/jit(dynamic_update_index_in_dim)/dynamic_update_slice | solution.py:106
  364.7 6.1 %all-to-all-start.4 = ((bf16[16,64,512]{2,1,0:T(8,128)(2,1)}), bf16[16,64,512]{2,1,0:T(8,128)(2,1)S(1)}, u32[]{:S(2)}, u32[]{:S(2)}) async-start(bf16[16,64,512]{2,1,0:T(8,128)(2,1)} %bitcast.28), calls=%async_computation.4 | async-start | bytes 2097152 | tf_op jit(solution)/shard_map/all_to_all | solution.py:118
  371.0 6.2 %gather_fusion.6 = f32[16,128,512]{2,1,0:T(8,128)} fusion(f32[32,128,512]{2,1,0:T(8,128)} %bitcast.168, s32[1024]{0:T(1024)S(1)} %get-tuple-element.293), kind=kCustom, calls=%fused_computation.6 | custom fusion | bytes 8388672 | tf_op jit(solution)/shard_map/gather | solution.py:116
  377.2 6.1 %gather_fusion.7 = f32[16,128,512]{2,1,0:T(8,128)} fusion(f32[32,128,512]{2,1,0:T(8,128)} %bitcast.169, s32[1024]{0:T(1024)S(1)} %get-tuple-element.292), kind=kCustom, calls=%fused_computation.7 | custom fusion | bytes 8388672 | tf_op jit(solution)/shard_map/gather | solution.py:116
  383.3 6.2 %gather_fusion.4 = f32[16,128,512]{2,1,0:T(8,128)} fusion(f32[32,128,512]{2,1,0:T(8,128)} %bitcast.166, s32[1024]{0:T(1024)S(1)} %get-tuple-element.293), kind=kCustom, calls=%fused_computation.4 | custom fusion | bytes 8388672 | tf_op jit(solution)/shard_map/gather | solution.py:115
  389.5 6.1 %gather_fusion.5 = f32[16,128,512]{2,1,0:T(8,128)} fusion(f32[32,128,512]{2,1,0:T(8,128)} %bitcast.167, s32[1024]{0:T(1024)S(1)} %get-tuple-element.292), kind=kCustom, calls=%fused_computation.5 | custom fusion | bytes 8388672 | tf_op jit(solution)/shard_map/gather | solution.py:115
  400.0 15.6 %copy.164 = bf16[2048,1,512]{2,1,0:T(2,128)(2,1)S(1)} copy(bf16[2048,1,512]{2,0,1:T(8,128)(2,1)S(1)} %bitcast.164) | data formatting | bytes 4194304 | tf_op jit(solution)/shard_map/convert_element_type | solution.py:116
  416.8 15.6 %copy.163 = bf16[2048,1,512]{2,1,0:T(2,128)(2,1)S(1)} copy(bf16[2048,1,512]{2,0,1:T(8,128)(2,1)S(1)} %bitcast.165) | data formatting | bytes 4194304 | tf_op jit(solution)/shard_map/convert_element_type | solution.py:115
  432.5 10.5 %pad_maximum_fusion = bf16[2048,2,512]{2,1,0:T(2,128)(2,1)} fusion(bf16[2048,1,512]{2,1,0:T(2,128)(2,1)S(1)} %copy.164, bf16[2048,1,512]{2,1,0:T(2,128)(2,1)S(1)} %copy.163), kind=kLoop, calls=%fused_computation.57 | loop fusion | flops 8388608 | bytes 8388608 | tf_op jit(solution)/shard_map/stack | solution.py:117
  443.0 6.0 %all-to-all-start.5 = ((bf16[2048,2,512]{2,1,0:T(2,128)(2,1)}), bf16[2048,2,512]{2,1,0:T(2,128)(2,1)}, u32[]{:S(2)}, u32[]{:S(2)}) async-start(bf16[2048,2,512]{2,1,0:T(2,128)(2,1)} %pad_maximum_fusion), calls=%async_computation.5 | async-start | bytes 8388608 | tf_op jit(solution)/shard_map/all_to_all | solution.py:119
  452.4 89.1 %all-to-all-done.5 = bf16[2048,2,512]{2,1,0:T(2,128)(2,1)} async-done(((bf16[2048,2,512]{2,1,0:T(2,128)(2,1)}), bf16[2048,2,512]{2,1,0:T(2,128)(2,1)}, u32[]{:S(2)}, u32[]{:S(2)}) %all-to-all-start.5) | async-done | bytes 4194336 | tf_op jit(solution)/shard_map/all_to_all | solution.py:119
  546.3 6.2 %copy.166 = bf16[128,2,16,512]{0,3,2,1:T(8,128)(2,1)} copy(bf16[128,2,16,512]{3,0,2,1:T(8,128)(2,1)} %bitcast.162) | data formatting | bytes 8388608 | tf_op jit(solution)/shard_map/all_to_all | solution.py:119
  552.5 11.1 %copy.167 = bf16[128,2,8192]{2,1,0:T(2,128)(2,1)} copy(bf16[128,2,8192]{0,2,1:T(8,128)(2,1)} %bitcast.163) | data formatting | bytes 8388608
  (133 shorter events, 199.2 us)
Async XLA Ops:
  0.6 9.0 %copy-start.8 = (bf16[64,8192]{1,0:T(8,128)(2,1)S(1)}, bf16[64,8192]{1,0:T(8,128)(2,1)}, u32[]{:S(2)}) copy-start(bf16[64,8192]{1,0:T(8,128)(2,1)} %param.9) | copy-start | bytes 3145732
  3.0 31.4 %all-to-all-start = ((bf16[64,16,512]{2,0,1:T(8,128)(2,1)}), bf16[64,16,512]{2,0,1:T(8,128)(2,1)S(1)}, u32[]{:S(2)}, u32[]{:S(2)}) async-start(bf16[64,16,512]{2,0,1:T(8,128)(2,1)} %bitcast.108), calls=%async_computation | async-start | bytes 2097152 | tf_op jit(solution)/shard_map/all_to_all | solution.py:79
  34.5 29.8 %all-to-all-start.3 = ((bf16[64,16,512]{2,0,1:T(8,128)(2,1)}), bf16[64,16,512]{2,0,1:T(8,128)(2,1)S(1)}, u32[]{:S(2)}, u32[]{:S(2)}) async-start(bf16[64,16,512]{2,0,1:T(8,128)(2,1)} %bitcast.107), calls=%async_computation.3 | async-start | bytes 2097152 | tf_op jit(solution)/shard_map/all_to_all | solution.py:98
  54.2 16.0 %copy-start.12 = (s32[32]{0:T(128)S(1)}, s32[32]{0:T(128)}, u32[]{:S(2)}) copy-start(s32[32]{0:T(128)} %param.11) | copy-start | bytes 388
  65.3 97.4 %all-to-all-start.1 = ((bf16[128,2,8192]{0,1,2:T(2,128)(2,1)}), bf16[128,2,8192]{0,1,2:T(2,128)(2,1)}, u32[]{:S(2)}, u32[]{:S(2)}) async-start(bf16[128,2,8192]{0,1,2:T(2,128)(2,1)} %copy.148), calls=%async_computation.1 | async-start | bytes 8388608 | tf_op jit(solution)/shard_map/all_to_all | solution.py:80
  73.3 1.2 copy-start.7
  242.1 122.6 %all-to-all-start.2 = ((bf16[16,64,512]{2,1,0:T(8,128)(2,1)}), bf16[16,64,512]{2,1,0:T(8,128)(2,1)}, u32[]{:S(2)}, u32[]{:S(2)}) async-start(bf16[16,64,512]{2,1,0:T(8,128)(2,1)} %bitcast.170), calls=%async_computation.2 | async-start | bytes 2097152 | tf_op jit(solution)/shard_map/all_to_all | solution.py:97
  247.0 5.6 copy-start.2
  252.6 3.0 copy-start
  262.6 2.5 copy-start.9
  265.6 1.0 copy-start.10
  276.1 5.6 copy-start.1
  296.2 8.3 %copy-start.3 = (bf16[2,8,64,4,128]{4,2,3,1,0:T(8,128)(2,1)S(1)}, bf16[2,8,64,4,128]{4,2,3,1,0:T(8,128)(2,1)}, u32[]{:S(2)}) copy-start(bf16[2,8,64,4,128]{4,2,3,1,0:T(8,128)(2,1)} %copy-done.2) | copy-start | bytes 3145732 | tf_op jit(solution)/shard_map/while
  304.5 5.6 copy-start.2
  310.1 3.0 copy-start
  320.1 2.5 copy-start.9
  323.0 1.0 copy-start.10
  333.6 5.6 copy-start.1
  353.7 8.4 %copy-start.3 = (bf16[2,8,64,4,128]{4,2,3,1,0:T(8,128)(2,1)S(1)}, bf16[2,8,64,4,128]{4,2,3,1,0:T(8,128)(2,1)}, u32[]{:S(2)}) copy-start(bf16[2,8,64,4,128]{4,2,3,1,0:T(8,128)(2,1)} %copy-done.2) | copy-start | bytes 3145732 | tf_op jit(solution)/shard_map/while
  363.5 7.3 %copy-start.11 = (s32[16,2]{1,0:T(8,128)S(1)}, s32[16,2]{1,0:T(8,128)}, u32[]{:S(2)}) copy-start(s32[16,2]{1,0:T(8,128)} %reshape.158) | copy-start | bytes 388
  364.7 78.3 %all-to-all-start.4 = ((bf16[16,64,512]{2,1,0:T(8,128)(2,1)}), bf16[16,64,512]{2,1,0:T(8,128)(2,1)S(1)}, u32[]{:S(2)}, u32[]{:S(2)}) async-start(bf16[16,64,512]{2,1,0:T(8,128)(2,1)} %bitcast.28), calls=%async_computation.4 | async-start | bytes 2097152 | tf_op jit(solution)/shard_map/all_to_all | solution.py:118
  395.6 20.0 %copy-start.5 = (f32[16,128,512]{2,1,0:T(8,128)S(1)}, f32[16,128,512]{2,1,0:T(8,128)}, u32[]{:S(2)}) copy-start(f32[16,128,512]{2,1,0:T(8,128)} %gather_fusion.5) | copy-start | bytes 12582916
  400.0 15.7 %copy-start.4 = (f32[16,128,512]{2,1,0:T(8,128)S(1)}, f32[16,128,512]{2,1,0:T(8,128)}, u32[]{:S(2)}) copy-start(f32[16,128,512]{2,1,0:T(8,128)} %gather_fusion.4) | copy-start | bytes 12582916
  443.0 98.5 %all-to-all-start.5 = ((bf16[2048,2,512]{2,1,0:T(2,128)(2,1)}), bf16[2048,2,512]{2,1,0:T(2,128)(2,1)}, u32[]{:S(2)}, u32[]{:S(2)}) async-start(bf16[2048,2,512]{2,1,0:T(2,128)(2,1)} %pad_maximum_fusion), calls=%async_computation.5 | async-start | bytes 8388608 | tf_op jit(solution)/shard_map/all_to_all | solution.py:119
  (1 other events, 1.0 us)
where the time goes:
time: 567 us; the launch traced here: 564 us
  local copies, waits for them, and re-layouts  233 us (41%)
  waiting for transfers between devices  210 us (37%)
  matrix products  57.1 us (10%)
  starting transfers between devices  33.4 us (6%)
  other arithmetic  29.4 us (5%)
    all_to_all x1, waiting for transfers between devices, body(): lax.all_to_all(row_grads, 'fsdp', split_axis=0, concat_axis=2, tiled=True)  89.1 us
    all_to_all x1, waiting for transfers between devices, body(): lax.all_to_all(neighbours, 'fsdp', split_axis=2, concat_axis=0, tiled=True)  86.7 us
    dynamic_update_slice x12, local copies, waits for them, and re-layouts, body(): lax.map(backward_step, (query_blocks, grad_blocks, id_blocks, softmax_all...  60.7 us
    unnamed x18, local copies, waits for them, and re-layouts  29.5 us
    all_to_all x1, waiting for transfers between devices, body(): lax.all_to_all(queries, 'fsdp', split_axis=1, concat_axis=0, tiled=True)  23.8 us
    gather x4, local copies, waits for them, and re-layouts, span_keys(): value_table[chosen_rows].reshape(per_block, 2 * NTOK, local_heads, HD)  21 us
    convert_element_type x1, local copies, waits for them, and re-layouts, body(): (value_slots[first_slot] + value_slots[second_slot]).astype(jnp.bfloat16)  15.6 us
    convert_element_type x1, local copies, waits for them, and re-layouts, body(): (key_slots[first_slot] + key_slots[second_slot]).astype(jnp.bfloat16)  15.6 us
  transfers between devices with their start and end apart: 6, of which 4 were waited for; matrix products, arithmetic and copies ran while one was open for 38% of the time, Pallas kernels for 0%

commit v1 on v0

v1 whole, which is shorter than its diff:
```python
import math

import jax
import jax.numpy as jnp
from jax import lax
from jax.experimental import pallas as pl
from jax.experimental.pallas import tpu as pltpu
from jax.sharding import PartitionSpec as P

HD = 128
SPAN = 64
NTOK = 128
ROWS = 2 * SPAN + 2 * NTOK
F32 = jnp.float32
BF16 = jnp.bfloat16


def pack_kernel(q_ref, g_ref, n_ref, out_ref):
    for h in range(out_ref.shape[1]):
        cols = pl.ds(h * HD, HD)
        out_ref[0, h, :SPAN] = q_ref[:, cols]
        out_ref[0, h, SPAN : 2 * SPAN] = g_ref[:, cols]
        out_ref[0, h, 2 * SPAN :] = n_ref[:, :, cols].reshape(2 * NTOK, HD)


def pack(queries, out_grad, neighbours, devices):
    width = queries.shape[1] // devices
    heads = width // HD
    return pl.pallas_call(
        pack_kernel,
        grid=(devices,),
        in_specs=[
            pl.BlockSpec((SPAN, width), lambda i: (0, i)),
            pl.BlockSpec((SPAN, width), lambda i: (0, i)),
            pl.BlockSpec((NTOK, 2, width), lambda i: (0, 0, i)),
        ],
        out_specs=pl.BlockSpec((1, heads, ROWS, HD), lambda i: (i, 0, 0, 0)),
        out_shape=jax.ShapeDtypeStruct((devices, heads, ROWS, HD), BF16),
        name="pack",
    )(queries, out_grad, neighbours)


def unpack_kernel(in_ref, o_ref, q_ref, n_ref):
    for h in range(in_ref.shape[1]):
        cols = pl.ds(h * HD, HD)
        o_ref[:, cols] = in_ref[0, h, :SPAN]
        q_ref[:, cols] = in_ref[0, h, SPAN : 2 * SPAN]
        n_ref[:, :, cols] = in_ref[0, h, 2 * SPAN :].reshape(NTOK, 2, HD)


def unpack(packed):
    devices, heads = packed.shape[:2]
    width = heads * HD
    total = devices * width
    return pl.pallas_call(
        unpack_kernel,
        grid=(devices,),
        in_specs=[pl.BlockSpec((1, heads, ROWS, HD), lambda i: (i, 0, 0, 0))],
        out_specs=[
            pl.BlockSpec((SPAN, width), lambda i: (0, i)),
            pl.BlockSpec((SPAN, width), lambda i: (0, i)),
            pl.BlockSpec((NTOK, 2, width), lambda i: (0, 0, i)),
        ],
        out_shape=[
            jax.ShapeDtypeStruct((SPAN, total), BF16),
            jax.ShapeDtypeStruct((SPAN, total), BF16),
            jax.ShapeDtypeStruct((NTOK, 2, total), BF16),
        ],
        name="unpack",
    )(packed)


def dot(a, b, dims):
    return lax.dot_general(a, b, (dims, ((), ())), preferred_element_type=F32)


def attention_kernel(ids_ref, in_ref, out_ref, table, sums, words):
    spans = in_ref.shape[0]
    scale = 1.0 / math.sqrt(HD)
    last = lax.broadcasted_iota(jnp.int32, (SPAN, HD), 0) == SPAN - 1
    even = pl.ds(0, NTOK, stride=2)
    odd = pl.ds(1, NTOK, stride=2)

    def split(row, carry):
        words[...] = in_ref[row, 0, 2 * SPAN :].astype(F32)
        table[row, :NTOK] = words[even, :].astype(BF16)
        table[row, NTOK:] = words[odd, :].astype(BF16)
        sums[row] = jnp.zeros((2 * NTOK, HD), F32)
        return carry

    lax.fori_loop(0, spans, split, 0, unroll=2)

    def arranged(c, start):
        own = in_ref[c, 0, pl.ds(start, SPAN)].astype(F32)
        after = in_ref[lax.rem(c + 1, spans), 0, pl.ds(start, SPAN)].astype(F32)
        after = after * jnp.where(c + 1 < spans, 1.0, 0.0)
        return jnp.where(last, own, after).astype(BF16)

    def one(c, carry):
        out_before, grad_before = carry
        q = arranged(c, 0)
        g = arranged(c, SPAN)
        rows = (ids_ref[2 * c], ids_ref[2 * c + 1])
        keys = [table[r, :NTOK] for r in rows]
        values = [table[r, NTOK:] for r in rows]
        scores = [dot(q, k, ((1,), (1,))) * scale for k in keys]
        top = jnp.maximum(
            jnp.max(scores[0], -1, keepdims=True), jnp.max(scores[1], -1, keepdims=True)
        )
        powers = [jnp.exp(s - top) for s in scores]
        total = jnp.sum(powers[0], -1, keepdims=True) + jnp.sum(powers[1], -1, keepdims=True)
        inverse = 1.0 / total
        soft = [p * inverse for p in powers]
        weights = [s.astype(BF16) for s in soft]
        attended = dot(weights[0], values[0], ((1,), (0,))) + dot(
            weights[1], values[1], ((1,), (0,))
        )
        delta = jnp.sum(g.astype(F32) * attended, -1, keepdims=True)
        score_grad = [
            (s * (dot(g, v, ((1,), (1,))) - delta)).astype(BF16) for s, v in zip(soft, values)
        ]
        query_grad = (
            dot(score_grad[0], keys[0], ((1,), (0,))) + dot(score_grad[1], keys[1], ((1,), (0,)))
        ) * scale
        for r, s, w in zip(rows, score_grad, weights):
            sums[r, :NTOK] += dot(s, q, ((0,), (0,))) * scale
            sums[r, NTOK:] += dot(w, g, ((0,), (0,)))
        out_ref[c, 0, :SPAN] = jnp.where(last, attended, out_before).astype(BF16)
        out_ref[c, 0, SPAN : 2 * SPAN] = jnp.where(last, query_grad, grad_before).astype(BF16)
        return attended, query_grad

    zero = jnp.zeros((SPAN, HD), F32)
    lax.fori_loop(0, spans, one, (zero, zero), unroll=4)

    def join(row, carry):
        words[even, :] = sums[row, :NTOK]
        words[odd, :] = sums[row, NTOK:]
        out_ref[row, 0, 2 * SPAN :] = words[...].astype(BF16)
        return carry

    lax.fori_loop(0, spans, join, 0, unroll=2)


def attention(ids, packed):
    spans, heads = packed.shape[:2]
    block = pl.BlockSpec((spans, 1, ROWS, HD), lambda h, ids: (0, h, 0, 0))
    return pl.pallas_call(
        attention_kernel,
        grid_spec=pltpu.PrefetchScalarGridSpec(
            num_scalar_prefetch=1,
            grid=(heads,),
            in_specs=[block],
            out_specs=block,
            scratch_shapes=[
                pltpu.VMEM((spans, 2 * NTOK, HD), BF16),
                pltpu.VMEM((spans, 2 * NTOK, HD), F32),
                pltpu.VMEM((2 * NTOK, HD), F32),
            ],
        ),
        out_shape=jax.ShapeDtypeStruct(packed.shape, BF16),
        compiler_params=pltpu.CompilerParams(vmem_limit_bytes=56 * 2**20),
        name="attention",
    )(ids, packed)


def body(queries, out_grad, neighbours, neighbour_ids):
    devices = lax.axis_size("fsdp")
    packed = pack(queries, out_grad, neighbours, devices)
    packed = lax.all_to_all(packed, "fsdp", split_axis=0, concat_axis=0, tiled=True)
    results = attention(neighbour_ids, packed)
    results = lax.all_to_all(results, "fsdp", split_axis=0, concat_axis=0, tiled=True)
    return tuple(unpack(results))


def solution(mesh):
    in_specs = (
        P(("groups", "fsdp"), None),
        P(("groups", "fsdp"), None),
        P(("groups", "fsdp"), None, None),
        P("groups"),
    )
    out_specs = (
        P(("groups", "fsdp"), None),
        P(("groups", "fsdp"), None),
        P(("groups", "fsdp"), None, None),
    )
    return jax.shard_map(body, mesh=mesh, in_specs=in_specs, out_specs=out_specs, check_vma=False)
```

time: 567 us -> 361 us (0.64)
  blocking collectives: 0 us -> 287 us
  local copies, waits for them, and re-layouts: 233 us -> 0 us
  waiting for transfers between devices: 210 us -> 0 us
  Pallas kernels: 0 us -> 72.1 us
  matrix products: 57.1 us -> 0 us
  starting transfers between devices: 33.4 us -> 0 us
  other arithmetic: 29.4 us -> 0 us
    all_to_all x0 -> x2, blocking collectives: none -> 287 us  [the longest x1 144 us: body(): lax.all_to_all(packed, 'fsdp', split_axis=0, concat_axis=0, tiled=True)]
    all_to_all x6 -> x0, waiting for transfers between devices: 210 us -> none  [the longest x1 89.1 us: body(): lax.all_to_all(row_grads, 'fsdp', split_axis=0, concat_axis=2, tiled=True)]
    pallas_call x0 -> x3, Pallas kernels: none -> 72.1 us  [the longest x1 47.6 us: attention(): pl.pallas_call(attention_kernel, grid_spec=pltpu.PrefetchScalarGridSpec(n...]
    dynamic_update_slice x12 -> x0, local copies, waits for them, and re-layouts: 60.7 us -> none  [body(): lax.map(backward_step, (query_blocks, grad_blocks, id_blocks, softmax_all...]
    gather x12 -> x0, local copies, waits for them, and re-layouts: 60 us -> none  [the longest x4 21 us: span_keys(): value_table[chosen_rows].reshape(per_block, 2 * NTOK, local_heads, HD)]
    dot_general x12 -> x0, matrix products: 49.3 us -> none  [the longest x2 13.8 us: forward_block(): jnp.einsum('ghqk,gkhd->gqhd', weights, value_block, preferred_element_typ...]
    all_to_all x6 -> x0, starting transfers between devices: 33.4 us -> none  [the longest x1 6.55 us: body(): lax.all_to_all(queries, 'fsdp', split_axis=1, concat_axis=0, tiled=True)]
    convert_element_type x3 -> x0, local copies, waits for them, and re-layouts: 32.1 us -> none  [the longest x1 15.6 us: body(): (value_slots[first_slot] + value_slots[second_slot]).astype(jnp.bfloat16)]
  transfers between devices with their start and end apart: 6 -> 0, of which waited for: 4 -> 0; matrix products, arithmetic and copies ran while one was open for 38% -> 0% of each run, Pallas kernels for 0% -> 0%
where the time goes in v1:
time: 361 us; the launch traced here: 359 us
  blocking collectives  287 us (80%)
  Pallas kernels  72.1 us (20%)
    all_to_all x1, blocking collectives, body(): lax.all_to_all(packed, 'fsdp', split_axis=0, concat_axis=0, tiled=True)  144 us
    all_to_all x1, blocking collectives, body(): lax.all_to_all(results, 'fsdp', split_axis=0, concat_axis=0, tiled=True)  143 us
    pallas_call x1, Pallas kernels, attention(): pl.pallas_call(attention_kernel, grid_spec=pltpu.PrefetchScalarGridSpec(n...  47.6 us
    pallas_call x1, Pallas kernels, unpack(): pl.pallas_call(unpack_kernel, grid=(devices,), in_specs=[pl.BlockSpec((1,...  12.3 us
    pallas_call x1, Pallas kernels, pack(): pl.pallas_call(pack_kernel, grid=(devices,), in_specs=[pl.BlockSpec((SPAN...  12.2 us

profile of v1, /device:TPU:15, one launch (start us, length us, event | category | flops | bytes accessed | tf_op | source)
XLA Modules:
  0.0 359.3 jit_solution(14374327733976109399)
XLA Ops:
  0.6 12.2 %pack.1 = bf16[16,4,384,128]{3,2,1,0:T(8,128)(2,1)} custom-call(bf16[64,8192]{1,0:T(8,128)(2,1)} %q_ref.1, bf16[64,8192]{1,0:T(8,128)(2,1)} %g_ref.1, bf16[128,2,8192]{2,1,0:T(2,128)(2,1)} %n_ref.1), custom_call_target="tpu_custom_call" | custom-call | tf_op jit(solution)/shard_map/pack/pallas_call | solution.py:29
  12.8 143.8 %all_to_all.10.in_ref = bf16[16,4,384,128]{3,2,1,0:T(8,128)(2,1)} all-to-all(bf16[16,4,384,128]{3,2,1,0:T(8,128)(2,1)} %pack.1), channel_id=1, replica_groups=mesh['groups'=2,'fsdp'=16] {'fsdp'}, dimensions={0} | all-to-all | bytes 12582912 | tf_op jit(solution)/shard_map/all_to_all | solution.py:169
  156.7 47.6 %attention.1 = bf16[16,4,384,128]{3,2,1,0:T(8,128)(2,1)} custom-call(s32[32]{0:T(128)} %ids_ref.1, bf16[16,4,384,128]{3,2,1,0:T(8,128)(2,1)} %all_to_all.10.in_ref), custom_call_target="tpu_custom_call" | custom-call | tf_op jit(solution)/shard_map/attention/pallas_call | solution.py:147
  204.3 142.8 %all_to_all.11.in_ref = bf16[16,4,384,128]{3,2,1,0:T(8,128)(2,1)} all-to-all(bf16[16,4,384,128]{3,2,1,0:T(8,128)(2,1)} %attention.1), channel_id=1, replica_groups=mesh['groups'=2,'fsdp'=16] {'fsdp'}, dimensions={0} | all-to-all | bytes 12582912 | tf_op jit(solution)/shard_map/all_to_all | solution.py:171
  347.1 12.3 %unpack.1 = (bf16[64,8192]{1,0:T(8,128)(2,1)}, bf16[64,8192]{1,0:T(8,128)(2,1)}, bf16[128,2,8192]{2,1,0:T(2,128)(2,1)}) custom-call(bf16[16,4,384,128]{3,2,1,0:T(8,128)(2,1)} %all_to_all.11.in_ref), custom_call_target="tpu_custom_call" | custom-call | tf_op jit(solution)/shard_map/unpack/pallas_call | solution.py:55

commit v2 on v0

v2 whole, which is shorter than its diff:
```python
import math

import jax
import jax.numpy as jnp
from jax import lax
from jax.experimental import pallas as pl
from jax.experimental.pallas import tpu as pltpu
from jax.sharding import PartitionSpec as P

HD = 128
SPAN = 64
NTOK = 128
F32 = jnp.float32
BF16 = jnp.bfloat16
ANY = pl.BlockSpec(memory_space=pl.ANY)
LIMIT = pltpu.CompilerParams(vmem_limit_bytes=56 * 2**20)


def dot(a, b, dims):
    return lax.dot_general(a, b, (dims, ((), ())), preferred_element_type=F32)


NT = ((1,), (1,))
NN = ((1,), (0,))
TN = ((0,), (0,))


def pack_tokens(queries, out_grad, devices):
    half = devices // 2
    width = queries.shape[1] // half

    def kernel(q_ref, g_ref, out_ref, sem):
        copies = []
        for i in range(devices):
            cols = pl.ds(i % half * width, width)
            for part, ref in enumerate((q_ref, g_ref)):
                rows = pl.ds(part * SPAN, SPAN)
                copies.append(pltpu.make_async_copy(ref.at[:, cols], out_ref.at[i, rows], sem.at[i, part]))
        for copy in copies:
            copy.start()
        for copy in copies:
            copy.wait()

    return pl.pallas_call(
        kernel,
        in_specs=[ANY, ANY],
        out_specs=ANY,
        out_shape=jax.ShapeDtypeStruct((devices, 2 * SPAN, width), BF16),
        scratch_shapes=[pltpu.SemaphoreType.DMA((devices, 2))],
        name="pack_tokens",
    )(queries, out_grad)


def place(half, step):
    return lax.rem(lax.rem(lax.axis_index("fsdp"), half) + step, half)


def pack_rows(neighbours, devices):
    half = devices // 2
    heads = neighbours.shape[2] // HD // half

    def kernel(n_ref, *refs):
        outs, sem = refs[:-1], refs[-1]
        copies = []
        for step, out in enumerate(outs):
            for h in range(heads):
                first = pl.multiple_of((place(half, step) * heads + h) * HD, HD)
                source = n_ref.at[:, :, pl.ds(first, HD)]
                copies.append(pltpu.make_async_copy(source, out.at[h], sem.at[step, h]))
        for copy in copies:
            copy.start()
        for copy in copies:
            copy.wait()

    shape = jax.ShapeDtypeStruct((heads, NTOK, 2, HD), BF16)
    return pl.pallas_call(
        kernel,
        in_specs=[ANY],
        out_specs=[ANY] * half,
        out_shape=[shape] * half,
        scratch_shapes=[pltpu.SemaphoreType.DMA((half, heads))],
        name="pack_rows",
    )(neighbours)


def unpack(tokens, rows, devices):
    half = devices // 2
    heads = rows[0].shape[0]
    width = heads * HD

    def kernel(t_ref, *refs):
        ins, (o_ref, q_ref, n_ref), sem = refs[:half], refs[half:-1], refs[-1]
        copies = []
        for step, ref in enumerate(ins):
            for h in range(heads):
                first = pl.multiple_of((place(half, -step + half) * heads + h) * HD, HD)
                target = n_ref.at[:, :, pl.ds(first, HD)]
                copies.append(pltpu.make_async_copy(ref.at[h], target, sem.at[step, h]))
        for copy in copies:
            copy.start()
        for i in range(half):
            cols = pl.ds(i * width, width)
            for part, out in enumerate((o_ref, q_ref)):
                some = pl.ds(part * SPAN, SPAN)
                total = t_ref[i, some].astype(F32) + t_ref[half + i, some].astype(F32)
                out[:, cols] = total.astype(BF16)
        for copy in copies:
            copy.wait()

    vmem = pl.BlockSpec(memory_space=pltpu.VMEM)
    tokens_out = jax.ShapeDtypeStruct((SPAN, half * width), BF16)
    return pl.pallas_call(
        kernel,
        in_specs=[vmem] + [ANY] * half,
        out_specs=[vmem, vmem, ANY],
        out_shape=[
            tokens_out,
            tokens_out,
            jax.ShapeDtypeStruct((NTOK, 2, half * width), BF16),
        ],
        scratch_shapes=[pltpu.SemaphoreType.DMA((half, heads))],
        compiler_params=LIMIT,
        name="unpack",
    )(tokens, *rows)


def last_rows():
    rows = lax.broadcasted_iota(jnp.int32, (2 * SPAN, HD), 0)
    return lax.rem(rows, SPAN) == SPAN - 1


def arrange(t_ref, spans_ref):
    devices = t_ref.shape[0]
    last = last_rows()
    for c in range(devices):
        own = t_ref[c].astype(F32)
        after = t_ref[c + 1].astype(F32) if c + 1 < devices else jnp.zeros_like(own)
        spans_ref[c] = jnp.where(last, own, after).astype(BF16)


def load_row(n_ref, words):
    words[...] = n_ref[0].astype(F32)
    keys = words[pl.ds(0, NTOK, stride=2), :].astype(BF16)
    values = words[pl.ds(1, NTOK, stride=2), :].astype(BF16)
    return keys, values


def pair(spans_ref, first, second, part):
    rows = pl.ds(part * SPAN, SPAN)
    return jnp.concatenate([spans_ref[first // 2, rows], spans_ref[second // 2, rows]], 0)


def slots_of(slots_ref, half, step):
    base = lax.axis_index("fsdp") // half * half
    local = place(half, step)
    return local, slots_ref[2 * (base + local)], slots_ref[2 * (base + local) + 1]


def products(keys, values, queries, grads):
    scores = dot(keys, queries, NT) * (1.0 / math.sqrt(HD))
    return scores, dot(values, grads, NT)


def stats_kernel(slots_ref, t_ref, *refs):
    half = t_ref.shape[0] // 2
    rows, out_ref, spans_ref, words = refs[:half], refs[half], refs[half + 1], refs[half + 2]
    arrange(t_ref, spans_ref)
    for step in range(half):
        local, first, second = slots_of(slots_ref, half, step)
        keys, values = load_row(rows[step], words.at[step % 4])
        queries = pair(spans_ref, first, second, 0)
        grads = pair(spans_ref, first, second, 1)
        scores, prob_grad = products(keys, values, queries, grads)
        top = jnp.max(scores, 0, keepdims=True)
        power = jnp.exp(scores - top)
        out_ref[0, 0, pl.ds(local, 1)] = top
        out_ref[0, 1, pl.ds(local, 1)] = jnp.sum(power, 0, keepdims=True)
        out_ref[0, 2, pl.ds(local, 1)] = jnp.sum(power * prob_grad, 0, keepdims=True)


def in_blocks(devices, heads):
    half = devices // 2
    tokens = pl.BlockSpec((devices, 2 * SPAN, HD), lambda h, slots: (0, 0, h))
    row = pl.BlockSpec((1, 2 * NTOK, HD), lambda h, slots: (h, 0, 0))
    return tokens, [row] * half


def row_stats(slots, tokens, rows):
    devices = tokens.shape[0]
    half = devices // 2
    heads = rows[0].shape[0]
    token_block, row_blocks = in_blocks(devices, heads)
    return pl.pallas_call(
        stats_kernel,
        grid_spec=pltpu.PrefetchScalarGridSpec(
            num_scalar_prefetch=1,
            grid=(heads,),
            in_specs=[token_block] + row_blocks,
            out_specs=pl.BlockSpec((1, 3, half, HD), lambda h, slots: (h, 0, 0, 0)),
            scratch_shapes=[
                pltpu.VMEM((devices, 2 * SPAN, HD), BF16),
                pltpu.VMEM((4, 2 * NTOK, HD), F32),
            ],
        ),
        out_shape=jax.ShapeDtypeStruct((heads, 3, half, HD), F32),
        compiler_params=LIMIT,
        name="row_stats",
    )(slots, tokens, *rows)


def grads_kernel(slots_ref, t_ref, *refs):
    devices = t_ref.shape[0]
    half = devices // 2
    rows, refs = refs[:half], refs[half:]
    own_ref, other_ref, out_ref = refs[:3]
    row_outs, refs = refs[3 : 3 + half], refs[3 + half :]
    spans_ref, words, by_slot, sums = refs
    scale = 1.0 / math.sqrt(HD)
    arrange(t_ref, spans_ref)
    sums[...] = jnp.zeros_like(sums)
    base = lax.axis_index("fsdp") // half * half
    left = lax.broadcasted_iota(jnp.int32, (1, HD), 1) < SPAN
    for ref, start in ((own_ref, base), (other_ref, half - base)):
        for i in range(3):
            block = ref[0, i]
            turned = pltpu.roll(block, SPAN, 1)
            firsts = jnp.where(left, block, turned)
            seconds = jnp.where(left, turned, block)
            for r in range(half):
                by_slot[i, pl.ds(slots_ref[2 * (start + r)], 1)] = firsts[r : r + 1]
                by_slot[i, pl.ds(slots_ref[2 * (start + r) + 1], 1)] = seconds[r : r + 1]

    def spread(first, second):
        def mate(slot):
            return slot + 1 - 2 * lax.rem(slot, 2)

        own = [jnp.where(left, by_slot[i, pl.ds(first, 1)], by_slot[i, pl.ds(second, 1)]) for i in range(3)]
        first, second = mate(first), mate(second)
        other = [jnp.where(left, by_slot[i, pl.ds(first, 1)], by_slot[i, pl.ds(second, 1)]) for i in range(3)]
        top = jnp.maximum(own[0], other[0])
        here, there = jnp.exp(own[0] - top), jnp.exp(other[0] - top)
        inverse = 1.0 / (own[1] * here + other[1] * there)
        return top, inverse, (own[2] * here + other[2] * there) * inverse

    for step in range(half):
        _, first, second = slots_of(slots_ref, half, step)
        keys, values = load_row(rows[step], words.at[step % 4])
        queries = pair(spans_ref, first, second, 0)
        grads = pair(spans_ref, first, second, 1)
        scores, prob_grad = products(keys, values, queries, grads)
        top, inverse, delta = spread(first, second)
        soft = jnp.exp(scores - top) * inverse
        weights = soft.astype(BF16)
        score_grad = (soft * (prob_grad - delta)).astype(BF16)
        joined = words.at[4 + step % 4]
        joined[pl.ds(0, NTOK, stride=2), :] = dot(score_grad, queries, NN) * scale
        joined[pl.ds(1, NTOK, stride=2), :] = dot(weights, grads, NN)
        row_outs[step][0] = joined[...].astype(BF16)
        attended = dot(weights, values, TN)
        query_grad = dot(score_grad, keys, TN) * scale
        for n, slot in enumerate((first, second)):
            piece = slice(n * SPAN, (n + 1) * SPAN)
            sums[slot // 2 + 1, :SPAN] += attended[piece]
            sums[slot // 2 + 1, SPAN:] += query_grad[piece]
    last = last_rows()
    for d in range(devices):
        out_ref[d] = jnp.where(last, sums[d + 1], sums[d]).astype(BF16)


def grads(slots, tokens, rows, own, other):
    devices = tokens.shape[0]
    half = devices // 2
    heads = rows[0].shape[0]
    token_block, row_blocks = in_blocks(devices, heads)
    stats_block = pl.BlockSpec((1, 3, half, HD), lambda h, slots: (h, 0, 0, 0))
    results = pl.pallas_call(
        grads_kernel,
        grid_spec=pltpu.PrefetchScalarGridSpec(
            num_scalar_prefetch=1,
            grid=(heads,),
            in_specs=[token_block] + row_blocks + [stats_block, stats_block],
            out_specs=[token_block] + row_blocks,
            scratch_shapes=[
                pltpu.VMEM((devices, 2 * SPAN, HD), BF16),
                pltpu.VMEM((8, 2 * NTOK, HD), F32),
                pltpu.VMEM((3, 2 * devices, HD), F32),
                pltpu.VMEM((devices + 1, 2 * SPAN, HD), F32),
            ],
        ),
        out_shape=[jax.ShapeDtypeStruct(tokens.shape, BF16)]
        + [jax.ShapeDtypeStruct(rows[0].shape, BF16)] * half,
        compiler_params=LIMIT,
        name="grads",
    )(slots, tokens, *rows, own, other)
    return results[0], results[1:]


def shifted(devices, step):
    half = devices // 2
    return [(b * half + j, b * half + (j + step) % half) for b in range(2) for j in range(half)]


def body(queries, out_grad, neighbours, neighbour_ids):
    devices = lax.axis_size("fsdp")
    half = devices // 2
    slots = jnp.argsort(neighbour_ids, stable=True).astype(jnp.int32)
    tokens = pack_tokens(queries, out_grad, devices)
    tokens = lax.all_to_all(tokens, "fsdp", split_axis=0, concat_axis=0, tiled=True)
    sent = pack_rows(neighbours, devices)
    rows = [sent[0]] + [lax.ppermute(sent[k], "fsdp", shifted(devices, k)) for k in range(1, half)]
    rows = [rows[0]] + [rows[half - k] for k in range(1, half)]
    rows = [row.reshape(-1, 2 * NTOK, HD) for row in rows]
    own = row_stats(slots, tokens, rows)
    across = [(i, (i + half) % devices) for i in range(devices)]
    other = lax.ppermute(own, "fsdp", across)
    token_grads, row_grads = grads(slots, tokens, rows, own, other)
    token_grads = lax.all_to_all(token_grads, "fsdp", split_axis=0, concat_axis=0, tiled=True)
    row_grads = [row.reshape(-1, NTOK, 2, HD) for row in row_grads]
    back = [row_grads[0]] + [
        lax.ppermute(row_grads[k], "fsdp", shifted(devices, k)) for k in range(1, half)
    ]
    return tuple(unpack(token_grads, back, devices))


def solution(mesh):
    in_specs = (
        P(("groups", "fsdp"), None),
        P(("groups", "fsdp"), None),
        P(("groups", "fsdp"), None, None),
        P("groups"),
    )
    out_specs = (
        P(("groups", "fsdp"), None),
        P(("groups", "fsdp"), None),
        P(("groups", "fsdp"), None, None),
    )
    return jax.shard_map(body, mesh=mesh, in_specs=in_specs, out_specs=out_specs, check_vma=False)
```

time: 567 us -> 613 us (1.081)
  Pallas kernels: 0 us -> 420 us
  local copies, waits for them, and re-layouts: 233 us -> 1.61 us
  waiting for transfers between devices: 210 us -> 150 us
  matrix products: 57.1 us -> 0 us
  other arithmetic: 29.4 us -> 1.63 us
    pallas_call x0 -> x5, Pallas kernels: none -> 420 us  [the longest x1 132 us: unpack(): pl.pallas_call(kernel, in_specs=[vmem] + [ANY] * half, out_specs=[vmem, v...]
    all_to_all x6 -> x2, waiting for transfers between devices: 210 us -> 0.01 us  [the longest x1 0.01 us: body(): lax.all_to_all(token_grads, 'fsdp', split_axis=0, concat_axis=0, tiled=True)]
    ppermute x0 -> x15, waiting for transfers between devices: none -> 150 us  [the longest x7 116 us: body(): lax.ppermute(row_grads[k], 'fsdp', shifted(devices, k))]
    dynamic_update_slice x12 -> x0, local copies, waits for them, and re-layouts: 60.7 us -> none  [body(): lax.map(backward_step, (query_blocks, grad_blocks, id_blocks, softmax_all...]
    gather x12 -> x0, local copies, waits for them, and re-layouts: 60 us -> none  [the longest x4 21 us: span_keys(): value_table[chosen_rows].reshape(per_block, 2 * NTOK, local_heads, HD)]
    dot_general x12 -> x0, matrix products: 49.3 us -> none  [the longest x2 13.8 us: forward_block(): jnp.einsum('ghqk,gkhd->gqhd', weights, value_block, preferred_element_typ...]
    convert_element_type x3 -> x0, local copies, waits for them, and re-layouts: 32.1 us -> none  [the longest x1 15.6 us: body(): (value_slots[first_slot] + value_slots[second_slot]).astype(jnp.bfloat16)]
    all_to_all x8 -> x0, local copies, waits for them, and re-layouts: 28.8 us -> none  [the longest x2 11.1 us: body(): lax.all_to_all(row_grads, 'fsdp', split_axis=0, concat_axis=2, tiled=True)]
  transfers between devices with their start and end apart: 6 -> 17, of which waited for: 4 -> 10; matrix products, arithmetic and copies ran while one was open for 38% -> 0% of each run, Pallas kernels for 0% -> 21%
where the time goes in v2:
time: 613 us
  Pallas kernels  420 us (69%)
  waiting for transfers between devices  150 us (24%)
  starting transfers between devices  38.5 us (6%)
    pallas_call x1, Pallas kernels, unpack(): pl.pallas_call(kernel, in_specs=[vmem] + [ANY] * half, out_specs=[vmem, v...  132 us
    pallas_call x1, Pallas kernels, pack_rows(): pl.pallas_call(kernel, in_specs=[ANY], out_specs=[ANY] * half, out_shape=...  129 us
    pallas_call x1, Pallas kernels, pack_tokens(): pl.pallas_call(kernel, in_specs=[ANY, ANY], out_specs=ANY, out_shape=jax....  128 us
    ppermute x7, waiting for transfers between devices, body(): lax.ppermute(row_grads[k], 'fsdp', shifted(devices, k))  116 us
    ppermute x7, waiting for transfers between devices, body(): lax.ppermute(sent[k], 'fsdp', shifted(devices, k))  31.8 us
    pallas_call x1, Pallas kernels, grads(): pl.pallas_call(grads_kernel, grid_spec=pltpu.PrefetchScalarGridSpec(num_s...  21.3 us
    ppermute x7, starting transfers between devices, body(): lax.ppermute(sent[k], 'fsdp', shifted(devices, k))  14.7 us
  transfers between devices with their start and end apart: 17, of which 10 were waited for; matrix products, arithmetic and copies ran while one was open for 0% of the time, Pallas kernels for 21%

profile of v2, /device:TPU:15, one launch (start us, length us, event | category | flops | bytes accessed | tf_op | source)
XLA Modules:
  0.0 612.7 jit_solution(8157486385571497259)
XLA Ops:
  0.6 128.4 %pack_tokens.1 = bf16[16,128,1024]{2,1,0:T(8,128)(2,1)} custom-call(bf16[64,8192]{1,0:T(8,128)(2,1)} %q_ref.1, bf16[64,8192]{1,0:T(8,128)(2,1)} %g_ref.1), custom_call_target="tpu_custom_call" | custom-call | tf_op jit(solution)/shard_map/pack_tokens/pallas_call | solution.py:44
  129.1 6.6 %all-to-all-start = ((bf16[16,128,1024]{2,1,0:T(8,128)(2,1)}), bf16[16,128,1024]{2,1,0:T(8,128)(2,1)}, u32[]{:S(2)}, u32[]{:S(2)}) async-start(bf16[16,128,1024]{2,1,0:T(8,128)(2,1)} %pack_tokens.1), calls=%async_computation | async-start | bytes 8388608 | tf_op jit(solution)/shard_map/all_to_all | solution.py:308
  135.7 128.7 %pack_rows.1 = (bf16[8,128,2,128]{3,2,1,0:T(2,128)(2,1)}, bf16[8,128,2,128]{3,2,1,0:T(2,128)(2,1)}, bf16[8,128,2,128]{3,2,1,0:T(2,128)(2,1)}, bf16[8,128,2,128]{...) custom-call(bf16[128,2,8192]{2,1,0:T(2,128)(2,1)} %n_ref.1), custom_call_target="tpu_custom_call" | custom-call | tf_op jit(solution)/shard_map/pack_rows/pallas_call | solution.py:76
  265.1 1.5 collective-permute-start.2
  266.6 1.4 collective-permute-start.3
  268.2 11.9 %collective-permute-done = bf16[8,128,2,128]{3,2,1,0:T(2,128)(2,1)S(1)} collective-permute-done((bf16[8,128,2,128]{3,2,1,0:T(2,128)(2,1)}, bf16[8,128,2,128]{3,2,1,0:T(2,128)(2,1)S(1)}, u32[]{:S(2)}, u32[]{:S(2)}) %collective-permute-start) | collective-permute-done | bytes 524320 | tf_op jit(solution)/shard_map/ppermute | solution.py:310
  280.2 10.9 %collective-permute-start.6 = (bf16[8,128,2,128]{3,2,1,0:T(2,128)(2,1)}, bf16[8,128,2,128]{3,2,1,0:T(2,128)(2,1)}, u32[]{:S(2)}, u32[]{:S(2)}) collective-permute-start(bf16[8,128,2,128]{3,2,1,0:T(2,128)(2,1)} %get-tuple-element.29), channel_id=1, source_target_pairs={{0,1},{1,2},{2,3},{3,4},{4,5},{5,6},{6,7},{7,0},{8,9},{9,10},{10,1... | collective-permute-start | bytes 1572872 | tf_op jit(solution)/shard_map/ppermute | solution.py:310
  291.0 1.6 sort.17
  292.7 9.3 %collective-permute-done.4 = bf16[8,128,2,128]{3,2,1,0:T(2,128)(2,1)S(1)} collective-permute-done((bf16[8,128,2,128]{3,2,1,0:T(2,128)(2,1)}, bf16[8,128,2,128]{3,2,1,0:T(2,128)(2,1)S(1)}, u32[]{:S(2)}, u32[]{:S(2)}) %collective-permute-start.4) | collective-permute-done | bytes 524320 | tf_op jit(solution)/shard_map/ppermute | solution.py:310
  302.5 10.0 %collective-permute-done.6 = bf16[8,128,2,128]{3,2,1,0:T(2,128)(2,1)} collective-permute-done((bf16[8,128,2,128]{3,2,1,0:T(2,128)(2,1)}, bf16[8,128,2,128]{3,2,1,0:T(2,128)(2,1)}, u32[]{:S(2)}, u32[]{:S(2)}) %collective-permute-start.6) | collective-permute-done | bytes 524320 | tf_op jit(solution)/shard_map/ppermute | solution.py:310
  312.6 9.4 %row_stats.1.refs_8_ = f32[8,3,8,128]{3,2,1,0:T(8,128)} custom-call(s32[32]{0:T(128)} %get-tuple-element.21.slots_ref, bf16[16,128,1024]{2,1,0:T(8,128)(2,1)} %all-to-all-done.t_ref, bf16[8,256,128]{2,1,0:T(8,128)(2,1)} %bitcast.16, bf16[8,256,128]{2,1,0:T(8,128)(2,1)} %bitcast.18, bf16[8,256,128]{2,1,0:T(8,128)(2,1)} %bitcast.20, ...), custom_call_target="tpu_custom_call" | custom-call | tf_op jit(solution)/shard_map/row_stats/pallas_call | solution.py:193
  322.0 2.1 collective-permute-start.7
  324.1 2.6 collective-permute-done.7.refs_9_
  326.7 0.6 copy-done.12
  327.3 21.3 %grads.1 = (bf16[16,128,1024]{2,1,0:T(8,128)(2,1)}, bf16[8,256,128]{2,1,0:T(8,128)(2,1)}, bf16[8,256,128]{2,1,0:T(8,128)(2,1)}, bf16[8,256,128]{2,1,0:T(8,128)(2...) custom-call(s32[32]{0:T(128)} %get-tuple-element.21.slots_ref, ...), custom_call_target="tpu_custom_call" | custom-call | tf_op jit(solution)/shard_map/grads/pallas_call | solution.py:276
  348.7 10.2 %all-to-all-start.1 = ((bf16[16,128,1024]{2,1,0:T(8,128)(2,1)}), bf16[16,128,1024]{2,1,0:T(8,128)(2,1)}, u32[]{:S(2)}, u32[]{:S(2)}) async-start(bf16[16,128,1024]{2,1,0:T(8,128)(2,1)} %get-tuple-element.30), calls=%async_computation.1 | async-start | bytes 8388608 | tf_op jit(solution)/shard_map/all_to_all | solution.py:317
  359.1 1.6 collective-permute-start.9
  361.1 0.8 collective-permute-start.11
  361.8 2.0 collective-permute-start.12
  363.9 57.2 %collective-permute-done.8.refs_1_ = bf16[8,128,2,128]{3,2,1,0:T(2,128)(2,1)S(1)} collective-permute-done((bf16[8,128,2,128]{3,2,1,0:T(2,128)(2,1)S(1)}, bf16[8,128,2,128]{3,2,1,0:T(2,128)(2,1)S(1)}, u32[]{:S(2)}, u32[]{:S(2)}) %collective-permute-start.8) | collective-permute-done | bytes 524320 | tf_op jit(solution)/shard_map/ppermute | solution.py:320
  421.1 28.3 %collective-permute-done.9.refs_2_ = bf16[8,128,2,128]{3,2,1,0:T(2,128)(2,1)S(1)} collective-permute-done((bf16[8,128,2,128]{3,2,1,0:T(2,128)(2,1)}, bf16[8,128,2,128]{3,2,1,0:T(2,128)(2,1)S(1)}, u32[]{:S(2)}, u32[]{:S(2)}) %collective-permute-start.9) | collective-permute-done | bytes 524320 | tf_op jit(solution)/shard_map/ppermute | solution.py:320
  449.3 11.2 %collective-permute-done.10.refs_3_ = bf16[8,128,2,128]{3,2,1,0:T(2,128)(2,1)S(1)} collective-permute-done((bf16[8,128,2,128]{3,2,1,0:T(2,128)(2,1)}, bf16[8,128,2,128]{3,2,1,0:T(2,128)(2,1)S(1)}, u32[]{:S(2)}, u32[]{:S(2)}) %collective-permute-start.10) | collective-permute-done | bytes 524320 | tf_op jit(solution)/shard_map/ppermute | solution.py:320
  460.6 18.5 %collective-permute-done.11.refs_4_ = bf16[8,128,2,128]{3,2,1,0:T(2,128)(2,1)S(1)} collective-permute-done((bf16[8,128,2,128]{3,2,1,0:T(2,128)(2,1)}, bf16[8,128,2,128]{3,2,1,0:T(2,128)(2,1)S(1)}, u32[]{:S(2)}, u32[]{:S(2)}) %collective-permute-start.11) | collective-permute-done | bytes 524320 | tf_op jit(solution)/shard_map/ppermute | solution.py:320
  480.5 132.2 %unpack.1 = (bf16[64,8192]{1,0:T(8,128)(2,1)}, bf16[64,8192]{1,0:T(8,128)(2,1)}, bf16[128,2,8192]{2,1,0:T(2,128)(2,1)}) custom-call(bf16[16,128,1024]{2,1,0:T(8,128)(2,1)} %all-to-all-done.1.t_ref, bf16[8,128,2,128]{3,2,1,0:T(2,128)(2,1)} %bitcast.30, bf16[8,128,2,128]{3,2,1,0:T(2,128)(2,1)} %copy-done.6, bf16[8,128,2,128]{3,2,1,0:T(2,128)(2,1)} %copy-done.7, ...), custom_call_target="tpu_custom_call" | custom-call | tf_op jit(solution)/shard_map/unpack/pallas_call | solution.py:112
  (47 shorter events, 3.6 us)
Async XLA Ops:
  129.1 183.5 %all-to-all-start = ((bf16[16,128,1024]{2,1,0:T(8,128)(2,1)}), bf16[16,128,1024]{2,1,0:T(8,128)(2,1)}, u32[]{:S(2)}, u32[]{:S(2)}) async-start(bf16[16,128,1024]{2,1,0:T(8,128)(2,1)} %pack_tokens.1), calls=%async_computation | async-start | bytes 8388608 | tf_op jit(solution)/shard_map/all_to_all | solution.py:308
  135.7 155.4 %copy-start.14 = (s32[32]{0:T(128)S(1)}, s32[32]{0:T(128)}, u32[]{:S(2)}) copy-start(s32[32]{0:T(128)} %param.7) | copy-start | bytes 388
  264.4 15.7 %collective-permute-start = (bf16[8,128,2,128]{3,2,1,0:T(2,128)(2,1)}, bf16[8,128,2,128]{3,2,1,0:T(2,128)(2,1)S(1)}, u32[]{:S(2)}, u32[]{:S(2)}) collective-permute-start(bf16[8,128,2,128]{3,2,1,0:T(2,128)(2,1)} %get-tuple-element.23), channel_id=1, source_target_pairs={{0,7},{1,0},{2,1},{3,2},{4,3},{5,4},{6,5},{7,6},{8,15},{9,8},{10,9... | collective-permute-start | bytes 1572872 | tf_op jit(solution)/shard_map/ppermute | solution.py:310
  264.8 15.3 %collective-permute-start.1 = (bf16[8,128,2,128]{3,2,1,0:T(2,128)(2,1)}, bf16[8,128,2,128]{3,2,1,0:T(2,128)(2,1)S(1)}, u32[]{:S(2)}, u32[]{:S(2)}) collective-permute-start(bf16[8,128,2,128]{3,2,1,0:T(2,128)(2,1)} %get-tuple-element.24), channel_id=1, source_target_pairs={{0,6},{1,7},{2,0},{3,1},{4,2},{5,3},{6,4},{7,5},{8,14},{9,15},{10,... | collective-permute-start | bytes 1572872 | tf_op jit(solution)/shard_map/ppermute | solution.py:310
  265.1 27.6 %collective-permute-start.2 = (bf16[8,128,2,128]{3,2,1,0:T(2,128)(2,1)}, bf16[8,128,2,128]{3,2,1,0:T(2,128)(2,1)S(1)}, u32[]{:S(2)}, u32[]{:S(2)}) collective-permute-start(bf16[8,128,2,128]{3,2,1,0:T(2,128)(2,1)} %get-tuple-element.25), channel_id=1, source_target_pairs={{0,5},{1,6},{2,7},{3,0},{4,1},{5,2},{6,3},{7,4},{8,13},{9,14},{10,... | collective-permute-start | bytes 1572872 | tf_op jit(solution)/shard_map/ppermute | solution.py:310
  266.6 26.1 %collective-permute-start.3 = (bf16[8,128,2,128]{3,2,1,0:T(2,128)(2,1)}, bf16[8,128,2,128]{3,2,1,0:T(2,128)(2,1)S(1)}, u32[]{:S(2)}, u32[]{:S(2)}) collective-permute-start(bf16[8,128,2,128]{3,2,1,0:T(2,128)(2,1)} %get-tuple-element.26), channel_id=1, source_target_pairs={{0,4},{1,5},{2,6},{3,7},{4,0},{5,1},{6,2},{7,3},{8,12},{9,13},{10,... | collective-permute-start | bytes 1572872 | tf_op jit(solution)/shard_map/ppermute | solution.py:310
  268.0 34.0 %collective-permute-start.4 = (bf16[8,128,2,128]{3,2,1,0:T(2,128)(2,1)}, bf16[8,128,2,128]{3,2,1,0:T(2,128)(2,1)S(1)}, u32[]{:S(2)}, u32[]{:S(2)}) collective-permute-start(bf16[8,128,2,128]{3,2,1,0:T(2,128)(2,1)} %get-tuple-element.27), channel_id=1, source_target_pairs={{0,3},{1,4},{2,5},{3,6},{4,7},{5,0},{6,1},{7,2},{8,11},{9,12},{10,... | collective-permute-start | bytes 1572872 | tf_op jit(solution)/shard_map/ppermute | solution.py:310
  280.1 32.4 %copy-start = (bf16[8,128,2,128]{3,2,1,0:T(2,128)(2,1)}, bf16[8,128,2,128]{3,2,1,0:T(2,128)(2,1)S(1)}, u32[]{:S(2)}) copy-start(bf16[8,128,2,128]{3,2,1,0:T(2,128)(2,1)S(1)} %collective-permute-done) | copy-start | bytes 1572868
  280.1 22.4 %collective-permute-start.5 = (bf16[8,128,2,128]{3,2,1,0:T(2,128)(2,1)}, bf16[8,128,2,128]{3,2,1,0:T(2,128)(2,1)S(1)}, u32[]{:S(2)}, u32[]{:S(2)}) collective-permute-start(bf16[8,128,2,128]{3,2,1,0:T(2,128)(2,1)} %get-tuple-element.28), channel_id=1, source_target_pairs={{0,2},{1,3},{2,4},{3,5},{4,6},{5,7},{6,0},{7,1},{8,10},{9,11},{10,... | collective-permute-start | bytes 1572872 | tf_op jit(solution)/shard_map/ppermute | solution.py:310
  280.1 32.4 %copy-start.1 = (bf16[8,128,2,128]{3,2,1,0:T(2,128)(2,1)}, bf16[8,128,2,128]{3,2,1,0:T(2,128)(2,1)S(1)}, u32[]{:S(2)}) copy-start(bf16[8,128,2,128]{3,2,1,0:T(2,128)(2,1)S(1)} %collective-permute-done.1) | copy-start | bytes 1572868
  280.2 32.4 %collective-permute-start.6 = (bf16[8,128,2,128]{3,2,1,0:T(2,128)(2,1)}, bf16[8,128,2,128]{3,2,1,0:T(2,128)(2,1)}, u32[]{:S(2)}, u32[]{:S(2)}) collective-permute-start(bf16[8,128,2,128]{3,2,1,0:T(2,128)(2,1)} %get-tuple-element.29), channel_id=1, source_target_pairs={{0,1},{1,2},{2,3},{3,4},{4,5},{5,6},{6,7},{7,0},{8,9},{9,10},{10,1... | collective-permute-start | bytes 1572872 | tf_op jit(solution)/shard_map/ppermute | solution.py:310
  292.7 19.9 %copy-start.2 = (bf16[8,128,2,128]{3,2,1,0:T(2,128)(2,1)}, bf16[8,128,2,128]{3,2,1,0:T(2,128)(2,1)S(1)}, u32[]{:S(2)}) copy-start(bf16[8,128,2,128]{3,2,1,0:T(2,128)(2,1)S(1)} %collective-permute-done.2) | copy-start | bytes 1572868
  292.7 19.9 %copy-start.3 = (bf16[8,128,2,128]{3,2,1,0:T(2,128)(2,1)}, bf16[8,128,2,128]{3,2,1,0:T(2,128)(2,1)S(1)}, u32[]{:S(2)}) copy-start(bf16[8,128,2,128]{3,2,1,0:T(2,128)(2,1)S(1)} %collective-permute-done.3) | copy-start | bytes 1572868
  322.0 4.7 collective-permute-start.7
  348.7 130.9 %all-to-all-start.1 = ((bf16[16,128,1024]{2,1,0:T(8,128)(2,1)}), bf16[16,128,1024]{2,1,0:T(8,128)(2,1)}, u32[]{:S(2)}, u32[]{:S(2)}) async-start(bf16[16,128,1024]{2,1,0:T(8,128)(2,1)} %get-tuple-element.30), calls=%async_computation.1 | async-start | bytes 8388608 | tf_op jit(solution)/shard_map/all_to_all | solution.py:317
  358.9 62.2 %collective-permute-start.8 = (bf16[8,128,2,128]{3,2,1,0:T(2,128)(2,1)S(1)}, bf16[8,128,2,128]{3,2,1,0:T(2,128)(2,1)S(1)}, u32[]{:S(2)}, u32[]{:S(2)}) collective-permute-start(bf16[8,128,2,128]{3,2,1,0:T(2,128)(2,1)S(1)} %bitcast.33), channel_id=1, source_target_pairs={{0,1},{1,2},{2,3},{3,4},{4,5},{5,6},{6,7},{7,0},{8,9},{9,10},{10,1... | collective-permute-start | bytes 1572872 | tf_op jit(solution)/shard_map/ppermute | solution.py:320
  359.1 90.3 %collective-permute-start.9 = (bf16[8,128,2,128]{3,2,1,0:T(2,128)(2,1)}, bf16[8,128,2,128]{3,2,1,0:T(2,128)(2,1)S(1)}, u32[]{:S(2)}, u32[]{:S(2)}) collective-permute-start(bf16[8,128,2,128]{3,2,1,0:T(2,128)(2,1)} %bitcast.10), channel_id=1, source_target_pairs={{0,2},{1,3},{2,4},{3,5},{4,6},{5,7},{6,0},{7,1},{8,10},{9,11},{10,... | collective-permute-start | bytes 1572872 | tf_op jit(solution)/shard_map/ppermute | solution.py:320
  360.7 99.9 %collective-permute-start.10 = (bf16[8,128,2,128]{3,2,1,0:T(2,128)(2,1)}, bf16[8,128,2,128]{3,2,1,0:T(2,128)(2,1)S(1)}, u32[]{:S(2)}, u32[]{:S(2)}) collective-permute-start(bf16[8,128,2,128]{3,2,1,0:T(2,128)(2,1)} %bitcast.11), channel_id=1, source_target_pairs={{0,3},{1,4},{2,5},{3,6},{4,7},{5,0},{6,1},{7,2},{8,11},{9,12},{10,... | collective-permute-start | bytes 1572872 | tf_op jit(solution)/shard_map/ppermute | solution.py:320
  361.1 118.0 %collective-permute-start.11 = (bf16[8,128,2,128]{3,2,1,0:T(2,128)(2,1)}, bf16[8,128,2,128]{3,2,1,0:T(2,128)(2,1)S(1)}, u32[]{:S(2)}, u32[]{:S(2)}) collective-permute-start(bf16[8,128,2,128]{3,2,1,0:T(2,128)(2,1)} %bitcast.12), channel_id=1, source_target_pairs={{0,4},{1,5},{2,6},{3,7},{4,0},{5,1},{6,2},{7,3},{8,12},{9,13},{10,... | collective-permute-start | bytes 1572872 | tf_op jit(solution)/shard_map/ppermute | solution.py:320
  361.8 117.7 %collective-permute-start.12 = (bf16[8,128,2,128]{3,2,1,0:T(2,128)(2,1)}, bf16[8,128,2,128]{3,2,1,0:T(2,128)(2,1)S(1)}, u32[]{:S(2)}, u32[]{:S(2)}) collective-permute-start(bf16[8,128,2,128]{3,2,1,0:T(2,128)(2,1)} %bitcast.13), channel_id=1, source_target_pairs={{0,5},{1,6},{2,7},{3,0},{4,1},{5,2},{6,3},{7,4},{8,13},{9,14},{10,... | collective-permute-start | bytes 1572872 | tf_op jit(solution)/shard_map/ppermute | solution.py:320
  421.1 58.5 %copy-start.6 = (bf16[8,128,2,128]{3,2,1,0:T(2,128)(2,1)}, bf16[8,128,2,128]{3,2,1,0:T(2,128)(2,1)S(1)}, u32[]{:S(2)}) copy-start(bf16[8,128,2,128]{3,2,1,0:T(2,128)(2,1)S(1)} %collective-permute-done.8.refs_1_) | copy-start | bytes 1572868
  421.1 58.5 %collective-permute-start.13 = (bf16[8,128,2,128]{3,2,1,0:T(2,128)(2,1)}, bf16[8,128,2,128]{3,2,1,0:T(2,128)(2,1)S(1)}, u32[]{:S(2)}, u32[]{:S(2)}) collective-permute-start(bf16[8,128,2,128]{3,2,1,0:T(2,128)(2,1)} %bitcast.32), channel_id=1, source_target_pairs={{0,6},{1,7},{2,0},{3,1},{4,2},{5,3},{6,4},{7,5},{8,14},{9,15},{10,... | collective-permute-start | bytes 1572872 | tf_op jit(solution)/shard_map/ppermute | solution.py:320
  449.3 30.2 %copy-start.7 = (bf16[8,128,2,128]{3,2,1,0:T(2,128)(2,1)}, bf16[8,128,2,128]{3,2,1,0:T(2,128)(2,1)S(1)}, u32[]{:S(2)}) copy-start(bf16[8,128,2,128]{3,2,1,0:T(2,128)(2,1)S(1)} %collective-permute-done.9.refs_2_) | copy-start | bytes 1572868
  449.3 30.2 %collective-permute-start.14 = (bf16[8,128,2,128]{3,2,1,0:T(2,128)(2,1)}, bf16[8,128,2,128]{3,2,1,0:T(2,128)(2,1)}, u32[]{:S(2)}, u32[]{:S(2)}) collective-permute-start(bf16[8,128,2,128]{3,2,1,0:T(2,128)(2,1)} %bitcast.31), channel_id=1, source_target_pairs={{0,7},{1,0},{2,1},{3,2},{4,3},{5,4},{6,5},{7,6},{8,15},{9,8},{10,9... | collective-permute-start | bytes 1572872 | tf_op jit(solution)/shard_map/ppermute | solution.py:320
  (8 other events, 53.2 us)

commit v3 on v2

--- a/solution.py
+++ b/solution.py
@@ -10,6 +10,7 @@
 HD = 128
 SPAN = 64
 NTOK = 128
+CHUNKS = 2
 F32 = jnp.float32
 BF16 = jnp.bfloat16
 ANY = pl.BlockSpec(memory_space=pl.ANY)
@@ -25,52 +26,66 @@
 TN = ((0,), (0,))
 
 
-def pack_tokens(queries, out_grad, devices):
-    half = devices // 2
-    width = queries.shape[1] // half
-
-    def kernel(q_ref, g_ref, out_ref, sem):
-        copies = []
-        for i in range(devices):
-            cols = pl.ds(i % half * width, width)
-            for part, ref in enumerate((q_ref, g_ref)):
-                rows = pl.ds(part * SPAN, SPAN)
-                copies.append(pltpu.make_async_copy(ref.at[:, cols], out_ref.at[i, rows], sem.at[i, part]))
-        for copy in copies:
-            copy.start()
-        for copy in copies:
-            copy.wait()
-
-    return pl.pallas_call(
+def vmem(*shape):
+    return pltpu.VMEM(shape, BF16)
+
+
+def partner(half, step):
+    return lax.rem(lax.axis_index("fsdp"), half) ^ step
+
+
+def pack_tokens(queries, out_grad, devices, chunk, chunks):
+    half = devices // 2
+    width = queries.shape[1] // half // chunks
+
+    def kernel(q_ref, g_ref, out_ref):
+        for b in range(2):
+            out_ref[b, 0, :SPAN] = q_ref[...]
+            out_ref[b, 0, SPAN:] = g_ref[...]
+
+    block = pl.BlockSpec((SPAN, width), lambda i: (0, i * chunks + chunk))
+    packed = pl.pallas_call(
         kernel,
-        in_specs=[ANY, ANY],
-        out_specs=ANY,
-        out_shape=jax.ShapeDtypeStruct((devices, 2 * SPAN, width), BF16),
-        scratch_shapes=[pltpu.SemaphoreType.DMA((devices, 2))],
+        grid=(half,),
+        in_specs=[block, block],
+        out_specs=pl.BlockSpec((2, 1, 2 * SPAN, width), lambda i: (0, i, 0, 0)),
+        out_shape=jax.ShapeDtypeStruct((2, half, 2 * SPAN, width), BF16),
         name="pack_tokens",
     )(queries, out_grad)
-
-
-def place(half, step):
-    return lax.rem(lax.rem(lax.axis_index("fsdp"), half) + step, half)
-
-
-def pack_rows(neighbours, devices):
-    half = devices // 2
-    heads = neighbours.shape[2] // HD // half
+    return packed.reshape(devices, 2 * SPAN, width)
+
+
+def pack_rows(neighbours, devices, chunk, chunks):
+    half = devices // 2
+    heads = neighbours.shape[2] // HD // half // chunks
+    width = heads * HD
 
     def kernel(n_ref, *refs):
-        outs, sem = refs[:-1], refs[-1]
-        copies = []
-        for step, out in enumerate(outs):
-            for h in range(heads):
-                first = pl.multiple_of((place(half, step) * heads + h) * HD, HD)
-                source = n_ref.at[:, :, pl.ds(first, HD)]
-                copies.append(pltpu.make_async_copy(source, out.at[h], sem.at[step, h]))
-        for copy in copies:
-            copy.start()
-        for copy in copies:
-            copy.wait()
+        outs, (buffer, come, go) = refs[:half], refs[half:]
+        first = [pl.multiple_of((partner(half, k) * chunks + chunk) * width, width) for k in range(half)]
+        loads = [
+            pltpu.make_async_copy(n_ref.at[:, :, pl.ds(first[k], width)], buffer.at[k], come.at[k])
+            for k in range(half)
+        ]
+        stores = [
+            [
+                pltpu.make_async_copy(
+                    buffer.at[k, :, :, pl.ds(h * HD, HD)], outs[k].at[h], go.at[k, h]
+                )
+                for h in range(heads)
+            ]
+            for k in range(half)
+        ]
+        order = range(half - 1, -1, -1)
+        for k in order:
+            loads[k].start()
+        for k in order:
+            loads[k].wait()
+            for store in stores[k]:
+                store.start()
+        for k in order:
+            for store in stores[k]:
+                store.wait()
 
     shape = jax.ShapeDtypeStruct((heads, NTOK, 2, HD), BF16)
     return pl.pallas_call(
@@ -78,50 +93,113 @@
         in_specs=[ANY],
         out_specs=[ANY] * half,
         out_shape=[shape] * half,
-        scratch_shapes=[pltpu.SemaphoreType.DMA((half, heads))],
+        scratch_shapes=[
+            vmem(half, NTOK, 2, width),
+            pltpu.SemaphoreType.DMA((half,)),
+            pltpu.SemaphoreType.DMA((half, heads)),
+        ],
+        compiler_params=LIMIT,
         name="pack_rows",
     )(neighbours)
 
 
-def unpack(tokens, rows, devices):
-    half = devices // 2
+def unpack_tokens(tokens, before, chunk, chunks):
+    devices, _, width = tokens.shape
+    half = devices // 2
+
+    def kernel(t_ref, *refs):
+        o_ref, q_ref, ins, outs, come, go = refs[-6:]
+        loads = [
+            [pltpu.make_async_copy(t_ref.at[i + b * half], ins.at[i, b], come.at[i, b]) for b in range(2)]
+            for i in range(half)
+        ]
+        stores = [
+            [
+                pltpu.make_async_copy(
+                    outs.at[i, part], ref.at[:, pl.ds((i * chunks + chunk) * width, width)], go.at[i, part]
+                )
+                for part, ref in enumerate((o_ref, q_ref))
+            ]
+            for i in range(half)
+        ]
+        for i in range(half):
+            for load in loads[i]:
+                load.start()
+        for i in range(half):
+            for load in loads[i]:
+                load.wait()
+            for part in range(2):
+                some = pl.ds(part * SPAN, SPAN)
+                total = ins[i, 0, some].astype(F32) + ins[i, 1, some].astype(F32)
+                outs[i, part] = total.astype(BF16)
+                stores[i][part].start()
+        for i in range(half):
+            for store in stores[i]:
+                store.wait()
+
+    shape = jax.ShapeDtypeStruct((SPAN, half * width * chunks), BF16)
+    return pl.pallas_call(
+        kernel,
+        in_specs=[ANY] * (1 + len(before)),
+        out_specs=[ANY] * 2,
+        out_shape=[shape] * 2,
+        input_output_aliases={1 + i: i for i in range(len(before))},
+        scratch_shapes=[
+            vmem(half, 2, 2 * SPAN, width),
+            vmem(half, 2, SPAN, width),
+            pltpu.SemaphoreType.DMA((half, 2)),
+            pltpu.SemaphoreType.DMA((half, 2)),
+        ],
+        compiler_params=LIMIT,
+        name="unpack_tokens",
+    )(tokens, *before)
+
+
+def unpack_rows(rows, before, chunk, chunks):
+    half = len(rows)
     heads = rows[0].shape[0]
     width = heads * HD
 
-    def kernel(t_ref, *refs):
-        ins, (o_ref, q_ref, n_ref), sem = refs[:half], refs[half:-1], refs[-1]
-        copies = []
-        for step, ref in enumerate(ins):
-            for h in range(heads):
-                first = pl.multiple_of((place(half, -step + half) * heads + h) * HD, HD)
-                target = n_ref.at[:, :, pl.ds(first, HD)]
-                copies.append(pltpu.make_async_copy(ref.at[h], target, sem.at[step, h]))
-        for copy in copies:
-            copy.start()
-        for i in range(half):
-            cols = pl.ds(i * width, width)
-            for part, out in enumerate((o_ref, q_ref)):
-                some = pl.ds(part * SPAN, SPAN)
-                total = t_ref[i, some].astype(F32) + t_ref[half + i, some].astype(F32)
-                out[:, cols] = total.astype(BF16)
-        for copy in copies:
-            copy.wait()
-
-    vmem = pl.BlockSpec(memory_space=pltpu.VMEM)
-    tokens_out = jax.ShapeDtypeStruct((SPAN, half * width), BF16)
+    def kernel(*refs):
+        ins, (n_ref, buffer, come, go) = refs[:half], refs[-4:]
+        loads = [
+            [
+                pltpu.make_async_copy(
+                    ins[k].at[h], buffer.at[k, :, :, pl.ds(h * HD, HD)], come.at[k, h]
+                )
+                for h in range(heads)
+            ]
+            for k in range(half)
+        ]
+        first = [pl.multiple_of((partner(half, k) * chunks + chunk) * width, width) for k in range(half)]
+        stores = [
+            pltpu.make_async_copy(buffer.at[k], n_ref.at[:, :, pl.ds(first[k], width)], go.at[k])
+            for k in range(half)
+        ]
+        for k in range(half):
+            for load in loads[k]:
+                load.start()
+        for k in range(half):
+            for load in loads[k]:
+                load.wait()
+            stores[k].start()
+        for k in range(half):
+            stores[k].wait()
+
     return pl.pallas_call(
         kernel,
-        in_specs=[vmem] + [ANY] * half,
-        out_specs=[vmem, vmem, ANY],
-        out_shape=[
-            tokens_out,
-            tokens_out,
-            jax.ShapeDtypeStruct((NTOK, 2, half * width), BF16),
+        in_specs=[ANY] * (half + len(before)),
+        out_specs=ANY,
+        out_shape=jax.ShapeDtypeStruct((NTOK, 2, half * width * chunks), BF16),
+        input_output_aliases={half: 0} if before else {},
+        scratch_shapes=[
+            vmem(half, NTOK, 2, width),
+            pltpu.SemaphoreType.DMA((half, heads)),
+            pltpu.SemaphoreType.DMA((half,)),
         ],
-        scratch_shapes=[pltpu.SemaphoreType.DMA((half, heads))],
         compiler_params=LIMIT,
-        name="unpack",
-    )(tokens, *rows)
+        name="unpack_rows",
+    )(*rows, *before)
 
 
 def last_rows():
@@ -152,7 +230,7 @@
 
 def slots_of(slots_ref, half, step):
     base = lax.axis_index("fsdp") // half * half
-    local = place(half, step)
+    local = partner(half, step)
     return local, slots_ref[2 * (base + local)], slots_ref[2 * (base + local) + 1]
 
 
@@ -295,31 +373,38 @@
     return results[0], results[1:]
 
 
-def shifted(devices, step):
-    half = devices // 2
-    return [(b * half + j, b * half + (j + step) % half) for b in range(2) for j in range(half)]
+def exchanged(devices, step):
+    return [(i, i ^ step) for i in range(devices)]
+
+
+def swap(rows, devices):
+    sent = {k: lax.ppermute(rows[k], "fsdp", exchanged(devices, k)) for k in range(len(rows) - 1, 0, -1)}
+    return [rows[0]] + [sent[k] for k in range(1, len(rows))]
 
 
 def body(queries, out_grad, neighbours, neighbour_ids):
     devices = lax.axis_size("fsdp")
     half = devices // 2
+    heads = queries.shape[1] // HD // half
+    chunks = math.gcd(heads, CHUNKS)
+    across = [(i, (i + half) % devices) for i in range(devices)]
     slots = jnp.argsort(neighbour_ids, stable=True).astype(jnp.int32)
-    tokens = pack_tokens(queries, out_grad, devices)
-    tokens = lax.all_to_all(tokens, "fsdp", split_axis=0, concat_axis=0, tiled=True)
-    sent = pack_rows(neighbours, devices)
-    rows = [sent[0]] + [lax.ppermute(sent[k], "fsdp", shifted(devices, k)) for k in range(1, half)]
-    rows = [rows[0]] + [rows[half - k] for k in range(1, half)]
-    rows = [row.reshape(-1, 2 * NTOK, HD) for row in rows]
-    own = row_stats(slots, tokens, rows)
-    across = [(i, (i + half) % devices) for i in range(devices)]
-    other = lax.ppermute(own, "fsdp", across)
-    token_grads, row_grads = grads(slots, tokens, rows, own, other)
-    token_grads = lax.all_to_all(token_grads, "fsdp", split_axis=0, concat_axis=0, tiled=True)
-    row_grads = [row.reshape(-1, NTOK, 2, HD) for row in row_grads]
-    back = [row_grads[0]] + [
-        lax.ppermute(row_grads[k], "fsdp", shifted(devices, k)) for k in range(1, half)
-    ]
-    return tuple(unpack(token_grads, back, devices))
+    arrived = []
+    for chunk in range(chunks):
+        tokens = pack_tokens(queries, out_grad, devices, chunk, chunks)
+        tokens = lax.all_to_all(tokens, "fsdp", split_axis=0, concat_axis=0, tiled=True)
+        rows = swap(pack_rows(neighbours, devices, chunk, chunks), devices)
+        arrived.append((tokens, [row.reshape(-1, 2 * NTOK, HD) for row in rows]))
+    out_tokens, out_rows = (), ()
+    for chunk, (tokens, rows) in enumerate(arrived):
+        own = row_stats(slots, tokens, rows)
+        other = lax.ppermute(own, "fsdp", across)
+        token_grads, row_grads = grads(slots, tokens, rows, own, other)
+        token_grads = lax.all_to_all(token_grads, "fsdp", split_axis=0, concat_axis=0, tiled=True)
+        row_grads = swap([row.reshape(-1, NTOK, 2, HD) for row in row_grads], devices)
+        out_tokens = tuple(unpack_tokens(token_grads, out_tokens, chunk, chunks))
+        out_rows = (unpack_rows(row_grads, out_rows, chunk, chunks),)
+    return out_tokens + out_rows
 
 
 def solution(mesh):

time: 613 us -> 340 us (0.55)
  Pallas kernels: 420 us -> 61.7 us
  waiting for transfers between devices: 150 us -> 196 us
  starting transfers between devices: 38.5 us -> 69.3 us
    pallas_call x2 -> x6, Pallas kernels: 261 us -> 21 us  [the longest x2 10.7 us: pack_tokens(): pl.pallas_call(kernel, grid=(half,), in_specs=[block, block], out_specs=p...]
    pallas_call x1 -> x2, Pallas kernels: 129 us -> 5.23 us  [pack_rows(): pl.pallas_call(kernel, in_specs=[ANY], out_specs=[ANY] * half, out_shape=...]
    all_to_all x1 -> x2, waiting for transfers between devices: 0.01 us -> 42.1 us  [body(): lax.all_to_all(tokens, 'fsdp', split_axis=0, concat_axis=0, tiled=True)]
    ppermute x14 -> x28, starting transfers between devices: 19.7 us -> 40.8 us  [swap(): lax.ppermute(rows[k], 'fsdp', exchanged(devices, k))]
    all_to_all x1 -> x2, starting transfers between devices: 10.2 us -> 14.7 us  [body(): lax.all_to_all(token_grads, 'fsdp', split_axis=0, concat_axis=0, tiled=True)]
    pallas_call x1 -> x2, Pallas kernels: 21.3 us -> 24.1 us  [grads(): pl.pallas_call(grads_kernel, grid_spec=pltpu.PrefetchScalarGridSpec(num_s...]
    ppermute x14 -> x28, waiting for transfers between devices: 147 us -> 148 us  [swap(): lax.ppermute(rows[k], 'fsdp', exchanged(devices, k))]
  transfers between devices with their start and end apart: 17 -> 34, of which waited for: 10 -> 25; matrix products, arithmetic and copies ran while one was open for 0% -> 0% of each run, Pallas kernels for 21% -> 16%
where the time goes in v3:
time: 340 us; the launch traced here: 336 us
  waiting for transfers between devices  196 us (58%)
  starting transfers between devices  69.3 us (20%)
  Pallas kernels  61.7 us (18%)
  local copies, waits for them, and re-layouts  6.64 us (2%)
    ppermute x28, waiting for transfers between devices, swap(): lax.ppermute(rows[k], 'fsdp', exchanged(devices, k))  148 us
    all_to_all x2, waiting for transfers between devices, body(): lax.all_to_all(tokens, 'fsdp', split_axis=0, concat_axis=0, tiled=True)  42.1 us
    ppermute x28, starting transfers between devices, swap(): lax.ppermute(rows[k], 'fsdp', exchanged(devices, k))  40.8 us
    pallas_call x2, Pallas kernels, grads(): pl.pallas_call(grads_kernel, grid_spec=pltpu.PrefetchScalarGridSpec(num_s...  24.1 us
    all_to_all x2, starting transfers between devices, body(): lax.all_to_all(token_grads, 'fsdp', split_axis=0, concat_axis=0, tiled=True)  14.7 us
    all_to_all x2, starting transfers between devices, body(): lax.all_to_all(tokens, 'fsdp', split_axis=0, concat_axis=0, tiled=True)  11.5 us
    pallas_call x2, Pallas kernels, row_stats(): pl.pallas_call(stats_kernel, grid_spec=pltpu.PrefetchScalarGridSpec(num_s...  11.3 us
    pallas_call x2, Pallas kernels, pack_tokens(): pl.pallas_call(kernel, grid=(half,), in_specs=[block, block], out_specs=p...  10.7 us
  transfers between devices with their start and end apart: 34, of which 25 were waited for; matrix products, arithmetic and copies ran while one was open for 0% of the time, Pallas kernels for 16%

profile of v3, /device:TPU:15, one launch (start us, length us, event | category | flops | bytes accessed | tf_op | source)
XLA Modules:
  0.0 336.5 jit_solution(11685120672570001297)
XLA Ops:
  6.0 6.6 %all-to-all-start.2 = ((bf16[16,128,512]{2,1,0:T(8,128)(2,1)}), bf16[16,128,512]{2,1,0:T(8,128)(2,1)S(1)}, u32[]{:S(2)}, u32[]{:S(2)}) async-start(bf16[16,128,512]{2,1,0:T(8,128)(2,1)} %bitcast.35), calls=%async_computation.2 | async-start | bytes 4194304 | tf_op jit(solution)/shard_map/all_to_all | solution.py:395
  17.8 42.1 %all-to-all-done.2.t_ref = bf16[16,128,512]{2,1,0:T(8,128)(2,1)S(1)} async-done(((bf16[16,128,512]{2,1,0:T(8,128)(2,1)}), bf16[16,128,512]{2,1,0:T(8,128)(2,1)S(1)}, u32[]{:S(2)}, u32[]{:S(2)}) %all-to-all-start.2) | async-done | bytes 2097184 | tf_op jit(solution)/shard_map/all_to_all | solution.py:395
  72.8 11.5 %collective-permute-done.9 = bf16[4,128,2,128]{3,2,1,0:T(2,128)(2,1)S(1)} collective-permute-done((bf16[4,128,2,128]{3,2,1,0:T(2,128)(2,1)}, bf16[4,128,2,128]{3,2,1,0:T(2,128)(2,1)S(1)}, u32[]{:S(2)}, u32[]{:S(2)}) %collective-permute-start.9) | collective-permute-done | bytes 262176 | tf_op jit(solution)/shard_map/ppermute | solution.py:381
  84.3 7.2 %collective-permute-start.14 = (bf16[4,128,2,128]{3,2,1,0:T(2,128)(2,1)}, bf16[4,128,2,128]{3,2,1,0:T(2,128)(2,1)}, u32[]{:S(2)}, u32[]{:S(2)}) collective-permute-start(bf16[4,128,2,128]{3,2,1,0:T(2,128)(2,1)} %get-tuple-element.59), channel_id=1, source_target_pairs={{0,7},{1,6},{2,5},{3,4},{4,3},{5,2},{6,1},{7,0},{8,15},{9,14},{10,... | collective-permute-start | bytes 786440 | tf_op jit(solution)/shard_map/ppermute | solution.py:381
  93.2 14.2 %collective-permute-done.11 = bf16[4,128,2,128]{3,2,1,0:T(2,128)(2,1)S(1)} collective-permute-done((bf16[4,128,2,128]{3,2,1,0:T(2,128)(2,1)}, bf16[4,128,2,128]{3,2,1,0:T(2,128)(2,1)S(1)}, u32[]{:S(2)}, u32[]{:S(2)}) %collective-permute-start.11) | collective-permute-done | bytes 262176 | tf_op jit(solution)/shard_map/ppermute | solution.py:381
  107.4 6.7 %collective-permute-done.12 = bf16[4,128,2,128]{3,2,1,0:T(2,128)(2,1)S(1)} collective-permute-done((bf16[4,128,2,128]{3,2,1,0:T(2,128)(2,1)}, bf16[4,128,2,128]{3,2,1,0:T(2,128)(2,1)S(1)}, u32[]{:S(2)}, u32[]{:S(2)}) %collective-permute-start.12) | collective-permute-done | bytes 262176 | tf_op jit(solution)/shard_map/ppermute | solution.py:381
  119.4 5.6 %collective-permute-done.14 = bf16[4,128,2,128]{3,2,1,0:T(2,128)(2,1)} collective-permute-done((bf16[4,128,2,128]{3,2,1,0:T(2,128)(2,1)}, bf16[4,128,2,128]{3,2,1,0:T(2,128)(2,1)}, u32[]{:S(2)}, u32[]{:S(2)}) %collective-permute-start.14) | collective-permute-done | bytes 262176 | tf_op jit(solution)/shard_map/ppermute | solution.py:381
  125.0 5.7 %row_stats.3.refs_8_ = f32[4,3,8,128]{3,2,1,0:T(8,128)} custom-call(s32[32]{0:T(128)} %get-tuple-element.42.slots_ref, bf16[16,128,512]{2,1,0:T(8,128)(2,1)} %copy-done.1, bf16[4,256,128]{2,1,0:T(8,128)(2,1)} %bitcast.36, bf16[4,256,128]{2,1,0:T(8,128)(2,1)} %bitcast.38, bf16[4,256,128]{2,1,0:T(8,128)(2,1)} %bitcast.40, bf16[4,256,128]{2,1,0:T(8,128)(2,1)} %bitcast.44, ...), custom_call_target="tpu_custom_call" | custom-call | tf_op jit(solution)/shard_map/row_stats/pallas_call | solution.py:271
  135.5 12.0 %grads.3 = (bf16[16,128,512]{2,1,0:T(8,128)(2,1)}, bf16[4,256,128]{2,1,0:T(8,128)(2,1)}, bf16[4,256,128]{2,1,0:T(8,128)(2,1)}, bf16[4,256,128]{2,1,0:T(8,128)(2,...) custom-call(s32[32]{0:T(128)} %get-tuple-element.42.slots_ref, ...), custom_call_target="tpu_custom_call" | custom-call | tf_op jit(solution)/shard_map/grads/pallas_call | solution.py:354
  148.8 7.4 %all-to-all-start.3 = ((bf16[16,128,512]{2,1,0:T(8,128)(2,1)}), bf16[16,128,512]{2,1,0:T(8,128)(2,1)}, u32[]{:S(2)}, u32[]{:S(2)}) async-start(bf16[16,128,512]{2,1,0:T(8,128)(2,1)} %get-tuple-element.60), calls=%async_computation.3 | async-start | bytes 4194304 | tf_op jit(solution)/shard_map/all_to_all | solution.py:403
  162.8 11.5 %collective-permute-done.1 = bf16[4,128,2,128]{3,2,1,0:T(2,128)(2,1)S(1)} collective-permute-done((bf16[4,128,2,128]{3,2,1,0:T(2,128)(2,1)}, bf16[4,128,2,128]{3,2,1,0:T(2,128)(2,1)S(1)}, u32[]{:S(2)}, u32[]{:S(2)}) %collective-permute-start.1) | collective-permute-done | bytes 262176 | tf_op jit(solution)/shard_map/ppermute | solution.py:381
  174.4 7.2 %collective-permute-start.6 = (bf16[4,128,2,128]{3,2,1,0:T(2,128)(2,1)}, bf16[4,128,2,128]{3,2,1,0:T(2,128)(2,1)S(1)}, u32[]{:S(2)}, u32[]{:S(2)}) collective-permute-start(bf16[4,128,2,128]{3,2,1,0:T(2,128)(2,1)} %get-tuple-element.50), channel_id=1, source_target_pairs={{0,7},{1,6},{2,5},{3,4},{4,3},{5,2},{6,1},{7,0},{8,15},{9,14},{10,... | collective-permute-start | bytes 786440 | tf_op jit(solution)/shard_map/ppermute | solution.py:381
  183.4 14.1 %collective-permute-done.3 = bf16[4,128,2,128]{3,2,1,0:T(2,128)(2,1)S(1)} collective-permute-done((bf16[4,128,2,128]{3,2,1,0:T(2,128)(2,1)}, bf16[4,128,2,128]{3,2,1,0:T(2,128)(2,1)S(1)}, u32[]{:S(2)}, u32[]{:S(2)}) %collective-permute-start.3) | collective-permute-done | bytes 262176 | tf_op jit(solution)/shard_map/ppermute | solution.py:381
  197.5 6.6 %collective-permute-done.4 = bf16[4,128,2,128]{3,2,1,0:T(2,128)(2,1)S(1)} collective-permute-done((bf16[4,128,2,128]{3,2,1,0:T(2,128)(2,1)}, bf16[4,128,2,128]{3,2,1,0:T(2,128)(2,1)S(1)}, u32[]{:S(2)}, u32[]{:S(2)}) %collective-permute-start.4) | collective-permute-done | bytes 262176 | tf_op jit(solution)/shard_map/ppermute | solution.py:381
  209.3 5.7 %collective-permute-done.6 = bf16[4,128,2,128]{3,2,1,0:T(2,128)(2,1)S(1)} collective-permute-done((bf16[4,128,2,128]{3,2,1,0:T(2,128)(2,1)}, bf16[4,128,2,128]{3,2,1,0:T(2,128)(2,1)S(1)}, u32[]{:S(2)}, u32[]{:S(2)}) %collective-permute-start.6) | collective-permute-done | bytes 262176 | tf_op jit(solution)/shard_map/ppermute | solution.py:381
  215.6 5.7 %row_stats.2.refs_8_ = f32[4,3,8,128]{3,2,1,0:T(8,128)} custom-call(s32[32]{0:T(128)} %get-tuple-element.42.slots_ref, bf16[16,128,512]{2,1,0:T(8,128)(2,1)} %copy-done, bf16[4,256,128]{2,1,0:T(8,128)(2,1)} %bitcast.42, bf16[4,256,128]{2,1,0:T(8,128)(2,1)} %bitcast.46, bf16[4,256,128]{2,1,0:T(8,128)(2,1)} %bitcast.50, bf16[4,256,128]{2,1,0:T(8,128)(2,1)} %bitcast.54, ...), custom_call_target="tpu_custom_call" | custom-call | tf_op jit(solution)/shard_map/row_stats/pallas_call | solution.py:271
  226.1 12.0 %grads.2 = (bf16[16,128,512]{2,1,0:T(8,128)(2,1)}, bf16[4,256,128]{2,1,0:T(8,128)(2,1)}, bf16[4,256,128]{2,1,0:T(8,128)(2,1)}, bf16[4,256,128]{2,1,0:T(8,128)(2,...) custom-call(s32[32]{0:T(128)} %get-tuple-element.42.slots_ref, ...), custom_call_target="tpu_custom_call" | custom-call | tf_op jit(solution)/shard_map/grads/pallas_call | solution.py:354
  238.2 7.2 %all-to-all-start.1 = ((bf16[16,128,512]{2,1,0:T(8,128)(2,1)}), bf16[16,128,512]{2,1,0:T(8,128)(2,1)S(1)}, u32[]{:S(2)}, u32[]{:S(2)}) async-start(bf16[16,128,512]{2,1,0:T(8,128)(2,1)} %get-tuple-element.51), calls=%async_computation.1 | async-start | bytes 4194304 | tf_op jit(solution)/shard_map/all_to_all | solution.py:403
  248.3 15.2 %collective-permute-done.17.refs_2_ = bf16[4,128,2,128]{3,2,1,0:T(2,128)(2,1)S(1)} collective-permute-done((bf16[4,128,2,128]{3,2,1,0:T(2,128)(2,1)}, bf16[4,128,2,128]{3,2,1,0:T(2,128)(2,1)S(1)}, u32[]{:S(2)}, u32[]{:S(2)}) %collective-permute-start.17) | collective-permute-done | bytes 262176 | tf_op jit(solution)/shard_map/ppermute | solution.py:381
  271.9 5.8 %collective-permute-start.29 = (bf16[4,128,2,128]{3,2,1,0:T(2,128)(2,1)S(1)}, bf16[4,128,2,128]{3,2,1,0:T(2,128)(2,1)S(1)}, u32[]{:S(2)}, u32[]{:S(2)}) collective-permute-start(bf16[4,128,2,128]{3,2,1,0:T(2,128)(2,1)S(1)} %bitcast.66), channel_id=1, source_target_pairs={{0,7},{1,6},{2,5},{3,4},{4,3},{5,2},{6,1},{7,0},{8,15},{9,14},{10,... | collective-permute-start | bytes 786440 | tf_op jit(solution)/shard_map/ppermute | solution.py:381
  277.7 5.9 %collective-permute-done.25.refs_3_ = bf16[4,128,2,128]{3,2,1,0:T(2,128)(2,1)S(1)} collective-permute-done((bf16[4,128,2,128]{3,2,1,0:T(2,128)(2,1)S(1)}, bf16[4,128,2,128]{3,2,1,0:T(2,128)(2,1)S(1)}, u32[]{:S(2)}, u32[]{:S(2)}) %collective-permute-start.25) | collective-permute-done | bytes 262176 | tf_op jit(solution)/shard_map/ppermute | solution.py:381
  287.4 5.8 %collective-permute-done.27.refs_5_ = bf16[4,128,2,128]{3,2,1,0:T(2,128)(2,1)S(1)} collective-permute-done((bf16[4,128,2,128]{3,2,1,0:T(2,128)(2,1)S(1)}, bf16[4,128,2,128]{3,2,1,0:T(2,128)(2,1)S(1)}, u32[]{:S(2)}, u32[]{:S(2)}) %collective-permute-start.27) | collective-permute-done | bytes 262176 | tf_op jit(solution)/shard_map/ppermute | solution.py:381
  309.2 6.3 %collective-permute-done.20.refs_5_ = bf16[4,128,2,128]{3,2,1,0:T(2,128)(2,1)S(1)} collective-permute-done((bf16[4,128,2,128]{3,2,1,0:T(2,128)(2,1)}, bf16[4,128,2,128]{3,2,1,0:T(2,128)(2,1)S(1)}, u32[]{:S(2)}, u32[]{:S(2)}) %collective-permute-start.20) | collective-permute-done | bytes 262176 | tf_op jit(solution)/shard_map/ppermute | solution.py:381
  315.5 5.6 %collective-permute-done.21.refs_6_ = bf16[4,128,2,128]{3,2,1,0:T(2,128)(2,1)S(1)} collective-permute-done((bf16[4,128,2,128]{3,2,1,0:T(2,128)(2,1)}, bf16[4,128,2,128]{3,2,1,0:T(2,128)(2,1)S(1)}, u32[]{:S(2)}, u32[]{:S(2)}) %collective-permute-start.21) | collective-permute-done | bytes 262176 | tf_op jit(solution)/shard_map/ppermute | solution.py:381
  (132 shorter events, 101.8 us)
Async XLA Ops:
  6.0 54.0 %all-to-all-start.2 = ((bf16[16,128,512]{2,1,0:T(8,128)(2,1)}), bf16[16,128,512]{2,1,0:T(8,128)(2,1)S(1)}, u32[]{:S(2)}, u32[]{:S(2)}) async-start(bf16[16,128,512]{2,1,0:T(8,128)(2,1)} %bitcast.35), calls=%async_computation.2 | async-start | bytes 4194304 | tf_op jit(solution)/shard_map/all_to_all | solution.py:395
  61.3 86.2 %all-to-all-start = ((bf16[16,128,512]{2,1,0:T(8,128)(2,1)}), bf16[16,128,512]{2,1,0:T(8,128)(2,1)S(1)}, u32[]{:S(2)}, u32[]{:S(2)}) async-start(bf16[16,128,512]{2,1,0:T(8,128)(2,1)} %bitcast.34), calls=%async_computation | async-start | bytes 4194304 | tf_op jit(solution)/shard_map/all_to_all | solution.py:395
  69.5 23.7 %collective-permute-start.10 = (bf16[4,128,2,128]{3,2,1,0:T(2,128)(2,1)}, bf16[4,128,2,128]{3,2,1,0:T(2,128)(2,1)S(1)}, u32[]{:S(2)}, u32[]{:S(2)}) collective-permute-start(bf16[4,128,2,128]{3,2,1,0:T(2,128)(2,1)} %get-tuple-element.55), channel_id=1, source_target_pairs={{0,3},{1,2},{2,1},{3,0},{4,7},{5,6},{6,5},{7,4},{8,11},{9,10},{10,... | collective-permute-start | bytes 786440 | tf_op jit(solution)/shard_map/ppermute | solution.py:381
  71.0 36.4 %collective-permute-start.11 = (bf16[4,128,2,128]{3,2,1,0:T(2,128)(2,1)}, bf16[4,128,2,128]{3,2,1,0:T(2,128)(2,1)S(1)}, u32[]{:S(2)}, u32[]{:S(2)}) collective-permute-start(bf16[4,128,2,128]{3,2,1,0:T(2,128)(2,1)} %get-tuple-element.56), channel_id=1, source_target_pairs={{0,4},{1,5},{2,6},{3,7},{4,0},{5,1},{6,2},{7,3},{8,12},{9,13},{10,... | collective-permute-start | bytes 786440 | tf_op jit(solution)/shard_map/ppermute | solution.py:381
  71.3 42.8 %collective-permute-start.12 = (bf16[4,128,2,128]{3,2,1,0:T(2,128)(2,1)}, bf16[4,128,2,128]{3,2,1,0:T(2,128)(2,1)S(1)}, u32[]{:S(2)}, u32[]{:S(2)}) collective-permute-start(bf16[4,128,2,128]{3,2,1,0:T(2,128)(2,1)} %get-tuple-element.57), channel_id=1, source_target_pairs={{0,5},{1,4},{2,7},{3,6},{4,1},{5,0},{6,3},{7,2},{8,13},{9,12},{10,... | collective-permute-start | bytes 786440 | tf_op jit(solution)/shard_map/ppermute | solution.py:381
  72.7 46.6 %collective-permute-start.13 = (bf16[4,128,2,128]{3,2,1,0:T(2,128)(2,1)}, bf16[4,128,2,128]{3,2,1,0:T(2,128)(2,1)}, u32[]{:S(2)}, u32[]{:S(2)}) collective-permute-start(bf16[4,128,2,128]{3,2,1,0:T(2,128)(2,1)} %get-tuple-element.58), channel_id=1, source_target_pairs={{0,6},{1,7},{2,4},{3,5},{4,2},{5,3},{6,0},{7,1},{8,14},{9,15},{10,... | collective-permute-start | bytes 786440 | tf_op jit(solution)/shard_map/ppermute | solution.py:381
  84.3 40.7 %collective-permute-start.14 = (bf16[4,128,2,128]{3,2,1,0:T(2,128)(2,1)}, bf16[4,128,2,128]{3,2,1,0:T(2,128)(2,1)}, u32[]{:S(2)}, u32[]{:S(2)}) collective-permute-start(bf16[4,128,2,128]{3,2,1,0:T(2,128)(2,1)} %get-tuple-element.59), channel_id=1, source_target_pairs={{0,7},{1,6},{2,5},{3,4},{4,3},{5,2},{6,1},{7,0},{8,15},{9,14},{10,... | collective-permute-start | bytes 786440 | tf_op jit(solution)/shard_map/ppermute | solution.py:381
  148.8 89.3 %all-to-all-start.3 = ((bf16[16,128,512]{2,1,0:T(8,128)(2,1)}), bf16[16,128,512]{2,1,0:T(8,128)(2,1)}, u32[]{:S(2)}, u32[]{:S(2)}) async-start(bf16[16,128,512]{2,1,0:T(8,128)(2,1)} %get-tuple-element.60), calls=%async_computation.3 | async-start | bytes 4194304 | tf_op jit(solution)/shard_map/all_to_all | solution.py:403
  159.6 23.8 %collective-permute-start.2 = (bf16[4,128,2,128]{3,2,1,0:T(2,128)(2,1)}, bf16[4,128,2,128]{3,2,1,0:T(2,128)(2,1)S(1)}, u32[]{:S(2)}, u32[]{:S(2)}) collective-permute-start(bf16[4,128,2,128]{3,2,1,0:T(2,128)(2,1)} %get-tuple-element.46), channel_id=1, source_target_pairs={{0,3},{1,2},{2,1},{3,0},{4,7},{5,6},{6,5},{7,4},{8,11},{9,10},{10,... | collective-permute-start | bytes 786440 | tf_op jit(solution)/shard_map/ppermute | solution.py:381
  161.1 36.4 %collective-permute-start.3 = (bf16[4,128,2,128]{3,2,1,0:T(2,128)(2,1)}, bf16[4,128,2,128]{3,2,1,0:T(2,128)(2,1)S(1)}, u32[]{:S(2)}, u32[]{:S(2)}) collective-permute-start(bf16[4,128,2,128]{3,2,1,0:T(2,128)(2,1)} %get-tuple-element.47), channel_id=1, source_target_pairs={{0,4},{1,5},{2,6},{3,7},{4,0},{5,1},{6,2},{7,3},{8,12},{9,13},{10,... | collective-permute-start | bytes 786440 | tf_op jit(solution)/shard_map/ppermute | solution.py:381
  161.4 42.7 %collective-permute-start.4 = (bf16[4,128,2,128]{3,2,1,0:T(2,128)(2,1)}, bf16[4,128,2,128]{3,2,1,0:T(2,128)(2,1)S(1)}, u32[]{:S(2)}, u32[]{:S(2)}) collective-permute-start(bf16[4,128,2,128]{3,2,1,0:T(2,128)(2,1)} %get-tuple-element.48), channel_id=1, source_target_pairs={{0,5},{1,4},{2,7},{3,6},{4,1},{5,0},{6,3},{7,2},{8,13},{9,12},{10,... | collective-permute-start | bytes 786440 | tf_op jit(solution)/shard_map/ppermute | solution.py:381
  162.8 46.4 %collective-permute-start.5 = (bf16[4,128,2,128]{3,2,1,0:T(2,128)(2,1)}, bf16[4,128,2,128]{3,2,1,0:T(2,128)(2,1)S(1)}, u32[]{:S(2)}, u32[]{:S(2)}) collective-permute-start(bf16[4,128,2,128]{3,2,1,0:T(2,128)(2,1)} %get-tuple-element.49), channel_id=1, source_target_pairs={{0,6},{1,7},{2,4},{3,5},{4,2},{5,3},{6,0},{7,1},{8,14},{9,15},{10,... | collective-permute-start | bytes 786440 | tf_op jit(solution)/shard_map/ppermute | solution.py:381
  174.4 40.6 %collective-permute-start.6 = (bf16[4,128,2,128]{3,2,1,0:T(2,128)(2,1)}, bf16[4,128,2,128]{3,2,1,0:T(2,128)(2,1)S(1)}, u32[]{:S(2)}, u32[]{:S(2)}) collective-permute-start(bf16[4,128,2,128]{3,2,1,0:T(2,128)(2,1)} %get-tuple-element.50), channel_id=1, source_target_pairs={{0,7},{1,6},{2,5},{3,4},{4,3},{5,2},{6,1},{7,0},{8,15},{9,14},{10,... | collective-permute-start | bytes 786440 | tf_op jit(solution)/shard_map/ppermute | solution.py:381
  238.2 94.5 %all-to-all-start.1 = ((bf16[16,128,512]{2,1,0:T(8,128)(2,1)}), bf16[16,128,512]{2,1,0:T(8,128)(2,1)S(1)}, u32[]{:S(2)}, u32[]{:S(2)}) async-start(bf16[16,128,512]{2,1,0:T(8,128)(2,1)} %get-tuple-element.51), calls=%async_computation.1 | async-start | bytes 4194304 | tf_op jit(solution)/shard_map/all_to_all | solution.py:403
  246.0 22.9 %collective-permute-start.23 = (bf16[4,128,2,128]{3,2,1,0:T(2,128)(2,1)}, bf16[4,128,2,128]{3,2,1,0:T(2,128)(2,1)S(1)}, u32[]{:S(2)}, u32[]{:S(2)}) collective-permute-start(bf16[4,128,2,128]{3,2,1,0:T(2,128)(2,1)} %bitcast.72), channel_id=1, source_target_pairs={{0,1},{1,0},{2,3},{3,2},{4,5},{5,4},{6,7},{7,6},{8,9},{9,8},{10,11... | collective-permute-start | bytes 786440 | tf_op jit(solution)/shard_map/ppermute | solution.py:381
  246.5 25.4 %collective-permute-start.24 = (bf16[4,128,2,128]{3,2,1,0:T(2,128)(2,1)}, bf16[4,128,2,128]{3,2,1,0:T(2,128)(2,1)S(1)}, u32[]{:S(2)}, u32[]{:S(2)}) collective-permute-start(bf16[4,128,2,128]{3,2,1,0:T(2,128)(2,1)} %bitcast.71), channel_id=1, source_target_pairs={{0,2},{1,3},{2,0},{3,1},{4,6},{5,7},{6,4},{7,5},{8,10},{9,11},{10,... | collective-permute-start | bytes 786440 | tf_op jit(solution)/shard_map/ppermute | solution.py:381
  247.7 36.0 %collective-permute-start.25 = (bf16[4,128,2,128]{3,2,1,0:T(2,128)(2,1)S(1)}, bf16[4,128,2,128]{3,2,1,0:T(2,128)(2,1)S(1)}, u32[]{:S(2)}, u32[]{:S(2)}) collective-permute-start(bf16[4,128,2,128]{3,2,1,0:T(2,128)(2,1)S(1)} %bitcast.70), channel_id=1, source_target_pairs={{0,3},{1,2},{2,1},{3,0},{4,7},{5,6},{6,5},{7,4},{8,11},{9,10},{10,... | collective-permute-start | bytes 786440 | tf_op jit(solution)/shard_map/ppermute | solution.py:381
  248.2 38.5 %collective-permute-start.26 = (bf16[4,128,2,128]{3,2,1,0:T(2,128)(2,1)S(1)}, bf16[4,128,2,128]{3,2,1,0:T(2,128)(2,1)S(1)}, u32[]{:S(2)}, u32[]{:S(2)}) collective-permute-start(bf16[4,128,2,128]{3,2,1,0:T(2,128)(2,1)S(1)} %bitcast.69), channel_id=1, source_target_pairs={{0,4},{1,5},{2,6},{3,7},{4,0},{5,1},{6,2},{7,3},{8,12},{9,13},{10,... | collective-permute-start | bytes 786440 | tf_op jit(solution)/shard_map/ppermute | solution.py:381
  263.5 29.7 %collective-permute-start.27 = (bf16[4,128,2,128]{3,2,1,0:T(2,128)(2,1)S(1)}, bf16[4,128,2,128]{3,2,1,0:T(2,128)(2,1)S(1)}, u32[]{:S(2)}, u32[]{:S(2)}) collective-permute-start(bf16[4,128,2,128]{3,2,1,0:T(2,128)(2,1)S(1)} %bitcast.68), channel_id=1, source_target_pairs={{0,5},{1,4},{2,7},{3,6},{4,1},{5,0},{6,3},{7,2},{8,13},{9,12},{10,... | collective-permute-start | bytes 786440 | tf_op jit(solution)/shard_map/ppermute | solution.py:381
  268.9 29.7 %collective-permute-start.28 = (bf16[4,128,2,128]{3,2,1,0:T(2,128)(2,1)S(1)}, bf16[4,128,2,128]{3,2,1,0:T(2,128)(2,1)S(1)}, u32[]{:S(2)}, u32[]{:S(2)}) collective-permute-start(bf16[4,128,2,128]{3,2,1,0:T(2,128)(2,1)S(1)} %bitcast.67), channel_id=1, source_target_pairs={{0,6},{1,7},{2,4},{3,5},{4,2},{5,3},{6,0},{7,1},{8,14},{9,15},{10,... | collective-permute-start | bytes 786440 | tf_op jit(solution)/shard_map/ppermute | solution.py:381
  271.9 32.4 %collective-permute-start.29 = (bf16[4,128,2,128]{3,2,1,0:T(2,128)(2,1)S(1)}, bf16[4,128,2,128]{3,2,1,0:T(2,128)(2,1)S(1)}, u32[]{:S(2)}, u32[]{:S(2)}) collective-permute-start(bf16[4,128,2,128]{3,2,1,0:T(2,128)(2,1)S(1)} %bitcast.66), channel_id=1, source_target_pairs={{0,7},{1,6},{2,5},{3,4},{4,3},{5,2},{6,1},{7,0},{8,15},{9,14},{10,... | collective-permute-start | bytes 786440 | tf_op jit(solution)/shard_map/ppermute | solution.py:381
  283.6 24.5 %collective-permute-start.18 = (bf16[4,128,2,128]{3,2,1,0:T(2,128)(2,1)}, bf16[4,128,2,128]{3,2,1,0:T(2,128)(2,1)S(1)}, u32[]{:S(2)}, u32[]{:S(2)}) collective-permute-start(bf16[4,128,2,128]{3,2,1,0:T(2,128)(2,1)} %bitcast.77), channel_id=1, source_target_pairs={{0,3},{1,2},{2,1},{3,0},{4,7},{5,6},{6,5},{7,4},{8,11},{9,10},{10,... | collective-permute-start | bytes 786440 | tf_op jit(solution)/shard_map/ppermute | solution.py:381
  286.7 22.5 %collective-permute-start.19 = (bf16[4,128,2,128]{3,2,1,0:T(2,128)(2,1)}, bf16[4,128,2,128]{3,2,1,0:T(2,128)(2,1)S(1)}, u32[]{:S(2)}, u32[]{:S(2)}) collective-permute-start(bf16[4,128,2,128]{3,2,1,0:T(2,128)(2,1)} %bitcast.76), channel_id=1, source_target_pairs={{0,4},{1,5},{2,6},{3,7},{4,0},{5,1},{6,2},{7,3},{8,12},{9,13},{10,... | collective-permute-start | bytes 786440 | tf_op jit(solution)/shard_map/ppermute | solution.py:381
  298.6 22.5 %collective-permute-start.21 = (bf16[4,128,2,128]{3,2,1,0:T(2,128)(2,1)}, bf16[4,128,2,128]{3,2,1,0:T(2,128)(2,1)S(1)}, u32[]{:S(2)}, u32[]{:S(2)}) collective-permute-start(bf16[4,128,2,128]{3,2,1,0:T(2,128)(2,1)} %bitcast.74), channel_id=1, source_target_pairs={{0,6},{1,7},{2,4},{3,5},{4,2},{5,3},{6,0},{7,1},{8,14},{9,15},{10,... | collective-permute-start | bytes 786440 | tf_op jit(solution)/shard_map/ppermute | solution.py:381
  (47 other events, 852.8 us)

commit v4 on v3

--- a/solution.py
+++ b/solution.py
@@ -34,25 +34,56 @@
     return lax.rem(lax.axis_index("fsdp"), half) ^ step
 
 
+def cost(microseconds):
+    return pl.CostEstimate(
+        flops=0, bytes_accessed=int(microseconds * 3.69e6), transcendentals=0
+    )
+
+
 def pack_tokens(queries, out_grad, devices, chunk, chunks):
     half = devices // 2
     width = queries.shape[1] // half // chunks
 
-    def kernel(q_ref, g_ref, out_ref):
-        for b in range(2):
-            out_ref[b, 0, :SPAN] = q_ref[...]
-            out_ref[b, 0, SPAN:] = g_ref[...]
-
-    block = pl.BlockSpec((SPAN, width), lambda i: (0, i * chunks + chunk))
-    packed = pl.pallas_call(
+    def kernel(q_ref, g_ref, out_ref, buffer, come, go):
+        loads = [
+            [
+                pltpu.make_async_copy(
+                    ref.at[:, pl.ds((i * chunks + chunk) * width, width)],
+                    buffer.at[i, pl.ds(part * SPAN, SPAN)],
+                    come.at[i, part],
+                )
+                for part, ref in enumerate((q_ref, g_ref))
+            ]
+            for i in range(half)
+        ]
+        stores = [
+            [pltpu.make_async_copy(buffer.at[i], out_ref.at[b * half + i], go.at[i, b]) for b in range(2)]
+            for i in range(half)
+        ]
+        for load in sum(loads, []):
+            load.start()
+        for i in range(half):
+            for load in loads[i]:
+                load.wait()
+            for store in stores[i]:
+                store.start()
+        for store in sum(stores, []):
+            store.wait()
+
+    return pl.pallas_call(
         kernel,
-        grid=(half,),
-        in_specs=[block, block],
-        out_specs=pl.BlockSpec((2, 1, 2 * SPAN, width), lambda i: (0, i, 0, 0)),
-        out_shape=jax.ShapeDtypeStruct((2, half, 2 * SPAN, width), BF16),
+        in_specs=[ANY, ANY],
+        out_specs=ANY,
+        out_shape=jax.ShapeDtypeStruct((devices, 2 * SPAN, width), BF16),
+        scratch_shapes=[
+            vmem(half, 2 * SPAN, width),
+            pltpu.SemaphoreType.DMA((half, 2)),
+            pltpu.SemaphoreType.DMA((half, 2)),
+        ],
+        compiler_params=LIMIT,
+        cost_estimate=cost(2.5),
         name="pack_tokens",
     )(queries, out_grad)
-    return packed.reshape(devices, 2 * SPAN, width)
 
 
 def pack_rows(neighbours, devices, chunk, chunks):
@@ -99,6 +130,7 @@
             pltpu.SemaphoreType.DMA((half, heads)),
         ],
         compiler_params=LIMIT,
+        cost_estimate=cost(2.6),
         name="pack_rows",
     )(neighbours)
 
@@ -151,6 +183,7 @@
             pltpu.SemaphoreType.DMA((half, 2)),
         ],
         compiler_params=LIMIT,
+        cost_estimate=cost(2.6),
         name="unpack_tokens",
     )(tokens, *before)
 
@@ -198,6 +231,7 @@
             pltpu.SemaphoreType.DMA((half,)),
         ],
         compiler_params=LIMIT,
+        cost_estimate=cost(2.6),
         name="unpack_rows",
     )(*rows, *before)
 
@@ -282,6 +316,7 @@
         ),
         out_shape=jax.ShapeDtypeStruct((heads, 3, half, HD), F32),
         compiler_params=LIMIT,
+        cost_estimate=cost(6),
         name="row_stats",
     )(slots, tokens, *rows)
 
@@ -368,6 +403,7 @@
         out_shape=[jax.ShapeDtypeStruct(tokens.shape, BF16)]
         + [jax.ShapeDtypeStruct(rows[0].shape, BF16)] * half,
         compiler_params=LIMIT,
+        cost_estimate=cost(12),
         name="grads",
     )(slots, tokens, *rows, own, other)
     return results[0], results[1:]

time: 340 us -> 337 us (level)
  Pallas kernels: 61.7 us -> 55.9 us
    pallas_call x2, Pallas kernels: 10.7 us -> 4.93 us  [pack_tokens(): pl.pallas_call(kernel, in_specs=[ANY, ANY], out_specs=ANY, out_shape=jax....]
  transfers between devices with their start and end apart: 34 -> 34, of which waited for: 25 -> 25; matrix products, arithmetic and copies ran while one was open for 0% -> 1% of each run, Pallas kernels for 16% -> 15%
where the time goes in v4:
time: 337 us; the launch traced here: 334 us
  waiting for transfers between devices  199 us (59%)
  starting transfers between devices  69.3 us (21%)
  Pallas kernels  55.9 us (17%)
  local copies, waits for them, and re-layouts  6.64 us (2%)
    ppermute x28, waiting for transfers between devices, swap(): lax.ppermute(rows[k], 'fsdp', exchanged(devices, k))  148 us
    all_to_all x2, waiting for transfers between devices, body(): lax.all_to_all(tokens, 'fsdp', split_axis=0, concat_axis=0, tiled=True)  45 us
    ppermute x28, starting transfers between devices, swap(): lax.ppermute(rows[k], 'fsdp', exchanged(devices, k))  40.8 us
    pallas_call x2, Pallas kernels, grads(): pl.pallas_call(grads_kernel, grid_spec=pltpu.PrefetchScalarGridSpec(num_s...  24.1 us
    all_to_all x2, starting transfers between devices, body(): lax.all_to_all(token_grads, 'fsdp', split_axis=0, concat_axis=0, tiled=True)  14.7 us
    all_to_all x2, starting transfers between devices, body(): lax.all_to_all(tokens, 'fsdp', split_axis=0, concat_axis=0, tiled=True)  11.5 us
    pallas_call x2, Pallas kernels, row_stats(): pl.pallas_call(stats_kernel, grid_spec=pltpu.PrefetchScalarGridSpec(num_s...  11.3 us
  transfers between devices with their start and end apart: 34, of which 25 were waited for; matrix products, arithmetic and copies ran while one was open for 1% of the time, Pallas kernels for 15%

profile of v4, /device:TPU:15, one launch (start us, length us, event | category | flops | bytes accessed | tf_op | source)
XLA Modules:
  0.0 333.6 jit_solution(13673867966027498842)
XLA Ops:
  3.1 6.6 %all-to-all-start.2 = ((bf16[16,128,512]{2,1,0:T(8,128)(2,1)}), bf16[16,128,512]{2,1,0:T(8,128)(2,1)S(1)}, u32[]{:S(2)}, u32[]{:S(2)}) async-start(bf16[16,128,512]{2,1,0:T(8,128)(2,1)} %pack_tokens.3), calls=%async_computation.2 | async-start | bytes 4194304 | tf_op jit(solution)/shard_map/all_to_all | solution.py:431
  12.1 45.0 %all-to-all-done.2.t_ref = bf16[16,128,512]{2,1,0:T(8,128)(2,1)S(1)} async-done(((bf16[16,128,512]{2,1,0:T(8,128)(2,1)}), bf16[16,128,512]{2,1,0:T(8,128)(2,1)S(1)}, u32[]{:S(2)}, u32[]{:S(2)}) %all-to-all-start.2) | async-done | bytes 2097184 | tf_op jit(solution)/shard_map/all_to_all | solution.py:431
  70.0 11.5 %collective-permute-done.9 = bf16[4,128,2,128]{3,2,1,0:T(2,128)(2,1)S(1)} collective-permute-done((bf16[4,128,2,128]{3,2,1,0:T(2,128)(2,1)}, bf16[4,128,2,128]{3,2,1,0:T(2,128)(2,1)S(1)}, u32[]{:S(2)}, u32[]{:S(2)}) %collective-permute-start.9) | collective-permute-done | bytes 262176 | tf_op jit(solution)/shard_map/ppermute | solution.py:417
  81.4 7.2 %collective-permute-start.14 = (bf16[4,128,2,128]{3,2,1,0:T(2,128)(2,1)}, bf16[4,128,2,128]{3,2,1,0:T(2,128)(2,1)}, u32[]{:S(2)}, u32[]{:S(2)}) collective-permute-start(bf16[4,128,2,128]{3,2,1,0:T(2,128)(2,1)} %get-tuple-element.59), channel_id=1, source_target_pairs={{0,7},{1,6},{2,5},{3,4},{4,3},{5,2},{6,1},{7,0},{8,15},{9,14},{10,... | collective-permute-start | bytes 786440 | tf_op jit(solution)/shard_map/ppermute | solution.py:417
  90.4 14.2 %collective-permute-done.11 = bf16[4,128,2,128]{3,2,1,0:T(2,128)(2,1)S(1)} collective-permute-done((bf16[4,128,2,128]{3,2,1,0:T(2,128)(2,1)}, bf16[4,128,2,128]{3,2,1,0:T(2,128)(2,1)S(1)}, u32[]{:S(2)}, u32[]{:S(2)}) %collective-permute-start.11) | collective-permute-done | bytes 262176 | tf_op jit(solution)/shard_map/ppermute | solution.py:417
  104.6 6.7 %collective-permute-done.12 = bf16[4,128,2,128]{3,2,1,0:T(2,128)(2,1)S(1)} collective-permute-done((bf16[4,128,2,128]{3,2,1,0:T(2,128)(2,1)}, bf16[4,128,2,128]{3,2,1,0:T(2,128)(2,1)S(1)}, u32[]{:S(2)}, u32[]{:S(2)}) %collective-permute-start.12) | collective-permute-done | bytes 262176 | tf_op jit(solution)/shard_map/ppermute | solution.py:417
  116.5 5.6 %collective-permute-done.14 = bf16[4,128,2,128]{3,2,1,0:T(2,128)(2,1)} collective-permute-done((bf16[4,128,2,128]{3,2,1,0:T(2,128)(2,1)}, bf16[4,128,2,128]{3,2,1,0:T(2,128)(2,1)}, u32[]{:S(2)}, u32[]{:S(2)}) %collective-permute-start.14) | collective-permute-done | bytes 262176 | tf_op jit(solution)/shard_map/ppermute | solution.py:417
  122.2 5.7 %row_stats.3.refs_8_ = f32[4,3,8,128]{3,2,1,0:T(8,128)} custom-call(s32[32]{0:T(128)} %get-tuple-element.42.slots_ref, bf16[16,128,512]{2,1,0:T(8,128)(2,1)} %copy-done.1, bf16[4,256,128]{2,1,0:T(8,128)(2,1)} %bitcast.32, bf16[4,256,128]{2,1,0:T(8,128)(2,1)} %bitcast.34, bf16[4,256,128]{2,1,0:T(8,128)(2,1)} %bitcast.36, bf16[4,256,128]{2,1,0:T(8,128)(2,1)} %bitcast.40, ...), custom_call_target="tpu_custom_call" | custom-call | bytes 22140000 | tf_op jit(solution)/shard_map/row_stats/pallas_call | solution.py:305
  132.6 12.0 %grads.3 = (bf16[16,128,512]{2,1,0:T(8,128)(2,1)}, bf16[4,256,128]{2,1,0:T(8,128)(2,1)}, bf16[4,256,128]{2,1,0:T(8,128)(2,1)}, bf16[4,256,128]{2,1,0:T(8,128)(2,...) custom-call(s32[32]{0:T(128)} %get-tuple-element.42.slots_ref, ...), custom_call_target="tpu_custom_call" | custom-call | bytes 44280000 | tf_op jit(solution)/shard_map/grads/pallas_call | solution.py:389
  146.0 7.4 %all-to-all-start.3 = ((bf16[16,128,512]{2,1,0:T(8,128)(2,1)}), bf16[16,128,512]{2,1,0:T(8,128)(2,1)}, u32[]{:S(2)}, u32[]{:S(2)}) async-start(bf16[16,128,512]{2,1,0:T(8,128)(2,1)} %get-tuple-element.60), calls=%async_computation.3 | async-start | bytes 4194304 | tf_op jit(solution)/shard_map/all_to_all | solution.py:439
  160.0 11.5 %collective-permute-done.1 = bf16[4,128,2,128]{3,2,1,0:T(2,128)(2,1)S(1)} collective-permute-done((bf16[4,128,2,128]{3,2,1,0:T(2,128)(2,1)}, bf16[4,128,2,128]{3,2,1,0:T(2,128)(2,1)S(1)}, u32[]{:S(2)}, u32[]{:S(2)}) %collective-permute-start.1) | collective-permute-done | bytes 262176 | tf_op jit(solution)/shard_map/ppermute | solution.py:417
  171.5 7.2 %collective-permute-start.6 = (bf16[4,128,2,128]{3,2,1,0:T(2,128)(2,1)}, bf16[4,128,2,128]{3,2,1,0:T(2,128)(2,1)S(1)}, u32[]{:S(2)}, u32[]{:S(2)}) collective-permute-start(bf16[4,128,2,128]{3,2,1,0:T(2,128)(2,1)} %get-tuple-element.50), channel_id=1, source_target_pairs={{0,7},{1,6},{2,5},{3,4},{4,3},{5,2},{6,1},{7,0},{8,15},{9,14},{10,... | collective-permute-start | bytes 786440 | tf_op jit(solution)/shard_map/ppermute | solution.py:417
  180.5 14.1 %collective-permute-done.3 = bf16[4,128,2,128]{3,2,1,0:T(2,128)(2,1)S(1)} collective-permute-done((bf16[4,128,2,128]{3,2,1,0:T(2,128)(2,1)}, bf16[4,128,2,128]{3,2,1,0:T(2,128)(2,1)S(1)}, u32[]{:S(2)}, u32[]{:S(2)}) %collective-permute-start.3) | collective-permute-done | bytes 262176 | tf_op jit(solution)/shard_map/ppermute | solution.py:417
  194.6 6.6 %collective-permute-done.4 = bf16[4,128,2,128]{3,2,1,0:T(2,128)(2,1)S(1)} collective-permute-done((bf16[4,128,2,128]{3,2,1,0:T(2,128)(2,1)}, bf16[4,128,2,128]{3,2,1,0:T(2,128)(2,1)S(1)}, u32[]{:S(2)}, u32[]{:S(2)}) %collective-permute-start.4) | collective-permute-done | bytes 262176 | tf_op jit(solution)/shard_map/ppermute | solution.py:417
  206.4 5.7 %collective-permute-done.6 = bf16[4,128,2,128]{3,2,1,0:T(2,128)(2,1)S(1)} collective-permute-done((bf16[4,128,2,128]{3,2,1,0:T(2,128)(2,1)}, bf16[4,128,2,128]{3,2,1,0:T(2,128)(2,1)S(1)}, u32[]{:S(2)}, u32[]{:S(2)}) %collective-permute-start.6) | collective-permute-done | bytes 262176 | tf_op jit(solution)/shard_map/ppermute | solution.py:417
  212.8 5.7 %row_stats.2.refs_8_ = f32[4,3,8,128]{3,2,1,0:T(8,128)} custom-call(s32[32]{0:T(128)} %get-tuple-element.42.slots_ref, bf16[16,128,512]{2,1,0:T(8,128)(2,1)} %copy-done, bf16[4,256,128]{2,1,0:T(8,128)(2,1)} %bitcast.38, bf16[4,256,128]{2,1,0:T(8,128)(2,1)} %bitcast.42, bf16[4,256,128]{2,1,0:T(8,128)(2,1)} %bitcast.46, bf16[4,256,128]{2,1,0:T(8,128)(2,1)} %bitcast.50, ...), custom_call_target="tpu_custom_call" | custom-call | bytes 22140000 | tf_op jit(solution)/shard_map/row_stats/pallas_call | solution.py:305
  223.2 12.0 %grads.2 = (bf16[16,128,512]{2,1,0:T(8,128)(2,1)}, bf16[4,256,128]{2,1,0:T(8,128)(2,1)}, bf16[4,256,128]{2,1,0:T(8,128)(2,1)}, bf16[4,256,128]{2,1,0:T(8,128)(2,...) custom-call(s32[32]{0:T(128)} %get-tuple-element.42.slots_ref, ...), custom_call_target="tpu_custom_call" | custom-call | bytes 44280000 | tf_op jit(solution)/shard_map/grads/pallas_call | solution.py:389
  235.3 7.2 %all-to-all-start.1 = ((bf16[16,128,512]{2,1,0:T(8,128)(2,1)}), bf16[16,128,512]{2,1,0:T(8,128)(2,1)S(1)}, u32[]{:S(2)}, u32[]{:S(2)}) async-start(bf16[16,128,512]{2,1,0:T(8,128)(2,1)} %get-tuple-element.51), calls=%async_computation.1 | async-start | bytes 4194304 | tf_op jit(solution)/shard_map/all_to_all | solution.py:439
  245.4 15.2 %collective-permute-done.17.refs_2_ = bf16[4,128,2,128]{3,2,1,0:T(2,128)(2,1)S(1)} collective-permute-done((bf16[4,128,2,128]{3,2,1,0:T(2,128)(2,1)}, bf16[4,128,2,128]{3,2,1,0:T(2,128)(2,1)S(1)}, u32[]{:S(2)}, u32[]{:S(2)}) %collective-permute-start.17) | collective-permute-done | bytes 262176 | tf_op jit(solution)/shard_map/ppermute | solution.py:417
  269.1 5.8 %collective-permute-start.29 = (bf16[4,128,2,128]{3,2,1,0:T(2,128)(2,1)S(1)}, bf16[4,128,2,128]{3,2,1,0:T(2,128)(2,1)S(1)}, u32[]{:S(2)}, u32[]{:S(2)}) collective-permute-start(bf16[4,128,2,128]{3,2,1,0:T(2,128)(2,1)S(1)} %bitcast.62), channel_id=1, source_target_pairs={{0,7},{1,6},{2,5},{3,4},{4,3},{5,2},{6,1},{7,0},{8,15},{9,14},{10,... | collective-permute-start | bytes 786440 | tf_op jit(solution)/shard_map/ppermute | solution.py:417
  274.8 5.9 %collective-permute-done.25.refs_3_ = bf16[4,128,2,128]{3,2,1,0:T(2,128)(2,1)S(1)} collective-permute-done((bf16[4,128,2,128]{3,2,1,0:T(2,128)(2,1)S(1)}, bf16[4,128,2,128]{3,2,1,0:T(2,128)(2,1)S(1)}, u32[]{:S(2)}, u32[]{:S(2)}) %collective-permute-start.25) | collective-permute-done | bytes 262176 | tf_op jit(solution)/shard_map/ppermute | solution.py:417
  284.6 5.8 %collective-permute-done.27.refs_5_ = bf16[4,128,2,128]{3,2,1,0:T(2,128)(2,1)S(1)} collective-permute-done((bf16[4,128,2,128]{3,2,1,0:T(2,128)(2,1)S(1)}, bf16[4,128,2,128]{3,2,1,0:T(2,128)(2,1)S(1)}, u32[]{:S(2)}, u32[]{:S(2)}) %collective-permute-start.27) | collective-permute-done | bytes 262176 | tf_op jit(solution)/shard_map/ppermute | solution.py:417
  306.3 6.3 %collective-permute-done.20.refs_5_ = bf16[4,128,2,128]{3,2,1,0:T(2,128)(2,1)S(1)} collective-permute-done((bf16[4,128,2,128]{3,2,1,0:T(2,128)(2,1)}, bf16[4,128,2,128]{3,2,1,0:T(2,128)(2,1)S(1)}, u32[]{:S(2)}, u32[]{:S(2)}) %collective-permute-start.20) | collective-permute-done | bytes 262176 | tf_op jit(solution)/shard_map/ppermute | solution.py:417
  312.6 5.6 %collective-permute-done.21.refs_6_ = bf16[4,128,2,128]{3,2,1,0:T(2,128)(2,1)S(1)} collective-permute-done((bf16[4,128,2,128]{3,2,1,0:T(2,128)(2,1)}, bf16[4,128,2,128]{3,2,1,0:T(2,128)(2,1)S(1)}, u32[]{:S(2)}, u32[]{:S(2)}) %collective-permute-start.21) | collective-permute-done | bytes 262176 | tf_op jit(solution)/shard_map/ppermute | solution.py:417
  (132 shorter events, 96.1 us)
Async XLA Ops:
  3.1 54.0 %all-to-all-start.2 = ((bf16[16,128,512]{2,1,0:T(8,128)(2,1)}), bf16[16,128,512]{2,1,0:T(8,128)(2,1)S(1)}, u32[]{:S(2)}, u32[]{:S(2)}) async-start(bf16[16,128,512]{2,1,0:T(8,128)(2,1)} %pack_tokens.3), calls=%async_computation.2 | async-start | bytes 4194304 | tf_op jit(solution)/shard_map/all_to_all | solution.py:431
  58.4 86.2 %all-to-all-start = ((bf16[16,128,512]{2,1,0:T(8,128)(2,1)}), bf16[16,128,512]{2,1,0:T(8,128)(2,1)S(1)}, u32[]{:S(2)}, u32[]{:S(2)}) async-start(bf16[16,128,512]{2,1,0:T(8,128)(2,1)} %pack_tokens.2), calls=%async_computation | async-start | bytes 4194304 | tf_op jit(solution)/shard_map/all_to_all | solution.py:431
  66.7 23.7 %collective-permute-start.10 = (bf16[4,128,2,128]{3,2,1,0:T(2,128)(2,1)}, bf16[4,128,2,128]{3,2,1,0:T(2,128)(2,1)S(1)}, u32[]{:S(2)}, u32[]{:S(2)}) collective-permute-start(bf16[4,128,2,128]{3,2,1,0:T(2,128)(2,1)} %get-tuple-element.55), channel_id=1, source_target_pairs={{0,3},{1,2},{2,1},{3,0},{4,7},{5,6},{6,5},{7,4},{8,11},{9,10},{10,... | collective-permute-start | bytes 786440 | tf_op jit(solution)/shard_map/ppermute | solution.py:417
  68.2 36.4 %collective-permute-start.11 = (bf16[4,128,2,128]{3,2,1,0:T(2,128)(2,1)}, bf16[4,128,2,128]{3,2,1,0:T(2,128)(2,1)S(1)}, u32[]{:S(2)}, u32[]{:S(2)}) collective-permute-start(bf16[4,128,2,128]{3,2,1,0:T(2,128)(2,1)} %get-tuple-element.56), channel_id=1, source_target_pairs={{0,4},{1,5},{2,6},{3,7},{4,0},{5,1},{6,2},{7,3},{8,12},{9,13},{10,... | collective-permute-start | bytes 786440 | tf_op jit(solution)/shard_map/ppermute | solution.py:417
  68.5 42.8 %collective-permute-start.12 = (bf16[4,128,2,128]{3,2,1,0:T(2,128)(2,1)}, bf16[4,128,2,128]{3,2,1,0:T(2,128)(2,1)S(1)}, u32[]{:S(2)}, u32[]{:S(2)}) collective-permute-start(bf16[4,128,2,128]{3,2,1,0:T(2,128)(2,1)} %get-tuple-element.57), channel_id=1, source_target_pairs={{0,5},{1,4},{2,7},{3,6},{4,1},{5,0},{6,3},{7,2},{8,13},{9,12},{10,... | collective-permute-start | bytes 786440 | tf_op jit(solution)/shard_map/ppermute | solution.py:417
  69.9 46.6 %collective-permute-start.13 = (bf16[4,128,2,128]{3,2,1,0:T(2,128)(2,1)}, bf16[4,128,2,128]{3,2,1,0:T(2,128)(2,1)}, u32[]{:S(2)}, u32[]{:S(2)}) collective-permute-start(bf16[4,128,2,128]{3,2,1,0:T(2,128)(2,1)} %get-tuple-element.58), channel_id=1, source_target_pairs={{0,6},{1,7},{2,4},{3,5},{4,2},{5,3},{6,0},{7,1},{8,14},{9,15},{10,... | collective-permute-start | bytes 786440 | tf_op jit(solution)/shard_map/ppermute | solution.py:417
  81.4 40.7 %collective-permute-start.14 = (bf16[4,128,2,128]{3,2,1,0:T(2,128)(2,1)}, bf16[4,128,2,128]{3,2,1,0:T(2,128)(2,1)}, u32[]{:S(2)}, u32[]{:S(2)}) collective-permute-start(bf16[4,128,2,128]{3,2,1,0:T(2,128)(2,1)} %get-tuple-element.59), channel_id=1, source_target_pairs={{0,7},{1,6},{2,5},{3,4},{4,3},{5,2},{6,1},{7,0},{8,15},{9,14},{10,... | collective-permute-start | bytes 786440 | tf_op jit(solution)/shard_map/ppermute | solution.py:417
  146.0 89.3 %all-to-all-start.3 = ((bf16[16,128,512]{2,1,0:T(8,128)(2,1)}), bf16[16,128,512]{2,1,0:T(8,128)(2,1)}, u32[]{:S(2)}, u32[]{:S(2)}) async-start(bf16[16,128,512]{2,1,0:T(8,128)(2,1)} %get-tuple-element.60), calls=%async_computation.3 | async-start | bytes 4194304 | tf_op jit(solution)/shard_map/all_to_all | solution.py:439
  156.7 23.8 %collective-permute-start.2 = (bf16[4,128,2,128]{3,2,1,0:T(2,128)(2,1)}, bf16[4,128,2,128]{3,2,1,0:T(2,128)(2,1)S(1)}, u32[]{:S(2)}, u32[]{:S(2)}) collective-permute-start(bf16[4,128,2,128]{3,2,1,0:T(2,128)(2,1)} %get-tuple-element.46), channel_id=1, source_target_pairs={{0,3},{1,2},{2,1},{3,0},{4,7},{5,6},{6,5},{7,4},{8,11},{9,10},{10,... | collective-permute-start | bytes 786440 | tf_op jit(solution)/shard_map/ppermute | solution.py:417
  158.3 36.4 %collective-permute-start.3 = (bf16[4,128,2,128]{3,2,1,0:T(2,128)(2,1)}, bf16[4,128,2,128]{3,2,1,0:T(2,128)(2,1)S(1)}, u32[]{:S(2)}, u32[]{:S(2)}) collective-permute-start(bf16[4,128,2,128]{3,2,1,0:T(2,128)(2,1)} %get-tuple-element.47), channel_id=1, source_target_pairs={{0,4},{1,5},{2,6},{3,7},{4,0},{5,1},{6,2},{7,3},{8,12},{9,13},{10,... | collective-permute-start | bytes 786440 | tf_op jit(solution)/shard_map/ppermute | solution.py:417
  158.5 42.7 %collective-permute-start.4 = (bf16[4,128,2,128]{3,2,1,0:T(2,128)(2,1)}, bf16[4,128,2,128]{3,2,1,0:T(2,128)(2,1)S(1)}, u32[]{:S(2)}, u32[]{:S(2)}) collective-permute-start(bf16[4,128,2,128]{3,2,1,0:T(2,128)(2,1)} %get-tuple-element.48), channel_id=1, source_target_pairs={{0,5},{1,4},{2,7},{3,6},{4,1},{5,0},{6,3},{7,2},{8,13},{9,12},{10,... | collective-permute-start | bytes 786440 | tf_op jit(solution)/shard_map/ppermute | solution.py:417
  160.0 46.4 %collective-permute-start.5 = (bf16[4,128,2,128]{3,2,1,0:T(2,128)(2,1)}, bf16[4,128,2,128]{3,2,1,0:T(2,128)(2,1)S(1)}, u32[]{:S(2)}, u32[]{:S(2)}) collective-permute-start(bf16[4,128,2,128]{3,2,1,0:T(2,128)(2,1)} %get-tuple-element.49), channel_id=1, source_target_pairs={{0,6},{1,7},{2,4},{3,5},{4,2},{5,3},{6,0},{7,1},{8,14},{9,15},{10,... | collective-permute-start | bytes 786440 | tf_op jit(solution)/shard_map/ppermute | solution.py:417
  171.5 40.6 %collective-permute-start.6 = (bf16[4,128,2,128]{3,2,1,0:T(2,128)(2,1)}, bf16[4,128,2,128]{3,2,1,0:T(2,128)(2,1)S(1)}, u32[]{:S(2)}, u32[]{:S(2)}) collective-permute-start(bf16[4,128,2,128]{3,2,1,0:T(2,128)(2,1)} %get-tuple-element.50), channel_id=1, source_target_pairs={{0,7},{1,6},{2,5},{3,4},{4,3},{5,2},{6,1},{7,0},{8,15},{9,14},{10,... | collective-permute-start | bytes 786440 | tf_op jit(solution)/shard_map/ppermute | solution.py:417
  235.3 94.5 %all-to-all-start.1 = ((bf16[16,128,512]{2,1,0:T(8,128)(2,1)}), bf16[16,128,512]{2,1,0:T(8,128)(2,1)S(1)}, u32[]{:S(2)}, u32[]{:S(2)}) async-start(bf16[16,128,512]{2,1,0:T(8,128)(2,1)} %get-tuple-element.51), calls=%async_computation.1 | async-start | bytes 4194304 | tf_op jit(solution)/shard_map/all_to_all | solution.py:439
  243.2 22.9 %collective-permute-start.23 = (bf16[4,128,2,128]{3,2,1,0:T(2,128)(2,1)}, bf16[4,128,2,128]{3,2,1,0:T(2,128)(2,1)S(1)}, u32[]{:S(2)}, u32[]{:S(2)}) collective-permute-start(bf16[4,128,2,128]{3,2,1,0:T(2,128)(2,1)} %bitcast.68), channel_id=1, source_target_pairs={{0,1},{1,0},{2,3},{3,2},{4,5},{5,4},{6,7},{7,6},{8,9},{9,8},{10,11... | collective-permute-start | bytes 786440 | tf_op jit(solution)/shard_map/ppermute | solution.py:417
  243.6 25.4 %collective-permute-start.24 = (bf16[4,128,2,128]{3,2,1,0:T(2,128)(2,1)}, bf16[4,128,2,128]{3,2,1,0:T(2,128)(2,1)S(1)}, u32[]{:S(2)}, u32[]{:S(2)}) collective-permute-start(bf16[4,128,2,128]{3,2,1,0:T(2,128)(2,1)} %bitcast.67), channel_id=1, source_target_pairs={{0,2},{1,3},{2,0},{3,1},{4,6},{5,7},{6,4},{7,5},{8,10},{9,11},{10,... | collective-permute-start | bytes 786440 | tf_op jit(solution)/shard_map/ppermute | solution.py:417
  244.8 36.0 %collective-permute-start.25 = (bf16[4,128,2,128]{3,2,1,0:T(2,128)(2,1)S(1)}, bf16[4,128,2,128]{3,2,1,0:T(2,128)(2,1)S(1)}, u32[]{:S(2)}, u32[]{:S(2)}) collective-permute-start(bf16[4,128,2,128]{3,2,1,0:T(2,128)(2,1)S(1)} %bitcast.66), channel_id=1, source_target_pairs={{0,3},{1,2},{2,1},{3,0},{4,7},{5,6},{6,5},{7,4},{8,11},{9,10},{10,... | collective-permute-start | bytes 786440 | tf_op jit(solution)/shard_map/ppermute | solution.py:417
  245.3 38.5 %collective-permute-start.26 = (bf16[4,128,2,128]{3,2,1,0:T(2,128)(2,1)S(1)}, bf16[4,128,2,128]{3,2,1,0:T(2,128)(2,1)S(1)}, u32[]{:S(2)}, u32[]{:S(2)}) collective-permute-start(bf16[4,128,2,128]{3,2,1,0:T(2,128)(2,1)S(1)} %bitcast.65), channel_id=1, source_target_pairs={{0,4},{1,5},{2,6},{3,7},{4,0},{5,1},{6,2},{7,3},{8,12},{9,13},{10,... | collective-permute-start | bytes 786440 | tf_op jit(solution)/shard_map/ppermute | solution.py:417
  260.7 29.7 %collective-permute-start.27 = (bf16[4,128,2,128]{3,2,1,0:T(2,128)(2,1)S(1)}, bf16[4,128,2,128]{3,2,1,0:T(2,128)(2,1)S(1)}, u32[]{:S(2)}, u32[]{:S(2)}) collective-permute-start(bf16[4,128,2,128]{3,2,1,0:T(2,128)(2,1)S(1)} %bitcast.64), channel_id=1, source_target_pairs={{0,5},{1,4},{2,7},{3,6},{4,1},{5,0},{6,3},{7,2},{8,13},{9,12},{10,... | collective-permute-start | bytes 786440 | tf_op jit(solution)/shard_map/ppermute | solution.py:417
  266.1 29.7 %collective-permute-start.28 = (bf16[4,128,2,128]{3,2,1,0:T(2,128)(2,1)S(1)}, bf16[4,128,2,128]{3,2,1,0:T(2,128)(2,1)S(1)}, u32[]{:S(2)}, u32[]{:S(2)}) collective-permute-start(bf16[4,128,2,128]{3,2,1,0:T(2,128)(2,1)S(1)} %bitcast.63), channel_id=1, source_target_pairs={{0,6},{1,7},{2,4},{3,5},{4,2},{5,3},{6,0},{7,1},{8,14},{9,15},{10,... | collective-permute-start | bytes 786440 | tf_op jit(solution)/shard_map/ppermute | solution.py:417
  269.1 32.4 %collective-permute-start.29 = (bf16[4,128,2,128]{3,2,1,0:T(2,128)(2,1)S(1)}, bf16[4,128,2,128]{3,2,1,0:T(2,128)(2,1)S(1)}, u32[]{:S(2)}, u32[]{:S(2)}) collective-permute-start(bf16[4,128,2,128]{3,2,1,0:T(2,128)(2,1)S(1)} %bitcast.62), channel_id=1, source_target_pairs={{0,7},{1,6},{2,5},{3,4},{4,3},{5,2},{6,1},{7,0},{8,15},{9,14},{10,... | collective-permute-start | bytes 786440 | tf_op jit(solution)/shard_map/ppermute | solution.py:417
  280.8 24.5 %collective-permute-start.18 = (bf16[4,128,2,128]{3,2,1,0:T(2,128)(2,1)}, bf16[4,128,2,128]{3,2,1,0:T(2,128)(2,1)S(1)}, u32[]{:S(2)}, u32[]{:S(2)}) collective-permute-start(bf16[4,128,2,128]{3,2,1,0:T(2,128)(2,1)} %bitcast.73), channel_id=1, source_target_pairs={{0,3},{1,2},{2,1},{3,0},{4,7},{5,6},{6,5},{7,4},{8,11},{9,10},{10,... | collective-permute-start | bytes 786440 | tf_op jit(solution)/shard_map/ppermute | solution.py:417
  283.8 22.5 %collective-permute-start.19 = (bf16[4,128,2,128]{3,2,1,0:T(2,128)(2,1)}, bf16[4,128,2,128]{3,2,1,0:T(2,128)(2,1)S(1)}, u32[]{:S(2)}, u32[]{:S(2)}) collective-permute-start(bf16[4,128,2,128]{3,2,1,0:T(2,128)(2,1)} %bitcast.72), channel_id=1, source_target_pairs={{0,4},{1,5},{2,6},{3,7},{4,0},{5,1},{6,2},{7,3},{8,12},{9,13},{10,... | collective-permute-start | bytes 786440 | tf_op jit(solution)/shard_map/ppermute | solution.py:417
  295.8 22.5 %collective-permute-start.21 = (bf16[4,128,2,128]{3,2,1,0:T(2,128)(2,1)}, bf16[4,128,2,128]{3,2,1,0:T(2,128)(2,1)S(1)}, u32[]{:S(2)}, u32[]{:S(2)}) collective-permute-start(bf16[4,128,2,128]{3,2,1,0:T(2,128)(2,1)} %bitcast.70), channel_id=1, source_target_pairs={{0,6},{1,7},{2,4},{3,5},{4,2},{5,3},{6,0},{7,1},{8,14},{9,15},{10,... | collective-permute-start | bytes 786440 | tf_op jit(solution)/shard_map/ppermute | solution.py:417
  (47 other events, 852.8 us)

commit v5 on v2

v5 whole, which is shorter than its diff:
```python
import math

import jax
import jax.numpy as jnp
from jax import lax
from jax.experimental import pallas as pl
from jax.experimental.pallas import tpu as pltpu
from jax.sharding import PartitionSpec as P

HD = 128
SPAN = 64
NTOK = 128
CHUNKS = 2
F32 = jnp.float32
BF16 = jnp.bfloat16
ANY = pl.BlockSpec(memory_space=pl.ANY)
LIMIT = pltpu.CompilerParams(vmem_limit_bytes=56 * 2**20)


def dot(a, b, dims):
    return lax.dot_general(a, b, (dims, ((), ())), preferred_element_type=F32)


NT = ((1,), (1,))
NN = ((1,), (0,))
TN = ((0,), (0,))


def cost(microseconds):
    return pl.CostEstimate(
        flops=0, bytes_accessed=int(microseconds * 3.69e6), transcendentals=0
    )


def vmem(*shape):
    return pltpu.VMEM(shape, BF16)


def partner(half, step):
    return lax.rem(lax.axis_index("fsdp"), half) ^ step


def cost(microseconds):
    return pl.CostEstimate(
        flops=0, bytes_accessed=int(microseconds * 3.69e6), transcendentals=0
    )


def pack(queries, out_grad, neighbours, devices, chunk, chunks):
    half = devices // 2
    heads = neighbours.shape[2] // HD // half // chunks
    width = heads * HD

    def kernel(q_ref, g_ref, n_ref, *refs):
        near, far, refs = refs[:half], refs[half : 2 * half], refs[2 * half :]
        plain, tokens, rows, come_t, come_r, go_n, go_f, go_r = refs
        first = [pl.multiple_of((partner(half, k) * chunks + chunk) * width, width) for k in range(half)]
        order = range(half - 1, -1, -1)
        token_loads = [
            [
                pltpu.make_async_copy(
                    ref.at[:, pl.ds(first[k], width)],
                    plain.at[k, pl.ds(part * SPAN, SPAN)],
                    come_t.at[k, part],
                )
                for part, ref in enumerate((q_ref, g_ref))
            ]
            for k in range(half)
        ]
        row_loads = [
            pltpu.make_async_copy(n_ref.at[:, :, pl.ds(first[k], width)], rows.at[k], come_r.at[k])
            for k in range(half)
        ]
        for k in order:
            for load in token_loads[k]:
                load.start()
        for k in order:
            row_loads[k].start()
        stores = []
        for k in order:
            for load in token_loads[k]:
                load.wait()
            for h in range(heads):
                folded = tokens.at[k, h].reshape(2 * SPAN, HD)
                folded[...] = plain[k, :, pl.ds(h * HD, HD)]
            stores.append(pltpu.make_async_copy(tokens.at[k], far[k], go_f.at[k]))
            stores.append(pltpu.make_async_copy(tokens.at[k], near[k].at[:, pl.ds(0, SPAN)], go_n.at[k]))
            for store in stores[-2:]:
                store.start()
        for k in order:
            row_loads[k].wait()
            for h in range(heads):
                source = rows.at[k, :, :, pl.ds(h * HD, HD)]
                stores.append(
                    pltpu.make_async_copy(source, near[k].at[h, pl.ds(SPAN, NTOK)], go_r.at[k, h])
                )
                stores[-1].start()
        for store in stores:
            store.wait()

    near = jax.ShapeDtypeStruct((heads, SPAN + NTOK, 2, HD), BF16)
    far = jax.ShapeDtypeStruct((heads, SPAN, 2, HD), BF16)
    results = pl.pallas_call(
        kernel,
        in_specs=[ANY] * 3,
        out_specs=[ANY] * (2 * half),
        out_shape=[near] * half + [far] * half,
        scratch_shapes=[
            vmem(half, 2 * SPAN, width),
            vmem(half, heads, SPAN, 2, HD),
            vmem(half, NTOK, 2, width),
            pltpu.SemaphoreType.DMA((half, 2)),
            pltpu.SemaphoreType.DMA((half,)),
            pltpu.SemaphoreType.DMA((half,)),
            pltpu.SemaphoreType.DMA((half,)),
            pltpu.SemaphoreType.DMA((half, heads)),
        ],
        compiler_params=LIMIT,
        cost_estimate=cost(5),
        name="pack",
    )(queries, out_grad, neighbours)
    return list(results)


def unpack(blocks, before, chunk, chunks):
    half = len(blocks) // 2
    heads = blocks[0].shape[0]
    width = heads * HD
    flat = [block.reshape(heads, -1, HD) for block in blocks]

    def kernel(*refs):
        near, flat = refs[:half], refs[half : 3 * half]
        o_ref, q_ref, n_ref, rows, ins, outs, come_r, come_t, go_r, go_t = refs[-10:]
        first = [pl.multiple_of((partner(half, k) * chunks + chunk) * width, width) for k in range(half)]
        token_loads = [
            [
                pltpu.make_async_copy(
                    flat[b * half + k].at[:, pl.ds(0, 2 * SPAN)], ins.at[k, b], come_t.at[k, b]
                )
                for b in range(2)
            ]
            for k in range(half)
        ]
        row_loads = [
            [
                pltpu.make_async_copy(
                    near[k].at[h, pl.ds(SPAN, NTOK)],
                    rows.at[k, :, :, pl.ds(h * HD, HD)],
                    come_r.at[k, h],
                )
                for h in range(heads)
            ]
            for k in range(half)
        ]
        stores = []
        for k in range(half):
            for load in row_loads[k]:
                load.start()
        for k in range(half):
            for load in token_loads[k]:
                load.start()
        for k in range(half):
            for load in row_loads[k]:
                load.wait()
            target = n_ref.at[:, :, pl.ds(first[k], width)]
            stores.append(pltpu.make_async_copy(rows.at[k], target, go_r.at[k]))
            stores[-1].start()
        for k in range(half):
            for load in token_loads[k]:
                load.wait()
            for h in range(heads):
                total = ins[k, 0, h].astype(F32) + ins[k, 1, h].astype(F32)
                outs[k, :, pl.ds(h * HD, HD)] = total.astype(BF16)
            for part, ref in enumerate((o_ref, q_ref)):
                source = outs.at[k, pl.ds(part * SPAN, SPAN)]
                target = ref.at[:, pl.ds(first[k], width)]
                stores.append(pltpu.make_async_copy(source, target, go_t.at[k, part]))
                stores[-1].start()
        for store in stores:
            store.wait()

    token_shape = jax.ShapeDtypeStruct((SPAN, half * width * chunks), BF16)
    row_shape = jax.ShapeDtypeStruct((NTOK, 2, half * width * chunks), BF16)
    return pl.pallas_call(
        kernel,
        in_specs=[ANY] * (3 * half + len(before)),
        out_specs=[ANY] * 3,
        out_shape=[token_shape, token_shape, row_shape],
        input_output_aliases={3 * half + i: i for i in range(len(before))},
        scratch_shapes=[
            vmem(half, NTOK, 2, width),
            vmem(half, 2, heads, 2 * SPAN, HD),
            vmem(half, 2 * SPAN, width),
            pltpu.SemaphoreType.DMA((half, heads)),
            pltpu.SemaphoreType.DMA((half, 2)),
            pltpu.SemaphoreType.DMA((half,)),
            pltpu.SemaphoreType.DMA((half, 2)),
        ],
        compiler_params=LIMIT,
        cost_estimate=cost(5),
        name="unpack",
    )(*blocks[:half], *flat, *before)


def last_rows():
    rows = lax.broadcasted_iota(jnp.int32, (2 * SPAN, HD), 0)
    return lax.rem(rows, SPAN) == SPAN - 1


def arrange(blocks, raw, spans_ref):
    devices = len(blocks)
    me = lax.axis_index("fsdp")
    for k, block in enumerate(blocks):
        raw[me ^ k] = block[0, : 2 * SPAN]
    last = last_rows()
    for c in range(devices):
        own = raw[c].astype(F32)
        after = raw[c + 1].astype(F32) if c + 1 < devices else jnp.zeros_like(own)
        spans_ref[c] = jnp.where(last, own, after).astype(BF16)


def load_row(n_ref, words):
    words[...] = n_ref[0, 2 * SPAN :].astype(F32)
    keys = words[pl.ds(0, NTOK, stride=2), :].astype(BF16)
    values = words[pl.ds(1, NTOK, stride=2), :].astype(BF16)
    return keys, values


def pair(spans_ref, first, second, part):
    rows = pl.ds(part * SPAN, SPAN)
    return jnp.concatenate([spans_ref[first // 2, rows], spans_ref[second // 2, rows]], 0)


def slots_of(slots_ref, half, step):
    base = lax.axis_index("fsdp") // half * half
    local = partner(half, step)
    return local, slots_ref[2 * (base + local)], slots_ref[2 * (base + local) + 1]


def products(keys, values, queries, grads):
    scores = dot(keys, queries, NT) * (1.0 / math.sqrt(HD))
    return scores, dot(values, grads, NT)


def stats_kernel(slots_ref, *refs):
    half = (len(refs) - 4) // 2
    blocks, (out_ref, raw, spans_ref, words) = refs[: 2 * half], refs[2 * half :]
    arrange(blocks, raw, spans_ref)
    for step in range(half):
        local, first, second = slots_of(slots_ref, half, step)
        keys, values = load_row(blocks[step], words.at[step % 4])
        queries = pair(spans_ref, first, second, 0)
        grads = pair(spans_ref, first, second, 1)
        scores, prob_grad = products(keys, values, queries, grads)
        top = jnp.max(scores, 0, keepdims=True)
        power = jnp.exp(scores - top)
        out_ref[0, 0, pl.ds(local, 1)] = top
        out_ref[0, 1, pl.ds(local, 1)] = jnp.sum(power, 0, keepdims=True)
        out_ref[0, 2, pl.ds(local, 1)] = jnp.sum(power * prob_grad, 0, keepdims=True)


def block_specs(blocks):
    return [pl.BlockSpec((1,) + block.shape[1:], lambda h, slots: (h, 0, 0)) for block in blocks]


def row_stats(slots, blocks):
    devices = len(blocks)
    half = devices // 2
    heads = blocks[0].shape[0]
    return pl.pallas_call(
        stats_kernel,
        grid_spec=pltpu.PrefetchScalarGridSpec(
            num_scalar_prefetch=1,
            grid=(heads,),
            in_specs=block_specs(blocks),
            out_specs=pl.BlockSpec((1, 3, half, HD), lambda h, slots: (h, 0, 0, 0)),
            scratch_shapes=[
                vmem(devices, 2 * SPAN, HD),
                vmem(devices, 2 * SPAN, HD),
                pltpu.VMEM((4, 2 * NTOK, HD), F32),
            ],
        ),
        out_shape=jax.ShapeDtypeStruct((heads, 3, half, HD), F32),
        compiler_params=LIMIT,
        cost_estimate=cost(6),
        name="row_stats",
    )(slots, *blocks)


def grads_kernel(slots_ref, *refs):
    devices = (len(refs) - 7) // 2
    half = devices // 2
    blocks, refs = refs[:devices], refs[devices:]
    (own_ref, other_ref), refs = refs[:2], refs[2:]
    outs, (raw, spans_ref, words, by_slot, sums) = refs[:devices], refs[devices:]
    scale = 1.0 / math.sqrt(HD)
    arrange(blocks, raw, spans_ref)
    sums[...] = jnp.zeros_like(sums)
    base = lax.axis_index("fsdp") // half * half
    left = lax.broadcasted_iota(jnp.int32, (1, HD), 1) < SPAN
    for ref, start in ((own_ref, base), (other_ref, half - base)):
        for i in range(3):
            block = ref[0, i]
            turned = pltpu.roll(block, SPAN, 1)
            firsts = jnp.where(left, block, turned)
            seconds = jnp.where(left, turned, block)
            for r in range(half):
                by_slot[i, pl.ds(slots_ref[2 * (start + r)], 1)] = firsts[r : r + 1]
                by_slot[i, pl.ds(slots_ref[2 * (start + r) + 1], 1)] = seconds[r : r + 1]

    def spread(first, second):
        def mate(slot):
            return slot + 1 - 2 * lax.rem(slot, 2)

        own = [jnp.where(left, by_slot[i, pl.ds(first, 1)], by_slot[i, pl.ds(second, 1)]) for i in range(3)]
        first, second = mate(first), mate(second)
        other = [jnp.where(left, by_slot[i, pl.ds(first, 1)], by_slot[i, pl.ds(second, 1)]) for i in range(3)]
        top = jnp.maximum(own[0], other[0])
        here, there = jnp.exp(own[0] - top), jnp.exp(other[0] - top)
        inverse = 1.0 / (own[1] * here + other[1] * there)
        return top, inverse, (own[2] * here + other[2] * there) * inverse

    for step in range(half):
        _, first, second = slots_of(slots_ref, half, step)
        keys, values = load_row(blocks[step], words.at[step % 4])
        queries = pair(spans_ref, first, second, 0)
        grads = pair(spans_ref, first, second, 1)
        scores, prob_grad = products(keys, values, queries, grads)
        top, inverse, delta = spread(first, second)
        soft = jnp.exp(scores - top) * inverse
        weights = soft.astype(BF16)
        score_grad = (soft * (prob_grad - delta)).astype(BF16)
        joined = words.at[4 + step % 4]
        joined[pl.ds(0, NTOK, stride=2), :] = dot(score_grad, queries, NN) * scale
        joined[pl.ds(1, NTOK, stride=2), :] = dot(weights, grads, NN)
        outs[step][0, 2 * SPAN :] = joined[...].astype(BF16)
        attended = dot(weights, values, TN)
        query_grad = dot(score_grad, keys, TN) * scale
        for n, slot in enumerate((first, second)):
            piece = slice(n * SPAN, (n + 1) * SPAN)
            sums[slot // 2 + 1, :SPAN] += attended[piece]
            sums[slot // 2 + 1, SPAN:] += query_grad[piece]
    last = last_rows()
    me = lax.axis_index("fsdp")
    for k, out in enumerate(outs):
        d = me ^ k
        out[0, : 2 * SPAN] = jnp.where(last, sums[d + 1], sums[d]).astype(BF16)


def grads(slots, blocks, own, other):
    devices = len(blocks)
    half = devices // 2
    heads = blocks[0].shape[0]
    stats_block = pl.BlockSpec((1, 3, half, HD), lambda h, slots: (h, 0, 0, 0))
    results = pl.pallas_call(
        grads_kernel,
        grid_spec=pltpu.PrefetchScalarGridSpec(
            num_scalar_prefetch=1,
            grid=(heads,),
            in_specs=block_specs(blocks) + [stats_block, stats_block],
            out_specs=block_specs(blocks),
            scratch_shapes=[
                vmem(devices, 2 * SPAN, HD),
                vmem(devices, 2 * SPAN, HD),
                pltpu.VMEM((8, 2 * NTOK, HD), F32),
                pltpu.VMEM((3, 2 * devices, HD), F32),
                pltpu.VMEM((devices + 1, 2 * SPAN, HD), F32),
            ],
        ),
        out_shape=[jax.ShapeDtypeStruct(block.shape, BF16) for block in blocks],
        compiler_params=LIMIT,
        cost_estimate=cost(12),
        name="grads",
    )(slots, *blocks, own, other)
    return list(results)


def swap(blocks):
    devices = len(blocks)
    half = devices // 2
    order = []
    for k in range(half):
        order += [half + k, (k + half // 2) % half]
    moved = list(blocks)
    for k in order:
        if k:
            moved[k] = lax.ppermute(blocks[k], "fsdp", [(i, i ^ k) for i in range(devices)])
    return moved


def after(later, earlier):
    both = lax.optimization_barrier((later, earlier))
    return both[0], both[1]


def body(queries, out_grad, neighbours, neighbour_ids):
    devices = lax.axis_size("fsdp")
    half = devices // 2
    heads = queries.shape[1] // HD // half
    chunks = math.gcd(heads, CHUNKS)
    across = [(i, i ^ half) for i in range(devices)]
    slots = jnp.argsort(neighbour_ids, stable=True).astype(jnp.int32)

    def compute(blocks):
        blocks = [block.reshape(block.shape[0], -1, HD) for block in blocks]
        own = row_stats(slots, blocks)
        other = lax.ppermute(own, "fsdp", across)
        results = grads(slots, blocks, own, other)
        return [block.reshape(block.shape[0], -1, 2, HD) for block in results]

    arrived, results, back = [], [], []
    for chunk in range(chunks):
        blocks = pack(queries, out_grad, neighbours, devices, chunk, chunks)
        if arrived:
            blocks, arrived[-1] = after(blocks, arrived[-1])
        arrived.append(swap(blocks))
    for chunk in range(chunks):
        blocks = compute(arrived[chunk])
        if chunk == 0 and chunks > 1:
            blocks, arrived[-1] = after(blocks, arrived[-1])
        if back:
            blocks, back[-1] = after(blocks, back[-1])
        back.append(swap(blocks))
    outputs = ()
    for chunk in range(chunks):
        outputs = tuple(unpack(back[chunk], outputs, chunk, chunks))
    return outputs


def solution(mesh):
    in_specs = (
        P(("groups", "fsdp"), None),
        P(("groups", "fsdp"), None),
        P(("groups", "fsdp"), None, None),
        P("groups"),
    )
    out_specs = (
        P(("groups", "fsdp"), None),
        P(("groups", "fsdp"), None),
        P(("groups", "fsdp"), None, None),
    )
    return jax.shard_map(body, mesh=mesh, in_specs=in_specs, out_specs=out_specs, check_vma=False)
```

time: 613 us -> 348 us (0.57)
  Pallas kernels: 420 us -> 54.4 us
  starting transfers between devices: 38.5 us -> 104 us
  waiting for transfers between devices: 150 us -> 185 us
    pallas_call x3 -> x4, Pallas kernels: 389 us -> 16.8 us  [the longest x2 8.74 us: unpack(): pl.pallas_call(kernel, in_specs=[ANY] * (3 * half + len(before)), out_spe...]
    ppermute x15 -> x62, starting transfers between devices: 21.8 us -> 104 us  [the longest x60 102 us: swap(): lax.ppermute(blocks[k], 'fsdp', [(i, i ^ k) for i in range(devices)])]
    ppermute x15 -> x62, waiting for transfers between devices: 150 us -> 185 us  [the longest x60 178 us: swap(): lax.ppermute(blocks[k], 'fsdp', [(i, i ^ k) for i in range(devices)])]
    all_to_all x2 -> x0, starting transfers between devices: 16.8 us -> none  [the longest x1 10.2 us: body(): lax.all_to_all(token_grads, 'fsdp', split_axis=0, concat_axis=0, tiled=True)]
    pallas_call x1 -> x2, Pallas kernels: 21.3 us -> 25.5 us  [grads(): pl.pallas_call(grads_kernel, grid_spec=pltpu.PrefetchScalarGridSpec(num_s...]
  transfers between devices with their start and end apart: 17 -> 62, of which waited for: 10 -> 40; matrix products, arithmetic and copies ran while one was open for 0% -> 0% of each run, Pallas kernels for 21% -> 13%
where the time goes in v5:
time: 348 us; the launch traced here: 347 us
  waiting for transfers between devices  185 us (53%)
  starting transfers between devices  104 us (30%)
  Pallas kernels  54.4 us (16%)
    ppermute x60, waiting for transfers between devices, swap(): lax.ppermute(blocks[k], 'fsdp', [(i, i ^ k) for i in range(devices)])  178 us
    ppermute x60, starting transfers between devices, swap(): lax.ppermute(blocks[k], 'fsdp', [(i, i ^ k) for i in range(devices)])  102 us
    pallas_call x2, Pallas kernels, grads(): pl.pallas_call(grads_kernel, grid_spec=pltpu.PrefetchScalarGridSpec(num_s...  25.5 us
    pallas_call x2, Pallas kernels, row_stats(): pl.pallas_call(stats_kernel, grid_spec=pltpu.PrefetchScalarGridSpec(num_s...  12.1 us
    pallas_call x2, Pallas kernels, unpack(): pl.pallas_call(kernel, in_specs=[ANY] * (3 * half + len(before)), out_spe...  8.74 us
    pallas_call x2, Pallas kernels, pack(): pl.pallas_call(kernel, in_specs=[ANY] * 3, out_specs=[ANY] * (2 * half),...  8.08 us
  transfers between devices with their start and end apart: 62, of which 40 were waited for; matrix products, arithmetic and copies ran while one was open for 0% of the time, Pallas kernels for 13%

profile of v5, /device:TPU:15, one launch (start us, length us, event | category | flops | bytes accessed | tf_op | source)
XLA Modules:
  0.0 346.9 jit_solution(17660144925760651012)
XLA Ops:
  11.5 7.5 %collective-permute-done.7 = bf16[4,64,2,128]{3,2,1,0:T(2,128)(2,1)S(1)} collective-permute-done((bf16[4,64,2,128]{3,2,1,0:T(2,128)(2,1)}, bf16[4,64,2,128]{3,2,1,0:T(2,128)(2,1)S(1)}, u32[]{:S(2)}, u32[]{:S(2)}) %collective-permute-start.7) | collective-permute-done | bytes 131104 | tf_op jit(solution)/shard_map/ppermute | solution.py:387
  27.8 5.1 %collective-permute-done.10 = bf16[4,64,2,128]{3,2,1,0:T(2,128)(2,1)S(1)} collective-permute-done((bf16[4,64,2,128]{3,2,1,0:T(2,128)(2,1)}, bf16[4,64,2,128]{3,2,1,0:T(2,128)(2,1)S(1)}, u32[]{:S(2)}, u32[]{:S(2)}) %collective-permute-start.10) | collective-permute-done | bytes 131104 | tf_op jit(solution)/shard_map/ppermute | solution.py:387
  32.8 5.6 %collective-permute-done.11 = bf16[4,64,2,128]{3,2,1,0:T(2,128)(2,1)S(1)} collective-permute-done((bf16[4,64,2,128]{3,2,1,0:T(2,128)(2,1)}, bf16[4,64,2,128]{3,2,1,0:T(2,128)(2,1)S(1)}, u32[]{:S(2)}, u32[]{:S(2)}) %collective-permute-start.11) | collective-permute-done | bytes 131104 | tf_op jit(solution)/shard_map/ppermute | solution.py:387
  38.4 8.3 %collective-permute-start.14 = (bf16[4,64,2,128]{3,2,1,0:T(2,128)(2,1)}, bf16[4,64,2,128]{3,2,1,0:T(2,128)(2,1)S(1)}, u32[]{:S(2)}, u32[]{:S(2)}) collective-permute-start(bf16[4,64,2,128]{3,2,1,0:T(2,128)(2,1)} %get-tuple-element.199), channel_id=1, source_target_pairs={{0,15},{1,14},{2,13},{3,12},{4,11},{5,10},{6,9},{7,8},{8,7},{9,6},... | collective-permute-start | bytes 393224 | tf_op jit(solution)/shard_map/ppermute | solution.py:387
  60.9 9.5 %collective-permute-done.4 = bf16[4,192,2,128]{3,2,1,0:T(2,128)(2,1)S(1)} collective-permute-done((bf16[4,192,2,128]{3,2,1,0:T(2,128)(2,1)}, bf16[4,192,2,128]{3,2,1,0:T(2,128)(2,1)S(1)}, u32[]{:S(2)}, u32[]{:S(2)}) %collective-permute-start.4) | collective-permute-done | bytes 393248 | tf_op jit(solution)/shard_map/ppermute | solution.py:387
  70.3 4.9 %collective-permute-done.5 = bf16[4,192,2,128]{3,2,1,0:T(2,128)(2,1)S(1)} collective-permute-done((bf16[4,192,2,128]{3,2,1,0:T(2,128)(2,1)}, bf16[4,192,2,128]{3,2,1,0:T(2,128)(2,1)S(1)}, u32[]{:S(2)}, u32[]{:S(2)}) %collective-permute-start.5) | collective-permute-done | bytes 393248 | tf_op jit(solution)/shard_map/ppermute | solution.py:387
  75.2 10.9 %collective-permute-done.6 = bf16[4,192,2,128]{3,2,1,0:T(2,128)(2,1)S(1)} collective-permute-done((bf16[4,192,2,128]{3,2,1,0:T(2,128)(2,1)}, bf16[4,192,2,128]{3,2,1,0:T(2,128)(2,1)S(1)}, u32[]{:S(2)}, u32[]{:S(2)}) %collective-permute-start.6) | collective-permute-done | bytes 393248 | tf_op jit(solution)/shard_map/ppermute | solution.py:387
  91.9 6.2 %row_stats.2.refs_16_ = f32[4,3,8,128]{3,2,1,0:T(8,128)} custom-call(s32[32]{0:T(128)} %get-tuple-element.167.slots_ref, bf16[4,384,128]{2,1,0:T(8,128)(2,1)} %bitcast.110, bf16[4,384,128]{2,1,0:T(8,128)(2,1)} %bitcast.112, bf16[4,384,128]{2,1,0:T(8,128)(2,1)} %bitcast.114, bf16[4,384,128]{2,1,0:T(8,128)(2,1)} %bitcast.120, bf16[4,384,128]{2,1,0:T(8,128)(2,1)} %bitcast.124, ...), custom_call_target="tpu_custom_call" | custom-call | bytes 22140000 | tf_op jit(solution)/shard_map/row_stats/pallas_call | solution.py:270
  109.1 8.6 %collective-permute-start.28 = (bf16[4,64,2,128]{3,2,1,0:T(2,128)(2,1)S(1)}, bf16[4,64,2,128]{3,2,1,0:T(2,128)(2,1)S(1)}, u32[]{:S(2)}, u32[]{:S(2)}) collective-permute-start(bf16[4,64,2,128]{3,2,1,0:T(2,128)(2,1)S(1)} %copy-done.72), channel_id=1, source_target_pairs={{0,13},{1,12},{2,15},{3,14},{4,9},{5,8},{6,11},{7,10},{8,5},{9,4},... | collective-permute-start | bytes 393224 | tf_op jit(solution)/shard_map/ppermute | solution.py:387
  122.7 12.2 %collective-permute-start.30 = (bf16[4,64,2,128]{3,2,1,0:T(2,128)(2,1)S(1)}, bf16[4,64,2,128]{3,2,1,0:T(2,128)(2,1)S(1)}, u32[]{:S(2)}, u32[]{:S(2)}) collective-permute-start(bf16[4,64,2,128]{3,2,1,0:T(2,128)(2,1)S(1)} %copy-done.68), channel_id=1, source_target_pairs={{0,15},{1,14},{2,13},{3,12},{4,11},{5,10},{6,9},{7,8},{8,7},{9,6},... | collective-permute-start | bytes 393224 | tf_op jit(solution)/shard_map/ppermute | solution.py:387
  142.8 12.8 %grads.2 = (bf16[4,384,128]{2,1,0:T(8,128)(2,1)}, bf16[4,384,128]{2,1,0:T(8,128)(2,1)}, bf16[4,384,128]{2,1,0:T(8,128)(2,1)}, bf16[4,384,128]{2,1,0:T(8,128)(2,1...) custom-call(s32[32]{0:T(128)} %get-tuple-element.167.slots_ref, ...), custom_call_target="tpu_custom_call" | custom-call | bytes 44280000 | tf_op jit(solution)/shard_map/grads/pallas_call | solution.py:355
  163.7 10.3 %collective-permute-done.22 = bf16[4,192,2,128]{3,2,1,0:T(2,128)(2,1)S(1)} collective-permute-done((bf16[4,192,2,128]{3,2,1,0:T(2,128)(2,1)S(1)}, bf16[4,192,2,128]{3,2,1,0:T(2,128)(2,1)S(1)}, u32[]{:S(2)}, u32[]{:S(2)}) %collective-permute-start.22) | collective-permute-done | bytes 393248 | tf_op jit(solution)/shard_map/ppermute | solution.py:387
  177.2 5.9 %row_stats.3.refs_16_ = f32[4,3,8,128]{3,2,1,0:T(8,128)} custom-call(s32[32]{0:T(128)} %get-tuple-element.167.slots_ref, bf16[4,384,128]{2,1,0:T(8,128)(2,1)} %bitcast.104, bf16[4,384,128]{2,1,0:T(8,128)(2,1)} %bitcast.106, bf16[4,384,128]{2,1,0:T(8,128)(2,1)} %bitcast.108, bf16[4,384,128]{2,1,0:T(8,128)(2,1)} %bitcast.116, bf16[4,384,128]{2,1,0:T(8,128)(2,1)} %bitcast.118, ...), custom_call_target="tpu_custom_call" | custom-call | bytes 22140000 | tf_op jit(solution)/shard_map/row_stats/pallas_call | solution.py:270
  192.8 9.0 %collective-permute-done.41 = bf16[4,64,2,128]{3,2,1,0:T(2,128)(2,1)S(1)} collective-permute-done((bf16[4,64,2,128]{3,2,1,0:T(2,128)(2,1)S(1)}, bf16[4,64,2,128]{3,2,1,0:T(2,128)(2,1)S(1)}, u32[]{:S(2)}, u32[]{:S(2)}) %collective-permute-start.41) | collective-permute-done | bytes 131104 | tf_op jit(solution)/shard_map/ppermute | solution.py:387
  205.4 11.8 %collective-permute-done.43 = bf16[4,64,2,128]{3,2,1,0:T(2,128)(2,1)S(1)} collective-permute-done((bf16[4,64,2,128]{3,2,1,0:T(2,128)(2,1)S(1)}, bf16[4,64,2,128]{3,2,1,0:T(2,128)(2,1)S(1)}, u32[]{:S(2)}, u32[]{:S(2)}) %collective-permute-start.43) | collective-permute-done | bytes 131104 | tf_op jit(solution)/shard_map/ppermute | solution.py:387
  229.0 12.8 %grads.3 = (bf16[4,384,128]{2,1,0:T(8,128)(2,1)}, bf16[4,384,128]{2,1,0:T(8,128)(2,1)}, bf16[4,384,128]{2,1,0:T(8,128)(2,1)}, bf16[4,384,128]{2,1,0:T(8,128)(2,1...) custom-call(s32[32]{0:T(128)} %get-tuple-element.167.slots_ref, ...), custom_call_target="tpu_custom_call" | custom-call | bytes 44280000 | tf_op jit(solution)/shard_map/grads/pallas_call | solution.py:355
  243.3 7.4 %collective-permute-done.37.refs_6_ = bf16[4,192,2,128]{3,2,1,0:T(2,128)(2,1)S(1)} collective-permute-done((bf16[4,192,2,128]{3,2,1,0:T(2,128)(2,1)S(1)}, bf16[4,192,2,128]{3,2,1,0:T(2,128)(2,1)S(1)}, u32[]{:S(2)}, u32[]{:S(2)}) %collective-permute-start.37) | collective-permute-done | bytes 393248 | tf_op jit(solution)/shard_map/ppermute | solution.py:387
  250.7 9.3 %collective-permute-done.38.refs_7_ = bf16[4,192,2,128]{3,2,1,0:T(2,128)(2,1)S(1)} collective-permute-done((bf16[4,192,2,128]{3,2,1,0:T(2,128)(2,1)S(1)}, bf16[4,192,2,128]{3,2,1,0:T(2,128)(2,1)S(1)}, u32[]{:S(2)}, u32[]{:S(2)}) %collective-permute-start.38) | collective-permute-done | bytes 393248 | tf_op jit(solution)/shard_map/ppermute | solution.py:387
  264.4 7.8 %collective-permute-done.54 = bf16[4,64,2,128]{3,2,1,0:T(2,128)(2,1)S(1)} collective-permute-done((bf16[4,64,2,128]{3,2,1,0:T(2,128)(2,1)}, bf16[4,64,2,128]{3,2,1,0:T(2,128)(2,1)S(1)}, u32[]{:S(2)}, u32[]{:S(2)}) %collective-permute-start.54) | collective-permute-done | bytes 131104 | tf_op jit(solution)/shard_map/ppermute | solution.py:387
  277.0 6.2 %collective-permute-done.56 = bf16[4,64,2,128]{3,2,1,0:T(2,128)(2,1)S(1)} collective-permute-done((bf16[4,64,2,128]{3,2,1,0:T(2,128)(2,1)}, bf16[4,64,2,128]{3,2,1,0:T(2,128)(2,1)S(1)}, u32[]{:S(2)}, u32[]{:S(2)}) %collective-permute-start.56) | collective-permute-done | bytes 131104 | tf_op jit(solution)/shard_map/ppermute | solution.py:387
  290.3 10.7 %collective-permute-start.61 = (bf16[4,64,2,128]{3,2,1,0:T(2,128)(2,1)}, bf16[4,64,2,128]{3,2,1,0:T(2,128)(2,1)S(1)}, u32[]{:S(2)}, u32[]{:S(2)}) collective-permute-start(bf16[4,64,2,128]{3,2,1,0:T(2,128)(2,1)} %bitcast.204), channel_id=1, source_target_pairs={{0,15},{1,14},{2,13},{3,12},{4,11},{5,10},{6,9},{7,8},{8,7},{9,6},... | collective-permute-start | bytes 393224 | tf_op jit(solution)/shard_map/ppermute | solution.py:387
  316.2 9.5 %collective-permute-done.51.refs_5_ = bf16[4,192,2,128]{3,2,1,0:T(2,128)(2,1)S(1)} collective-permute-done((bf16[4,192,2,128]{3,2,1,0:T(2,128)(2,1)}, bf16[4,192,2,128]{3,2,1,0:T(2,128)(2,1)S(1)}, u32[]{:S(2)}, u32[]{:S(2)}) %collective-permute-start.51) | collective-permute-done | bytes 393248 | tf_op jit(solution)/shard_map/ppermute | solution.py:387
  325.7 6.1 %collective-permute-done.52.refs_6_ = bf16[4,192,2,128]{3,2,1,0:T(2,128)(2,1)S(1)} collective-permute-done((bf16[4,192,2,128]{3,2,1,0:T(2,128)(2,1)}, bf16[4,192,2,128]{3,2,1,0:T(2,128)(2,1)S(1)}, u32[]{:S(2)}, u32[]{:S(2)}) %collective-permute-start.52) | collective-permute-done | bytes 393248 | tf_op jit(solution)/shard_map/ppermute | solution.py:387
  331.8 9.8 %collective-permute-done.53.refs_7_ = bf16[4,192,2,128]{3,2,1,0:T(2,128)(2,1)S(1)} collective-permute-done((bf16[4,192,2,128]{3,2,1,0:T(2,128)(2,1)}, bf16[4,192,2,128]{3,2,1,0:T(2,128)(2,1)S(1)}, u32[]{:S(2)}, u32[]{:S(2)}) %collective-permute-start.53) | collective-permute-done | bytes 393248 | tf_op jit(solution)/shard_map/ppermute | solution.py:387
  (268 shorter events, 137.4 us)
Async XLA Ops:
  8.0 44.7 %collective-permute-start = (bf16[4,192,2,128]{3,2,1,0:T(2,128)(2,1)}, bf16[4,192,2,128]{3,2,1,0:T(2,128)(2,1)S(1)}, u32[]{:S(2)}, u32[]{:S(2)}) collective-permute-start(bf16[4,192,2,128]{3,2,1,0:T(2,128)(2,1)} %get-tuple-element.185), channel_id=1, source_target_pairs={{0,1},{1,0},{2,3},{3,2},{4,5},{5,4},{6,7},{7,6},{8,9},{9,8},{10,11... | collective-permute-start | bytes 1179656 | tf_op jit(solution)/shard_map/ppermute | solution.py:387
  8.0 46.4 %collective-permute-start.1 = (bf16[4,192,2,128]{3,2,1,0:T(2,128)(2,1)}, bf16[4,192,2,128]{3,2,1,0:T(2,128)(2,1)S(1)}, u32[]{:S(2)}, u32[]{:S(2)}) collective-permute-start(bf16[4,192,2,128]{3,2,1,0:T(2,128)(2,1)} %get-tuple-element.186), channel_id=1, source_target_pairs={{0,2},{1,3},{2,0},{3,1},{4,6},{5,7},{6,4},{7,5},{8,10},{9,11},{10,... | collective-permute-start | bytes 1179656 | tf_op jit(solution)/shard_map/ppermute | solution.py:387
  8.3 19.1 %collective-permute-start.9 = (bf16[4,64,2,128]{3,2,1,0:T(2,128)(2,1)}, bf16[4,64,2,128]{3,2,1,0:T(2,128)(2,1)S(1)}, u32[]{:S(2)}, u32[]{:S(2)}) collective-permute-start(bf16[4,64,2,128]{3,2,1,0:T(2,128)(2,1)} %get-tuple-element.194), channel_id=1, source_target_pairs={{0,10},{1,11},{2,8},{3,9},{4,14},{5,15},{6,12},{7,13},{8,2},{9,3},... | collective-permute-start | bytes 393224 | tf_op jit(solution)/shard_map/ppermute | solution.py:387
  27.4 20.4 %collective-permute-start.12 = (bf16[4,64,2,128]{3,2,1,0:T(2,128)(2,1)}, bf16[4,64,2,128]{3,2,1,0:T(2,128)(2,1)S(1)}, u32[]{:S(2)}, u32[]{:S(2)}) collective-permute-start(bf16[4,64,2,128]{3,2,1,0:T(2,128)(2,1)} %get-tuple-element.197), channel_id=1, source_target_pairs={{0,13},{1,12},{2,15},{3,14},{4,9},{5,8},{6,11},{7,10},{8,5},{9,4},... | collective-permute-start | bytes 393224 | tf_op jit(solution)/shard_map/ppermute | solution.py:387
  52.7 22.5 %collective-permute-start.5 = (bf16[4,192,2,128]{3,2,1,0:T(2,128)(2,1)}, bf16[4,192,2,128]{3,2,1,0:T(2,128)(2,1)S(1)}, u32[]{:S(2)}, u32[]{:S(2)}) collective-permute-start(bf16[4,192,2,128]{3,2,1,0:T(2,128)(2,1)} %get-tuple-element.190), channel_id=1, source_target_pairs={{0,6},{1,7},{2,4},{3,5},{4,2},{5,3},{6,0},{7,1},{8,14},{9,15},{10,... | collective-permute-start | bytes 1179656 | tf_op jit(solution)/shard_map/ppermute | solution.py:387
  54.5 31.6 %collective-permute-start.6 = (bf16[4,192,2,128]{3,2,1,0:T(2,128)(2,1)}, bf16[4,192,2,128]{3,2,1,0:T(2,128)(2,1)S(1)}, u32[]{:S(2)}, u32[]{:S(2)}) collective-permute-start(bf16[4,192,2,128]{3,2,1,0:T(2,128)(2,1)} %get-tuple-element.191), channel_id=1, source_target_pairs={{0,7},{1,6},{2,5},{3,4},{4,3},{5,2},{6,1},{7,0},{8,15},{9,14},{10,... | collective-permute-start | bytes 1179656 | tf_op jit(solution)/shard_map/ppermute | solution.py:387
  88.9 51.8 %collective-permute-start.16 = (bf16[4,192,2,128]{3,2,1,0:T(2,128)(2,1)}, bf16[4,192,2,128]{3,2,1,0:T(2,128)(2,1)S(1)}, u32[]{:S(2)}, u32[]{:S(2)}) collective-permute-start(bf16[4,192,2,128]{3,2,1,0:T(2,128)(2,1)} %get-tuple-element.233), channel_id=1, source_target_pairs={{0,1},{1,0},{2,3},{3,2},{4,5},{5,4},{6,7},{7,6},{8,9},{9,8},{10,11... | collective-permute-start | bytes 1179656 | tf_op jit(solution)/shard_map/ppermute | solution.py:387
  89.3 53.0 %collective-permute-start.17 = (bf16[4,192,2,128]{3,2,1,0:T(2,128)(2,1)}, bf16[4,192,2,128]{3,2,1,0:T(2,128)(2,1)S(1)}, u32[]{:S(2)}, u32[]{:S(2)}) collective-permute-start(bf16[4,192,2,128]{3,2,1,0:T(2,128)(2,1)} %get-tuple-element.234), channel_id=1, source_target_pairs={{0,2},{1,3},{2,0},{3,1},{4,6},{5,7},{6,4},{7,5},{8,10},{9,11},{10,... | collective-permute-start | bytes 1179656 | tf_op jit(solution)/shard_map/ppermute | solution.py:387
  109.1 25.7 %collective-permute-start.28 = (bf16[4,64,2,128]{3,2,1,0:T(2,128)(2,1)S(1)}, bf16[4,64,2,128]{3,2,1,0:T(2,128)(2,1)S(1)}, u32[]{:S(2)}, u32[]{:S(2)}) collective-permute-start(bf16[4,64,2,128]{3,2,1,0:T(2,128)(2,1)S(1)} %copy-done.72), channel_id=1, source_target_pairs={{0,13},{1,12},{2,15},{3,14},{4,9},{5,8},{6,11},{7,10},{8,5},{9,4},... | collective-permute-start | bytes 393224 | tf_op jit(solution)/shard_map/ppermute | solution.py:387
  117.8 19.0 %collective-permute-start.29 = (bf16[4,64,2,128]{3,2,1,0:T(2,128)(2,1)S(1)}, bf16[4,64,2,128]{3,2,1,0:T(2,128)(2,1)S(1)}, u32[]{:S(2)}, u32[]{:S(2)}) collective-permute-start(bf16[4,64,2,128]{3,2,1,0:T(2,128)(2,1)S(1)} %copy-done.70), channel_id=1, source_target_pairs={{0,14},{1,15},{2,12},{3,13},{4,10},{5,11},{6,8},{7,9},{8,6},{9,7},... | collective-permute-start | bytes 393224 | tf_op jit(solution)/shard_map/ppermute | solution.py:387
  134.9 20.8 %collective-permute-start.18 = (bf16[4,192,2,128]{3,2,1,0:T(2,128)(2,1)}, bf16[4,192,2,128]{3,2,1,0:T(2,128)(2,1)S(1)}, u32[]{:S(2)}, u32[]{:S(2)}) collective-permute-start(bf16[4,192,2,128]{3,2,1,0:T(2,128)(2,1)} %get-tuple-element.235), channel_id=1, source_target_pairs={{0,3},{1,2},{2,1},{3,0},{4,7},{5,6},{6,5},{7,4},{8,11},{9,10},{10,... | collective-permute-start | bytes 1179656 | tf_op jit(solution)/shard_map/ppermute | solution.py:387
  140.7 23.0 %collective-permute-start.21 = (bf16[4,192,2,128]{3,2,1,0:T(2,128)(2,1)}, bf16[4,192,2,128]{3,2,1,0:T(2,128)(2,1)S(1)}, u32[]{:S(2)}, u32[]{:S(2)}) collective-permute-start(bf16[4,192,2,128]{3,2,1,0:T(2,128)(2,1)} %get-tuple-element.238), channel_id=1, source_target_pairs={{0,6},{1,7},{2,4},{3,5},{4,2},{5,3},{6,0},{7,1},{8,14},{9,15},{10,... | collective-permute-start | bytes 1179656 | tf_op jit(solution)/shard_map/ppermute | solution.py:387
  142.3 31.7 %collective-permute-start.22 = (bf16[4,192,2,128]{3,2,1,0:T(2,128)(2,1)S(1)}, bf16[4,192,2,128]{3,2,1,0:T(2,128)(2,1)S(1)}, u32[]{:S(2)}, u32[]{:S(2)}) collective-permute-start(bf16[4,192,2,128]{3,2,1,0:T(2,128)(2,1)S(1)} %copy-done.64), channel_id=1, source_target_pairs={{0,7},{1,6},{2,5},{3,4},{4,3},{5,2},{6,1},{7,0},{8,15},{9,14},{10,... | collective-permute-start | bytes 1179656 | tf_op jit(solution)/shard_map/ppermute | solution.py:387
  175.0 50.9 %collective-permute-start.32 = (bf16[4,192,2,128]{3,2,1,0:T(2,128)(2,1)}, bf16[4,192,2,128]{3,2,1,0:T(2,128)(2,1)S(1)}, u32[]{:S(2)}, u32[]{:S(2)}) collective-permute-start(bf16[4,192,2,128]{3,2,1,0:T(2,128)(2,1)} %bitcast.199), channel_id=1, source_target_pairs={{0,1},{1,0},{2,3},{3,2},{4,5},{5,4},{6,7},{7,6},{8,9},{9,8},{10,11... | collective-permute-start | bytes 1179656 | tf_op jit(solution)/shard_map/ppermute | solution.py:387
  176.7 51.8 %collective-permute-start.33 = (bf16[4,192,2,128]{3,2,1,0:T(2,128)(2,1)}, bf16[4,192,2,128]{3,2,1,0:T(2,128)(2,1)S(1)}, u32[]{:S(2)}, u32[]{:S(2)}) collective-permute-start(bf16[4,192,2,128]{3,2,1,0:T(2,128)(2,1)} %bitcast.198), channel_id=1, source_target_pairs={{0,2},{1,3},{2,0},{3,1},{4,6},{5,7},{6,4},{7,5},{8,10},{9,11},{10,... | collective-permute-start | bytes 1179656 | tf_op jit(solution)/shard_map/ppermute | solution.py:387
  192.2 25.1 %collective-permute-start.43 = (bf16[4,64,2,128]{3,2,1,0:T(2,128)(2,1)S(1)}, bf16[4,64,2,128]{3,2,1,0:T(2,128)(2,1)S(1)}, u32[]{:S(2)}, u32[]{:S(2)}) collective-permute-start(bf16[4,64,2,128]{3,2,1,0:T(2,128)(2,1)S(1)} %bitcast.207), channel_id=1, source_target_pairs={{0,12},{1,13},{2,14},{3,15},{4,8},{5,9},{6,10},{7,11},{8,4},{9,5},... | collective-permute-start | bytes 393224 | tf_op jit(solution)/shard_map/ppermute | solution.py:387
  220.1 21.7 %collective-permute-start.34 = (bf16[4,192,2,128]{3,2,1,0:T(2,128)(2,1)S(1)}, bf16[4,192,2,128]{3,2,1,0:T(2,128)(2,1)S(1)}, u32[]{:S(2)}, u32[]{:S(2)}) collective-permute-start(bf16[4,192,2,128]{3,2,1,0:T(2,128)(2,1)S(1)} %bitcast.192), channel_id=1, source_target_pairs={{0,3},{1,2},{2,1},{3,0},{4,7},{5,6},{6,5},{7,4},{8,11},{9,10},{10,... | collective-permute-start | bytes 1179656 | tf_op jit(solution)/shard_map/ppermute | solution.py:387
  225.9 24.7 %collective-permute-start.37 = (bf16[4,192,2,128]{3,2,1,0:T(2,128)(2,1)S(1)}, bf16[4,192,2,128]{3,2,1,0:T(2,128)(2,1)S(1)}, u32[]{:S(2)}, u32[]{:S(2)}) collective-permute-start(bf16[4,192,2,128]{3,2,1,0:T(2,128)(2,1)S(1)} %bitcast.189), channel_id=1, source_target_pairs={{0,6},{1,7},{2,4},{3,5},{4,2},{5,3},{6,0},{7,1},{8,14},{9,15},{10,... | collective-permute-start | bytes 1179656 | tf_op jit(solution)/shard_map/ppermute | solution.py:387
  228.5 31.4 %collective-permute-start.38 = (bf16[4,192,2,128]{3,2,1,0:T(2,128)(2,1)S(1)}, bf16[4,192,2,128]{3,2,1,0:T(2,128)(2,1)S(1)}, u32[]{:S(2)}, u32[]{:S(2)}) collective-permute-start(bf16[4,192,2,128]{3,2,1,0:T(2,128)(2,1)S(1)} %bitcast.188), channel_id=1, source_target_pairs={{0,7},{1,6},{2,5},{3,4},{4,3},{5,2},{6,1},{7,0},{8,15},{9,14},{10,... | collective-permute-start | bytes 1179656 | tf_op jit(solution)/shard_map/ppermute | solution.py:387
  262.0 45.5 %collective-permute-start.47 = (bf16[4,192,2,128]{3,2,1,0:T(2,128)(2,1)}, bf16[4,192,2,128]{3,2,1,0:T(2,128)(2,1)S(1)}, u32[]{:S(2)}, u32[]{:S(2)}) collective-permute-start(bf16[4,192,2,128]{3,2,1,0:T(2,128)(2,1)} %bitcast.201), channel_id=1, source_target_pairs={{0,1},{1,0},{2,3},{3,2},{4,5},{5,4},{6,7},{7,6},{8,9},{9,8},{10,11... | collective-permute-start | bytes 1179656 | tf_op jit(solution)/shard_map/ppermute | solution.py:387
  262.7 47.2 %collective-permute-start.48 = (bf16[4,192,2,128]{3,2,1,0:T(2,128)(2,1)}, bf16[4,192,2,128]{3,2,1,0:T(2,128)(2,1)S(1)}, u32[]{:S(2)}, u32[]{:S(2)}) collective-permute-start(bf16[4,192,2,128]{3,2,1,0:T(2,128)(2,1)} %bitcast.200), channel_id=1, source_target_pairs={{0,2},{1,3},{2,0},{3,1},{4,6},{5,7},{6,4},{7,5},{8,10},{9,11},{10,... | collective-permute-start | bytes 1179656 | tf_op jit(solution)/shard_map/ppermute | solution.py:387
  263.1 20.1 %collective-permute-start.56 = (bf16[4,64,2,128]{3,2,1,0:T(2,128)(2,1)}, bf16[4,64,2,128]{3,2,1,0:T(2,128)(2,1)S(1)}, u32[]{:S(2)}, u32[]{:S(2)}) collective-permute-start(bf16[4,64,2,128]{3,2,1,0:T(2,128)(2,1)} %bitcast.214), channel_id=1, source_target_pairs={{0,10},{1,11},{2,8},{3,9},{4,14},{5,15},{6,12},{7,13},{8,2},{9,3},... | collective-permute-start | bytes 393224 | tf_op jit(solution)/shard_map/ppermute | solution.py:387
  307.6 24.2 %collective-permute-start.52 = (bf16[4,192,2,128]{3,2,1,0:T(2,128)(2,1)}, bf16[4,192,2,128]{3,2,1,0:T(2,128)(2,1)S(1)}, u32[]{:S(2)}, u32[]{:S(2)}) collective-permute-start(bf16[4,192,2,128]{3,2,1,0:T(2,128)(2,1)} %bitcast.194), channel_id=1, source_target_pairs={{0,6},{1,7},{2,4},{3,5},{4,2},{5,3},{6,0},{7,1},{8,14},{9,15},{10,... | collective-permute-start | bytes 1179656 | tf_op jit(solution)/shard_map/ppermute | solution.py:387
  309.9 31.7 %collective-permute-start.53 = (bf16[4,192,2,128]{3,2,1,0:T(2,128)(2,1)}, bf16[4,192,2,128]{3,2,1,0:T(2,128)(2,1)S(1)}, u32[]{:S(2)}, u32[]{:S(2)}) collective-permute-start(bf16[4,192,2,128]{3,2,1,0:T(2,128)(2,1)} %bitcast.193), channel_id=1, source_target_pairs={{0,7},{1,6},{2,5},{3,4},{4,3},{5,2},{6,1},{7,0},{8,15},{9,14},{10,... | collective-permute-start | bytes 1179656 | tf_op jit(solution)/shard_map/ppermute | solution.py:387
  (117 other events, 4126.4 us)

commit v6 on v5

--- a/solution.py
+++ b/solution.py
@@ -11,6 +11,7 @@
 SPAN = 64
 NTOK = 128
 CHUNKS = 2
+WINDOW = 5
 F32 = jnp.float32
 BF16 = jnp.bfloat16
 ANY = pl.BlockSpec(memory_space=pl.ANY)
@@ -375,22 +376,29 @@
     return list(results)
 
 
-def swap(blocks):
+def turns(devices):
+    half, quarter = devices // 2, devices // 4
+    far = list(range(half, devices))
+    near = list(range(quarter, half))
+    inner = list(range(1, quarter))
+    order = []
+    while far or near or inner:
+        for kind in (far, near, far, inner):
+            if kind:
+                order.append(kind.pop(0))
+    return order
+
+
+def swap(blocks, flight):
     devices = len(blocks)
-    half = devices // 2
-    order = []
-    for k in range(half):
-        order += [half + k, (k + half // 2) % half]
     moved = list(blocks)
-    for k in order:
-        if k:
-            moved[k] = lax.ppermute(blocks[k], "fsdp", [(i, i ^ k) for i in range(devices)])
+    for k in turns(devices):
+        block = blocks[k]
+        if len(flight) >= WINDOW:
+            block, _ = lax.optimization_barrier((block, flight[-WINDOW]))
+        moved[k] = lax.ppermute(block, "fsdp", [(i, i ^ k) for i in range(devices)])
+        flight.append(moved[k])
     return moved
-
-
-def after(later, earlier):
-    both = lax.optimization_barrier((later, earlier))
-    return both[0], both[1]
 
 
 def body(queries, out_grad, neighbours, neighbour_ids):
@@ -408,19 +416,10 @@
         results = grads(slots, blocks, own, other)
         return [block.reshape(block.shape[0], -1, 2, HD) for block in results]
 
-    arrived, results, back = [], [], []
-    for chunk in range(chunks):
-        blocks = pack(queries, out_grad, neighbours, devices, chunk, chunks)
-        if arrived:
-            blocks, arrived[-1] = after(blocks, arrived[-1])
-        arrived.append(swap(blocks))
-    for chunk in range(chunks):
-        blocks = compute(arrived[chunk])
-        if chunk == 0 and chunks > 1:
-            blocks, arrived[-1] = after(blocks, arrived[-1])
-        if back:
-            blocks, back[-1] = after(blocks, back[-1])
-        back.append(swap(blocks))
+    flight = []
+    packed = [pack(queries, out_grad, neighbours, devices, chunk, chunks) for chunk in range(chunks)]
+    arrived = [swap(blocks, flight) for blocks in packed]
+    back = [swap(compute(blocks), flight) for blocks in arrived]
     outputs = ()
     for chunk in range(chunks):
         outputs = tuple(unpack(back[chunk], outputs, chunk, chunks))

time: 348 us -> 317 us (0.911)
  waiting for transfers between devices: 185 us -> 144 us
  starting transfers between devices: 104 us -> 112 us
    ppermute x60, waiting for transfers between devices: 178 us -> 142 us  [swap(): moved[k] = lax.ppermute(block, 'fsdp', [(i, i ^ k) for i in range(devices)])]
    ppermute x2, waiting for transfers between devices: 6.46 us -> 1.23 us  [compute(): other = lax.ppermute(own, 'fsdp', across)]
    ppermute x2, starting transfers between devices: 1.98 us -> 6.15 us  [compute(): other = lax.ppermute(own, 'fsdp', across)]
    ppermute x60, starting transfers between devices: 102 us -> 106 us  [swap(): moved[k] = lax.ppermute(block, 'fsdp', [(i, i ^ k) for i in range(devices)])]
  transfers between devices with their start and end apart: 62 -> 62, of which waited for: 40 -> 24; matrix products, arithmetic and copies ran while one was open for 0% -> 1% of each run, Pallas kernels for 13% -> 15%
where the time goes in v6:
time: 317 us; the launch traced here: 316 us
  waiting for transfers between devices  144 us (45%)
  starting transfers between devices  112 us (35%)
  Pallas kernels  54.6 us (17%)
    ppermute x60, waiting for transfers between devices, swap(): moved[k] = lax.ppermute(block, 'fsdp', [(i, i ^ k) for i in range(devices)])  142 us
    ppermute x60, starting transfers between devices, swap(): moved[k] = lax.ppermute(block, 'fsdp', [(i, i ^ k) for i in range(devices)])  106 us
    pallas_call x2, Pallas kernels, grads(): pl.pallas_call(grads_kernel, grid_spec=pltpu.PrefetchScalarGridSpec(num_s...  25.6 us
    pallas_call x2, Pallas kernels, row_stats(): pl.pallas_call(stats_kernel, grid_spec=pltpu.PrefetchScalarGridSpec(num_s...  12.2 us
    pallas_call x2, Pallas kernels, unpack(): pl.pallas_call(kernel, in_specs=[ANY] * (3 * half + len(before)), out_spe...  8.74 us
    pallas_call x2, Pallas kernels, pack(): pl.pallas_call(kernel, in_specs=[ANY] * 3, out_specs=[ANY] * (2 * half),...  8.07 us
  transfers between devices with their start and end apart: 62, of which 24 were waited for; matrix products, arithmetic and copies ran while one was open for 1% of the time, Pallas kernels for 15%

profile of v6, /device:TPU:15, one launch (start us, length us, event | category | flops | bytes accessed | tf_op | source)
XLA Modules:
  0.0 316.3 jit_solution(8161937731937653835)
XLA Ops:
  0.6 4.0 %pack.3 = (bf16[4,192,2,128]{3,2,1,0:T(2,128)(2,1)}, bf16[4,192,2,128]{3,2,1,0:T(2,128)(2,1)}, bf16[4,192,2,128]{3,2,1,0:T(2,128)(2,1)}, bf16[4,192,2,128]{3,2,1...) custom-call(bf16[64,8192]{1,0:T(8,128)(2,1)} %q_ref.3, ...), custom_call_target="tpu_custom_call" | custom-call | bytes 18450000 | tf_op jit(solution)/shard_map/pack/pallas_call | solution.py:104
  6.0 9.1 %collective-permute-done.9 = bf16[4,192,2,128]{3,2,1,0:T(2,128)(2,1)S(1)} collective-permute-done((bf16[4,192,2,128]{3,2,1,0:T(2,128)(2,1)}, bf16[4,192,2,128]{3,2,1,0:T(2,128)(2,1)S(1)}, u32[]{:S(2)}, u32[]{:S(2)}) %collective-permute-start.9) | collective-permute-done | bytes 393248 | tf_op jit(solution)/shard_map/ppermute | solution.py:399
  18.7 8.3 %collective-permute-done.10 = bf16[4,64,2,128]{3,2,1,0:T(2,128)(2,1)S(1)} collective-permute-done((bf16[4,64,2,128]{3,2,1,0:T(2,128)(2,1)}, bf16[4,64,2,128]{3,2,1,0:T(2,128)(2,1)S(1)}, u32[]{:S(2)}, u32[]{:S(2)}) %collective-permute-start.10) | collective-permute-done | bytes 131104 | tf_op jit(solution)/shard_map/ppermute | solution.py:399
  31.0 4.0 %pack.2 = (bf16[4,192,2,128]{3,2,1,0:T(2,128)(2,1)}, bf16[4,192,2,128]{3,2,1,0:T(2,128)(2,1)}, bf16[4,192,2,128]{3,2,1,0:T(2,128)(2,1)}, bf16[4,192,2,128]{3,2,1...) custom-call(bf16[64,8192]{1,0:T(8,128)(2,1)} %q_ref.3, ...), custom_call_target="tpu_custom_call" | custom-call | bytes 18450000 | tf_op jit(solution)/shard_map/pack/pallas_call | solution.py:104
  35.0 11.7 %collective-permute-done.11 = bf16[4,192,2,128]{3,2,1,0:T(2,128)(2,1)S(1)} collective-permute-done((bf16[4,192,2,128]{3,2,1,0:T(2,128)(2,1)}, bf16[4,192,2,128]{3,2,1,0:T(2,128)(2,1)S(1)}, u32[]{:S(2)}, u32[]{:S(2)}) %collective-permute-start.11) | collective-permute-done | bytes 393248 | tf_op jit(solution)/shard_map/ppermute | solution.py:399
  54.3 8.8 %collective-permute-done.20 = bf16[4,64,2,128]{3,2,1,0:T(2,128)(2,1)S(1)} collective-permute-done((bf16[4,64,2,128]{3,2,1,0:T(2,128)(2,1)S(1)}, bf16[4,64,2,128]{3,2,1,0:T(2,128)(2,1)S(1)}, u32[]{:S(2)}, u32[]{:S(2)}) %collective-permute-start.20) | collective-permute-done | bytes 131104 | tf_op jit(solution)/shard_map/ppermute | solution.py:399
  73.8 15.4 %collective-permute-done.13 = bf16[4,64,2,128]{3,2,1,0:T(2,128)(2,1)S(1)} collective-permute-done((bf16[4,64,2,128]{3,2,1,0:T(2,128)(2,1)}, bf16[4,64,2,128]{3,2,1,0:T(2,128)(2,1)S(1)}, u32[]{:S(2)}, u32[]{:S(2)}) %collective-permute-start.13) | collective-permute-done | bytes 131104 | tf_op jit(solution)/shard_map/ppermute | solution.py:399
  96.7 5.8 %collective-permute-done.22 = bf16[4,64,2,128]{3,2,1,0:T(2,128)(2,1)} collective-permute-done((bf16[4,64,2,128]{3,2,1,0:T(2,128)(2,1)S(1)}, bf16[4,64,2,128]{3,2,1,0:T(2,128)(2,1)}, u32[]{:S(2)}, u32[]{:S(2)}) %collective-permute-start.22) | collective-permute-done | bytes 131104 | tf_op jit(solution)/shard_map/ppermute | solution.py:399
  102.5 11.3 %collective-permute-start.23 = (bf16[4,64,2,128]{3,2,1,0:T(2,128)(2,1)}, bf16[4,64,2,128]{3,2,1,0:T(2,128)(2,1)}, u32[]{:S(2)}, u32[]{:S(2)}) collective-permute-start(bf16[4,64,2,128]{3,2,1,0:T(2,128)(2,1)} %get-tuple-element.171), channel_id=1, source_target_pairs={{0,10},{1,11},{2,8},{3,9},{4,14},{5,15},{6,12},{7,13},{8,2},{9,3},... | collective-permute-start | bytes 393224 | tf_op jit(solution)/shard_map/ppermute | solution.py:399
  115.8 4.4 %collective-permute-start.7 = (bf16[4,64,2,128]{3,2,1,0:T(2,128)(2,1)}, bf16[4,64,2,128]{3,2,1,0:T(2,128)(2,1)}, u32[]{:S(2)}, u32[]{:S(2)}) collective-permute-start(bf16[4,64,2,128]{3,2,1,0:T(2,128)(2,1)} %get-tuple-element.142), channel_id=1, source_target_pairs={{0,9},{1,8},{2,11},{3,10},{4,13},{5,12},{6,15},{7,14},{8,1},{9,0},... | collective-permute-start | bytes 393224 | tf_op jit(solution)/shard_map/ppermute | solution.py:399
  121.9 6.2 %row_stats.3.refs_16_ = f32[4,3,8,128]{3,2,1,0:T(8,128)} custom-call(s32[32]{0:T(128)} %get-tuple-element.126.slots_ref, bf16[4,384,128]{2,1,0:T(8,128)(2,1)} %bitcast.112, bf16[4,384,128]{2,1,0:T(8,128)(2,1)} %bitcast.116, bf16[4,384,128]{2,1,0:T(8,128)(2,1)} %bitcast.20.refs_2_, bf16[4,384,128]{2,1,0:T(8,128)(2,1)} %bitcast.118, ...), custom_call_target="tpu_custom_call" | custom-call | bytes 22140000 | tf_op jit(solution)/shard_map/row_stats/pallas_call | solution.py:271
  136.0 12.8 %grads.3 = (bf16[4,384,128]{2,1,0:T(8,128)(2,1)}, bf16[4,384,128]{2,1,0:T(8,128)(2,1)}, bf16[4,384,128]{2,1,0:T(8,128)(2,1)}, bf16[4,384,128]{2,1,0:T(8,128)(2,1...) custom-call(s32[32]{0:T(128)} %get-tuple-element.126.slots_ref, ...), custom_call_target="tpu_custom_call" | custom-call | bytes 44280000 | tf_op jit(solution)/shard_map/grads/pallas_call | solution.py:356
  156.2 3.9 %collective-permute-done.41.refs_4_ = bf16[4,192,2,128]{3,2,1,0:T(2,128)(2,1)S(1)} collective-permute-done((bf16[4,192,2,128]{3,2,1,0:T(2,128)(2,1)}, bf16[4,192,2,128]{3,2,1,0:T(2,128)(2,1)S(1)}, u32[]{:S(2)}, u32[]{:S(2)}) %collective-permute-start.41) | collective-permute-done | bytes 393248 | tf_op jit(solution)/shard_map/ppermute | solution.py:399
  160.2 12.6 %collective-permute-start.42 = (bf16[4,64,2,128]{3,2,1,0:T(2,128)(2,1)}, bf16[4,64,2,128]{3,2,1,0:T(2,128)(2,1)S(1)}, u32[]{:S(2)}, u32[]{:S(2)}) collective-permute-start(bf16[4,64,2,128]{3,2,1,0:T(2,128)(2,1)} %bitcast.200), channel_id=1, source_target_pairs={{0,11},{1,10},{2,9},{3,8},{4,15},{5,14},{6,13},{7,12},{8,3},{9,2},... | collective-permute-start | bytes 393224 | tf_op jit(solution)/shard_map/ppermute | solution.py:399
  175.9 11.8 %collective-permute-done.42 = bf16[4,64,2,128]{3,2,1,0:T(2,128)(2,1)S(1)} collective-permute-done((bf16[4,64,2,128]{3,2,1,0:T(2,128)(2,1)}, bf16[4,64,2,128]{3,2,1,0:T(2,128)(2,1)S(1)}, u32[]{:S(2)}, u32[]{:S(2)}) %collective-permute-start.42) | collective-permute-done | bytes 131104 | tf_op jit(solution)/shard_map/ppermute | solution.py:399
  192.0 6.0 %row_stats.2.refs_16_ = f32[4,3,8,128]{3,2,1,0:T(8,128)} custom-call(s32[32]{0:T(128)} %get-tuple-element.126.slots_ref, bf16[4,384,128]{2,1,0:T(8,128)(2,1)} %bitcast.102, bf16[4,384,128]{2,1,0:T(8,128)(2,1)} %bitcast.106, bf16[4,384,128]{2,1,0:T(8,128)(2,1)} %bitcast.126, bf16[4,384,128]{2,1,0:T(8,128)(2,1)} %bitcast.108, bf16[4,384,128]{2,1,0:T(8,128)(2,1)} %bitcast.104, ...), custom_call_target="tpu_custom_call" | custom-call | bytes 22140000 | tf_op jit(solution)/shard_map/row_stats/pallas_call | solution.py:271
  207.3 12.8 %grads.2 = (bf16[4,384,128]{2,1,0:T(8,128)(2,1)}, bf16[4,384,128]{2,1,0:T(8,128)(2,1)}, bf16[4,384,128]{2,1,0:T(8,128)(2,1)}, bf16[4,384,128]{2,1,0:T(8,128)(2,1...) custom-call(s32[32]{0:T(128)} %get-tuple-element.126.slots_ref, ...), custom_call_target="tpu_custom_call" | custom-call | bytes 44280000 | tf_op jit(solution)/shard_map/grads/pallas_call | solution.py:356
  228.3 10.6 %collective-permute-start.55 = (bf16[4,64,2,128]{3,2,1,0:T(2,128)(2,1)}, bf16[4,64,2,128]{3,2,1,0:T(2,128)(2,1)S(1)}, u32[]{:S(2)}, u32[]{:S(2)}) collective-permute-start(bf16[4,64,2,128]{3,2,1,0:T(2,128)(2,1)} %bitcast.203), channel_id=1, source_target_pairs={{0,10},{1,11},{2,8},{3,9},{4,14},{5,15},{6,12},{7,13},{8,2},{9,3},... | collective-permute-start | bytes 393224 | tf_op jit(solution)/shard_map/ppermute | solution.py:399
  242.4 5.9 %collective-permute-done.38 = bf16[4,64,2,128]{3,2,1,0:T(2,128)(2,1)S(1)} collective-permute-done((bf16[4,64,2,128]{3,2,1,0:T(2,128)(2,1)S(1)}, bf16[4,64,2,128]{3,2,1,0:T(2,128)(2,1)S(1)}, u32[]{:S(2)}, u32[]{:S(2)}) %collective-permute-start.38) | collective-permute-done | bytes 131104 | tf_op jit(solution)/shard_map/ppermute | solution.py:399
  251.0 5.7 %collective-permute-done.50 = bf16[4,64,2,128]{3,2,1,0:T(2,128)(2,1)S(1)} collective-permute-done((bf16[4,64,2,128]{3,2,1,0:T(2,128)(2,1)}, bf16[4,64,2,128]{3,2,1,0:T(2,128)(2,1)S(1)}, u32[]{:S(2)}, u32[]{:S(2)}) %collective-permute-start.50) | collective-permute-done | bytes 131104 | tf_op jit(solution)/shard_map/ppermute | solution.py:399
  265.5 19.9 %collective-permute-done.45 = bf16[4,64,2,128]{3,2,1,0:T(2,128)(2,1)S(1)} collective-permute-done((bf16[4,64,2,128]{3,2,1,0:T(2,128)(2,1)}, bf16[4,64,2,128]{3,2,1,0:T(2,128)(2,1)S(1)}, u32[]{:S(2)}, u32[]{:S(2)}) %collective-permute-start.45) | collective-permute-done | bytes 131104 | tf_op jit(solution)/shard_map/ppermute | solution.py:399
  292.3 4.4 %unpack.2 = (bf16[64,8192]{1,0:T(8,128)(2,1)}, bf16[64,8192]{1,0:T(8,128)(2,1)}, bf16[128,2,8192]{2,1,0:T(2,128)(2,1)}) custom-call(bf16[4,192,2,128]{3,2,1,0:T(2,128)(2,1)} %bitcast.94, bf16[4,192,2,128]{3,2,1,0:T(2,128)(2,1)} %copy-done.1, bf16[4,192,2,128]{3,2,1,0:T(2,128)(2,1)} %copy-done.6, bf16[4,192,2,128]{3,2,1,0:T(2,128)(2,1)} %copy-done.2, ...), custom_call_target="tpu_custom_call" | custom-call | bytes 18450000 | tf_op jit(solution)/shard_map/unpack/pallas_call | solution.py:185
  299.0 11.9 %collective-permute-done.61 = bf16[4,64,2,128]{3,2,1,0:T(2,128)(2,1)S(1)} collective-permute-done((bf16[4,64,2,128]{3,2,1,0:T(2,128)(2,1)}, bf16[4,64,2,128]{3,2,1,0:T(2,128)(2,1)S(1)}, u32[]{:S(2)}, u32[]{:S(2)}) %collective-permute-start.61) | collective-permute-done | bytes 131104 | tf_op jit(solution)/shard_map/ppermute | solution.py:399
  311.8 4.3 %unpack.3 = (bf16[64,8192]{1,0:T(8,128)(2,1)}, bf16[64,8192]{1,0:T(8,128)(2,1)}, bf16[128,2,8192]{2,1,0:T(2,128)(2,1)}) custom-call(bf16[4,192,2,128]{3,2,1,0:T(2,128)(2,1)} %bitcast.130, bf16[4,192,2,128]{3,2,1,0:T(2,128)(2,1)} %copy-done.20, bf16[4,192,2,128]{3,2,1,0:T(2,128)(2,1)} %copy-done.21, ...), custom_call_target="tpu_custom_call", output_to_operand_aliasing={{0}: (24, {}), {1}: (25, {}), {2}: (26, {})} | custom-call | bytes 18450000 | tf_op jit(solution)/shard_map/unpack/pallas_call | solution.py:185
  (262 shorter events, 103.1 us)
Async XLA Ops:
  46.7 23.4 %collective-permute-start.12 = (bf16[4,192,2,128]{3,2,1,0:T(2,128)(2,1)}, bf16[4,192,2,128]{3,2,1,0:T(2,128)(2,1)S(1)}, u32[]{:S(2)}, u32[]{:S(2)}) collective-permute-start(bf16[4,192,2,128]{3,2,1,0:T(2,128)(2,1)} %get-tuple-element.152), channel_id=1, source_target_pairs={{0,4},{1,5},{2,6},{3,7},{4,0},{5,1},{6,2},{7,3},{8,12},{9,13},{10,... | collective-permute-start | bytes 1179656 | tf_op jit(solution)/shard_map/ppermute | solution.py:399
  47.7 25.6 %collective-permute-start.3 = (bf16[4,192,2,128]{3,2,1,0:T(2,128)(2,1)}, bf16[4,192,2,128]{3,2,1,0:T(2,128)(2,1)S(1)}, u32[]{:S(2)}, u32[]{:S(2)}) collective-permute-start(bf16[4,192,2,128]{3,2,1,0:T(2,128)(2,1)} %get-tuple-element.134), channel_id=1, source_target_pairs={{0,1},{1,0},{2,3},{3,2},{4,5},{5,4},{6,7},{7,6},{8,9},{9,8},{10,11... | collective-permute-start | bytes 1179656 | tf_op jit(solution)/shard_map/ppermute | solution.py:399
  63.1 30.8 %collective-permute-start.21 = (bf16[4,192,2,128]{3,2,1,0:T(2,128)(2,1)S(1)}, bf16[4,192,2,128]{3,2,1,0:T(2,128)(2,1)S(1)}, u32[]{:S(2)}, u32[]{:S(2)}) collective-permute-start(bf16[4,192,2,128]{3,2,1,0:T(2,128)(2,1)S(1)} %copy-done.62), channel_id=1, source_target_pairs={{0,6},{1,7},{2,4},{3,5},{4,2},{5,3},{6,0},{7,1},{8,14},{9,15},{10,... | collective-permute-start | bytes 1179656 | tf_op jit(solution)/shard_map/ppermute | solution.py:399
  66.0 28.0 %collective-permute-start.16 = (bf16[4,192,2,128]{3,2,1,0:T(2,128)(2,1)S(1)}, bf16[4,192,2,128]{3,2,1,0:T(2,128)(2,1)}, u32[]{:S(2)}, u32[]{:S(2)}) collective-permute-start(bf16[4,192,2,128]{3,2,1,0:T(2,128)(2,1)S(1)} %copy-done.61), channel_id=1, source_target_pairs={{0,5},{1,4},{2,7},{3,6},{4,1},{5,0},{6,3},{7,2},{8,13},{9,12},{10,... | collective-permute-start | bytes 1179656 | tf_op jit(solution)/shard_map/ppermute | solution.py:399
  69.8 26.8 %collective-permute-start.5 = (bf16[4,192,2,128]{3,2,1,0:T(2,128)(2,1)S(1)}, bf16[4,192,2,128]{3,2,1,0:T(2,128)(2,1)}, u32[]{:S(2)}, u32[]{:S(2)}) collective-permute-start(bf16[4,192,2,128]{3,2,1,0:T(2,128)(2,1)S(1)} %copy-done.60), channel_id=1, source_target_pairs={{0,2},{1,3},{2,0},{3,1},{4,6},{5,7},{6,4},{7,5},{8,10},{9,11},{10,... | collective-permute-start | bytes 1179656 | tf_op jit(solution)/shard_map/ppermute | solution.py:399
  89.8 59.1 %collective-permute-start.14 = (bf16[4,192,2,128]{3,2,1,0:T(2,128)(2,1)}, bf16[4,192,2,128]{3,2,1,0:T(2,128)(2,1)S(1)}, u32[]{:S(2)}, u32[]{:S(2)}) collective-permute-start(bf16[4,192,2,128]{3,2,1,0:T(2,128)(2,1)} %get-tuple-element.154), channel_id=1, source_target_pairs={{0,3},{1,2},{2,1},{3,0},{4,7},{5,6},{6,5},{7,4},{8,11},{9,10},{10,... | collective-permute-start | bytes 1179656 | tf_op jit(solution)/shard_map/ppermute | solution.py:399
  91.3 58.6 %collective-permute-start.26 = (bf16[4,192,2,128]{3,2,1,0:T(2,128)(2,1)}, bf16[4,192,2,128]{3,2,1,0:T(2,128)(2,1)S(1)}, u32[]{:S(2)}, u32[]{:S(2)}) collective-permute-start(bf16[4,192,2,128]{3,2,1,0:T(2,128)(2,1)} %get-tuple-element.176), channel_id=1, source_target_pairs={{0,7},{1,6},{2,5},{3,4},{4,3},{5,2},{6,1},{7,0},{8,15},{9,14},{10,... | collective-permute-start | bytes 1179656 | tf_op jit(solution)/shard_map/ppermute | solution.py:399
  102.5 25.6 %collective-permute-start.23 = (bf16[4,64,2,128]{3,2,1,0:T(2,128)(2,1)}, bf16[4,64,2,128]{3,2,1,0:T(2,128)(2,1)}, u32[]{:S(2)}, u32[]{:S(2)}) collective-permute-start(bf16[4,64,2,128]{3,2,1,0:T(2,128)(2,1)} %get-tuple-element.171), channel_id=1, source_target_pairs={{0,10},{1,11},{2,8},{3,9},{4,14},{5,15},{6,12},{7,13},{8,2},{9,3},... | collective-permute-start | bytes 393224 | tf_op jit(solution)/shard_map/ppermute | solution.py:399
  149.9 22.9 %collective-permute-start.32 = (bf16[4,192,2,128]{3,2,1,0:T(2,128)(2,1)}, bf16[4,192,2,128]{3,2,1,0:T(2,128)(2,1)S(1)}, u32[]{:S(2)}, u32[]{:S(2)}) collective-permute-start(bf16[4,192,2,128]{3,2,1,0:T(2,128)(2,1)} %bitcast.186), channel_id=1, source_target_pairs={{0,1},{1,0},{2,3},{3,2},{4,5},{5,4},{6,7},{7,6},{8,9},{9,8},{10,11... | collective-permute-start | bytes 1179656 | tf_op jit(solution)/shard_map/ppermute | solution.py:399
  160.2 27.5 %collective-permute-start.42 = (bf16[4,64,2,128]{3,2,1,0:T(2,128)(2,1)}, bf16[4,64,2,128]{3,2,1,0:T(2,128)(2,1)S(1)}, u32[]{:S(2)}, u32[]{:S(2)}) collective-permute-start(bf16[4,64,2,128]{3,2,1,0:T(2,128)(2,1)} %bitcast.200), channel_id=1, source_target_pairs={{0,11},{1,10},{2,9},{3,8},{4,15},{5,14},{6,13},{7,12},{8,3},{9,2},... | collective-permute-start | bytes 393224 | tf_op jit(solution)/shard_map/ppermute | solution.py:399
  172.8 25.2 %collective-permute-start.52 = (bf16[4,64,2,128]{3,2,1,0:T(2,128)(2,1)}, bf16[4,64,2,128]{3,2,1,0:T(2,128)(2,1)S(1)}, u32[]{:S(2)}, u32[]{:S(2)}) collective-permute-start(bf16[4,64,2,128]{3,2,1,0:T(2,128)(2,1)} %bitcast.198), channel_id=1, source_target_pairs={{0,10},{1,11},{2,8},{3,9},{4,14},{5,15},{6,12},{7,13},{8,2},{9,3},... | collective-permute-start | bytes 393224 | tf_op jit(solution)/shard_map/ppermute | solution.py:399
  174.4 26.8 %collective-permute-start.47 = (bf16[4,64,2,128]{3,2,1,0:T(2,128)(2,1)}, bf16[4,64,2,128]{3,2,1,0:T(2,128)(2,1)S(1)}, u32[]{:S(2)}, u32[]{:S(2)}) collective-permute-start(bf16[4,64,2,128]{3,2,1,0:T(2,128)(2,1)} %bitcast.196), channel_id=1, source_target_pairs={{0,8},{1,9},{2,10},{3,11},{4,12},{5,13},{6,14},{7,15},{8,0},{9,1},... | collective-permute-start | bytes 393224 | tf_op jit(solution)/shard_map/ppermute | solution.py:399
  175.4 25.9 %collective-permute-start.36 = (bf16[4,64,2,128]{3,2,1,0:T(2,128)(2,1)}, bf16[4,64,2,128]{3,2,1,0:T(2,128)(2,1)S(1)}, u32[]{:S(2)}, u32[]{:S(2)}) collective-permute-start(bf16[4,64,2,128]{3,2,1,0:T(2,128)(2,1)} %bitcast.194), channel_id=1, source_target_pairs={{0,9},{1,8},{2,11},{3,10},{4,13},{5,12},{6,15},{7,14},{8,1},{9,0},... | collective-permute-start | bytes 393224 | tf_op jit(solution)/shard_map/ppermute | solution.py:399
  187.7 32.4 %collective-permute-start.43 = (bf16[4,192,2,128]{3,2,1,0:T(2,128)(2,1)}, bf16[4,192,2,128]{3,2,1,0:T(2,128)(2,1)S(1)}, u32[]{:S(2)}, u32[]{:S(2)}) collective-permute-start(bf16[4,192,2,128]{3,2,1,0:T(2,128)(2,1)} %bitcast.180), channel_id=1, source_target_pairs={{0,3},{1,2},{2,1},{3,0},{4,7},{5,6},{6,5},{7,4},{8,11},{9,10},{10,... | collective-permute-start | bytes 1179656 | tf_op jit(solution)/shard_map/ppermute | solution.py:399
  191.9 28.8 %collective-permute-start.34 = (bf16[4,192,2,128]{3,2,1,0:T(2,128)(2,1)}, bf16[4,192,2,128]{3,2,1,0:T(2,128)(2,1)S(1)}, u32[]{:S(2)}, u32[]{:S(2)}) collective-permute-start(bf16[4,192,2,128]{3,2,1,0:T(2,128)(2,1)} %bitcast.178), channel_id=1, source_target_pairs={{0,7},{1,6},{2,5},{3,4},{4,3},{5,2},{6,1},{7,0},{8,15},{9,14},{10,... | collective-permute-start | bytes 1179656 | tf_op jit(solution)/shard_map/ppermute | solution.py:399
  201.4 23.7 %collective-permute-start.48 = (bf16[4,192,2,128]{3,2,1,0:T(2,128)(2,1)S(1)}, bf16[4,192,2,128]{3,2,1,0:T(2,128)(2,1)S(1)}, u32[]{:S(2)}, u32[]{:S(2)}) collective-permute-start(bf16[4,192,2,128]{3,2,1,0:T(2,128)(2,1)S(1)} %bitcast.175), channel_id=1, source_target_pairs={{0,5},{1,4},{2,7},{3,6},{4,1},{5,0},{6,3},{7,2},{8,13},{9,12},{10,... | collective-permute-start | bytes 1179656 | tf_op jit(solution)/shard_map/ppermute | solution.py:399
  220.1 42.8 %collective-permute-start.44 = (bf16[4,192,2,128]{3,2,1,0:T(2,128)(2,1)}, bf16[4,192,2,128]{3,2,1,0:T(2,128)(2,1)S(1)}, u32[]{:S(2)}, u32[]{:S(2)}) collective-permute-start(bf16[4,192,2,128]{3,2,1,0:T(2,128)(2,1)} %bitcast.185), channel_id=1, source_target_pairs={{0,4},{1,5},{2,6},{3,7},{4,0},{5,1},{6,2},{7,3},{8,12},{9,13},{10,... | collective-permute-start | bytes 1179656 | tf_op jit(solution)/shard_map/ppermute | solution.py:399
  220.7 44.7 %collective-permute-start.35 = (bf16[4,192,2,128]{3,2,1,0:T(2,128)(2,1)}, bf16[4,192,2,128]{3,2,1,0:T(2,128)(2,1)S(1)}, u32[]{:S(2)}, u32[]{:S(2)}) collective-permute-start(bf16[4,192,2,128]{3,2,1,0:T(2,128)(2,1)} %bitcast.184), channel_id=1, source_target_pairs={{0,1},{1,0},{2,3},{3,2},{4,5},{5,4},{6,7},{7,6},{8,9},{9,8},{10,11... | collective-permute-start | bytes 1179656 | tf_op jit(solution)/shard_map/ppermute | solution.py:399
  228.3 22.8 %collective-permute-start.55 = (bf16[4,64,2,128]{3,2,1,0:T(2,128)(2,1)}, bf16[4,64,2,128]{3,2,1,0:T(2,128)(2,1)S(1)}, u32[]{:S(2)}, u32[]{:S(2)}) collective-permute-start(bf16[4,64,2,128]{3,2,1,0:T(2,128)(2,1)} %bitcast.203), channel_id=1, source_target_pairs={{0,10},{1,11},{2,8},{3,9},{4,14},{5,15},{6,12},{7,13},{8,2},{9,3},... | collective-permute-start | bytes 393224 | tf_op jit(solution)/shard_map/ppermute | solution.py:399
  259.5 29.6 %collective-permute-start.40 = (bf16[4,192,2,128]{3,2,1,0:T(2,128)(2,1)}, bf16[4,192,2,128]{3,2,1,0:T(2,128)(2,1)S(1)}, u32[]{:S(2)}, u32[]{:S(2)}) collective-permute-start(bf16[4,192,2,128]{3,2,1,0:T(2,128)(2,1)} %bitcast.183), channel_id=1, source_target_pairs={{0,2},{1,3},{2,0},{3,1},{4,6},{5,7},{6,4},{7,5},{8,10},{9,11},{10,... | collective-permute-start | bytes 1179656 | tf_op jit(solution)/shard_map/ppermute | solution.py:399
  259.5 29.8 %collective-permute-start.51 = (bf16[4,192,2,128]{3,2,1,0:T(2,128)(2,1)}, bf16[4,192,2,128]{3,2,1,0:T(2,128)(2,1)S(1)}, u32[]{:S(2)}, u32[]{:S(2)}) collective-permute-start(bf16[4,192,2,128]{3,2,1,0:T(2,128)(2,1)} %bitcast.182), channel_id=1, source_target_pairs={{0,5},{1,4},{2,7},{3,6},{4,1},{5,0},{6,3},{7,2},{8,13},{9,12},{10,... | collective-permute-start | bytes 1179656 | tf_op jit(solution)/shard_map/ppermute | solution.py:399
  261.6 28.4 %collective-permute-start.56 = (bf16[4,192,2,128]{3,2,1,0:T(2,128)(2,1)}, bf16[4,192,2,128]{3,2,1,0:T(2,128)(2,1)S(1)}, u32[]{:S(2)}, u32[]{:S(2)}) collective-permute-start(bf16[4,192,2,128]{3,2,1,0:T(2,128)(2,1)} %bitcast.181), channel_id=1, source_target_pairs={{0,6},{1,7},{2,4},{3,5},{4,2},{5,3},{6,0},{7,1},{8,14},{9,15},{10,... | collective-permute-start | bytes 1179656 | tf_op jit(solution)/shard_map/ppermute | solution.py:399
  285.3 25.5 %collective-permute-start.46 = (bf16[4,192,2,128]{3,2,1,0:T(2,128)(2,1)}, bf16[4,192,2,128]{3,2,1,0:T(2,128)(2,1)S(1)}, u32[]{:S(2)}, u32[]{:S(2)}) collective-permute-start(bf16[4,192,2,128]{3,2,1,0:T(2,128)(2,1)} %bitcast.179), channel_id=1, source_target_pairs={{0,3},{1,2},{2,1},{3,0},{4,7},{5,6},{6,5},{7,4},{8,11},{9,10},{10,... | collective-permute-start | bytes 1179656 | tf_op jit(solution)/shard_map/ppermute | solution.py:399
  285.4 25.5 %collective-permute-start.58 = (bf16[4,192,2,128]{3,2,1,0:T(2,128)(2,1)}, bf16[4,192,2,128]{3,2,1,0:T(2,128)(2,1)S(1)}, u32[]{:S(2)}, u32[]{:S(2)}) collective-permute-start(bf16[4,192,2,128]{3,2,1,0:T(2,128)(2,1)} %bitcast.177), channel_id=1, source_target_pairs={{0,7},{1,6},{2,5},{3,4},{4,3},{5,2},{6,1},{7,0},{8,15},{9,14},{10,... | collective-permute-start | bytes 1179656 | tf_op jit(solution)/shard_map/ppermute | solution.py:399
  (114 other events, 3910.8 us)

commit v7 on v0

v7 whole, which is shorter than its diff:
```python
import math

import jax
import jax.numpy as jnp
from jax import lax
from jax.experimental import pallas as pl
from jax.experimental.pallas import tpu as pltpu
from jax.sharding import PartitionSpec as P

HD = 128
SPAN = 64
NTOK = 128
CHUNKS = 2
F32 = jnp.float32
BF16 = jnp.bfloat16
ANY = pl.BlockSpec(memory_space=pl.ANY)
LIMIT = pltpu.CompilerParams(vmem_limit_bytes=56 * 2**20)


def dot(a, b, dims):
    return lax.dot_general(a, b, (dims, ((), ())), preferred_element_type=F32)


NT = ((1,), (1,))
NN = ((1,), (0,))
TN = ((0,), (0,))


def cost(microseconds):
    return pl.CostEstimate(
        flops=0, bytes_accessed=int(microseconds * 3.69e6), transcendentals=0
    )


def vmem(*shape):
    return pltpu.VMEM(shape, BF16)


def pack(queries, out_grad, neighbours, devices, chunk, chunks):
    heads = neighbours.shape[2] // HD // devices // chunks
    width = heads * HD

    def kernel(q_ref, g_ref, n_ref, out_ref, plain, tokens, rows, come_t, come_r, go_t, go_r):
        every = range(devices)
        columns = [pl.ds((i * chunks + chunk) * width, width) for i in every]
        token_loads = [
            [
                pltpu.make_async_copy(
                    ref.at[:, columns[i]], plain.at[i, pl.ds(part * SPAN, SPAN)], come_t.at[i, part]
                )
                for part, ref in enumerate((q_ref, g_ref))
            ]
            for i in every
        ]
        row_loads = [
            pltpu.make_async_copy(n_ref.at[:, :, columns[i]], rows.at[i], come_r.at[i]) for i in every
        ]
        for i in every:
            row_loads[i].start()
        for i in every:
            for load in token_loads[i]:
                load.start()
        stores = []
        for i in every:
            row_loads[i].wait()
            for h in range(heads):
                source = rows.at[i, :, :, pl.ds(h * HD, HD)]
                stores.append(
                    pltpu.make_async_copy(source, out_ref.at[i, h, pl.ds(SPAN, NTOK)], go_r.at[i, h])
                )
                stores[-1].start()
        for i in every:
            for load in token_loads[i]:
                load.wait()
            for h in range(heads):
                folded = tokens.at[i, h].reshape(2 * SPAN, HD)
                folded[...] = plain[i, :, pl.ds(h * HD, HD)]
            stores.append(pltpu.make_async_copy(tokens.at[i], out_ref.at[i, :, pl.ds(0, SPAN)], go_t.at[i]))
            stores[-1].start()
        for store in stores:
            store.wait()

    return pl.pallas_call(
        kernel,
        in_specs=[ANY] * 3,
        out_specs=ANY,
        out_shape=jax.ShapeDtypeStruct((devices, heads, SPAN + NTOK, 2, HD), BF16),
        scratch_shapes=[
            vmem(devices, 2 * SPAN, width),
            vmem(devices, heads, SPAN, 2, HD),
            vmem(devices, NTOK, 2, width),
            pltpu.SemaphoreType.DMA((devices, 2)),
            pltpu.SemaphoreType.DMA((devices,)),
            pltpu.SemaphoreType.DMA((devices,)),
            pltpu.SemaphoreType.DMA((devices, heads)),
        ],
        compiler_params=LIMIT,
        cost_estimate=cost(4),
        name="pack",
    )(queries, out_grad, neighbours)


def unpack(blocks, before, chunk, chunks):
    devices, heads = blocks.shape[:2]
    width = heads * HD

    def kernel(b_ref, t_ref, *refs):
        o_ref, q_ref, n_ref, rows, tokens, come_r, come_t, go_r, go_t = refs[-9:]
        every = range(devices)
        columns = [pl.ds((i * chunks + chunk) * width, width) for i in every]
        row_loads = [
            [
                pltpu.make_async_copy(
                    b_ref.at[i, h, pl.ds(SPAN, NTOK)],
                    rows.at[i, :, :, pl.ds(h * HD, HD)],
                    come_r.at[i, h],
                )
                for h in range(heads)
            ]
            for i in every
        ]
        token_loads = [
            [
                pltpu.make_async_copy(
                    t_ref.at[i, h, pl.ds(0, 2 * SPAN)],
                    tokens.at[i, :, pl.ds(h * HD, HD)],
                    come_t.at[i, h],
                )
                for h in range(heads)
            ]
            for i in every
        ]
        for i in every:
            for load in row_loads[i] + token_loads[i]:
                load.start()
        stores = []
        for i in every:
            for load in row_loads[i]:
                load.wait()
            stores.append(pltpu.make_async_copy(rows.at[i], n_ref.at[:, :, columns[i]], go_r.at[i]))
            stores[-1].start()
            for load in token_loads[i]:
                load.wait()
            for part, ref in enumerate((o_ref, q_ref)):
                source = tokens.at[i, pl.ds(part * SPAN, SPAN)]
                stores.append(pltpu.make_async_copy(source, ref.at[:, columns[i]], go_t.at[i, part]))
                stores[-1].start()
        for store in stores:
            store.wait()

    total = devices * width * chunks
    return pl.pallas_call(
        kernel,
        in_specs=[ANY] * (2 + len(before)),
        out_specs=[ANY] * 3,
        out_shape=[
            jax.ShapeDtypeStruct((SPAN, total), BF16),
            jax.ShapeDtypeStruct((SPAN, total), BF16),
            jax.ShapeDtypeStruct((NTOK, 2, total), BF16),
        ],
        input_output_aliases={2 + i: i for i in range(len(before))},
        scratch_shapes=[
            vmem(devices, NTOK, 2, width),
            vmem(devices, 2 * SPAN, width),
            pltpu.SemaphoreType.DMA((devices, heads)),
            pltpu.SemaphoreType.DMA((devices, heads)),
            pltpu.SemaphoreType.DMA((devices,)),
            pltpu.SemaphoreType.DMA((devices, 2)),
        ],
        compiler_params=LIMIT,
        cost_estimate=cost(5),
        name="unpack",
    )(blocks, blocks.reshape(devices, heads, -1, HD), *before)


def last_rows():
    rows = lax.broadcasted_iota(jnp.int32, (2 * SPAN, HD), 0)
    return lax.rem(rows, SPAN) == SPAN - 1


def load_row(block, words):
    words[...] = block.astype(F32)
    keys = words[pl.ds(0, NTOK, stride=2), :].astype(BF16)
    values = words[pl.ds(1, NTOK, stride=2), :].astype(BF16)
    return keys, values


def pair(spans_ref, first, second, part):
    rows = pl.ds(part * SPAN, SPAN)
    return jnp.concatenate([spans_ref[first // 2, rows], spans_ref[second // 2, rows]], 0)


def attention_kernel(slots_ref, in_ref, out_ref, spans_ref, words, table, powers, probs, stats, sums):
    devices = in_ref.shape[0]
    scale = 1.0 / math.sqrt(HD)
    last = last_rows()
    left = lax.broadcasted_iota(jnp.int32, (1, HD), 1) < SPAN
    for c in range(devices):
        own = in_ref[c, 0, : 2 * SPAN].astype(F32)
        after = in_ref[c + 1, 0, : 2 * SPAN].astype(F32) if c + 1 < devices else jnp.zeros_like(own)
        spans_ref[c] = jnp.where(last, own, after).astype(BF16)
    sums[...] = jnp.zeros_like(sums)

    def measure(r, lane):
        first, second = slots_ref[2 * r], slots_ref[2 * r + 1]
        keys, values = load_row(in_ref[r, 0, 2 * SPAN :], words.at[lane])
        table[r, :NTOK] = keys
        table[r, NTOK:] = values
        scores = dot(keys, pair(spans_ref, first, second, 0), NT) * scale
        prob_grad = dot(values, pair(spans_ref, first, second, 1), NT)
        top = jnp.max(scores, 0, keepdims=True)
        power = jnp.exp(scores - top)
        powers[r] = power
        probs[r] = prob_grad
        found = (top, jnp.sum(power, 0, keepdims=True), jnp.sum(power * prob_grad, 0, keepdims=True))
        for i, value in enumerate(found):
            turned = pltpu.roll(value, SPAN, 1)
            stats[i, pl.ds(first, 1)] = jnp.where(left, value, turned)
            stats[i, pl.ds(second, 1)] = jnp.where(left, turned, value)

    def spread(first, second):
        return [
            jnp.where(left, stats[i, pl.ds(first, 1)], stats[i, pl.ds(second, 1)]) for i in range(3)
        ]

    def mate(slot):
        return slot + 1 - 2 * lax.rem(slot, 2)

    def derive(r, lane):
        first, second = slots_ref[2 * r], slots_ref[2 * r + 1]
        own = spread(first, second)
        other = spread(mate(first), mate(second))
        top = jnp.maximum(own[0], other[0])
        here, there = jnp.exp(own[0] - top), jnp.exp(other[0] - top)
        inverse = 1.0 / (own[1] * here + other[1] * there)
        delta = (own[2] * here + other[2] * there) * inverse
        soft = powers[r] * (here * inverse)
        weights = soft.astype(BF16)
        score_grad = (soft * (probs[r] - delta)).astype(BF16)
        joined = words.at[lane]
        joined[pl.ds(0, NTOK, stride=2), :] = dot(score_grad, pair(spans_ref, first, second, 0), NN) * scale
        joined[pl.ds(1, NTOK, stride=2), :] = dot(weights, pair(spans_ref, first, second, 1), NN)
        out_ref[r, 0, 2 * SPAN :] = joined[...].astype(BF16)
        attended = dot(weights, table[r, NTOK:], TN)
        query_grad = dot(score_grad, table[r, :NTOK], TN) * scale
        for n, slot in enumerate((first, second)):
            piece = slice(n * SPAN, (n + 1) * SPAN)
            sums[slot // 2 + 1, :SPAN] += attended[piece]
            sums[slot // 2 + 1, SPAN:] += query_grad[piece]

    for step in (measure, derive):
        for r in range(devices):
            step(r, r % 4)
    for d in range(devices):
        out_ref[d, 0, : 2 * SPAN] = jnp.where(last, sums[d + 1], sums[d]).astype(BF16)


def attention(slots, blocks):
    devices, heads, rows, _ = blocks.shape
    block = pl.BlockSpec((devices, 1, rows, HD), lambda h, slots: (0, h, 0, 0))
    return pl.pallas_call(
        attention_kernel,
        grid_spec=pltpu.PrefetchScalarGridSpec(
            num_scalar_prefetch=1,
            grid=(heads,),
            in_specs=[block],
            out_specs=block,
            scratch_shapes=[
                vmem(devices, 2 * SPAN, HD),
                pltpu.VMEM((4, 2 * NTOK, HD), F32),
                vmem(devices, 2 * NTOK, HD),
                pltpu.VMEM((devices, NTOK, HD), F32),
                pltpu.VMEM((devices, NTOK, HD), F32),
                pltpu.VMEM((3, 2 * devices, HD), F32),
                pltpu.VMEM((devices + 1, 2 * SPAN, HD), F32),
            ],
        ),
        out_shape=jax.ShapeDtypeStruct(blocks.shape, BF16),
        compiler_params=LIMIT,
        cost_estimate=cost(14),
        name="attention",
    )(slots, blocks)


def body(queries, out_grad, neighbours, neighbour_ids):
    devices = lax.axis_size("fsdp")
    heads = queries.shape[1] // HD // devices
    chunks = math.gcd(heads, CHUNKS)
    slots = jnp.argsort(neighbour_ids, stable=True).astype(jnp.int32)

    def exchange(blocks):
        return lax.all_to_all(blocks, "fsdp", split_axis=0, concat_axis=0, tiled=True)

    arrived = [
        exchange(pack(queries, out_grad, neighbours, devices, chunk, chunks)) for chunk in range(chunks)
    ]
    outputs = ()
    for chunk, blocks in enumerate(arrived):
        results = attention(slots, blocks.reshape(devices, heads // chunks, -1, HD))
        back = exchange(results.reshape(blocks.shape))
        outputs = tuple(unpack(back, outputs, chunk, chunks))
    return outputs


def solution(mesh):
    in_specs = (
        P(("groups", "fsdp"), None),
        P(("groups", "fsdp"), None),
        P(("groups", "fsdp"), None, None),
        P("groups"),
    )
    out_specs = (
        P(("groups", "fsdp"), None),
        P(("groups", "fsdp"), None),
        P(("groups", "fsdp"), None, None),
    )
    return jax.shard_map(body, mesh=mesh, in_specs=in_specs, out_specs=out_specs, check_vma=False)
```

time: 567 us -> 315 us (0.56)
  local copies, waits for them, and re-layouts: 233 us -> 5.01 us
  matrix products: 57.1 us -> 0 us
  waiting for transfers between devices: 210 us -> 254 us
  Pallas kernels: 0 us -> 32.1 us
  other arithmetic: 29.4 us -> 1.61 us
  starting transfers between devices: 33.4 us -> 21.3 us
    dynamic_update_slice x12 -> x0, local copies, waits for them, and re-layouts: 60.7 us -> none  [body(): lax.map(backward_step, (query_blocks, grad_blocks, id_blocks, softmax_all...]
    gather x12 -> x0, local copies, waits for them, and re-layouts: 60 us -> none  [the longest x4 21 us: span_keys(): value_table[chosen_rows].reshape(per_block, 2 * NTOK, local_heads, HD)]
    dot_general x12 -> x0, matrix products: 49.3 us -> none  [the longest x2 13.8 us: forward_block(): jnp.einsum('ghqk,gkhd->gqhd', weights, value_block, preferred_element_typ...]
    all_to_all x6 -> x4, waiting for transfers between devices: 210 us -> 254 us  [exchange(): lax.all_to_all(blocks, 'fsdp', split_axis=0, concat_axis=0, tiled=True)]
    convert_element_type x3 -> x0, local copies, waits for them, and re-layouts: 32.1 us -> none  [the longest x1 15.6 us: body(): (value_slots[first_slot] + value_slots[second_slot]).astype(jnp.bfloat16)]
    pallas_call x0 -> x6, Pallas kernels: none -> 32.1 us  [the longest x2 15.6 us: attention(): pl.pallas_call(attention_kernel, grid_spec=pltpu.PrefetchScalarGridSpec(n...]
    all_to_all x8 -> x0, local copies, waits for them, and re-layouts: 28.8 us -> none  [the longest x2 11.1 us: body(): lax.all_to_all(row_grads, 'fsdp', split_axis=0, concat_axis=2, tiled=True)]
    unnamed x18 -> x8, local copies, waits for them, and re-layouts: 29.5 us -> 5.01 us
  transfers between devices with their start and end apart: 6 -> 4, of which waited for: 4 -> 4; matrix products, arithmetic and copies ran while one was open for 38% -> 1% of each run, Pallas kernels for 0% -> 8%
where the time goes in v7:
time: 315 us
  waiting for transfers between devices  254 us (81%)
  Pallas kernels  32.1 us (10%)
  starting transfers between devices  21.3 us (7%)
  local copies, waits for them, and re-layouts  5.01 us (2%)
    all_to_all x4, waiting for transfers between devices, exchange(): lax.all_to_all(blocks, 'fsdp', split_axis=0, concat_axis=0, tiled=True)  254 us
    all_to_all x4, starting transfers between devices, exchange(): lax.all_to_all(blocks, 'fsdp', split_axis=0, concat_axis=0, tiled=True)  21.3 us
    pallas_call x2, Pallas kernels, attention(): pl.pallas_call(attention_kernel, grid_spec=pltpu.PrefetchScalarGridSpec(n...  15.6 us
    pallas_call x2, Pallas kernels, pack(): pl.pallas_call(kernel, in_specs=[ANY] * 3, out_specs=ANY, out_shape=jax.S...  8.81 us
    pallas_call x2, Pallas kernels, unpack(): pl.pallas_call(kernel, in_specs=[ANY] * (2 + len(before)), out_specs=[ANY...  7.68 us
  transfers between devices with their start and end apart: 4, of which 4 were waited for; matrix products, arithmetic and copies ran while one was open for 1% of the time, Pallas kernels for 8%

profile of v7, /device:TPU:15, one launch (start us, length us, event | category | flops | bytes accessed | tf_op | source)
XLA Modules:
  0.0 314.9 jit_solution(9061167436455264577)
XLA Ops:
  0.6 4.4 %pack.3 = bf16[16,2,192,2,128]{4,3,2,1,0:T(2,128)(2,1)} custom-call(bf16[64,8192]{1,0:T(8,128)(2,1)} %q_ref.3, bf16[64,8192]{1,0:T(8,128)(2,1)} %g_ref.3, bf16[128,2,8192]{2,1,0:T(2,128)(2,1)} %n_ref.3), custom_call_target="tpu_custom_call" | custom-call | bytes 14760000 | tf_op jit(solution)/shard_map/pack/pallas_call | solution.py:83
  5.0 6.6 %all-to-all-start.2 = ((bf16[16,2,192,2,128]{4,3,2,1,0:T(2,128)(2,1)}), bf16[16,2,192,2,128]{4,3,2,1,0:T(2,128)(2,1)S(1)}, u32[]{:S(2)}, u32[]{:S(2)}) async-start(bf16[16,2,192,2,128]{4,3,2,1,0:T(2,128)(2,1)} %pack.3), calls=%async_computation.2 | async-start | bytes 6291456 | tf_op jit(solution)/shard_map/all_to_all | solution.py:292
  11.6 4.4 %pack.2 = bf16[16,2,192,2,128]{4,3,2,1,0:T(2,128)(2,1)} custom-call(bf16[64,8192]{1,0:T(8,128)(2,1)} %q_ref.3, bf16[64,8192]{1,0:T(8,128)(2,1)} %g_ref.3, bf16[128,2,8192]{2,1,0:T(2,128)(2,1)} %n_ref.3), custom_call_target="tpu_custom_call" | custom-call | bytes 14760000 | tf_op jit(solution)/shard_map/pack/pallas_call | solution.py:83
  16.0 0.0 copy-start.3
  16.0 65.5 %all-to-all-done.2 = bf16[16,2,192,2,128]{4,3,2,1,0:T(2,128)(2,1)S(1)} async-done(((bf16[16,2,192,2,128]{4,3,2,1,0:T(2,128)(2,1)}), bf16[16,2,192,2,128]{4,3,2,1,0:T(2,128)(2,1)S(1)}, u32[]{:S(2)}, u32[]{:S(2)}) %all-to-all-start.2) | async-done | bytes 3145760 | tf_op jit(solution)/shard_map/all_to_all | solution.py:292
  81.5 0.0 copy-start.2
  81.5 1.7 copy-done.2
  83.2 4.9 %all-to-all-start = ((bf16[16,2,192,2,128]{4,3,2,1,0:T(2,128)(2,1)}), bf16[16,2,192,2,128]{4,3,2,1,0:T(2,128)(2,1)S(1)}, u32[]{:S(2)}, u32[]{:S(2)}) async-start(bf16[16,2,192,2,128]{4,3,2,1,0:T(2,128)(2,1)} %pack.2), calls=%async_computation | async-start | bytes 6291456 | tf_op jit(solution)/shard_map/all_to_all | solution.py:292
  88.1 0.0 copy-done.3
  88.1 1.6 sort.17
  89.7 7.8 %attention.3 = bf16[16,2,384,128]{3,2,1,0:T(8,128)(2,1)} custom-call(s32[32]{0:T(128)} %get-tuple-element.7.slots_ref, bf16[16,2,384,128]{3,2,1,0:T(8,128)(2,1)} %bitcast.8), custom_call_target="tpu_custom_call" | custom-call | bytes 51660000 | tf_op jit(solution)/shard_map/attention/pallas_call | solution.py:261
  97.5 60.5 %all-to-all-done = bf16[16,2,192,2,128]{4,3,2,1,0:T(2,128)(2,1)S(1)} async-done(((bf16[16,2,192,2,128]{4,3,2,1,0:T(2,128)(2,1)}), bf16[16,2,192,2,128]{4,3,2,1,0:T(2,128)(2,1)S(1)}, u32[]{:S(2)}, u32[]{:S(2)}) %all-to-all-start) | async-done | bytes 3145760 | tf_op jit(solution)/shard_map/all_to_all | solution.py:292
  158.0 0.0 copy-start.1
  158.0 1.7 copy-done.1
  159.6 4.9 %all-to-all-start.3 = ((bf16[16,2,192,2,128]{4,3,2,1,0:T(2,128)(2,1)}), bf16[16,2,192,2,128]{4,3,2,1,0:T(2,128)(2,1)S(1)}, u32[]{:S(2)}, u32[]{:S(2)}) async-start(bf16[16,2,192,2,128]{4,3,2,1,0:T(2,128)(2,1)} %bitcast.10), calls=%async_computation.3 | async-start | bytes 6291456 | tf_op jit(solution)/shard_map/all_to_all | solution.py:292
  164.5 7.8 %attention.2 = bf16[16,2,384,128]{3,2,1,0:T(8,128)(2,1)} custom-call(s32[32]{0:T(128)} %get-tuple-element.7.slots_ref, bf16[16,2,384,128]{3,2,1,0:T(8,128)(2,1)} %bitcast.7), custom_call_target="tpu_custom_call" | custom-call | bytes 51660000 | tf_op jit(solution)/shard_map/attention/pallas_call | solution.py:261
  172.3 62.1 %all-to-all-done.3.b_ref = bf16[16,2,192,2,128]{4,3,2,1,0:T(2,128)(2,1)S(1)} async-done(((bf16[16,2,192,2,128]{4,3,2,1,0:T(2,128)(2,1)}), bf16[16,2,192,2,128]{4,3,2,1,0:T(2,128)(2,1)S(1)}, u32[]{:S(2)}, u32[]{:S(2)}) %all-to-all-start.3) | async-done | bytes 3145760 | tf_op jit(solution)/shard_map/all_to_all | solution.py:292
  234.4 0.0 copy-start
  234.4 1.7 copy-done
  236.1 4.9 %all-to-all-start.1 = ((bf16[16,2,192,2,128]{4,3,2,1,0:T(2,128)(2,1)}), bf16[16,2,192,2,128]{4,3,2,1,0:T(2,128)(2,1)}, u32[]{:S(2)}, u32[]{:S(2)}) async-start(bf16[16,2,192,2,128]{4,3,2,1,0:T(2,128)(2,1)} %bitcast.9), calls=%async_computation.1 | async-start | bytes 6291456 | tf_op jit(solution)/shard_map/all_to_all | solution.py:292
  241.0 3.8 %unpack.2 = (bf16[64,8192]{1,0:T(8,128)(2,1)}, bf16[64,8192]{1,0:T(8,128)(2,1)}, bf16[128,2,8192]{2,1,0:T(2,128)(2,1)}) custom-call(bf16[16,2,192,2,128]{4,3,2,1,0:T(2,128)(2,1)} %copy-done, bf16[16,2,384,128]{3,2,1,0:T(8,128)(2,1)} %bitcast.6), custom_call_target="tpu_custom_call" | custom-call | bytes 18450000 | tf_op jit(solution)/shard_map/unpack/pallas_call | solution.py:152
  244.9 66.1 %all-to-all-done.1.b_ref = bf16[16,2,192,2,128]{4,3,2,1,0:T(2,128)(2,1)} async-done(((bf16[16,2,192,2,128]{4,3,2,1,0:T(2,128)(2,1)}), bf16[16,2,192,2,128]{4,3,2,1,0:T(2,128)(2,1)}, u32[]{:S(2)}, u32[]{:S(2)}) %all-to-all-start.1) | async-done | bytes 3145760 | tf_op jit(solution)/shard_map/all_to_all | solution.py:292
  311.0 3.8 %unpack.3 = (bf16[64,8192]{1,0:T(8,128)(2,1)}, bf16[64,8192]{1,0:T(8,128)(2,1)}, bf16[128,2,8192]{2,1,0:T(2,128)(2,1)}) custom-call(bf16[16,2,192,2,128]{4,3,2,1,0:T(2,128)(2,1)} %all-to-all-done.1.b_ref, bf16[16,2,384,128]{3,2,1,0:T(8,128)(2,1)} %bitcast.2.t_ref, ...), custom_call_target="tpu_custom_call", output_to_operand_aliasing={{0}: (2, {}), {1}: (3, {}), {2}: (4, {})} | custom-call | bytes 18450000 | tf_op jit(solution)/shard_map/unpack/pallas_call | solution.py:152
  (1 shorter events, 0.0 us)
Async XLA Ops:
  5.0 76.5 %all-to-all-start.2 = ((bf16[16,2,192,2,128]{4,3,2,1,0:T(2,128)(2,1)}), bf16[16,2,192,2,128]{4,3,2,1,0:T(2,128)(2,1)S(1)}, u32[]{:S(2)}, u32[]{:S(2)}) async-start(bf16[16,2,192,2,128]{4,3,2,1,0:T(2,128)(2,1)} %pack.3), calls=%async_computation.2 | async-start | bytes 6291456 | tf_op jit(solution)/shard_map/all_to_all | solution.py:292
  16.0 72.1 %copy-start.3 = (s32[32]{0:T(128)S(1)}, s32[32]{0:T(128)}, u32[]{:S(2)}) copy-start(s32[32]{0:T(128)} %param.7) | copy-start | bytes 388
  81.5 1.7 copy-start.2
  83.2 74.8 %all-to-all-start = ((bf16[16,2,192,2,128]{4,3,2,1,0:T(2,128)(2,1)}), bf16[16,2,192,2,128]{4,3,2,1,0:T(2,128)(2,1)S(1)}, u32[]{:S(2)}, u32[]{:S(2)}) async-start(bf16[16,2,192,2,128]{4,3,2,1,0:T(2,128)(2,1)} %pack.2), calls=%async_computation | async-start | bytes 6291456 | tf_op jit(solution)/shard_map/all_to_all | solution.py:292
  158.0 1.7 copy-start.1
  159.6 74.8 %all-to-all-start.3 = ((bf16[16,2,192,2,128]{4,3,2,1,0:T(2,128)(2,1)}), bf16[16,2,192,2,128]{4,3,2,1,0:T(2,128)(2,1)S(1)}, u32[]{:S(2)}, u32[]{:S(2)}) async-start(bf16[16,2,192,2,128]{4,3,2,1,0:T(2,128)(2,1)} %bitcast.10), calls=%async_computation.3 | async-start | bytes 6291456 | tf_op jit(solution)/shard_map/all_to_all | solution.py:292
  234.4 1.7 copy-start
  236.1 74.9 %all-to-all-start.1 = ((bf16[16,2,192,2,128]{4,3,2,1,0:T(2,128)(2,1)}), bf16[16,2,192,2,128]{4,3,2,1,0:T(2,128)(2,1)}, u32[]{:S(2)}, u32[]{:S(2)}) async-start(bf16[16,2,192,2,128]{4,3,2,1,0:T(2,128)(2,1)} %bitcast.9), calls=%async_computation.1 | async-start | bytes 6291456 | tf_op jit(solution)/shard_map/all_to_all | solution.py:292

commit v8 on v7

--- a/solution.py
+++ b/solution.py
@@ -10,11 +10,11 @@
 HD = 128
 SPAN = 64
 NTOK = 128
-CHUNKS = 2
+CHUNKS = 1
 F32 = jnp.float32
 BF16 = jnp.bfloat16
 ANY = pl.BlockSpec(memory_space=pl.ANY)
-LIMIT = pltpu.CompilerParams(vmem_limit_bytes=56 * 2**20)
+LIMIT = pltpu.CompilerParams(vmem_limit_bytes=63 * 2**20)
 
 
 def dot(a, b, dims):
@@ -277,7 +277,7 @@
         ),
         out_shape=jax.ShapeDtypeStruct(blocks.shape, BF16),
         compiler_params=LIMIT,
-        cost_estimate=cost(14),
+        cost_estimate=cost(16),
         name="attention",
     )(slots, blocks)
 
@@ -289,7 +289,9 @@
     slots = jnp.argsort(neighbour_ids, stable=True).astype(jnp.int32)
 
     def exchange(blocks):
-        return lax.all_to_all(blocks, "fsdp", split_axis=0, concat_axis=0, tiled=True)
+        pieces = blocks.reshape(-1, 2, HD)
+        pieces = lax.all_to_all(pieces, "fsdp", split_axis=0, concat_axis=0, tiled=True)
+        return pieces.reshape(blocks.shape)
 
     arrived = [
         exchange(pack(queries, out_grad, neighbours, devices, chunk, chunks)) for chunk in range(chunks)

time: 315 us -> 315 us (level)
  blocking collectives: 0 us -> 142 us
  waiting for transfers between devices: 254 us -> 136 us
  starting transfers between devices: 21.3 us -> 6.57 us
  Pallas kernels: 32.1 us -> 26.5 us
  local copies, waits for them, and re-layouts: 5.01 us -> 0.01 us
    all_to_all x0 -> x1, blocking collectives: none -> 142 us  [exchange(): lax.all_to_all(pieces, 'fsdp', split_axis=0, concat_axis=0, tiled=True)]
    all_to_all x4 -> x1, waiting for transfers between devices: 254 us -> 136 us  [exchange(): lax.all_to_all(pieces, 'fsdp', split_axis=0, concat_axis=0, tiled=True)]
    all_to_all x4 -> x1, starting transfers between devices: 21.3 us -> 6.57 us  [exchange(): lax.all_to_all(pieces, 'fsdp', split_axis=0, concat_axis=0, tiled=True)]
    unnamed x8 -> x2, local copies, waits for them, and re-layouts: 5.01 us -> 0.01 us
    pallas_call x2 -> x1, Pallas kernels: 15.6 us -> 12.4 us  [attention(): pl.pallas_call(attention_kernel, grid_spec=pltpu.PrefetchScalarGridSpec(n...]
    pallas_call x2 -> x1, Pallas kernels: 8.81 us -> 7.47 us  [pack(): pl.pallas_call(kernel, in_specs=[ANY] * 3, out_specs=ANY, out_shape=jax.S...]
    pallas_call x2 -> x1, Pallas kernels: 7.68 us -> 6.65 us  [unpack(): pl.pallas_call(kernel, in_specs=[ANY] * (2 + len(before)), out_specs=[ANY...]
  transfers between devices with their start and end apart: 4 -> 1, of which waited for: 4 -> 1; matrix products, arithmetic and copies ran while one was open for 1% -> 1% of each run, Pallas kernels for 8% -> 0%
where the time goes in v8:
time: 315 us; the launch traced here: 313 us
  blocking collectives  142 us (45%)
  waiting for transfers between devices  136 us (43%)
  Pallas kernels  26.5 us (8%)
  starting transfers between devices  6.57 us (2%)
    all_to_all x1, blocking collectives, exchange(): lax.all_to_all(pieces, 'fsdp', split_axis=0, concat_axis=0, tiled=True)  142 us
    all_to_all x1, waiting for transfers between devices, exchange(): lax.all_to_all(pieces, 'fsdp', split_axis=0, concat_axis=0, tiled=True)  136 us
    pallas_call x1, Pallas kernels, attention(): pl.pallas_call(attention_kernel, grid_spec=pltpu.PrefetchScalarGridSpec(n...  12.4 us
    pallas_call x1, Pallas kernels, pack(): pl.pallas_call(kernel, in_specs=[ANY] * 3, out_specs=ANY, out_shape=jax.S...  7.47 us
    pallas_call x1, Pallas kernels, unpack(): pl.pallas_call(kernel, in_specs=[ANY] * (2 + len(before)), out_specs=[ANY...  6.65 us
    all_to_all x1, starting transfers between devices, exchange(): lax.all_to_all(pieces, 'fsdp', split_axis=0, concat_axis=0, tiled=True)  6.57 us
  transfers between devices with their start and end apart: 1, of which 1 were waited for; matrix products, arithmetic and copies ran while one was open for 1% of the time, Pallas kernels for 0%

profile of v8, /device:TPU:15, one launch (start us, length us, event | category | flops | bytes accessed | tf_op | source)
XLA Modules:
  0.0 313.3 jit_solution(8653227701305970576)
XLA Ops:
  0.6 7.5 %pack.1 = bf16[16,4,192,2,128]{4,3,2,1,0:T(2,128)(2,1)} custom-call(bf16[64,8192]{1,0:T(8,128)(2,1)} %q_ref.1, bf16[64,8192]{1,0:T(8,128)(2,1)} %g_ref.1, bf16[128,2,8192]{2,1,0:T(2,128)(2,1)} %n_ref.1), custom_call_target="tpu_custom_call" | custom-call | bytes 14760000 | tf_op jit(solution)/shard_map/pack/pallas_call | solution.py:83
  8.1 0.0 copy-start
  8.1 6.6 %all-to-all-start = ((bf16[12288,2,128]{2,1,0:T(2,128)(2,1)}), bf16[12288,2,128]{2,1,0:T(2,128)(2,1)}, u32[]{:S(2)}, u32[]{:S(2)}) async-start(bf16[12288,2,128]{2,1,0:T(2,128)(2,1)} %bitcast.7), calls=%async_computation | async-start | bytes 12582912 | tf_op jit(solution)/shard_map/all_to_all | solution.py:293
  14.7 0.0 copy-done
  14.7 1.6 sort.17
  16.3 135.8 %all-to-all-done = bf16[12288,2,128]{2,1,0:T(2,128)(2,1)} async-done(((bf16[12288,2,128]{2,1,0:T(2,128)(2,1)}), bf16[12288,2,128]{2,1,0:T(2,128)(2,1)}, u32[]{:S(2)}, u32[]{:S(2)}) %all-to-all-start) | async-done | bytes 6291488 | tf_op jit(solution)/shard_map/all_to_all | solution.py:293
  152.1 12.4 %attention.1 = bf16[16,4,384,128]{3,2,1,0:T(8,128)(2,1)} custom-call(s32[32]{0:T(128)} %get-tuple-element.4.slots_ref, bf16[16,4,384,128]{3,2,1,0:T(8,128)(2,1)} %bitcast.1.in_ref), custom_call_target="tpu_custom_call" | custom-call | bytes 59040000 | tf_op jit(solution)/shard_map/attention/pallas_call | solution.py:261
  164.5 142.2 %all_to_all.10 = bf16[12288,2,128]{2,1,0:T(2,128)(2,1)} all-to-all(bf16[12288,2,128]{2,1,0:T(2,128)(2,1)} %bitcast.8), channel_id=1, replica_groups=mesh['groups'=2,'fsdp'=16] {'fsdp'}, dimensions={0} | all-to-all | bytes 12582912 | tf_op jit(solution)/shard_map/all_to_all | solution.py:293
  306.7 6.7 %unpack.1 = (bf16[64,8192]{1,0:T(8,128)(2,1)}, bf16[64,8192]{1,0:T(8,128)(2,1)}, bf16[128,2,8192]{2,1,0:T(2,128)(2,1)}) custom-call(bf16[16,4,192,2,128]{4,3,2,1,0:T(2,128)(2,1)} %bitcast.5, bf16[16,4,384,128]{3,2,1,0:T(8,128)(2,1)} %bitcast.6), custom_call_target="tpu_custom_call" | custom-call | bytes 18450000 | tf_op jit(solution)/shard_map/unpack/pallas_call | solution.py:152
  (1 shorter events, 0.0 us)
Async XLA Ops:
  8.1 6.6 %copy-start = (s32[32]{0:T(128)S(1)}, s32[32]{0:T(128)}, u32[]{:S(2)}) copy-start(s32[32]{0:T(128)} %param.7) | copy-start | bytes 388
  8.1 144.0 %all-to-all-start = ((bf16[12288,2,128]{2,1,0:T(2,128)(2,1)}), bf16[12288,2,128]{2,1,0:T(2,128)(2,1)}, u32[]{:S(2)}, u32[]{:S(2)}) async-start(bf16[12288,2,128]{2,1,0:T(2,128)(2,1)} %bitcast.7), calls=%async_computation | async-start | bytes 12582912 | tf_op jit(solution)/shard_map/all_to_all | solution.py:293

commit v9 on v4

--- a/solution.py
+++ b/solution.py
@@ -14,7 +14,7 @@
 F32 = jnp.float32
 BF16 = jnp.bfloat16
 ANY = pl.BlockSpec(memory_space=pl.ANY)
-LIMIT = pltpu.CompilerParams(vmem_limit_bytes=56 * 2**20)
+LIMIT = pltpu.CompilerParams(vmem_limit_bytes=63 * 2**20)
 
 
 def dot(a, b, dims):
@@ -409,13 +409,19 @@
     return results[0], results[1:]
 
 
-def exchanged(devices, step):
-    return [(i, i ^ step) for i in range(devices)]
-
-
-def swap(rows, devices):
-    sent = {k: lax.ppermute(rows[k], "fsdp", exchanged(devices, k)) for k in range(len(rows) - 1, 0, -1)}
-    return [rows[0]] + [sent[k] for k in range(1, len(rows))]
+def after(later, earlier):
+    return lax.optimization_barrier((later, earlier))
+
+
+def swap(tokens, rows, devices):
+    half = len(rows)
+    quarter = half // 2
+    moved = list(rows)
+    for k in list(range(quarter, half)) + list(range(1, quarter)):
+        moved[k] = lax.ppermute(rows[k], "fsdp", [(i, i ^ k) for i in range(devices)])
+    tokens, moved[quarter] = after(tokens, moved[quarter])
+    tokens = lax.all_to_all(tokens, "fsdp", split_axis=0, concat_axis=0, tiled=True)
+    return tokens, moved
 
 
 def body(queries, out_grad, neighbours, neighbour_ids):
@@ -423,23 +429,34 @@
     half = devices // 2
     heads = queries.shape[1] // HD // half
     chunks = math.gcd(heads, CHUNKS)
-    across = [(i, (i + half) % devices) for i in range(devices)]
+    across = [(i, i ^ half) for i in range(devices)]
     slots = jnp.argsort(neighbour_ids, stable=True).astype(jnp.int32)
-    arrived = []
-    for chunk in range(chunks):
-        tokens = pack_tokens(queries, out_grad, devices, chunk, chunks)
-        tokens = lax.all_to_all(tokens, "fsdp", split_axis=0, concat_axis=0, tiled=True)
-        rows = swap(pack_rows(neighbours, devices, chunk, chunks), devices)
-        arrived.append((tokens, [row.reshape(-1, 2 * NTOK, HD) for row in rows]))
-    out_tokens, out_rows = (), ()
-    for chunk, (tokens, rows) in enumerate(arrived):
+
+    def compute(tokens, rows):
+        rows = [row.reshape(-1, 2 * NTOK, HD) for row in rows]
         own = row_stats(slots, tokens, rows)
         other = lax.ppermute(own, "fsdp", across)
         token_grads, row_grads = grads(slots, tokens, rows, own, other)
-        token_grads = lax.all_to_all(token_grads, "fsdp", split_axis=0, concat_axis=0, tiled=True)
-        row_grads = swap([row.reshape(-1, NTOK, 2, HD) for row in row_grads], devices)
-        out_tokens = tuple(unpack_tokens(token_grads, out_tokens, chunk, chunks))
-        out_rows = (unpack_rows(row_grads, out_rows, chunk, chunks),)
+        return token_grads, [row.reshape(-1, NTOK, 2, HD) for row in row_grads]
+
+    arrived, back = [], []
+    for chunk in range(chunks):
+        rows = pack_rows(neighbours, devices, chunk, chunks)
+        tokens = pack_tokens(queries, out_grad, devices, chunk, chunks)
+        if arrived:
+            (tokens, rows), arrived[-1] = after((tokens, rows), arrived[-1])
+        arrived.append(swap(tokens, rows, devices))
+    for chunk in range(chunks):
+        results = compute(*arrived[chunk])
+        if back:
+            results, back[-1] = after(results, back[-1])
+        elif chunks > 1:
+            results, arrived[-1] = after(results, arrived[-1])
+        back.append(swap(*results, devices))
+    out_tokens, out_rows = (), ()
+    for chunk, (tokens, rows) in enumerate(back):
+        out_rows = (unpack_rows(rows, out_rows, chunk, chunks),)
+        out_tokens = tuple(unpack_tokens(tokens, out_tokens, chunk, chunks))
     return out_tokens + out_rows
 
 

time: 337 us -> 310 us (0.920)
  waiting for transfers between devices: 199 us -> 187 us
  starting transfers between devices: 69.3 us -> 60.6 us
  local copies, waits for them, and re-layouts: 6.64 us -> 1.48 us
    all_to_all x4, waiting for transfers between devices: 45 us -> 0.01 us  [swap(): lax.all_to_all(tokens, 'fsdp', split_axis=0, concat_axis=0, tiled=True)]
    ppermute x30, waiting for transfers between devices: 154 us -> 187 us  [the longest x28 114 us: swap(): lax.ppermute(rows[k], 'fsdp', [(i, i ^ k) for i in range(devices)])]
    ppermute x30, starting transfers between devices: 43.2 us -> 33.5 us  [the longest x28 29.3 us: swap(): lax.ppermute(rows[k], 'fsdp', [(i, i ^ k) for i in range(devices)])]
    unnamed x74 -> x42, local copies, waits for them, and re-layouts: 6.63 us -> 1.47 us
  transfers between devices with their start and end apart: 34 -> 34, of which waited for: 25 -> 16; matrix products, arithmetic and copies ran while one was open for 1% -> 1% of each run, Pallas kernels for 15% -> 17%
where the time goes in v9:
time: 310 us; the launch traced here: 307 us
  waiting for transfers between devices  187 us (60%)
  starting transfers between devices  60.6 us (20%)
  Pallas kernels  56 us (18%)
    ppermute x28, waiting for transfers between devices, swap(): lax.ppermute(rows[k], 'fsdp', [(i, i ^ k) for i in range(devices)])  114 us
    ppermute x2, waiting for transfers between devices, compute(): other = lax.ppermute(own, 'fsdp', across)  72.8 us
    ppermute x28, starting transfers between devices, swap(): lax.ppermute(rows[k], 'fsdp', [(i, i ^ k) for i in range(devices)])  29.3 us
    all_to_all x4, starting transfers between devices, swap(): lax.all_to_all(tokens, 'fsdp', split_axis=0, concat_axis=0, tiled=True)  27 us
    pallas_call x2, Pallas kernels, grads(): pl.pallas_call(grads_kernel, grid_spec=pltpu.PrefetchScalarGridSpec(num_s...  24.1 us
    pallas_call x2, Pallas kernels, row_stats(): pl.pallas_call(stats_kernel, grid_spec=pltpu.PrefetchScalarGridSpec(num_s...  11.4 us
  transfers between devices with their start and end apart: 34, of which 16 were waited for; matrix products, arithmetic and copies ran while one was open for 1% of the time, Pallas kernels for 17%

profile of v9, /device:TPU:15, one launch (start us, length us, event | category | flops | bytes accessed | tf_op | source)
XLA Modules:
  0.0 307.3 jit_solution(11528231023053650497)
XLA Ops:
  6.0 4.7 %collective-permute-done = bf16[4,128,2,128]{3,2,1,0:T(2,128)(2,1)S(1)} collective-permute-done((bf16[4,128,2,128]{3,2,1,0:T(2,128)(2,1)}, bf16[4,128,2,128]{3,2,1,0:T(2,128)(2,1)S(1)}, u32[]{:S(2)}, u32[]{:S(2)}) %collective-permute-start) | collective-permute-done | bytes 262176 | tf_op jit(solution)/shard_map/ppermute | solution.py:421
  10.7 7.4 %all-to-all-start = ((bf16[16,128,512]{2,1,0:T(8,128)(2,1)}), bf16[16,128,512]{2,1,0:T(8,128)(2,1)}, u32[]{:S(2)}, u32[]{:S(2)}) async-start(bf16[16,128,512]{2,1,0:T(8,128)(2,1)} %pack_tokens.3), calls=%async_computation | async-start | bytes 4194304 | tf_op jit(solution)/shard_map/all_to_all | solution.py:423
  28.7 7.6 %collective-permute-done.2 = bf16[4,128,2,128]{3,2,1,0:T(2,128)(2,1)S(1)} collective-permute-done((bf16[4,128,2,128]{3,2,1,0:T(2,128)(2,1)}, bf16[4,128,2,128]{3,2,1,0:T(2,128)(2,1)S(1)}, u32[]{:S(2)}, u32[]{:S(2)}) %collective-permute-start.2) | collective-permute-done | bytes 262176 | tf_op jit(solution)/shard_map/ppermute | solution.py:421
  36.2 9.0 %collective-permute-done.3 = bf16[4,128,2,128]{3,2,1,0:T(2,128)(2,1)S(1)} collective-permute-done((bf16[4,128,2,128]{3,2,1,0:T(2,128)(2,1)}, bf16[4,128,2,128]{3,2,1,0:T(2,128)(2,1)S(1)}, u32[]{:S(2)}, u32[]{:S(2)}) %collective-permute-start.3) | collective-permute-done | bytes 262176 | tf_op jit(solution)/shard_map/ppermute | solution.py:421
  45.2 15.2 %collective-permute-done.4 = bf16[4,128,2,128]{3,2,1,0:T(2,128)(2,1)S(1)} collective-permute-done((bf16[4,128,2,128]{3,2,1,0:T(2,128)(2,1)}, bf16[4,128,2,128]{3,2,1,0:T(2,128)(2,1)S(1)}, u32[]{:S(2)}, u32[]{:S(2)}) %collective-permute-start.4) | collective-permute-done | bytes 262176 | tf_op jit(solution)/shard_map/ppermute | solution.py:421
  60.4 5.9 %collective-permute-done.5 = bf16[4,128,2,128]{3,2,1,0:T(2,128)(2,1)} collective-permute-done((bf16[4,128,2,128]{3,2,1,0:T(2,128)(2,1)}, bf16[4,128,2,128]{3,2,1,0:T(2,128)(2,1)}, u32[]{:S(2)}, u32[]{:S(2)}) %collective-permute-start.5) | collective-permute-done | bytes 262176 | tf_op jit(solution)/shard_map/ppermute | solution.py:421
  66.3 6.9 %collective-permute-done.6 = bf16[4,128,2,128]{3,2,1,0:T(2,128)(2,1)} collective-permute-done((bf16[4,128,2,128]{3,2,1,0:T(2,128)(2,1)}, bf16[4,128,2,128]{3,2,1,0:T(2,128)(2,1)}, u32[]{:S(2)}, u32[]{:S(2)}) %collective-permute-start.6) | collective-permute-done | bytes 262176 | tf_op jit(solution)/shard_map/ppermute | solution.py:421
  73.3 7.6 %collective-permute-done.8 = bf16[4,128,2,128]{3,2,1,0:T(2,128)(2,1)S(1)} collective-permute-done((bf16[4,128,2,128]{3,2,1,0:T(2,128)(2,1)}, bf16[4,128,2,128]{3,2,1,0:T(2,128)(2,1)S(1)}, u32[]{:S(2)}, u32[]{:S(2)}) %collective-permute-start.8) | collective-permute-done | bytes 262176 | tf_op jit(solution)/shard_map/ppermute | solution.py:421
  80.9 7.2 %all-to-all-start.1 = ((bf16[16,128,512]{2,1,0:T(8,128)(2,1)}), bf16[16,128,512]{2,1,0:T(8,128)(2,1)}, u32[]{:S(2)}, u32[]{:S(2)}) async-start(bf16[16,128,512]{2,1,0:T(8,128)(2,1)} %pack_tokens.2), calls=%async_computation.1 | async-start | bytes 4194304 | tf_op jit(solution)/shard_map/all_to_all | solution.py:423
  90.1 5.7 %row_stats.2.refs_8_ = f32[4,3,8,128]{3,2,1,0:T(8,128)} custom-call(s32[32]{0:T(128)} %get-tuple-element.104.slots_ref, bf16[16,128,512]{2,1,0:T(8,128)(2,1)} %all-to-all-done.t_ref, bf16[4,256,128]{2,1,0:T(8,128)(2,1)} %bitcast.38, bf16[4,256,128]{2,1,0:T(8,128)(2,1)} %bitcast.1.refs_1_, bf16[4,256,128]{2,1,0:T(8,128)(2,1)} %bitcast.46, ...), custom_call_target="tpu_custom_call" | custom-call | bytes 22140000 | tf_op jit(solution)/shard_map/row_stats/pallas_call | solution.py:305
  100.0 35.6 %collective-permute-done.7.refs_9_ = f32[4,3,8,128]{3,2,1,0:T(8,128)S(1)} collective-permute-done((f32[4,3,8,128]{3,2,1,0:T(8,128)}, f32[4,3,8,128]{3,2,1,0:T(8,128)S(1)}, u32[]{:S(2)}, u32[]{:S(2)}) %collective-permute-start.7) | collective-permute-done | bytes 49184 | tf_op jit(solution)/shard_map/ppermute | solution.py:438
  139.4 12.0 %grads.2 = (bf16[16,128,512]{2,1,0:T(8,128)(2,1)}, bf16[4,256,128]{2,1,0:T(8,128)(2,1)}, bf16[4,256,128]{2,1,0:T(8,128)(2,1)}, bf16[4,256,128]{2,1,0:T(8,128)(2,...) custom-call(s32[32]{0:T(128)} %get-tuple-element.104.slots_ref, ...), custom_call_target="tpu_custom_call" | custom-call | bytes 44280000 | tf_op jit(solution)/shard_map/grads/pallas_call | solution.py:389
  154.4 6.3 %collective-permute-done.16.refs_4_ = bf16[4,128,2,128]{3,2,1,0:T(2,128)(2,1)S(1)} collective-permute-done((bf16[4,128,2,128]{3,2,1,0:T(2,128)(2,1)}, bf16[4,128,2,128]{3,2,1,0:T(2,128)(2,1)S(1)}, u32[]{:S(2)}, u32[]{:S(2)}) %collective-permute-start.16) | collective-permute-done | bytes 262176 | tf_op jit(solution)/shard_map/ppermute | solution.py:421
  161.4 6.2 %all-to-all-start.2 = ((bf16[16,128,512]{2,1,0:T(8,128)(2,1)}), bf16[16,128,512]{2,1,0:T(8,128)(2,1)}, u32[]{:S(2)}, u32[]{:S(2)}) async-start(bf16[16,128,512]{2,1,0:T(8,128)(2,1)} %get-tuple-element.172), calls=%async_computation.2 | async-start | bytes 4194304 | tf_op jit(solution)/shard_map/all_to_all | solution.py:423
  168.0 5.7 %row_stats.3.refs_8_ = f32[4,3,8,128]{3,2,1,0:T(8,128)} custom-call(s32[32]{0:T(128)} %get-tuple-element.104.slots_ref, bf16[16,128,512]{2,1,0:T(8,128)(2,1)} %all-to-all-done.1.t_ref, bf16[4,256,128]{2,1,0:T(8,128)(2,1)} %bitcast.32, bf16[4,256,128]{2,1,0:T(8,128)(2,1)} %bitcast.36, bf16[4,256,128]{2,1,0:T(8,128)(2,1)} %bitcast.42, ...), custom_call_target="tpu_custom_call" | custom-call | bytes 22140000 | tf_op jit(solution)/shard_map/row_stats/pallas_call | solution.py:305
  177.8 37.2 %collective-permute-done.15.refs_9_ = f32[4,3,8,128]{3,2,1,0:T(8,128)S(1)} collective-permute-done((f32[4,3,8,128]{3,2,1,0:T(8,128)}, f32[4,3,8,128]{3,2,1,0:T(8,128)S(1)}, u32[]{:S(2)}, u32[]{:S(2)}) %collective-permute-start.15) | collective-permute-done | bytes 49184 | tf_op jit(solution)/shard_map/ppermute | solution.py:438
  218.9 12.0 %grads.3 = (bf16[16,128,512]{2,1,0:T(8,128)(2,1)}, bf16[4,256,128]{2,1,0:T(8,128)(2,1)}, bf16[4,256,128]{2,1,0:T(8,128)(2,1)}, bf16[4,256,128]{2,1,0:T(8,128)(2,...) custom-call(s32[32]{0:T(128)} %get-tuple-element.104.slots_ref, ...), custom_call_target="tpu_custom_call" | custom-call | bytes 44280000 | tf_op jit(solution)/shard_map/grads/pallas_call | solution.py:389
  233.9 6.3 %collective-permute-done.23.refs_4_ = bf16[4,128,2,128]{3,2,1,0:T(2,128)(2,1)S(1)} collective-permute-done((bf16[4,128,2,128]{3,2,1,0:T(2,128)(2,1)}, bf16[4,128,2,128]{3,2,1,0:T(2,128)(2,1)S(1)}, u32[]{:S(2)}, u32[]{:S(2)}) %collective-permute-start.23) | collective-permute-done | bytes 262176 | tf_op jit(solution)/shard_map/ppermute | solution.py:421
  240.9 6.2 %all-to-all-start.3 = ((bf16[16,128,512]{2,1,0:T(8,128)(2,1)}), bf16[16,128,512]{2,1,0:T(8,128)(2,1)}, u32[]{:S(2)}, u32[]{:S(2)}) async-start(bf16[16,128,512]{2,1,0:T(8,128)(2,1)} %get-tuple-element.183), calls=%async_computation.3 | async-start | bytes 4194304 | tf_op jit(solution)/shard_map/all_to_all | solution.py:423
  257.8 7.5 %collective-permute-done.25.refs_2_ = bf16[4,128,2,128]{3,2,1,0:T(2,128)(2,1)S(1)} collective-permute-done((bf16[4,128,2,128]{3,2,1,0:T(2,128)(2,1)}, bf16[4,128,2,128]{3,2,1,0:T(2,128)(2,1)S(1)}, u32[]{:S(2)}, u32[]{:S(2)}) %collective-permute-start.25) | collective-permute-done | bytes 262176 | tf_op jit(solution)/shard_map/ppermute | solution.py:421
  265.2 9.0 %collective-permute-done.26.refs_3_ = bf16[4,128,2,128]{3,2,1,0:T(2,128)(2,1)S(1)} collective-permute-done((bf16[4,128,2,128]{3,2,1,0:T(2,128)(2,1)}, bf16[4,128,2,128]{3,2,1,0:T(2,128)(2,1)S(1)}, u32[]{:S(2)}, u32[]{:S(2)}) %collective-permute-start.26) | collective-permute-done | bytes 262176 | tf_op jit(solution)/shard_map/ppermute | solution.py:421
  274.2 15.1 %collective-permute-done.27.refs_5_ = bf16[4,128,2,128]{3,2,1,0:T(2,128)(2,1)} collective-permute-done((bf16[4,128,2,128]{3,2,1,0:T(2,128)(2,1)}, bf16[4,128,2,128]{3,2,1,0:T(2,128)(2,1)}, u32[]{:S(2)}, u32[]{:S(2)}) %collective-permute-start.27) | collective-permute-done | bytes 262176 | tf_op jit(solution)/shard_map/ppermute | solution.py:421
  289.4 5.6 %collective-permute-done.28.refs_6_ = bf16[4,128,2,128]{3,2,1,0:T(2,128)(2,1)} collective-permute-done((bf16[4,128,2,128]{3,2,1,0:T(2,128)(2,1)}, bf16[4,128,2,128]{3,2,1,0:T(2,128)(2,1)}, u32[]{:S(2)}, u32[]{:S(2)}) %collective-permute-start.28) | collective-permute-done | bytes 262176 | tf_op jit(solution)/shard_map/ppermute | solution.py:421
  294.9 7.2 %collective-permute-done.29.refs_7_ = bf16[4,128,2,128]{3,2,1,0:T(2,128)(2,1)} collective-permute-done((bf16[4,128,2,128]{3,2,1,0:T(2,128)(2,1)}, bf16[4,128,2,128]{3,2,1,0:T(2,128)(2,1)}, u32[]{:S(2)}, u32[]{:S(2)}) %collective-permute-start.29) | collective-permute-done | bytes 262176 | tf_op jit(solution)/shard_map/ppermute | solution.py:421
  (100 shorter events, 57.3 us)
Async XLA Ops:
  10.7 62.5 %all-to-all-start = ((bf16[16,128,512]{2,1,0:T(8,128)(2,1)}), bf16[16,128,512]{2,1,0:T(8,128)(2,1)}, u32[]{:S(2)}, u32[]{:S(2)}) async-start(bf16[16,128,512]{2,1,0:T(8,128)(2,1)} %pack_tokens.3), calls=%async_computation | async-start | bytes 4194304 | tf_op jit(solution)/shard_map/all_to_all | solution.py:423
  18.6 17.7 %collective-permute-start.2 = (bf16[4,128,2,128]{3,2,1,0:T(2,128)(2,1)}, bf16[4,128,2,128]{3,2,1,0:T(2,128)(2,1)S(1)}, u32[]{:S(2)}, u32[]{:S(2)}) collective-permute-start(bf16[4,128,2,128]{3,2,1,0:T(2,128)(2,1)} %get-tuple-element.117), channel_id=1, source_target_pairs={{0,2},{1,3},{2,0},{3,1},{4,6},{5,7},{6,4},{7,5},{8,10},{9,11},{10,... | collective-permute-start | bytes 786440 | tf_op jit(solution)/shard_map/ppermute | solution.py:421
  18.9 26.4 %collective-permute-start.3 = (bf16[4,128,2,128]{3,2,1,0:T(2,128)(2,1)}, bf16[4,128,2,128]{3,2,1,0:T(2,128)(2,1)S(1)}, u32[]{:S(2)}, u32[]{:S(2)}) collective-permute-start(bf16[4,128,2,128]{3,2,1,0:T(2,128)(2,1)} %get-tuple-element.118), channel_id=1, source_target_pairs={{0,3},{1,2},{2,1},{3,0},{4,7},{5,6},{6,5},{7,4},{8,11},{9,10},{10,... | collective-permute-start | bytes 786440 | tf_op jit(solution)/shard_map/ppermute | solution.py:421
  20.4 40.1 %collective-permute-start.4 = (bf16[4,128,2,128]{3,2,1,0:T(2,128)(2,1)}, bf16[4,128,2,128]{3,2,1,0:T(2,128)(2,1)S(1)}, u32[]{:S(2)}, u32[]{:S(2)}) collective-permute-start(bf16[4,128,2,128]{3,2,1,0:T(2,128)(2,1)} %get-tuple-element.120), channel_id=1, source_target_pairs={{0,5},{1,4},{2,7},{3,6},{4,1},{5,0},{6,3},{7,2},{8,13},{9,12},{10,... | collective-permute-start | bytes 786440 | tf_op jit(solution)/shard_map/ppermute | solution.py:421
  20.6 45.7 %collective-permute-start.5 = (bf16[4,128,2,128]{3,2,1,0:T(2,128)(2,1)}, bf16[4,128,2,128]{3,2,1,0:T(2,128)(2,1)}, u32[]{:S(2)}, u32[]{:S(2)}) collective-permute-start(bf16[4,128,2,128]{3,2,1,0:T(2,128)(2,1)} %get-tuple-element.121), channel_id=1, source_target_pairs={{0,6},{1,7},{2,4},{3,5},{4,2},{5,3},{6,0},{7,1},{8,14},{9,15},{10,... | collective-permute-start | bytes 786440 | tf_op jit(solution)/shard_map/ppermute | solution.py:421
  21.8 51.4 %collective-permute-start.6 = (bf16[4,128,2,128]{3,2,1,0:T(2,128)(2,1)}, bf16[4,128,2,128]{3,2,1,0:T(2,128)(2,1)}, u32[]{:S(2)}, u32[]{:S(2)}) collective-permute-start(bf16[4,128,2,128]{3,2,1,0:T(2,128)(2,1)} %get-tuple-element.122), channel_id=1, source_target_pairs={{0,7},{1,6},{2,5},{3,4},{4,3},{5,2},{6,1},{7,0},{8,15},{9,14},{10,... | collective-permute-start | bytes 786440 | tf_op jit(solution)/shard_map/ppermute | solution.py:421
  80.9 70.7 %all-to-all-start.1 = ((bf16[16,128,512]{2,1,0:T(8,128)(2,1)}), bf16[16,128,512]{2,1,0:T(8,128)(2,1)}, u32[]{:S(2)}, u32[]{:S(2)}) async-start(bf16[16,128,512]{2,1,0:T(8,128)(2,1)} %pack_tokens.2), calls=%async_computation.1 | async-start | bytes 4194304 | tf_op jit(solution)/shard_map/all_to_all | solution.py:423
  88.1 50.5 %collective-permute-start.9 = (bf16[4,128,2,128]{3,2,1,0:T(2,128)(2,1)}, bf16[4,128,2,128]{3,2,1,0:T(2,128)(2,1)S(1)}, u32[]{:S(2)}, u32[]{:S(2)}) collective-permute-start(bf16[4,128,2,128]{3,2,1,0:T(2,128)(2,1)} %get-tuple-element.145), channel_id=1, source_target_pairs={{0,1},{1,0},{2,3},{3,2},{4,5},{5,4},{6,7},{7,6},{8,9},{9,8},{10,11... | collective-permute-start | bytes 786440 | tf_op jit(solution)/shard_map/ppermute | solution.py:421
  95.8 39.7 %collective-permute-start.7 = (f32[4,3,8,128]{3,2,1,0:T(8,128)}, f32[4,3,8,128]{3,2,1,0:T(8,128)S(1)}, u32[]{:S(2)}, u32[]{:S(2)}) collective-permute-start(f32[4,3,8,128]{3,2,1,0:T(8,128)} %row_stats.2.refs_8_), channel_id=1, source_target_pairs={{0,8},{1,9},{2,10},{3,11},{4,12},{5,13},{6,14},{7,15},{8,0},{9,1},... | collective-permute-start | bytes 147464 | tf_op jit(solution)/shard_map/ppermute | solution.py:438
  97.9 53.6 %collective-permute-start.10 = (bf16[4,128,2,128]{3,2,1,0:T(2,128)(2,1)}, bf16[4,128,2,128]{3,2,1,0:T(2,128)(2,1)S(1)}, u32[]{:S(2)}, u32[]{:S(2)}) collective-permute-start(bf16[4,128,2,128]{3,2,1,0:T(2,128)(2,1)} %get-tuple-element.146), channel_id=1, source_target_pairs={{0,2},{1,3},{2,0},{3,1},{4,6},{5,7},{6,4},{7,5},{8,10},{9,11},{10,... | collective-permute-start | bytes 786440 | tf_op jit(solution)/shard_map/ppermute | solution.py:421
  98.2 53.3 %collective-permute-start.11 = (bf16[4,128,2,128]{3,2,1,0:T(2,128)(2,1)}, bf16[4,128,2,128]{3,2,1,0:T(2,128)(2,1)S(1)}, u32[]{:S(2)}, u32[]{:S(2)}) collective-permute-start(bf16[4,128,2,128]{3,2,1,0:T(2,128)(2,1)} %get-tuple-element.147), channel_id=1, source_target_pairs={{0,3},{1,2},{2,1},{3,0},{4,7},{5,6},{6,5},{7,4},{8,11},{9,10},{10,... | collective-permute-start | bytes 786440 | tf_op jit(solution)/shard_map/ppermute | solution.py:421
  100.0 51.6 %collective-permute-start.12 = (bf16[4,128,2,128]{3,2,1,0:T(2,128)(2,1)}, bf16[4,128,2,128]{3,2,1,0:T(2,128)(2,1)}, u32[]{:S(2)}, u32[]{:S(2)}) collective-permute-start(bf16[4,128,2,128]{3,2,1,0:T(2,128)(2,1)} %get-tuple-element.149), channel_id=1, source_target_pairs={{0,5},{1,4},{2,7},{3,6},{4,1},{5,0},{6,3},{7,2},{8,13},{9,12},{10,... | collective-permute-start | bytes 786440 | tf_op jit(solution)/shard_map/ppermute | solution.py:421
  161.4 69.7 %all-to-all-start.2 = ((bf16[16,128,512]{2,1,0:T(8,128)(2,1)}), bf16[16,128,512]{2,1,0:T(8,128)(2,1)}, u32[]{:S(2)}, u32[]{:S(2)}) async-start(bf16[16,128,512]{2,1,0:T(8,128)(2,1)} %get-tuple-element.172), calls=%async_computation.2 | async-start | bytes 4194304 | tf_op jit(solution)/shard_map/all_to_all | solution.py:423
  167.6 50.5 %collective-permute-start.17 = (bf16[4,128,2,128]{3,2,1,0:T(2,128)(2,1)}, bf16[4,128,2,128]{3,2,1,0:T(2,128)(2,1)S(1)}, u32[]{:S(2)}, u32[]{:S(2)}) collective-permute-start(bf16[4,128,2,128]{3,2,1,0:T(2,128)(2,1)} %bitcast.9), channel_id=1, source_target_pairs={{0,1},{1,0},{2,3},{3,2},{4,5},{5,4},{6,7},{7,6},{8,9},{9,8},{10,11... | collective-permute-start | bytes 786440 | tf_op jit(solution)/shard_map/ppermute | solution.py:421
  173.6 41.4 %collective-permute-start.15 = (f32[4,3,8,128]{3,2,1,0:T(8,128)}, f32[4,3,8,128]{3,2,1,0:T(8,128)S(1)}, u32[]{:S(2)}, u32[]{:S(2)}) collective-permute-start(f32[4,3,8,128]{3,2,1,0:T(8,128)} %row_stats.3.refs_8_), channel_id=1, source_target_pairs={{0,8},{1,9},{2,10},{3,11},{4,12},{5,13},{6,14},{7,15},{8,0},{9,1},... | collective-permute-start | bytes 147464 | tf_op jit(solution)/shard_map/ppermute | solution.py:438
  175.8 55.2 %collective-permute-start.18 = (bf16[4,128,2,128]{3,2,1,0:T(2,128)(2,1)}, bf16[4,128,2,128]{3,2,1,0:T(2,128)(2,1)S(1)}, u32[]{:S(2)}, u32[]{:S(2)}) collective-permute-start(bf16[4,128,2,128]{3,2,1,0:T(2,128)(2,1)} %bitcast.10), channel_id=1, source_target_pairs={{0,2},{1,3},{2,0},{3,1},{4,6},{5,7},{6,4},{7,5},{8,10},{9,11},{10,... | collective-permute-start | bytes 786440 | tf_op jit(solution)/shard_map/ppermute | solution.py:421
  176.0 55.0 %collective-permute-start.19 = (bf16[4,128,2,128]{3,2,1,0:T(2,128)(2,1)}, bf16[4,128,2,128]{3,2,1,0:T(2,128)(2,1)S(1)}, u32[]{:S(2)}, u32[]{:S(2)}) collective-permute-start(bf16[4,128,2,128]{3,2,1,0:T(2,128)(2,1)} %bitcast.57), channel_id=1, source_target_pairs={{0,3},{1,2},{2,1},{3,0},{4,7},{5,6},{6,5},{7,4},{8,11},{9,10},{10,... | collective-permute-start | bytes 786440 | tf_op jit(solution)/shard_map/ppermute | solution.py:421
  177.8 53.2 %collective-permute-start.20 = (bf16[4,128,2,128]{3,2,1,0:T(2,128)(2,1)}, bf16[4,128,2,128]{3,2,1,0:T(2,128)(2,1)}, u32[]{:S(2)}, u32[]{:S(2)}) collective-permute-start(bf16[4,128,2,128]{3,2,1,0:T(2,128)(2,1)} %bitcast.56), channel_id=1, source_target_pairs={{0,5},{1,4},{2,7},{3,6},{4,1},{5,0},{6,3},{7,2},{8,13},{9,12},{10,... | collective-permute-start | bytes 786440 | tf_op jit(solution)/shard_map/ppermute | solution.py:421
  240.9 63.9 %all-to-all-start.3 = ((bf16[16,128,512]{2,1,0:T(8,128)(2,1)}), bf16[16,128,512]{2,1,0:T(8,128)(2,1)}, u32[]{:S(2)}, u32[]{:S(2)}) async-start(bf16[16,128,512]{2,1,0:T(8,128)(2,1)} %get-tuple-element.183), calls=%async_computation.3 | async-start | bytes 4194304 | tf_op jit(solution)/shard_map/all_to_all | solution.py:423
  247.6 17.7 %collective-permute-start.25 = (bf16[4,128,2,128]{3,2,1,0:T(2,128)(2,1)}, bf16[4,128,2,128]{3,2,1,0:T(2,128)(2,1)S(1)}, u32[]{:S(2)}, u32[]{:S(2)}) collective-permute-start(bf16[4,128,2,128]{3,2,1,0:T(2,128)(2,1)} %bitcast.26), channel_id=1, source_target_pairs={{0,2},{1,3},{2,0},{3,1},{4,6},{5,7},{6,4},{7,5},{8,10},{9,11},{10,... | collective-permute-start | bytes 786440 | tf_op jit(solution)/shard_map/ppermute | solution.py:421
  247.8 26.4 %collective-permute-start.26 = (bf16[4,128,2,128]{3,2,1,0:T(2,128)(2,1)}, bf16[4,128,2,128]{3,2,1,0:T(2,128)(2,1)S(1)}, u32[]{:S(2)}, u32[]{:S(2)}) collective-permute-start(bf16[4,128,2,128]{3,2,1,0:T(2,128)(2,1)} %bitcast.27), channel_id=1, source_target_pairs={{0,3},{1,2},{2,1},{3,0},{4,7},{5,6},{6,5},{7,4},{8,11},{9,10},{10,... | collective-permute-start | bytes 786440 | tf_op jit(solution)/shard_map/ppermute | solution.py:421
  249.4 40.0 %collective-permute-start.27 = (bf16[4,128,2,128]{3,2,1,0:T(2,128)(2,1)}, bf16[4,128,2,128]{3,2,1,0:T(2,128)(2,1)}, u32[]{:S(2)}, u32[]{:S(2)}) collective-permute-start(bf16[4,128,2,128]{3,2,1,0:T(2,128)(2,1)} %bitcast.29), channel_id=1, source_target_pairs={{0,5},{1,4},{2,7},{3,6},{4,1},{5,0},{6,3},{7,2},{8,13},{9,12},{10,... | collective-permute-start | bytes 786440 | tf_op jit(solution)/shard_map/ppermute | solution.py:421
  249.6 45.4 %collective-permute-start.28 = (bf16[4,128,2,128]{3,2,1,0:T(2,128)(2,1)}, bf16[4,128,2,128]{3,2,1,0:T(2,128)(2,1)}, u32[]{:S(2)}, u32[]{:S(2)}) collective-permute-start(bf16[4,128,2,128]{3,2,1,0:T(2,128)(2,1)} %bitcast.30), channel_id=1, source_target_pairs={{0,6},{1,7},{2,4},{3,5},{4,2},{5,3},{6,0},{7,1},{8,14},{9,15},{10,... | collective-permute-start | bytes 786440 | tf_op jit(solution)/shard_map/ppermute | solution.py:421
  250.8 51.4 %collective-permute-start.29 = (bf16[4,128,2,128]{3,2,1,0:T(2,128)(2,1)}, bf16[4,128,2,128]{3,2,1,0:T(2,128)(2,1)}, u32[]{:S(2)}, u32[]{:S(2)}) collective-permute-start(bf16[4,128,2,128]{3,2,1,0:T(2,128)(2,1)} %bitcast.31), channel_id=1, source_target_pairs={{0,7},{1,6},{2,5},{3,4},{4,3},{5,2},{6,1},{7,0},{8,15},{9,14},{10,... | collective-permute-start | bytes 786440 | tf_op jit(solution)/shard_map/ppermute | solution.py:421
  (31 other events, 393.8 us)

commit v10 on v9

--- a/solution.py
+++ b/solution.py
@@ -192,13 +192,15 @@
     half = len(rows)
     heads = rows[0].shape[0]
     width = heads * HD
+    rows = [row if k < half // 2 else row.reshape(2, heads, NTOK, 2, HD) for k, row in enumerate(rows)]
 
     def kernel(*refs):
         ins, (n_ref, buffer, come, go) = refs[:half], refs[-4:]
+        taken = [ref if len(ref.shape) == 4 else ref.at[other_place(half)] for ref in ins]
         loads = [
             [
                 pltpu.make_async_copy(
-                    ins[k].at[h], buffer.at[k, :, :, pl.ds(h * HD, HD)], come.at[k, h]
+                    taken[k].at[h], buffer.at[k, :, :, pl.ds(h * HD, HD)], come.at[k, h]
                 )
                 for h in range(heads)
             ]
@@ -273,7 +275,7 @@
     return scores, dot(values, grads, NT)
 
 
-def stats_kernel(slots_ref, t_ref, *refs):
+def stats_kernel(slots_ref, other_ref, t_ref, *refs):
     half = t_ref.shape[0] // 2
     rows, out_ref, spans_ref, words = refs[:half], refs[half], refs[half + 1], refs[half + 2]
     arrange(t_ref, spans_ref)
@@ -290,25 +292,30 @@
         out_ref[0, 2, pl.ds(local, 1)] = jnp.sum(power * prob_grad, 0, keepdims=True)
 
 
-def in_blocks(devices, heads):
-    half = devices // 2
-    tokens = pl.BlockSpec((devices, 2 * SPAN, HD), lambda h, slots: (0, 0, h))
-    row = pl.BlockSpec((1, 2 * NTOK, HD), lambda h, slots: (h, 0, 0))
-    return tokens, [row] * half
+def in_blocks(devices, rows):
+    tokens = pl.BlockSpec((devices, 2 * SPAN, HD), lambda h, slots, other: (0, 0, h))
+    row = pl.BlockSpec((1, 2 * NTOK, HD), lambda h, slots, other: (h, 0, 0))
+    gathered = pl.BlockSpec((None, 1, 2 * NTOK, HD), lambda h, slots, other: (other[0], h, 0, 0))
+    return tokens, row, [gathered if block.ndim == 4 else row for block in rows]
+
+
+def other_place(half):
+    return 1 - lax.rem(lax.axis_index("fsdp"), half) // (half // 2)
 
 
 def row_stats(slots, tokens, rows):
     devices = tokens.shape[0]
     half = devices // 2
     heads = rows[0].shape[0]
-    token_block, row_blocks = in_blocks(devices, heads)
+    token_block, row_block, row_blocks = in_blocks(devices, rows)
+    other_slot = jnp.stack([other_place(half), 1 - lax.axis_index("fsdp") // half]).astype(jnp.int32)
     return pl.pallas_call(
         stats_kernel,
         grid_spec=pltpu.PrefetchScalarGridSpec(
-            num_scalar_prefetch=1,
+            num_scalar_prefetch=2,
             grid=(heads,),
             in_specs=[token_block] + row_blocks,
-            out_specs=pl.BlockSpec((1, 3, half, HD), lambda h, slots: (h, 0, 0, 0)),
+            out_specs=pl.BlockSpec((1, 3, half, HD), lambda h, slots, other: (h, 0, 0, 0)),
             scratch_shapes=[
                 pltpu.VMEM((devices, 2 * SPAN, HD), BF16),
                 pltpu.VMEM((4, 2 * NTOK, HD), F32),
@@ -318,10 +325,10 @@
         compiler_params=LIMIT,
         cost_estimate=cost(6),
         name="row_stats",
-    )(slots, tokens, *rows)
-
-
-def grads_kernel(slots_ref, t_ref, *refs):
+    )(slots, other_slot, tokens, *rows)
+
+
+def grads_kernel(slots_ref, place_ref, t_ref, *refs):
     devices = t_ref.shape[0]
     half = devices // 2
     rows, refs = refs[:half], refs[half:]
@@ -384,15 +391,19 @@
     devices = tokens.shape[0]
     half = devices // 2
     heads = rows[0].shape[0]
-    token_block, row_blocks = in_blocks(devices, heads)
-    stats_block = pl.BlockSpec((1, 3, half, HD), lambda h, slots: (h, 0, 0, 0))
+    token_block, row_block, row_blocks = in_blocks(devices, rows)
+    other_slot = jnp.stack([other_place(half), 1 - lax.axis_index("fsdp") // half]).astype(jnp.int32)
+    stats_block = pl.BlockSpec((1, 3, half, HD), lambda h, slots, other: (h, 0, 0, 0))
+    other_block = pl.BlockSpec(
+        (None, 1, 3, half, HD), lambda h, slots, other: (other[1], h, 0, 0, 0)
+    )
     results = pl.pallas_call(
         grads_kernel,
         grid_spec=pltpu.PrefetchScalarGridSpec(
-            num_scalar_prefetch=1,
+            num_scalar_prefetch=2,
             grid=(heads,),
-            in_specs=[token_block] + row_blocks + [stats_block, stats_block],
-            out_specs=[token_block] + row_blocks,
+            in_specs=[token_block] + row_blocks + [stats_block, other_block],
+            out_specs=[token_block] + [row_block] * half,
             scratch_shapes=[
                 pltpu.VMEM((devices, 2 * SPAN, HD), BF16),
                 pltpu.VMEM((8, 2 * NTOK, HD), F32),
@@ -401,11 +412,11 @@
             ],
         ),
         out_shape=[jax.ShapeDtypeStruct(tokens.shape, BF16)]
-        + [jax.ShapeDtypeStruct(rows[0].shape, BF16)] * half,
+        + [jax.ShapeDtypeStruct((heads, 2 * NTOK, HD), BF16)] * half,
         compiler_params=LIMIT,
         cost_estimate=cost(12),
         name="grads",
-    )(slots, tokens, *rows, own, other)
+    )(slots, other_slot, tokens, *rows, own, other)
     return results[0], results[1:]
 
 
@@ -417,9 +428,12 @@
     half = len(rows)
     quarter = half // 2
     moved = list(rows)
-    for k in list(range(quarter, half)) + list(range(1, quarter)):
+    for k in range(quarter, half):
+        pairs = [[i, i ^ k] for i in range(devices) if i < i ^ k]
+        block = rows[k].reshape(-1, 2 * NTOK, HD)
+        moved[k] = lax.all_gather(block, "fsdp", axis_index_groups=pairs)
+    for k in range(1, quarter):
         moved[k] = lax.ppermute(rows[k], "fsdp", [(i, i ^ k) for i in range(devices)])
-    tokens, moved[quarter] = after(tokens, moved[quarter])
     tokens = lax.all_to_all(tokens, "fsdp", split_axis=0, concat_axis=0, tiled=True)
     return tokens, moved
 
@@ -429,13 +443,13 @@
     half = devices // 2
     heads = queries.shape[1] // HD // half
     chunks = math.gcd(heads, CHUNKS)
-    across = [(i, i ^ half) for i in range(devices)]
+    across = [[i, i + half] for i in range(half)]
     slots = jnp.argsort(neighbour_ids, stable=True).astype(jnp.int32)
 
     def compute(tokens, rows):
-        rows = [row.reshape(-1, 2 * NTOK, HD) for row in rows]
+        rows = [row if k >= half // 2 else row.reshape(-1, 2 * NTOK, HD) for k, row in enumerate(rows)]
         own = row_stats(slots, tokens, rows)
-        other = lax.ppermute(own, "fsdp", across)
+        other = lax.all_gather(own, "fsdp", axis_index_groups=across)
         token_grads, row_grads = grads(slots, tokens, rows, own, other)
         return token_grads, [row.reshape(-1, NTOK, 2, HD) for row in row_grads]
 

time: 310 us -> 385 us (1.24)
  blocking collectives: 0 us -> 285 us
  waiting for transfers between devices: 187 us -> 0.04 us
  starting transfers between devices: 60.6 us -> 33.5 us
    all_gather x0 -> x18, blocking collectives: none -> 285 us  [the longest x16 205 us: swap(): moved[k] = lax.all_gather(block, 'fsdp', axis_index_groups=pairs)]
    ppermute x28 -> x12, waiting for transfers between devices: 114 us -> 0.03 us  [swap(): lax.ppermute(rows[k], 'fsdp', [(i, i ^ k) for i in range(devices)])]
    ppermute x2 -> x0, waiting for transfers between devices: 72.8 us -> none  [compute(): other = lax.ppermute(own, 'fsdp', across)]
    ppermute x28 -> x12, starting transfers between devices: 29.3 us -> 9.67 us  [swap(): lax.ppermute(rows[k], 'fsdp', [(i, i ^ k) for i in range(devices)])]
    ppermute x2 -> x0, starting transfers between devices: 4.22 us -> none  [compute(): other = lax.ppermute(own, 'fsdp', across)]
  transfers between devices with their start and end apart: 34 -> 16, of which waited for: 16 -> 0; matrix products, arithmetic and copies ran while one was open for 1% -> 1% of each run, Pallas kernels for 17% -> 14%
where the time goes in v10:
time: 385 us; the launch traced here: 381 us
  blocking collectives  285 us (74%)
  Pallas kernels  56.8 us (15%)
  starting transfers between devices  33.5 us (9%)
    all_gather x16, blocking collectives, swap(): moved[k] = lax.all_gather(block, 'fsdp', axis_index_groups=pairs)  205 us
    all_gather x2, blocking collectives, compute(): other = lax.all_gather(own, 'fsdp', axis_index_groups=across)  81 us
    pallas_call x2, Pallas kernels, grads(): pl.pallas_call(grads_kernel, grid_spec=pltpu.PrefetchScalarGridSpec(num_s...  24.7 us
    all_to_all x4, starting transfers between devices, swap(): lax.all_to_all(tokens, 'fsdp', split_axis=0, concat_axis=0, tiled=True)  23.8 us
    pallas_call x2, Pallas kernels, row_stats(): pl.pallas_call(stats_kernel, grid_spec=pltpu.PrefetchScalarGridSpec(num_s...  11.5 us
    ppermute x12, starting transfers between devices, swap(): lax.ppermute(rows[k], 'fsdp', [(i, i ^ k) for i in range(devices)])  9.67 us
  transfers between devices with their start and end apart: 16, of which 0 were waited for; matrix products, arithmetic and copies ran while one was open for 1% of the time, Pallas kernels for 14%

profile of v10, /device:TPU:15, one launch (start us, length us, event | category | flops | bytes accessed | tf_op | source)
XLA Modules:
  0.0 380.7 jit_solution(50105638267851721)
XLA Ops:
  3.1 6.6 %all-to-all-start = ((bf16[16,128,512]{2,1,0:T(8,128)(2,1)}), bf16[16,128,512]{2,1,0:T(8,128)(2,1)}, u32[]{:S(2)}, u32[]{:S(2)}) async-start(bf16[16,128,512]{2,1,0:T(8,128)(2,1)} %pack_tokens.3), calls=%async_computation | async-start | bytes 4194304 | tf_op jit(solution)/shard_map/all_to_all | solution.py:437
  19.7 31.4 %all_gather.60.refs_4_ = bf16[2,4,256,128]{3,2,1,0:T(8,128)(2,1)} all-gather(bf16[1,4,256,128]{3,2,1,0:T(8,128)(2,1)} %bitcast.95), channel_id=1, replica_groups={{0,4},{1,5},{2,6},{3,7},{8,12},{9,13},{10,14},{11,15},{16,20},{17,21},{..., dimensions={0}, use_global_device_ids=true | all-gather | bytes 786432 | tf_op jit(solution)/shard_map/all_gather | solution.py:434
  51.1 9.8 %all_gather.61.refs_5_ = bf16[2,4,256,128]{3,2,1,0:T(8,128)(2,1)} all-gather(bf16[1,4,256,128]{3,2,1,0:T(8,128)(2,1)} %bitcast.94), channel_id=1, replica_groups={{0,5},{1,4},{2,7},{3,6},{8,13},{9,12},{10,15},{11,14},{16,21},{17,20},{..., dimensions={0}, use_global_device_ids=true | all-gather | bytes 786432 | tf_op jit(solution)/shard_map/all_gather | solution.py:434
  60.8 12.5 %all_gather.62.refs_6_ = bf16[2,4,256,128]{3,2,1,0:T(8,128)(2,1)} all-gather(bf16[1,4,256,128]{3,2,1,0:T(8,128)(2,1)} %bitcast.93), channel_id=1, replica_groups={{0,6},{1,7},{2,4},{3,5},{8,14},{9,15},{10,12},{11,13},{16,22},{17,23},{..., dimensions={0}, use_global_device_ids=true | all-gather | bytes 786432 | tf_op jit(solution)/shard_map/all_gather | solution.py:434
  73.3 10.3 %all_gather.63.refs_7_ = bf16[2,4,256,128]{3,2,1,0:T(8,128)(2,1)} all-gather(bf16[1,4,256,128]{3,2,1,0:T(8,128)(2,1)S(1)} %bitcast.92), channel_id=1, replica_groups={{0,7},{1,6},{2,5},{3,4},{8,15},{9,14},{10,13},{11,12},{16,23},{17,22},{..., dimensions={0}, use_global_device_ids=true | all-gather | bytes 786432 | tf_op jit(solution)/shard_map/all_gather | solution.py:434
  92.2 5.7 %row_stats.2.refs_8_ = f32[4,3,8,128]{3,2,1,0:T(8,128)} custom-call(s32[32]{0:T(128)} %get-tuple-element.96.slots_ref, s32[2]{0:T(128)} %pad_add_fusion.other_ref.place_ref, bf16[16,128,512]{2,1,0:T(8,128)(2,1)} %all-to-all-done.t_ref, bf16[4,256,128]{2,1,0:T(8,128)(2,1)} %bitcast.62, bf16[4,256,128]{2,1,0:T(8,128)(2,1)} %bitcast.64, ...), custom_call_target="tpu_custom_call" | custom-call | bytes 22140000 | tf_op jit(solution)/shard_map/row_stats/pallas_call | solution.py:312
  98.0 39.4 %all-gather = f32[8,3,8,128]{3,2,1,0:T(8,128)} all-gather(f32[4,3,8,128]{3,2,1,0:T(8,128)} %row_stats.2.refs_8_), channel_id=2, replica_groups={{0,8},{1,9},{2,10},{3,11},{4,12},{5,13},{6,14},{7,15},{16,24},{17,25},{..., dimensions={0}, use_global_device_ids=true | all-gather | bytes 147456 | tf_op jit(solution)/shard_map/all_gather | solution.py:452
  137.4 12.4 %grads.2 = (bf16[16,128,512]{2,1,0:T(8,128)(2,1)}, bf16[4,256,128]{2,1,0:T(8,128)(2,1)}, bf16[4,256,128]{2,1,0:T(8,128)(2,1)}, bf16[4,256,128]{2,1,0:T(8,128)(2,...) custom-call(s32[32]{0:T(128)} %get-tuple-element.96.slots_ref, ...), custom_call_target="tpu_custom_call" | custom-call | bytes 44280000 | tf_op jit(solution)/shard_map/grads/pallas_call | solution.py:400
  152.4 10.7 %all_gather.66.refs_4_ = bf16[2,4,256,128]{3,2,1,0:T(8,128)(2,1)} all-gather(bf16[1,4,256,128]{3,2,1,0:T(8,128)(2,1)S(1)} %bitcast.81), channel_id=1, replica_groups={{0,4},{1,5},{2,6},{3,7},{8,12},{9,13},{10,14},{11,15},{16,20},{17,21},{..., dimensions={0}, use_global_device_ids=true | all-gather | bytes 786432 | tf_op jit(solution)/shard_map/all_gather | solution.py:434
  163.0 9.3 %all_gather.67.refs_5_ = bf16[2,4,256,128]{3,2,1,0:T(8,128)(2,1)} all-gather(bf16[1,4,256,128]{3,2,1,0:T(8,128)(2,1)S(1)} %bitcast.80), channel_id=1, replica_groups={{0,5},{1,4},{2,7},{3,6},{8,13},{9,12},{10,15},{11,14},{16,21},{17,20},{..., dimensions={0}, use_global_device_ids=true | all-gather | bytes 786432 | tf_op jit(solution)/shard_map/all_gather | solution.py:434
  172.4 9.2 %all_gather.68.refs_6_ = bf16[2,4,256,128]{3,2,1,0:T(8,128)(2,1)} all-gather(bf16[1,4,256,128]{3,2,1,0:T(8,128)(2,1)S(1)} %bitcast.79), channel_id=1, replica_groups={{0,6},{1,7},{2,4},{3,5},{8,14},{9,15},{10,12},{11,13},{16,22},{17,23},{..., dimensions={0}, use_global_device_ids=true | all-gather | bytes 786432 | tf_op jit(solution)/shard_map/all_gather | solution.py:434
  181.5 10.1 %all_gather.69.refs_7_ = bf16[2,4,256,128]{3,2,1,0:T(8,128)(2,1)} all-gather(bf16[1,4,256,128]{3,2,1,0:T(8,128)(2,1)S(1)} %bitcast.78), channel_id=1, replica_groups={{0,7},{1,6},{2,5},{3,4},{8,15},{9,14},{10,13},{11,12},{16,23},{17,22},{..., dimensions={0}, use_global_device_ids=true | all-gather | bytes 786432 | tf_op jit(solution)/shard_map/all_gather | solution.py:434
  192.5 5.8 %all-to-all-start.2 = ((bf16[16,128,512]{2,1,0:T(8,128)(2,1)}), bf16[16,128,512]{2,1,0:T(8,128)(2,1)}, u32[]{:S(2)}, u32[]{:S(2)}) async-start(bf16[16,128,512]{2,1,0:T(8,128)(2,1)} %get-tuple-element.158), calls=%async_computation.2 | async-start | bytes 4194304 | tf_op jit(solution)/shard_map/all_to_all | solution.py:437
  204.1 41.6 %all-gather.1 = f32[8,3,8,128]{3,2,1,0:T(8,128)} all-gather(f32[4,3,8,128]{3,2,1,0:T(8,128)} %row_stats.3.refs_8_), channel_id=3, replica_groups={{0,8},{1,9},{2,10},{3,11},{4,12},{5,13},{6,14},{7,15},{16,24},{17,25},{..., dimensions={0}, use_global_device_ids=true | all-gather | bytes 147456 | tf_op jit(solution)/shard_map/all_gather | solution.py:452
  245.7 12.4 %grads.3 = (bf16[16,128,512]{2,1,0:T(8,128)(2,1)}, bf16[4,256,128]{2,1,0:T(8,128)(2,1)}, bf16[4,256,128]{2,1,0:T(8,128)(2,1)}, bf16[4,256,128]{2,1,0:T(8,128)(2,...) custom-call(s32[32]{0:T(128)} %get-tuple-element.96.slots_ref, ...), custom_call_target="tpu_custom_call" | custom-call | bytes 44280000 | tf_op jit(solution)/shard_map/grads/pallas_call | solution.py:400
  260.7 10.6 %all_gather.72 = bf16[2,4,256,128]{3,2,1,0:T(8,128)(2,1)} all-gather(bf16[1,4,256,128]{3,2,1,0:T(8,128)(2,1)S(1)} %bitcast.87), channel_id=1, replica_groups={{0,4},{1,5},{2,6},{3,7},{8,12},{9,13},{10,14},{11,15},{16,20},{17,21},{..., dimensions={0}, use_global_device_ids=true | all-gather | bytes 786432 | tf_op jit(solution)/shard_map/all_gather | solution.py:434
  271.3 9.4 %all_gather.73 = bf16[2,4,256,128]{3,2,1,0:T(8,128)(2,1)} all-gather(bf16[1,4,256,128]{3,2,1,0:T(8,128)(2,1)S(1)} %bitcast.86), channel_id=1, replica_groups={{0,5},{1,4},{2,7},{3,6},{8,13},{9,12},{10,15},{11,14},{16,21},{17,20},{..., dimensions={0}, use_global_device_ids=true | all-gather | bytes 786432 | tf_op jit(solution)/shard_map/all_gather | solution.py:434
  280.7 9.2 %all_gather.74 = bf16[2,4,256,128]{3,2,1,0:T(8,128)(2,1)} all-gather(bf16[1,4,256,128]{3,2,1,0:T(8,128)(2,1)S(1)} %bitcast.85), channel_id=1, replica_groups={{0,6},{1,7},{2,4},{3,5},{8,14},{9,15},{10,12},{11,13},{16,22},{17,23},{..., dimensions={0}, use_global_device_ids=true | all-gather | bytes 786432 | tf_op jit(solution)/shard_map/all_gather | solution.py:434
  289.9 10.1 %all_gather.75 = bf16[2,4,256,128]{3,2,1,0:T(8,128)(2,1)} all-gather(bf16[1,4,256,128]{3,2,1,0:T(8,128)(2,1)S(1)} %bitcast.83), channel_id=1, replica_groups={{0,7},{1,6},{2,5},{3,4},{8,15},{9,14},{10,13},{11,12},{16,23},{17,22},{..., dimensions={0}, use_global_device_ids=true | all-gather | bytes 786432 | tf_op jit(solution)/shard_map/all_gather | solution.py:434
  300.0 5.8 %all-to-all-start.3 = ((bf16[16,128,512]{2,1,0:T(8,128)(2,1)}), bf16[16,128,512]{2,1,0:T(8,128)(2,1)}, u32[]{:S(2)}, u32[]{:S(2)}) async-start(bf16[16,128,512]{2,1,0:T(8,128)(2,1)} %get-tuple-element.167), calls=%async_computation.3 | async-start | bytes 4194304 | tf_op jit(solution)/shard_map/all_to_all | solution.py:437
  313.3 33.8 %all_gather.76 = bf16[2,4,256,128]{3,2,1,0:T(8,128)(2,1)} all-gather(bf16[1,4,256,128]{3,2,1,0:T(8,128)(2,1)S(1)} %bitcast.91), channel_id=1, replica_groups={{0,4},{1,5},{2,6},{3,7},{8,12},{9,13},{10,14},{11,15},{16,20},{17,21},{..., dimensions={0}, use_global_device_ids=true | all-gather | bytes 786432 | tf_op jit(solution)/shard_map/all_gather | solution.py:434
  347.2 9.5 %all_gather.77 = bf16[2,4,256,128]{3,2,1,0:T(8,128)(2,1)} all-gather(bf16[1,4,256,128]{3,2,1,0:T(8,128)(2,1)S(1)} %bitcast.90), channel_id=1, replica_groups={{0,5},{1,4},{2,7},{3,6},{8,13},{9,12},{10,15},{11,14},{16,21},{17,20},{..., dimensions={0}, use_global_device_ids=true | all-gather | bytes 786432 | tf_op jit(solution)/shard_map/all_gather | solution.py:434
  356.7 8.9 %all_gather.78 = bf16[2,4,256,128]{3,2,1,0:T(8,128)(2,1)} all-gather(bf16[1,4,256,128]{3,2,1,0:T(8,128)(2,1)S(1)} %bitcast.89), channel_id=1, replica_groups={{0,6},{1,7},{2,4},{3,5},{8,14},{9,15},{10,12},{11,13},{16,22},{17,23},{..., dimensions={0}, use_global_device_ids=true | all-gather | bytes 786432 | tf_op jit(solution)/shard_map/all_gather | solution.py:434
  365.6 9.9 %all_gather.79 = bf16[2,4,256,128]{3,2,1,0:T(8,128)(2,1)} all-gather(bf16[1,4,256,128]{3,2,1,0:T(8,128)(2,1)S(1)} %bitcast.88), channel_id=1, replica_groups={{0,7},{1,6},{2,5},{3,4},{8,15},{9,14},{10,13},{11,12},{16,23},{17,22},{..., dimensions={0}, use_global_device_ids=true | all-gather | bytes 786432 | tf_op jit(solution)/shard_map/all_gather | solution.py:434
  (81 shorter events, 45.6 us)
Async XLA Ops:
  3.1 80.5 %all-to-all-start = ((bf16[16,128,512]{2,1,0:T(8,128)(2,1)}), bf16[16,128,512]{2,1,0:T(8,128)(2,1)}, u32[]{:S(2)}, u32[]{:S(2)}) async-start(bf16[16,128,512]{2,1,0:T(8,128)(2,1)} %pack_tokens.3), calls=%async_computation | async-start | bytes 4194304 | tf_op jit(solution)/shard_map/all_to_all | solution.py:437
  12.4 71.2 %collective-permute-start = (bf16[4,128,2,128]{3,2,1,0:T(2,128)(2,1)}, bf16[4,128,2,128]{3,2,1,0:T(2,128)(2,1)S(1)}, u32[]{:S(2)}, u32[]{:S(2)}) collective-permute-start(bf16[4,128,2,128]{3,2,1,0:T(2,128)(2,1)} %get-tuple-element.106), channel_id=1, source_target_pairs={{0,1},{1,0},{2,3},{3,2},{4,5},{5,4},{6,7},{7,6},{8,9},{9,8},{10,11... | collective-permute-start | bytes 786440 | tf_op jit(solution)/shard_map/ppermute | solution.py:436
  12.8 70.8 %collective-permute-start.1 = (bf16[4,128,2,128]{3,2,1,0:T(2,128)(2,1)}, bf16[4,128,2,128]{3,2,1,0:T(2,128)(2,1)S(1)}, u32[]{:S(2)}, u32[]{:S(2)}) collective-permute-start(bf16[4,128,2,128]{3,2,1,0:T(2,128)(2,1)} %get-tuple-element.107), channel_id=1, source_target_pairs={{0,2},{1,3},{2,0},{3,1},{4,6},{5,7},{6,4},{7,5},{8,10},{9,11},{10,... | collective-permute-start | bytes 786440 | tf_op jit(solution)/shard_map/ppermute | solution.py:436
  13.1 70.5 %collective-permute-start.2 = (bf16[4,128,2,128]{3,2,1,0:T(2,128)(2,1)}, bf16[4,128,2,128]{3,2,1,0:T(2,128)(2,1)S(1)}, u32[]{:S(2)}, u32[]{:S(2)}) collective-permute-start(bf16[4,128,2,128]{3,2,1,0:T(2,128)(2,1)} %get-tuple-element.108), channel_id=1, source_target_pairs={{0,3},{1,2},{2,1},{3,0},{4,7},{5,6},{6,5},{7,4},{8,11},{9,10},{10,... | collective-permute-start | bytes 786440 | tf_op jit(solution)/shard_map/ppermute | solution.py:436
  19.7 53.6 %copy-start.18 = (bf16[4,128,2,128]{3,2,1,0:T(2,128)(2,1)S(1)}, bf16[4,128,2,128]{3,2,1,0:T(2,128)(2,1)}, u32[]{:S(2)}) copy-start(bf16[4,128,2,128]{3,2,1,0:T(2,128)(2,1)} %get-tuple-element.112) | copy-start | bytes 786436
  84.4 107.2 %all-to-all-start.1 = ((bf16[16,128,512]{2,1,0:T(8,128)(2,1)}), bf16[16,128,512]{2,1,0:T(8,128)(2,1)}, u32[]{:S(2)}, u32[]{:S(2)}) async-start(bf16[16,128,512]{2,1,0:T(8,128)(2,1)} %pack_tokens.2), calls=%async_computation.1 | async-start | bytes 4194304 | tf_op jit(solution)/shard_map/all_to_all | solution.py:437
  137.3 35.0 %copy-start.7 = (bf16[4,128,2,128]{3,2,1,0:T(2,128)(2,1)S(1)}, bf16[4,128,2,128]{3,2,1,0:T(2,128)(2,1)}, u32[]{:S(2)}) copy-start(bf16[4,128,2,128]{3,2,1,0:T(2,128)(2,1)} %get-tuple-element.138) | copy-start | bytes 786436
  149.7 31.8 %copy-start.6 = (bf16[4,128,2,128]{3,2,1,0:T(2,128)(2,1)S(1)}, bf16[4,128,2,128]{3,2,1,0:T(2,128)(2,1)}, u32[]{:S(2)}) copy-start(bf16[4,128,2,128]{3,2,1,0:T(2,128)(2,1)} %get-tuple-element.139) | copy-start | bytes 786436
  149.7 41.9 %collective-permute-start.3 = (bf16[4,128,2,128]{3,2,1,0:T(2,128)(2,1)}, bf16[4,128,2,128]{3,2,1,0:T(2,128)(2,1)S(1)}, u32[]{:S(2)}, u32[]{:S(2)}) collective-permute-start(bf16[4,128,2,128]{3,2,1,0:T(2,128)(2,1)} %get-tuple-element.133), channel_id=1, source_target_pairs={{0,1},{1,0},{2,3},{3,2},{4,5},{5,4},{6,7},{7,6},{8,9},{9,8},{10,11... | collective-permute-start | bytes 786440 | tf_op jit(solution)/shard_map/ppermute | solution.py:436
  150.7 41.0 %collective-permute-start.4 = (bf16[4,128,2,128]{3,2,1,0:T(2,128)(2,1)}, bf16[4,128,2,128]{3,2,1,0:T(2,128)(2,1)S(1)}, u32[]{:S(2)}, u32[]{:S(2)}) collective-permute-start(bf16[4,128,2,128]{3,2,1,0:T(2,128)(2,1)} %get-tuple-element.134), channel_id=1, source_target_pairs={{0,2},{1,3},{2,0},{3,1},{4,6},{5,7},{6,4},{7,5},{8,10},{9,11},{10,... | collective-permute-start | bytes 786440 | tf_op jit(solution)/shard_map/ppermute | solution.py:436
  151.0 40.7 %collective-permute-start.5 = (bf16[4,128,2,128]{3,2,1,0:T(2,128)(2,1)}, bf16[4,128,2,128]{3,2,1,0:T(2,128)(2,1)S(1)}, u32[]{:S(2)}, u32[]{:S(2)}) collective-permute-start(bf16[4,128,2,128]{3,2,1,0:T(2,128)(2,1)} %get-tuple-element.135), channel_id=1, source_target_pairs={{0,3},{1,2},{2,1},{3,0},{4,7},{5,6},{6,5},{7,4},{8,11},{9,10},{10,... | collective-permute-start | bytes 786440 | tf_op jit(solution)/shard_map/ppermute | solution.py:436
  192.5 107.5 %all-to-all-start.2 = ((bf16[16,128,512]{2,1,0:T(8,128)(2,1)}), bf16[16,128,512]{2,1,0:T(8,128)(2,1)}, u32[]{:S(2)}, u32[]{:S(2)}) async-start(bf16[16,128,512]{2,1,0:T(8,128)(2,1)} %get-tuple-element.158), calls=%async_computation.2 | async-start | bytes 4194304 | tf_op jit(solution)/shard_map/all_to_all | solution.py:437
  245.7 35.0 %copy-start.11 = (bf16[4,256,128]{2,1,0:T(8,128)(2,1)S(1)}, bf16[4,256,128]{2,1,0:T(8,128)(2,1)}, u32[]{:S(2)}) copy-start(bf16[4,256,128]{2,1,0:T(8,128)(2,1)} %get-tuple-element.129) | copy-start | bytes 786436
  258.1 31.8 %copy-start.10 = (bf16[4,256,128]{2,1,0:T(8,128)(2,1)S(1)}, bf16[4,256,128]{2,1,0:T(8,128)(2,1)}, u32[]{:S(2)}) copy-start(bf16[4,256,128]{2,1,0:T(8,128)(2,1)} %get-tuple-element.130) | copy-start | bytes 786436
  258.1 41.9 %collective-permute-start.6 = (bf16[4,128,2,128]{3,2,1,0:T(2,128)(2,1)}, bf16[4,128,2,128]{3,2,1,0:T(2,128)(2,1)}, u32[]{:S(2)}, u32[]{:S(2)}) collective-permute-start(bf16[4,128,2,128]{3,2,1,0:T(2,128)(2,1)} %bitcast.98), channel_id=1, source_target_pairs={{0,1},{1,0},{2,3},{3,2},{4,5},{5,4},{6,7},{7,6},{8,9},{9,8},{10,11... | collective-permute-start | bytes 786440 | tf_op jit(solution)/shard_map/ppermute | solution.py:436
  259.0 41.0 %collective-permute-start.7 = (bf16[4,128,2,128]{3,2,1,0:T(2,128)(2,1)}, bf16[4,128,2,128]{3,2,1,0:T(2,128)(2,1)}, u32[]{:S(2)}, u32[]{:S(2)}) collective-permute-start(bf16[4,128,2,128]{3,2,1,0:T(2,128)(2,1)} %bitcast.97), channel_id=1, source_target_pairs={{0,2},{1,3},{2,0},{3,1},{4,6},{5,7},{6,4},{7,5},{8,10},{9,11},{10,... | collective-permute-start | bytes 786440 | tf_op jit(solution)/shard_map/ppermute | solution.py:436
  259.3 40.7 %collective-permute-start.8 = (bf16[4,128,2,128]{3,2,1,0:T(2,128)(2,1)}, bf16[4,128,2,128]{3,2,1,0:T(2,128)(2,1)}, u32[]{:S(2)}, u32[]{:S(2)}) collective-permute-start(bf16[4,128,2,128]{3,2,1,0:T(2,128)(2,1)} %bitcast.96), channel_id=1, source_target_pairs={{0,3},{1,2},{2,1},{3,0},{4,7},{5,6},{6,5},{7,4},{8,11},{9,10},{10,... | collective-permute-start | bytes 786440 | tf_op jit(solution)/shard_map/ppermute | solution.py:436
  300.0 78.1 %all-to-all-start.3 = ((bf16[16,128,512]{2,1,0:T(8,128)(2,1)}), bf16[16,128,512]{2,1,0:T(8,128)(2,1)}, u32[]{:S(2)}, u32[]{:S(2)}) async-start(bf16[16,128,512]{2,1,0:T(8,128)(2,1)} %get-tuple-element.167), calls=%async_computation.3 | async-start | bytes 4194304 | tf_op jit(solution)/shard_map/all_to_all | solution.py:437
  305.9 69.6 %collective-permute-start.9 = (bf16[4,128,2,128]{3,2,1,0:T(2,128)(2,1)}, bf16[4,128,2,128]{3,2,1,0:T(2,128)(2,1)}, u32[]{:S(2)}, u32[]{:S(2)}) collective-permute-start(bf16[4,128,2,128]{3,2,1,0:T(2,128)(2,1)} %bitcast.29), channel_id=1, source_target_pairs={{0,1},{1,0},{2,3},{3,2},{4,5},{5,4},{6,7},{7,6},{8,9},{9,8},{10,11... | collective-permute-start | bytes 786440 | tf_op jit(solution)/shard_map/ppermute | solution.py:436
  306.2 69.2 %collective-permute-start.10 = (bf16[4,128,2,128]{3,2,1,0:T(2,128)(2,1)}, bf16[4,128,2,128]{3,2,1,0:T(2,128)(2,1)}, u32[]{:S(2)}, u32[]{:S(2)}) collective-permute-start(bf16[4,128,2,128]{3,2,1,0:T(2,128)(2,1)} %bitcast.30), channel_id=1, source_target_pairs={{0,2},{1,3},{2,0},{3,1},{4,6},{5,7},{6,4},{7,5},{8,10},{9,11},{10,... | collective-permute-start | bytes 786440 | tf_op jit(solution)/shard_map/ppermute | solution.py:436
  306.5 69.0 %collective-permute-start.11 = (bf16[4,128,2,128]{3,2,1,0:T(2,128)(2,1)}, bf16[4,128,2,128]{3,2,1,0:T(2,128)(2,1)}, u32[]{:S(2)}, u32[]{:S(2)}) collective-permute-start(bf16[4,128,2,128]{3,2,1,0:T(2,128)(2,1)} %bitcast.31), channel_id=1, source_target_pairs={{0,3},{1,2},{2,1},{3,0},{4,7},{5,6},{6,5},{7,4},{8,11},{9,10},{10,... | collective-permute-start | bytes 786440 | tf_op jit(solution)/shard_map/ppermute | solution.py:436
  310.6 36.6 %copy-start.16 = (bf16[4,256,128]{2,1,0:T(8,128)(2,1)S(1)}, bf16[4,256,128]{2,1,0:T(8,128)(2,1)}, u32[]{:S(2)}) copy-start(bf16[4,256,128]{2,1,0:T(8,128)(2,1)} %get-tuple-element.155) | copy-start | bytes 786436
  310.6 46.1 %copy-start.15 = (bf16[4,256,128]{2,1,0:T(8,128)(2,1)S(1)}, bf16[4,256,128]{2,1,0:T(8,128)(2,1)}, u32[]{:S(2)}) copy-start(bf16[4,256,128]{2,1,0:T(8,128)(2,1)} %get-tuple-element.156) | copy-start | bytes 786436
  313.3 52.3 %copy-start.14 = (bf16[4,256,128]{2,1,0:T(8,128)(2,1)S(1)}, bf16[4,256,128]{2,1,0:T(8,128)(2,1)}, u32[]{:S(2)}) copy-start(bf16[4,256,128]{2,1,0:T(8,128)(2,1)} %get-tuple-element.157) | copy-start | bytes 786436
  (12 other events, 95.2 us)

commit v11 on v7

--- a/solution.py
+++ b/solution.py
@@ -14,7 +14,7 @@
 F32 = jnp.float32
 BF16 = jnp.bfloat16
 ANY = pl.BlockSpec(memory_space=pl.ANY)
-LIMIT = pltpu.CompilerParams(vmem_limit_bytes=56 * 2**20)
+LIMIT = pltpu.CompilerParams(vmem_limit_bytes=63 * 2**20)
 
 
 def dot(a, b, dims):
@@ -36,13 +36,39 @@
     return pltpu.VMEM(shape, BF16)
 
 
+def moves(devices):
+    quarter = devices // 4
+    return [(kind, offset) for offset in range(quarter) for kind in (0, 1, 2, 3)]
+
+
+def reached(index, devices, move):
+    kind, offset = move
+    quarter = devices // 4
+    plane, inner = index // quarter, index % quarter
+    plane = (plane, (2 * plane + 1) % 5, (3 * plane + 2) % 5, 3 - plane)[kind]
+    return plane * quarter + (inner ^ offset)
+
+
+def target(devices, move):
+    return reached(lax.axis_index("fsdp"), devices, move)
+
+
+def source(devices, move):
+    kind, offset = move
+    return reached(lax.axis_index("fsdp"), devices, ((0, 2, 1, 3)[kind], offset))
+
+
 def pack(queries, out_grad, neighbours, devices, chunk, chunks):
     heads = neighbours.shape[2] // HD // devices // chunks
     width = heads * HD
 
-    def kernel(q_ref, g_ref, n_ref, out_ref, plain, tokens, rows, come_t, come_r, go_t, go_r):
+    def kernel(q_ref, g_ref, n_ref, *refs):
+        outs, (plain, tokens, rows, come_t, come_r, go_t, go_r) = refs[:devices], refs[devices:]
         every = range(devices)
-        columns = [pl.ds((i * chunks + chunk) * width, width) for i in every]
+        columns = [
+            pl.ds(pl.multiple_of((target(devices, move) * chunks + chunk) * width, width), width)
+            for move in moves(devices)
+        ]
         token_loads = [
             [
                 pltpu.make_async_copy(
@@ -64,9 +90,9 @@
         for i in every:
             row_loads[i].wait()
             for h in range(heads):
-                source = rows.at[i, :, :, pl.ds(h * HD, HD)]
+                piece = rows.at[i, :, :, pl.ds(h * HD, HD)]
                 stores.append(
-                    pltpu.make_async_copy(source, out_ref.at[i, h, pl.ds(SPAN, NTOK)], go_r.at[i, h])
+                    pltpu.make_async_copy(piece, outs[i].at[h, pl.ds(SPAN, NTOK)], go_r.at[i, h])
                 )
                 stores[-1].start()
         for i in every:
@@ -75,16 +101,17 @@
             for h in range(heads):
                 folded = tokens.at[i, h].reshape(2 * SPAN, HD)
                 folded[...] = plain[i, :, pl.ds(h * HD, HD)]
-            stores.append(pltpu.make_async_copy(tokens.at[i], out_ref.at[i, :, pl.ds(0, SPAN)], go_t.at[i]))
+            stores.append(pltpu.make_async_copy(tokens.at[i], outs[i].at[:, pl.ds(0, SPAN)], go_t.at[i]))
             stores[-1].start()
         for store in stores:
             store.wait()
 
-    return pl.pallas_call(
+    shape = jax.ShapeDtypeStruct((heads, SPAN + NTOK, 2, HD), BF16)
+    results = pl.pallas_call(
         kernel,
         in_specs=[ANY] * 3,
-        out_specs=ANY,
-        out_shape=jax.ShapeDtypeStruct((devices, heads, SPAN + NTOK, 2, HD), BF16),
+        out_specs=[ANY] * devices,
+        out_shape=[shape] * devices,
         scratch_shapes=[
             vmem(devices, 2 * SPAN, width),
             vmem(devices, heads, SPAN, 2, HD),
@@ -98,20 +125,25 @@
         cost_estimate=cost(4),
         name="pack",
     )(queries, out_grad, neighbours)
+    return list(results)
 
 
 def unpack(blocks, before, chunk, chunks):
-    devices, heads = blocks.shape[:2]
+    devices, heads = len(blocks), blocks[0].shape[0]
     width = heads * HD
 
-    def kernel(b_ref, t_ref, *refs):
+    def kernel(*refs):
+        ins, flat = refs[:devices], refs[devices : 2 * devices]
         o_ref, q_ref, n_ref, rows, tokens, come_r, come_t, go_r, go_t = refs[-9:]
         every = range(devices)
-        columns = [pl.ds((i * chunks + chunk) * width, width) for i in every]
+        columns = [
+            pl.ds(pl.multiple_of((source(devices, move) * chunks + chunk) * width, width), width)
+            for move in moves(devices)
+        ]
         row_loads = [
             [
                 pltpu.make_async_copy(
-                    b_ref.at[i, h, pl.ds(SPAN, NTOK)],
+                    ins[i].at[h, pl.ds(SPAN, NTOK)],
                     rows.at[i, :, :, pl.ds(h * HD, HD)],
                     come_r.at[i, h],
                 )
@@ -122,7 +154,7 @@
         token_loads = [
             [
                 pltpu.make_async_copy(
-                    t_ref.at[i, h, pl.ds(0, 2 * SPAN)],
+                    flat[i].at[h, pl.ds(0, 2 * SPAN)],
                     tokens.at[i, :, pl.ds(h * HD, HD)],
                     come_t.at[i, h],
                 )
@@ -142,8 +174,8 @@
             for load in token_loads[i]:
                 load.wait()
             for part, ref in enumerate((o_ref, q_ref)):
-                source = tokens.at[i, pl.ds(part * SPAN, SPAN)]
-                stores.append(pltpu.make_async_copy(source, ref.at[:, columns[i]], go_t.at[i, part]))
+                piece = tokens.at[i, pl.ds(part * SPAN, SPAN)]
+                stores.append(pltpu.make_async_copy(piece, ref.at[:, columns[i]], go_t.at[i, part]))
                 stores[-1].start()
         for store in stores:
             store.wait()
@@ -151,14 +183,14 @@
     total = devices * width * chunks
     return pl.pallas_call(
         kernel,
-        in_specs=[ANY] * (2 + len(before)),
+        in_specs=[ANY] * (2 * devices + len(before)),
         out_specs=[ANY] * 3,
         out_shape=[
             jax.ShapeDtypeStruct((SPAN, total), BF16),
             jax.ShapeDtypeStruct((SPAN, total), BF16),
             jax.ShapeDtypeStruct((NTOK, 2, total), BF16),
         ],
-        input_output_aliases={2 + i: i for i in range(len(before))},
+        input_output_aliases={2 * devices + i: i for i in range(len(before))},
         scratch_shapes=[
             vmem(devices, NTOK, 2, width),
             vmem(devices, 2 * SPAN, width),
@@ -168,9 +200,9 @@
             pltpu.SemaphoreType.DMA((devices, 2)),
         ],
         compiler_params=LIMIT,
-        cost_estimate=cost(5),
+        cost_estimate=cost(4),
         name="unpack",
-    )(blocks, blocks.reshape(devices, heads, -1, HD), *before)
+    )(*blocks, *[block.reshape(heads, -1, HD) for block in blocks], *before)
 
 
 def last_rows():
@@ -190,20 +222,26 @@
     return jnp.concatenate([spans_ref[first // 2, rows], spans_ref[second // 2, rows]], 0)
 
 
-def attention_kernel(slots_ref, in_ref, out_ref, spans_ref, words, table, powers, probs, stats, sums):
-    devices = in_ref.shape[0]
+def attention_kernel(slots_ref, *refs):
+    devices = (len(refs) - 8) // 2
+    blocks, outs, refs = refs[:devices], refs[devices : 2 * devices], refs[2 * devices :]
+    raw, spans_ref, words, table, powers, probs, stats, sums = refs
+    order = moves(devices)
     scale = 1.0 / math.sqrt(HD)
     last = last_rows()
     left = lax.broadcasted_iota(jnp.int32, (1, HD), 1) < SPAN
+    for block, move in zip(blocks, order):
+        raw[source(devices, move)] = block[0, : 2 * SPAN]
     for c in range(devices):
-        own = in_ref[c, 0, : 2 * SPAN].astype(F32)
-        after = in_ref[c + 1, 0, : 2 * SPAN].astype(F32) if c + 1 < devices else jnp.zeros_like(own)
+        own = raw[c].astype(F32)
+        after = raw[c + 1].astype(F32) if c + 1 < devices else jnp.zeros_like(own)
         spans_ref[c] = jnp.where(last, own, after).astype(BF16)
     sums[...] = jnp.zeros_like(sums)
 
-    def measure(r, lane):
+    def measure(i, lane):
+        r = source(devices, order[i])
         first, second = slots_ref[2 * r], slots_ref[2 * r + 1]
-        keys, values = load_row(in_ref[r, 0, 2 * SPAN :], words.at[lane])
+        keys, values = load_row(blocks[i][0, 2 * SPAN :], words.at[lane])
         table[r, :NTOK] = keys
         table[r, NTOK:] = values
         scores = dot(keys, pair(spans_ref, first, second, 0), NT) * scale
@@ -226,7 +264,8 @@
     def mate(slot):
         return slot + 1 - 2 * lax.rem(slot, 2)
 
-    def derive(r, lane):
+    def derive(i, lane):
+        r = target(devices, order[i])
         first, second = slots_ref[2 * r], slots_ref[2 * r + 1]
         own = spread(first, second)
         other = spread(mate(first), mate(second))
@@ -240,7 +279,7 @@
         joined = words.at[lane]
         joined[pl.ds(0, NTOK, stride=2), :] = dot(score_grad, pair(spans_ref, first, second, 0), NN) * scale
         joined[pl.ds(1, NTOK, stride=2), :] = dot(weights, pair(spans_ref, first, second, 1), NN)
-        out_ref[r, 0, 2 * SPAN :] = joined[...].astype(BF16)
+        outs[i][0, 2 * SPAN :] = joined[...].astype(BF16)
         attended = dot(weights, table[r, NTOK:], TN)
         query_grad = dot(score_grad, table[r, :NTOK], TN) * scale
         for n, slot in enumerate((first, second)):
@@ -249,23 +288,26 @@
             sums[slot // 2 + 1, SPAN:] += query_grad[piece]
 
     for step in (measure, derive):
-        for r in range(devices):
-            step(r, r % 4)
-    for d in range(devices):
-        out_ref[d, 0, : 2 * SPAN] = jnp.where(last, sums[d + 1], sums[d]).astype(BF16)
+        for i in range(devices):
+            step(i, i % 4)
+    for out, move in zip(outs, order):
+        d = target(devices, move)
+        out[0, : 2 * SPAN] = jnp.where(last, sums[d + 1], sums[d]).astype(BF16)
 
 
 def attention(slots, blocks):
-    devices, heads, rows, _ = blocks.shape
-    block = pl.BlockSpec((devices, 1, rows, HD), lambda h, slots: (0, h, 0, 0))
-    return pl.pallas_call(
+    devices = len(blocks)
+    heads, rows, _ = blocks[0].shape
+    block = pl.BlockSpec((1, rows, HD), lambda h, slots: (h, 0, 0))
+    results = pl.pallas_call(
         attention_kernel,
         grid_spec=pltpu.PrefetchScalarGridSpec(
             num_scalar_prefetch=1,
             grid=(heads,),
-            in_specs=[block],
-            out_specs=block,
+            in_specs=[block] * devices,
+            out_specs=[block] * devices,
             scratch_shapes=[
+                vmem(devices, 2 * SPAN, HD),
                 vmem(devices, 2 * SPAN, HD),
                 pltpu.VMEM((4, 2 * NTOK, HD), F32),
                 vmem(devices, 2 * NTOK, HD),
@@ -275,11 +317,24 @@
                 pltpu.VMEM((devices + 1, 2 * SPAN, HD), F32),
             ],
         ),
-        out_shape=jax.ShapeDtypeStruct(blocks.shape, BF16),
+        out_shape=[jax.ShapeDtypeStruct(block.shape, BF16) for block in blocks],
         compiler_params=LIMIT,
-        cost_estimate=cost(14),
+        cost_estimate=cost(16 / CHUNKS),
         name="attention",
-    )(slots, blocks)
+    )(slots, *blocks)
+    return list(results)
+
+
+def after(later, earlier):
+    return lax.optimization_barrier((later, earlier))
+
+
+def swap(blocks):
+    devices = len(blocks)
+    return blocks[:1] + [
+        lax.ppermute(block, "fsdp", [(i, reached(i, devices, move)) for i in range(devices)])
+        for block, move in list(zip(blocks, moves(devices)))[1:]
+    ]
 
 
 def body(queries, out_grad, neighbours, neighbour_ids):
@@ -287,18 +342,23 @@
     heads = queries.shape[1] // HD // devices
     chunks = math.gcd(heads, CHUNKS)
     slots = jnp.argsort(neighbour_ids, stable=True).astype(jnp.int32)
-
-    def exchange(blocks):
-        return lax.all_to_all(blocks, "fsdp", split_axis=0, concat_axis=0, tiled=True)
-
-    arrived = [
-        exchange(pack(queries, out_grad, neighbours, devices, chunk, chunks)) for chunk in range(chunks)
-    ]
+    arrived, back = [], []
+    for chunk in range(chunks):
+        blocks = pack(queries, out_grad, neighbours, devices, chunk, chunks)
+        if arrived:
+            blocks, arrived[-1] = after(blocks, arrived[-1])
+        arrived.append(swap(blocks))
+    for chunk in range(chunks):
+        blocks = attention(slots, [block.reshape(block.shape[0], -1, HD) for block in arrived[chunk]])
+        blocks = [block.reshape(block.shape[0], -1, 2, HD) for block in blocks]
+        if back:
+            blocks, back[-1] = after(blocks, back[-1])
+        elif chunks > 1:
+            blocks, arrived[-1] = after(blocks, arrived[-1])
+        back.append(swap(blocks))
     outputs = ()
-    for chunk, blocks in enumerate(arrived):
-        results = attention(slots, blocks.reshape(devices, heads // chunks, -1, HD))
-        back = exchange(results.reshape(blocks.shape))
-        outputs = tuple(unpack(back, outputs, chunk, chunks))
+    for chunk in range(chunks):
+        outputs = tuple(unpack(back[chunk], outputs, chunk, chunks))
     return outputs
 
 

time: 315 us -> 307 us (0.975)
  waiting for transfers between devices: 254 us -> 157 us
  starting transfers between devices: 21.3 us -> 113 us
  local copies, waits for them, and re-layouts: 5.01 us -> 0.04 us
    all_to_all x4 -> x0, waiting for transfers between devices: 254 us -> none  [exchange(): lax.all_to_all(blocks, 'fsdp', split_axis=0, concat_axis=0, tiled=True)]
    ppermute x0 -> x60, waiting for transfers between devices: none -> 157 us  [swap(): lax.ppermute(block, 'fsdp', [(i, reached(i, devices, move)) for i in rang...]
    ppermute x0 -> x60, starting transfers between devices: none -> 113 us  [swap(): lax.ppermute(block, 'fsdp', [(i, reached(i, devices, move)) for i in rang...]
    all_to_all x4 -> x0, starting transfers between devices: 21.3 us -> none  [exchange(): lax.all_to_all(blocks, 'fsdp', split_axis=0, concat_axis=0, tiled=True)]
    unnamed x8 -> x20, local copies, waits for them, and re-layouts: 5.01 us -> 0.04 us
  transfers between devices with their start and end apart: 4 -> 60, of which waited for: 4 -> 31; matrix products, arithmetic and copies ran while one was open for 1% -> 1% of each run, Pallas kernels for 8% -> 8%
where the time goes in v11:
time: 307 us; the launch traced here: 306 us
  waiting for transfers between devices  157 us (51%)
  starting transfers between devices  113 us (37%)
  Pallas kernels  33.5 us (11%)
    ppermute x60, waiting for transfers between devices, swap(): lax.ppermute(block, 'fsdp', [(i, reached(i, devices, move)) for i in rang...  157 us
    ppermute x60, starting transfers between devices, swap(): lax.ppermute(block, 'fsdp', [(i, reached(i, devices, move)) for i in rang...  113 us
    pallas_call x2, Pallas kernels, attention(): pl.pallas_call(attention_kernel, grid_spec=pltpu.PrefetchScalarGridSpec(n...  17 us
    pallas_call x2, Pallas kernels, pack(): pl.pallas_call(kernel, in_specs=[ANY] * 3, out_specs=[ANY] * devices, out...  8.82 us
    pallas_call x2, Pallas kernels, unpack(): pl.pallas_call(kernel, in_specs=[ANY] * (2 * devices + len(before)), out_...  7.7 us
  transfers between devices with their start and end apart: 60, of which 31 were waited for; matrix products, arithmetic and copies ran while one was open for 1% of the time, Pallas kernels for 8%

profile of v11, /device:TPU:15, one launch (start us, length us, event | category | flops | bytes accessed | tf_op | source)
XLA Modules:
  0.0 306.4 jit_solution(16614478238081208619)
XLA Ops:
  0.6 4.4 %pack.3 = (bf16[2,192,2,128]{3,2,1,0:T(2,128)(2,1)}, bf16[2,192,2,128]{3,2,1,0:T(2,128)(2,1)}, bf16[2,192,2,128]{3,2,1,0:T(2,128)(2,1)}, bf16[2,192,2,128]{3,2,1...) custom-call(bf16[64,8192]{1,0:T(8,128)(2,1)} %q_ref.3, ...), custom_call_target="tpu_custom_call" | custom-call | bytes 14760000 | tf_op jit(solution)/shard_map/pack/pallas_call | solution.py:110
  19.2 5.6 %collective-permute-done.2 = bf16[2,192,2,128]{3,2,1,0:T(2,128)(2,1)S(1)} collective-permute-done((bf16[2,192,2,128]{3,2,1,0:T(2,128)(2,1)}, bf16[2,192,2,128]{3,2,1,0:T(2,128)(2,1)S(1)}, u32[]{:S(2)}, u32[]{:S(2)}) %collective-permute-start.2) | collective-permute-done | bytes 196640 | tf_op jit(solution)/shard_map/ppermute | solution.py:335
  26.0 10.7 %collective-permute-done.4 = bf16[2,192,2,128]{3,2,1,0:T(2,128)(2,1)S(1)} collective-permute-done((bf16[2,192,2,128]{3,2,1,0:T(2,128)(2,1)}, bf16[2,192,2,128]{3,2,1,0:T(2,128)(2,1)S(1)}, u32[]{:S(2)}, u32[]{:S(2)}) %collective-permute-start.4) | collective-permute-done | bytes 196640 | tf_op jit(solution)/shard_map/ppermute | solution.py:335
  42.9 9.2 %collective-permute-start.11 = (bf16[2,192,2,128]{3,2,1,0:T(2,128)(2,1)}, bf16[2,192,2,128]{3,2,1,0:T(2,128)(2,1)}, u32[]{:S(2)}, u32[]{:S(2)}) collective-permute-start(bf16[2,192,2,128]{3,2,1,0:T(2,128)(2,1)} %get-tuple-element.196), channel_id=1, source_target_pairs={{0,3},{1,2},{2,1},{3,0},{4,7},{5,6},{6,5},{7,4},{8,11},{9,10},{10,... | collective-permute-start | bytes 589832 | tf_op jit(solution)/shard_map/ppermute | solution.py:335
  58.1 4.4 %pack.2 = (bf16[2,192,2,128]{3,2,1,0:T(2,128)(2,1)}, bf16[2,192,2,128]{3,2,1,0:T(2,128)(2,1)}, bf16[2,192,2,128]{3,2,1,0:T(2,128)(2,1)}, bf16[2,192,2,128]{3,2,1...) custom-call(bf16[64,8192]{1,0:T(8,128)(2,1)} %q_ref.3, ...), custom_call_target="tpu_custom_call" | custom-call | bytes 14760000 | tf_op jit(solution)/shard_map/pack/pallas_call | solution.py:110
  62.5 7.0 %collective-permute-done.10 = bf16[2,192,2,128]{3,2,1,0:T(2,128)(2,1)} collective-permute-done((bf16[2,192,2,128]{3,2,1,0:T(2,128)(2,1)}, bf16[2,192,2,128]{3,2,1,0:T(2,128)(2,1)}, u32[]{:S(2)}, u32[]{:S(2)}) %collective-permute-start.10) | collective-permute-done | bytes 196640 | tf_op jit(solution)/shard_map/ppermute | solution.py:335
  92.8 6.3 %collective-permute-done.17 = bf16[2,192,2,128]{3,2,1,0:T(2,128)(2,1)} collective-permute-done((bf16[2,192,2,128]{3,2,1,0:T(2,128)(2,1)}, bf16[2,192,2,128]{3,2,1,0:T(2,128)(2,1)}, u32[]{:S(2)}, u32[]{:S(2)}) %collective-permute-start.17) | collective-permute-done | bytes 196640 | tf_op jit(solution)/shard_map/ppermute | solution.py:335
  99.0 7.0 %collective-permute-start.22 = (bf16[2,192,2,128]{3,2,1,0:T(2,128)(2,1)}, bf16[2,192,2,128]{3,2,1,0:T(2,128)(2,1)}, u32[]{:S(2)}, u32[]{:S(2)}) collective-permute-start(bf16[2,192,2,128]{3,2,1,0:T(2,128)(2,1)} %get-tuple-element.240), channel_id=1, source_target_pairs={{0,2},{1,3},{2,0},{3,1},{4,6},{5,7},{6,4},{7,5},{8,10},{9,11},{10,... | collective-permute-start | bytes 589832 | tf_op jit(solution)/shard_map/ppermute | solution.py:335
  108.2 5.6 %collective-permute-start.24 = (bf16[2,192,2,128]{3,2,1,0:T(2,128)(2,1)}, bf16[2,192,2,128]{3,2,1,0:T(2,128)(2,1)}, u32[]{:S(2)}, u32[]{:S(2)}) collective-permute-start(bf16[2,192,2,128]{3,2,1,0:T(2,128)(2,1)} %get-tuple-element.242), channel_id=1, source_target_pairs={{0,10},{1,11},{2,8},{3,9},{4,2},{5,3},{6,0},{7,1},{8,14},{9,15},{1... | collective-permute-start | bytes 589832 | tf_op jit(solution)/shard_map/ppermute | solution.py:335
  113.8 10.3 %collective-permute-done.21 = bf16[2,192,2,128]{3,2,1,0:T(2,128)(2,1)} collective-permute-done((bf16[2,192,2,128]{3,2,1,0:T(2,128)(2,1)}, bf16[2,192,2,128]{3,2,1,0:T(2,128)(2,1)}, u32[]{:S(2)}, u32[]{:S(2)}) %collective-permute-start.21) | collective-permute-done | bytes 196640 | tf_op jit(solution)/shard_map/ppermute | solution.py:335
  126.3 4.4 %collective-permute-start.28 = (bf16[2,192,2,128]{3,2,1,0:T(2,128)(2,1)}, bf16[2,192,2,128]{3,2,1,0:T(2,128)(2,1)}, u32[]{:S(2)}, u32[]{:S(2)}) collective-permute-start(bf16[2,192,2,128]{3,2,1,0:T(2,128)(2,1)} %get-tuple-element.246), channel_id=1, source_target_pairs={{0,11},{1,10},{2,9},{3,8},{4,3},{5,2},{6,1},{7,0},{8,15},{9,14},{1... | collective-permute-start | bytes 589832 | tf_op jit(solution)/shard_map/ppermute | solution.py:335
  133.5 8.5 %attention.2 = (bf16[2,384,128]{2,1,0:T(8,128)(2,1)}, bf16[2,384,128]{2,1,0:T(8,128)(2,1)}, bf16[2,384,128]{2,1,0:T(8,128)(2,1)}, bf16[2,384,128]{2,1,0:T(8,128)...) custom-call(s32[32]{0:T(128)} %get-tuple-element.167.slots_ref, ...), custom_call_target="tpu_custom_call" | custom-call | bytes 29520000 | tf_op jit(solution)/shard_map/attention/pallas_call | solution.py:302
  146.4 8.2 %collective-permute-done.29 = bf16[2,192,2,128]{3,2,1,0:T(2,128)(2,1)} collective-permute-done((bf16[2,192,2,128]{3,2,1,0:T(2,128)(2,1)}, bf16[2,192,2,128]{3,2,1,0:T(2,128)(2,1)}, u32[]{:S(2)}, u32[]{:S(2)}) %collective-permute-start.29) | collective-permute-done | bytes 196640 | tf_op jit(solution)/shard_map/ppermute | solution.py:335
  163.7 4.9 %collective-permute-start.36 = (bf16[2,192,2,128]{3,2,1,0:T(2,128)(2,1)}, bf16[2,192,2,128]{3,2,1,0:T(2,128)(2,1)}, u32[]{:S(2)}, u32[]{:S(2)}) collective-permute-start(bf16[2,192,2,128]{3,2,1,0:T(2,128)(2,1)} %bitcast.127), channel_id=1, source_target_pairs={{0,13},{1,12},{2,15},{3,14},{4,9},{5,8},{6,11},{7,10},{8,5},{9,4},... | collective-permute-start | bytes 589832 | tf_op jit(solution)/shard_map/ppermute | solution.py:335
  172.4 11.8 %collective-permute-done.34.refs_5_ = bf16[2,192,2,128]{3,2,1,0:T(2,128)(2,1)S(1)} collective-permute-done((bf16[2,192,2,128]{3,2,1,0:T(2,128)(2,1)}, bf16[2,192,2,128]{3,2,1,0:T(2,128)(2,1)S(1)}, u32[]{:S(2)}, u32[]{:S(2)}) %collective-permute-start.34) | collective-permute-done | bytes 196640 | tf_op jit(solution)/shard_map/ppermute | solution.py:335
  189.7 7.2 %collective-permute-done.36.refs_7_ = bf16[2,192,2,128]{3,2,1,0:T(2,128)(2,1)} collective-permute-done((bf16[2,192,2,128]{3,2,1,0:T(2,128)(2,1)}, bf16[2,192,2,128]{3,2,1,0:T(2,128)(2,1)}, u32[]{:S(2)}, u32[]{:S(2)}) %collective-permute-start.36) | collective-permute-done | bytes 196640 | tf_op jit(solution)/shard_map/ppermute | solution.py:335
  205.5 8.5 %attention.3 = (bf16[2,384,128]{2,1,0:T(8,128)(2,1)}, bf16[2,384,128]{2,1,0:T(8,128)(2,1)}, bf16[2,384,128]{2,1,0:T(8,128)(2,1)}, bf16[2,384,128]{2,1,0:T(8,128)...) custom-call(s32[32]{0:T(128)} %get-tuple-element.167.slots_ref, ...), custom_call_target="tpu_custom_call" | custom-call | bytes 29520000 | tf_op jit(solution)/shard_map/attention/pallas_call | solution.py:302
  240.3 6.4 %collective-permute-done.47.refs_3_ = bf16[2,192,2,128]{3,2,1,0:T(2,128)(2,1)} collective-permute-done((bf16[2,192,2,128]{3,2,1,0:T(2,128)(2,1)}, bf16[2,192,2,128]{3,2,1,0:T(2,128)(2,1)}, u32[]{:S(2)}, u32[]{:S(2)}) %collective-permute-start.47) | collective-permute-done | bytes 196640 | tf_op jit(solution)/shard_map/ppermute | solution.py:335
  247.9 7.9 %collective-permute-done.49.refs_5_ = bf16[2,192,2,128]{3,2,1,0:T(2,128)(2,1)} collective-permute-done((bf16[2,192,2,128]{3,2,1,0:T(2,128)(2,1)}, bf16[2,192,2,128]{3,2,1,0:T(2,128)(2,1)}, u32[]{:S(2)}, u32[]{:S(2)}) %collective-permute-start.49) | collective-permute-done | bytes 196640 | tf_op jit(solution)/shard_map/ppermute | solution.py:335
  255.7 5.7 %collective-permute-start.54 = (bf16[2,192,2,128]{3,2,1,0:T(2,128)(2,1)}, bf16[2,192,2,128]{3,2,1,0:T(2,128)(2,1)}, u32[]{:S(2)}, u32[]{:S(2)}) collective-permute-start(bf16[2,192,2,128]{3,2,1,0:T(2,128)(2,1)} %bitcast.120), channel_id=1, source_target_pairs={{0,10},{1,11},{2,8},{3,9},{4,2},{5,3},{6,0},{7,1},{8,14},{9,15},{1... | collective-permute-start | bytes 589832 | tf_op jit(solution)/shard_map/ppermute | solution.py:335
  261.4 10.6 %collective-permute-done.51.refs_7_ = bf16[2,192,2,128]{3,2,1,0:T(2,128)(2,1)} collective-permute-done((bf16[2,192,2,128]{3,2,1,0:T(2,128)(2,1)}, bf16[2,192,2,128]{3,2,1,0:T(2,128)(2,1)}, u32[]{:S(2)}, u32[]{:S(2)}) %collective-permute-start.51) | collective-permute-done | bytes 196640 | tf_op jit(solution)/shard_map/ppermute | solution.py:335
  273.4 5.3 %collective-permute-start.58 = (bf16[2,192,2,128]{3,2,1,0:T(2,128)(2,1)}, bf16[2,192,2,128]{3,2,1,0:T(2,128)(2,1)}, u32[]{:S(2)}, u32[]{:S(2)}) collective-permute-start(bf16[2,192,2,128]{3,2,1,0:T(2,128)(2,1)} %bitcast.116), channel_id=1, source_target_pairs={{0,11},{1,10},{2,9},{3,8},{4,3},{5,2},{6,1},{7,0},{8,15},{9,14},{1... | collective-permute-start | bytes 589832 | tf_op jit(solution)/shard_map/ppermute | solution.py:335
  282.6 11.3 %collective-permute-done.55.refs_11_ = bf16[2,192,2,128]{3,2,1,0:T(2,128)(2,1)} collective-permute-done((bf16[2,192,2,128]{3,2,1,0:T(2,128)(2,1)}, bf16[2,192,2,128]{3,2,1,0:T(2,128)(2,1)}, u32[]{:S(2)}, u32[]{:S(2)}) %collective-permute-start.55) | collective-permute-done | bytes 196640 | tf_op jit(solution)/shard_map/ppermute | solution.py:335
  294.0 8.4 %collective-permute-done.59.refs_15_ = bf16[2,192,2,128]{3,2,1,0:T(2,128)(2,1)} collective-permute-done((bf16[2,192,2,128]{3,2,1,0:T(2,128)(2,1)}, bf16[2,192,2,128]{3,2,1,0:T(2,128)(2,1)}, u32[]{:S(2)}, u32[]{:S(2)}) %collective-permute-start.59) | collective-permute-done | bytes 196640 | tf_op jit(solution)/shard_map/ppermute | solution.py:335
  (124 shorter events, 125.8 us)
Async XLA Ops:
  9.4 27.3 %collective-permute-start.4 = (bf16[2,192,2,128]{3,2,1,0:T(2,128)(2,1)}, bf16[2,192,2,128]{3,2,1,0:T(2,128)(2,1)S(1)}, u32[]{:S(2)}, u32[]{:S(2)}) collective-permute-start(bf16[2,192,2,128]{3,2,1,0:T(2,128)(2,1)} %get-tuple-element.189), channel_id=1, source_target_pairs={{0,5},{1,4},{2,7},{3,6},{4,13},{5,12},{6,15},{7,14},{8,1},{9,0},{1... | collective-permute-start | bytes 589832 | tf_op jit(solution)/shard_map/ppermute | solution.py:335
  12.1 27.3 %collective-permute-start.5 = (bf16[2,192,2,128]{3,2,1,0:T(2,128)(2,1)}, bf16[2,192,2,128]{3,2,1,0:T(2,128)(2,1)}, u32[]{:S(2)}, u32[]{:S(2)}) collective-permute-start(bf16[2,192,2,128]{3,2,1,0:T(2,128)(2,1)} %get-tuple-element.190), channel_id=1, source_target_pairs={{0,9},{1,8},{2,11},{3,10},{4,1},{5,0},{6,3},{7,2},{8,13},{9,12},{1... | collective-permute-start | bytes 589832 | tf_op jit(solution)/shard_map/ppermute | solution.py:335
  16.4 26.5 %collective-permute-start.6 = (bf16[2,192,2,128]{3,2,1,0:T(2,128)(2,1)}, bf16[2,192,2,128]{3,2,1,0:T(2,128)(2,1)}, u32[]{:S(2)}, u32[]{:S(2)}) collective-permute-start(bf16[2,192,2,128]{3,2,1,0:T(2,128)(2,1)} %get-tuple-element.191), channel_id=1, source_target_pairs={{0,13},{1,12},{2,15},{3,14},{4,9},{5,8},{6,11},{7,10},{8,5},{9,4},... | collective-permute-start | bytes 589832 | tf_op jit(solution)/shard_map/ppermute | solution.py:335
  24.7 27.3 %collective-permute-start.7 = (bf16[2,192,2,128]{3,2,1,0:T(2,128)(2,1)}, bf16[2,192,2,128]{3,2,1,0:T(2,128)(2,1)}, u32[]{:S(2)}, u32[]{:S(2)}) collective-permute-start(bf16[2,192,2,128]{3,2,1,0:T(2,128)(2,1)} %get-tuple-element.192), channel_id=1, source_target_pairs={{0,2},{1,3},{2,0},{3,1},{4,6},{5,7},{6,4},{7,5},{8,10},{9,11},{10,... | collective-permute-start | bytes 589832 | tf_op jit(solution)/shard_map/ppermute | solution.py:335
  25.0 28.6 %collective-permute-start.8 = (bf16[2,192,2,128]{3,2,1,0:T(2,128)(2,1)}, bf16[2,192,2,128]{3,2,1,0:T(2,128)(2,1)}, u32[]{:S(2)}, u32[]{:S(2)}) collective-permute-start(bf16[2,192,2,128]{3,2,1,0:T(2,128)(2,1)} %get-tuple-element.193), channel_id=1, source_target_pairs={{0,6},{1,7},{2,4},{3,5},{4,14},{5,15},{6,12},{7,13},{8,2},{9,3},{1... | collective-permute-start | bytes 589832 | tf_op jit(solution)/shard_map/ppermute | solution.py:335
  39.4 30.1 %collective-permute-start.10 = (bf16[2,192,2,128]{3,2,1,0:T(2,128)(2,1)}, bf16[2,192,2,128]{3,2,1,0:T(2,128)(2,1)}, u32[]{:S(2)}, u32[]{:S(2)}) collective-permute-start(bf16[2,192,2,128]{3,2,1,0:T(2,128)(2,1)} %get-tuple-element.195), channel_id=1, source_target_pairs={{0,14},{1,15},{2,12},{3,13},{4,10},{5,11},{6,8},{7,9},{8,6},{9,7},... | collective-permute-start | bytes 589832 | tf_op jit(solution)/shard_map/ppermute | solution.py:335
  42.9 28.7 %collective-permute-start.11 = (bf16[2,192,2,128]{3,2,1,0:T(2,128)(2,1)}, bf16[2,192,2,128]{3,2,1,0:T(2,128)(2,1)}, u32[]{:S(2)}, u32[]{:S(2)}) collective-permute-start(bf16[2,192,2,128]{3,2,1,0:T(2,128)(2,1)} %get-tuple-element.196), channel_id=1, source_target_pairs={{0,3},{1,2},{2,1},{3,0},{4,7},{5,6},{6,5},{7,4},{8,11},{9,10},{10,... | collective-permute-start | bytes 589832 | tf_op jit(solution)/shard_map/ppermute | solution.py:335
  82.8 25.4 %collective-permute-start.19 = (bf16[2,192,2,128]{3,2,1,0:T(2,128)(2,1)}, bf16[2,192,2,128]{3,2,1,0:T(2,128)(2,1)}, u32[]{:S(2)}, u32[]{:S(2)}) collective-permute-start(bf16[2,192,2,128]{3,2,1,0:T(2,128)(2,1)} %get-tuple-element.237), channel_id=1, source_target_pairs={{0,5},{1,4},{2,7},{3,6},{4,13},{5,12},{6,15},{7,14},{8,1},{9,0},{1... | collective-permute-start | bytes 589832 | tf_op jit(solution)/shard_map/ppermute | solution.py:335
  84.5 29.3 %collective-permute-start.20 = (bf16[2,192,2,128]{3,2,1,0:T(2,128)(2,1)}, bf16[2,192,2,128]{3,2,1,0:T(2,128)(2,1)}, u32[]{:S(2)}, u32[]{:S(2)}) collective-permute-start(bf16[2,192,2,128]{3,2,1,0:T(2,128)(2,1)} %get-tuple-element.238), channel_id=1, source_target_pairs={{0,9},{1,8},{2,11},{3,10},{4,1},{5,0},{6,3},{7,2},{8,13},{9,12},{1... | collective-permute-start | bytes 589832 | tf_op jit(solution)/shard_map/ppermute | solution.py:335
  92.0 32.1 %collective-permute-start.21 = (bf16[2,192,2,128]{3,2,1,0:T(2,128)(2,1)}, bf16[2,192,2,128]{3,2,1,0:T(2,128)(2,1)}, u32[]{:S(2)}, u32[]{:S(2)}) collective-permute-start(bf16[2,192,2,128]{3,2,1,0:T(2,128)(2,1)} %get-tuple-element.239), channel_id=1, source_target_pairs={{0,13},{1,12},{2,15},{3,14},{4,9},{5,8},{6,11},{7,10},{8,5},{9,4},... | collective-permute-start | bytes 589832 | tf_op jit(solution)/shard_map/ppermute | solution.py:335
  99.0 27.3 %collective-permute-start.22 = (bf16[2,192,2,128]{3,2,1,0:T(2,128)(2,1)}, bf16[2,192,2,128]{3,2,1,0:T(2,128)(2,1)}, u32[]{:S(2)}, u32[]{:S(2)}) collective-permute-start(bf16[2,192,2,128]{3,2,1,0:T(2,128)(2,1)} %get-tuple-element.240), channel_id=1, source_target_pairs={{0,2},{1,3},{2,0},{3,1},{4,6},{5,7},{6,4},{7,5},{8,10},{9,11},{10,... | collective-permute-start | bytes 589832 | tf_op jit(solution)/shard_map/ppermute | solution.py:335
  113.8 32.6 %collective-permute-start.25 = (bf16[2,192,2,128]{3,2,1,0:T(2,128)(2,1)}, bf16[2,192,2,128]{3,2,1,0:T(2,128)(2,1)}, u32[]{:S(2)}, u32[]{:S(2)}) collective-permute-start(bf16[2,192,2,128]{3,2,1,0:T(2,128)(2,1)} %get-tuple-element.243), channel_id=1, source_target_pairs={{0,14},{1,15},{2,12},{3,13},{4,10},{5,11},{6,8},{7,9},{8,6},{9,7},... | collective-permute-start | bytes 589832 | tf_op jit(solution)/shard_map/ppermute | solution.py:335
  157.3 26.9 %collective-permute-start.34 = (bf16[2,192,2,128]{3,2,1,0:T(2,128)(2,1)}, bf16[2,192,2,128]{3,2,1,0:T(2,128)(2,1)S(1)}, u32[]{:S(2)}, u32[]{:S(2)}) collective-permute-start(bf16[2,192,2,128]{3,2,1,0:T(2,128)(2,1)} %bitcast.131), channel_id=1, source_target_pairs={{0,5},{1,4},{2,7},{3,6},{4,13},{5,12},{6,15},{7,14},{8,1},{9,0},{1... | collective-permute-start | bytes 589832 | tf_op jit(solution)/shard_map/ppermute | solution.py:335
  160.6 26.1 %collective-permute-start.35 = (bf16[2,192,2,128]{3,2,1,0:T(2,128)(2,1)}, bf16[2,192,2,128]{3,2,1,0:T(2,128)(2,1)}, u32[]{:S(2)}, u32[]{:S(2)}) collective-permute-start(bf16[2,192,2,128]{3,2,1,0:T(2,128)(2,1)} %bitcast.129), channel_id=1, source_target_pairs={{0,9},{1,8},{2,11},{3,10},{4,1},{5,0},{6,3},{7,2},{8,13},{9,12},{1... | collective-permute-start | bytes 589832 | tf_op jit(solution)/shard_map/ppermute | solution.py:335
  163.7 33.1 %collective-permute-start.36 = (bf16[2,192,2,128]{3,2,1,0:T(2,128)(2,1)}, bf16[2,192,2,128]{3,2,1,0:T(2,128)(2,1)}, u32[]{:S(2)}, u32[]{:S(2)}) collective-permute-start(bf16[2,192,2,128]{3,2,1,0:T(2,128)(2,1)} %bitcast.127), channel_id=1, source_target_pairs={{0,13},{1,12},{2,15},{3,14},{4,9},{5,8},{6,11},{7,10},{8,5},{9,4},... | collective-permute-start | bytes 589832 | tf_op jit(solution)/shard_map/ppermute | solution.py:335
  171.6 27.3 %collective-permute-start.37 = (bf16[2,192,2,128]{3,2,1,0:T(2,128)(2,1)}, bf16[2,192,2,128]{3,2,1,0:T(2,128)(2,1)}, u32[]{:S(2)}, u32[]{:S(2)}) collective-permute-start(bf16[2,192,2,128]{3,2,1,0:T(2,128)(2,1)} %bitcast.125), channel_id=1, source_target_pairs={{0,2},{1,3},{2,0},{3,1},{4,6},{5,7},{6,4},{7,5},{8,10},{9,11},{10,... | collective-permute-start | bytes 589832 | tf_op jit(solution)/shard_map/ppermute | solution.py:335
  172.0 29.0 %collective-permute-start.38 = (bf16[2,192,2,128]{3,2,1,0:T(2,128)(2,1)}, bf16[2,192,2,128]{3,2,1,0:T(2,128)(2,1)}, u32[]{:S(2)}, u32[]{:S(2)}) collective-permute-start(bf16[2,192,2,128]{3,2,1,0:T(2,128)(2,1)} %bitcast.123), channel_id=1, source_target_pairs={{0,6},{1,7},{2,4},{3,5},{4,14},{5,15},{6,12},{7,13},{8,2},{9,3},{1... | collective-permute-start | bytes 589832 | tf_op jit(solution)/shard_map/ppermute | solution.py:335
  186.7 30.4 %collective-permute-start.40 = (bf16[2,192,2,128]{3,2,1,0:T(2,128)(2,1)}, bf16[2,192,2,128]{3,2,1,0:T(2,128)(2,1)}, u32[]{:S(2)}, u32[]{:S(2)}) collective-permute-start(bf16[2,192,2,128]{3,2,1,0:T(2,128)(2,1)} %bitcast.114), channel_id=1, source_target_pairs={{0,14},{1,15},{2,12},{3,13},{4,10},{5,11},{6,8},{7,9},{8,6},{9,7},... | collective-permute-start | bytes 589832 | tf_op jit(solution)/shard_map/ppermute | solution.py:335
  230.5 25.2 %collective-permute-start.49 = (bf16[2,192,2,128]{3,2,1,0:T(2,128)(2,1)}, bf16[2,192,2,128]{3,2,1,0:T(2,128)(2,1)}, u32[]{:S(2)}, u32[]{:S(2)}) collective-permute-start(bf16[2,192,2,128]{3,2,1,0:T(2,128)(2,1)} %bitcast.130), channel_id=1, source_target_pairs={{0,5},{1,4},{2,7},{3,6},{4,13},{5,12},{6,15},{7,14},{8,1},{9,0},{1... | collective-permute-start | bytes 589832 | tf_op jit(solution)/shard_map/ppermute | solution.py:335
  232.0 29.4 %collective-permute-start.50 = (bf16[2,192,2,128]{3,2,1,0:T(2,128)(2,1)}, bf16[2,192,2,128]{3,2,1,0:T(2,128)(2,1)}, u32[]{:S(2)}, u32[]{:S(2)}) collective-permute-start(bf16[2,192,2,128]{3,2,1,0:T(2,128)(2,1)} %bitcast.128), channel_id=1, source_target_pairs={{0,9},{1,8},{2,11},{3,10},{4,1},{5,0},{6,3},{7,2},{8,13},{9,12},{1... | collective-permute-start | bytes 589832 | tf_op jit(solution)/shard_map/ppermute | solution.py:335
  239.3 32.7 %collective-permute-start.51 = (bf16[2,192,2,128]{3,2,1,0:T(2,128)(2,1)}, bf16[2,192,2,128]{3,2,1,0:T(2,128)(2,1)}, u32[]{:S(2)}, u32[]{:S(2)}) collective-permute-start(bf16[2,192,2,128]{3,2,1,0:T(2,128)(2,1)} %bitcast.126), channel_id=1, source_target_pairs={{0,13},{1,12},{2,15},{3,14},{4,9},{5,8},{6,11},{7,10},{8,5},{9,4},... | collective-permute-start | bytes 589832 | tf_op jit(solution)/shard_map/ppermute | solution.py:335
  246.7 26.7 %collective-permute-start.52 = (bf16[2,192,2,128]{3,2,1,0:T(2,128)(2,1)}, bf16[2,192,2,128]{3,2,1,0:T(2,128)(2,1)}, u32[]{:S(2)}, u32[]{:S(2)}) collective-permute-start(bf16[2,192,2,128]{3,2,1,0:T(2,128)(2,1)} %bitcast.124), channel_id=1, source_target_pairs={{0,2},{1,3},{2,0},{3,1},{4,6},{5,7},{6,4},{7,5},{8,10},{9,11},{10,... | collective-permute-start | bytes 589832 | tf_op jit(solution)/shard_map/ppermute | solution.py:335
  247.8 25.6 %collective-permute-start.53 = (bf16[2,192,2,128]{3,2,1,0:T(2,128)(2,1)}, bf16[2,192,2,128]{3,2,1,0:T(2,128)(2,1)}, u32[]{:S(2)}, u32[]{:S(2)}) collective-permute-start(bf16[2,192,2,128]{3,2,1,0:T(2,128)(2,1)} %bitcast.122), channel_id=1, source_target_pairs={{0,6},{1,7},{2,4},{3,5},{4,14},{5,15},{6,12},{7,13},{8,2},{9,3},{1... | collective-permute-start | bytes 589832 | tf_op jit(solution)/shard_map/ppermute | solution.py:335
  261.4 32.6 %collective-permute-start.55 = (bf16[2,192,2,128]{3,2,1,0:T(2,128)(2,1)}, bf16[2,192,2,128]{3,2,1,0:T(2,128)(2,1)}, u32[]{:S(2)}, u32[]{:S(2)}) collective-permute-start(bf16[2,192,2,128]{3,2,1,0:T(2,128)(2,1)} %bitcast.119), channel_id=1, source_target_pairs={{0,14},{1,15},{2,12},{3,13},{4,10},{5,11},{6,8},{7,9},{8,6},{9,7},... | collective-permute-start | bytes 589832 | tf_op jit(solution)/shard_map/ppermute | solution.py:335
  (46 other events, 1738.6 us)

commit v12 on v11

--- a/solution.py
+++ b/solution.py
@@ -326,7 +326,9 @@
 
 
 def after(later, earlier):
-    return lax.optimization_barrier((later, earlier))
+    some = len(earlier) * 3 // 4
+    later, earlier[:some] = lax.optimization_barrier((later, earlier[:some]))
+    return later
 
 
 def swap(blocks):
@@ -346,15 +348,15 @@
     for chunk in range(chunks):
         blocks = pack(queries, out_grad, neighbours, devices, chunk, chunks)
         if arrived:
-            blocks, arrived[-1] = after(blocks, arrived[-1])
+            blocks = after(blocks, arrived[-1])
         arrived.append(swap(blocks))
     for chunk in range(chunks):
         blocks = attention(slots, [block.reshape(block.shape[0], -1, HD) for block in arrived[chunk]])
         blocks = [block.reshape(block.shape[0], -1, 2, HD) for block in blocks]
         if back:
-            blocks, back[-1] = after(blocks, back[-1])
+            blocks = after(blocks, back[-1])
         elif chunks > 1:
-            blocks, arrived[-1] = after(blocks, arrived[-1])
+            blocks = after(blocks, arrived[-1])
         back.append(swap(blocks))
     outputs = ()
     for chunk in range(chunks):

time: 307 us -> 297 us (0.967)
  waiting for transfers between devices: 157 us -> 143 us
    ppermute x60, waiting for transfers between devices: 157 us -> 143 us  [swap(): lax.ppermute(block, 'fsdp', [(i, reached(i, devices, move)) for i in rang...]
  transfers between devices with their start and end apart: 60 -> 60, of which waited for: 31 -> 34; matrix products, arithmetic and copies ran while one was open for 1% -> 1% of each run, Pallas kernels for 8% -> 9%
where the time goes in v12:
time: 297 us; the launch traced here: 294 us
  waiting for transfers between devices  143 us (48%)
  starting transfers between devices  115 us (39%)
  Pallas kernels  33.5 us (11%)
    ppermute x60, waiting for transfers between devices, swap(): lax.ppermute(block, 'fsdp', [(i, reached(i, devices, move)) for i in rang...  143 us
    ppermute x60, starting transfers between devices, swap(): lax.ppermute(block, 'fsdp', [(i, reached(i, devices, move)) for i in rang...  115 us
    pallas_call x2, Pallas kernels, attention(): pl.pallas_call(attention_kernel, grid_spec=pltpu.PrefetchScalarGridSpec(n...  17 us
    pallas_call x2, Pallas kernels, pack(): pl.pallas_call(kernel, in_specs=[ANY] * 3, out_specs=[ANY] * devices, out...  8.83 us
    pallas_call x2, Pallas kernels, unpack(): pl.pallas_call(kernel, in_specs=[ANY] * (2 * devices + len(before)), out_...  7.7 us
  transfers between devices with their start and end apart: 60, of which 34 were waited for; matrix products, arithmetic and copies ran while one was open for 1% of the time, Pallas kernels for 9%

profile of v12, /device:TPU:15, one launch (start us, length us, event | category | flops | bytes accessed | tf_op | source)
XLA Modules:
  0.0 294.3 jit_solution(4296593813819965197)
XLA Ops:
  0.6 4.4 %pack.3 = (bf16[2,192,2,128]{3,2,1,0:T(2,128)(2,1)}, bf16[2,192,2,128]{3,2,1,0:T(2,128)(2,1)}, bf16[2,192,2,128]{3,2,1,0:T(2,128)(2,1)}, bf16[2,192,2,128]{3,2,1...) custom-call(bf16[64,8192]{1,0:T(8,128)(2,1)} %q_ref.3, ...), custom_call_target="tpu_custom_call" | custom-call | bytes 14760000 | tf_op jit(solution)/shard_map/pack/pallas_call | solution.py:110
  19.2 5.6 %collective-permute-done.2 = bf16[2,192,2,128]{3,2,1,0:T(2,128)(2,1)S(1)} collective-permute-done((bf16[2,192,2,128]{3,2,1,0:T(2,128)(2,1)}, bf16[2,192,2,128]{3,2,1,0:T(2,128)(2,1)S(1)}, u32[]{:S(2)}, u32[]{:S(2)}) %collective-permute-start.2) | collective-permute-done | bytes 196640 | tf_op jit(solution)/shard_map/ppermute | solution.py:337
  26.0 10.7 %collective-permute-done.4 = bf16[2,192,2,128]{3,2,1,0:T(2,128)(2,1)S(1)} collective-permute-done((bf16[2,192,2,128]{3,2,1,0:T(2,128)(2,1)}, bf16[2,192,2,128]{3,2,1,0:T(2,128)(2,1)S(1)}, u32[]{:S(2)}, u32[]{:S(2)}) %collective-permute-start.4) | collective-permute-done | bytes 196640 | tf_op jit(solution)/shard_map/ppermute | solution.py:337
  42.9 9.2 %collective-permute-start.11 = (bf16[2,192,2,128]{3,2,1,0:T(2,128)(2,1)}, bf16[2,192,2,128]{3,2,1,0:T(2,128)(2,1)}, u32[]{:S(2)}, u32[]{:S(2)}) collective-permute-start(bf16[2,192,2,128]{3,2,1,0:T(2,128)(2,1)} %get-tuple-element.196), channel_id=1, source_target_pairs={{0,3},{1,2},{2,1},{3,0},{4,7},{5,6},{6,5},{7,4},{8,11},{9,10},{10,... | collective-permute-start | bytes 589832 | tf_op jit(solution)/shard_map/ppermute | solution.py:337
  62.5 7.0 %collective-permute-done.10 = bf16[2,192,2,128]{3,2,1,0:T(2,128)(2,1)} collective-permute-done((bf16[2,192,2,128]{3,2,1,0:T(2,128)(2,1)}, bf16[2,192,2,128]{3,2,1,0:T(2,128)(2,1)}, u32[]{:S(2)}, u32[]{:S(2)}) %collective-permute-start.10) | collective-permute-done | bytes 196640 | tf_op jit(solution)/shard_map/ppermute | solution.py:337
  73.9 4.7 %collective-permute-start.18 = (bf16[2,192,2,128]{3,2,1,0:T(2,128)(2,1)}, bf16[2,192,2,128]{3,2,1,0:T(2,128)(2,1)}, u32[]{:S(2)}, u32[]{:S(2)}) collective-permute-start(bf16[2,192,2,128]{3,2,1,0:T(2,128)(2,1)} %get-tuple-element.220), channel_id=1, source_target_pairs={{0,1},{1,0},{2,3},{3,2},{4,5},{5,4},{6,7},{7,6},{8,9},{9,8},{10,11... | collective-permute-start | bytes 589832 | tf_op jit(solution)/shard_map/ppermute | solution.py:337
  78.6 5.9 %collective-permute-done.14 = bf16[2,192,2,128]{3,2,1,0:T(2,128)(2,1)} collective-permute-done((bf16[2,192,2,128]{3,2,1,0:T(2,128)(2,1)}, bf16[2,192,2,128]{3,2,1,0:T(2,128)(2,1)}, u32[]{:S(2)}, u32[]{:S(2)}) %collective-permute-start.14) | collective-permute-done | bytes 196640 | tf_op jit(solution)/shard_map/ppermute | solution.py:337
  84.5 6.3 %collective-permute-done.15 = bf16[2,192,2,128]{3,2,1,0:T(2,128)(2,1)} collective-permute-done((bf16[2,192,2,128]{3,2,1,0:T(2,128)(2,1)}, bf16[2,192,2,128]{3,2,1,0:T(2,128)(2,1)}, u32[]{:S(2)}, u32[]{:S(2)}) %collective-permute-start.15) | collective-permute-done | bytes 196640 | tf_op jit(solution)/shard_map/ppermute | solution.py:337
  94.4 9.0 %collective-permute-done.17 = bf16[2,192,2,128]{3,2,1,0:T(2,128)(2,1)} collective-permute-done((bf16[2,192,2,128]{3,2,1,0:T(2,128)(2,1)}, bf16[2,192,2,128]{3,2,1,0:T(2,128)(2,1)}, u32[]{:S(2)}, u32[]{:S(2)}) %collective-permute-start.17) | collective-permute-done | bytes 196640 | tf_op jit(solution)/shard_map/ppermute | solution.py:337
  107.6 8.3 %collective-permute-start.25 = (bf16[2,192,2,128]{3,2,1,0:T(2,128)(2,1)}, bf16[2,192,2,128]{3,2,1,0:T(2,128)(2,1)}, u32[]{:S(2)}, u32[]{:S(2)}) collective-permute-start(bf16[2,192,2,128]{3,2,1,0:T(2,128)(2,1)} %get-tuple-element.227), channel_id=1, source_target_pairs={{0,14},{1,15},{2,12},{3,13},{4,10},{5,11},{6,8},{7,9},{8,6},{9,7},... | collective-permute-start | bytes 589832 | tf_op jit(solution)/shard_map/ppermute | solution.py:337
  115.9 6.7 %collective-permute-start.26 = (bf16[2,192,2,128]{3,2,1,0:T(2,128)(2,1)}, bf16[2,192,2,128]{3,2,1,0:T(2,128)(2,1)}, u32[]{:S(2)}, u32[]{:S(2)}) collective-permute-start(bf16[2,192,2,128]{3,2,1,0:T(2,128)(2,1)} %get-tuple-element.240), channel_id=1, source_target_pairs={{0,3},{1,2},{2,1},{3,0},{4,7},{5,6},{6,5},{7,4},{8,11},{9,10},{10,... | collective-permute-start | bytes 589832 | tf_op jit(solution)/shard_map/ppermute | solution.py:337
  131.1 8.5 %attention.2 = (bf16[2,384,128]{2,1,0:T(8,128)(2,1)}, bf16[2,384,128]{2,1,0:T(8,128)(2,1)}, bf16[2,384,128]{2,1,0:T(8,128)(2,1)}, bf16[2,384,128]{2,1,0:T(8,128)...) custom-call(s32[32]{0:T(128)} %get-tuple-element.155.slots_ref, ...), custom_call_target="tpu_custom_call" | custom-call | bytes 29520000 | tf_op jit(solution)/shard_map/attention/pallas_call | solution.py:302
  147.6 9.7 %collective-permute-done.29 = bf16[2,192,2,128]{3,2,1,0:T(2,128)(2,1)} collective-permute-done((bf16[2,192,2,128]{3,2,1,0:T(2,128)(2,1)}, bf16[2,192,2,128]{3,2,1,0:T(2,128)(2,1)}, u32[]{:S(2)}, u32[]{:S(2)}) %collective-permute-start.29) | collective-permute-done | bytes 196640 | tf_op jit(solution)/shard_map/ppermute | solution.py:337
  165.0 9.1 %collective-permute-done.32.refs_3_ = bf16[2,192,2,128]{3,2,1,0:T(2,128)(2,1)S(1)} collective-permute-done((bf16[2,192,2,128]{3,2,1,0:T(2,128)(2,1)}, bf16[2,192,2,128]{3,2,1,0:T(2,128)(2,1)S(1)}, u32[]{:S(2)}, u32[]{:S(2)}) %collective-permute-start.32) | collective-permute-done | bytes 196640 | tf_op jit(solution)/shard_map/ppermute | solution.py:337
  178.3 8.2 %collective-permute-start.40 = (bf16[2,192,2,128]{3,2,1,0:T(2,128)(2,1)}, bf16[2,192,2,128]{3,2,1,0:T(2,128)(2,1)}, u32[]{:S(2)}, u32[]{:S(2)}) collective-permute-start(bf16[2,192,2,128]{3,2,1,0:T(2,128)(2,1)} %bitcast.114), channel_id=1, source_target_pairs={{0,14},{1,15},{2,12},{3,13},{4,10},{5,11},{6,8},{7,9},{8,6},{9,7},... | collective-permute-start | bytes 589832 | tf_op jit(solution)/shard_map/ppermute | solution.py:337
  186.5 6.8 %collective-permute-start.56 = (bf16[2,192,2,128]{3,2,1,0:T(2,128)(2,1)}, bf16[2,192,2,128]{3,2,1,0:T(2,128)(2,1)}, u32[]{:S(2)}, u32[]{:S(2)}) collective-permute-start(bf16[2,192,2,128]{3,2,1,0:T(2,128)(2,1)} %bitcast.113), channel_id=1, source_target_pairs={{0,3},{1,2},{2,1},{3,0},{4,7},{5,6},{6,5},{7,4},{8,11},{9,10},{10,... | collective-permute-start | bytes 589832 | tf_op jit(solution)/shard_map/ppermute | solution.py:337
  199.3 8.5 %attention.3 = (bf16[2,384,128]{2,1,0:T(8,128)(2,1)}, bf16[2,384,128]{2,1,0:T(8,128)(2,1)}, bf16[2,384,128]{2,1,0:T(8,128)(2,1)}, bf16[2,384,128]{2,1,0:T(8,128)...) custom-call(s32[32]{0:T(128)} %get-tuple-element.155.slots_ref, ...), custom_call_target="tpu_custom_call" | custom-call | bytes 29520000 | tf_op jit(solution)/shard_map/attention/pallas_call | solution.py:302
  215.3 4.7 %collective-permute-start.44 = (bf16[2,192,2,128]{3,2,1,0:T(2,128)(2,1)}, bf16[2,192,2,128]{3,2,1,0:T(2,128)(2,1)}, u32[]{:S(2)}, u32[]{:S(2)}) collective-permute-start(bf16[2,192,2,128]{3,2,1,0:T(2,128)(2,1)} %bitcast.132), channel_id=1, source_target_pairs={{0,1},{1,0},{2,3},{3,2},{4,5},{5,4},{6,7},{7,6},{8,9},{9,8},{10,11... | collective-permute-start | bytes 589832 | tf_op jit(solution)/shard_map/ppermute | solution.py:337
  220.0 8.1 %collective-permute-done.59.refs_15_ = bf16[2,192,2,128]{3,2,1,0:T(2,128)(2,1)} collective-permute-done((bf16[2,192,2,128]{3,2,1,0:T(2,128)(2,1)}, bf16[2,192,2,128]{3,2,1,0:T(2,128)(2,1)}, u32[]{:S(2)}, u32[]{:S(2)}) %collective-permute-start.59) | collective-permute-done | bytes 196640 | tf_op jit(solution)/shard_map/ppermute | solution.py:337
  235.9 4.8 %collective-permute-done.43.refs_3_ = bf16[2,192,2,128]{3,2,1,0:T(2,128)(2,1)} collective-permute-done((bf16[2,192,2,128]{3,2,1,0:T(2,128)(2,1)}, bf16[2,192,2,128]{3,2,1,0:T(2,128)(2,1)}, u32[]{:S(2)}, u32[]{:S(2)}) %collective-permute-start.43) | collective-permute-done | bytes 196640 | tf_op jit(solution)/shard_map/ppermute | solution.py:337
  240.8 8.4 %collective-permute-done.45.refs_5_ = bf16[2,192,2,128]{3,2,1,0:T(2,128)(2,1)} collective-permute-done((bf16[2,192,2,128]{3,2,1,0:T(2,128)(2,1)}, bf16[2,192,2,128]{3,2,1,0:T(2,128)(2,1)}, u32[]{:S(2)}, u32[]{:S(2)}) %collective-permute-start.45) | collective-permute-done | bytes 196640 | tf_op jit(solution)/shard_map/ppermute | solution.py:337
  249.1 8.3 %collective-permute-start.51 = (bf16[2,192,2,128]{3,2,1,0:T(2,128)(2,1)}, bf16[2,192,2,128]{3,2,1,0:T(2,128)(2,1)}, u32[]{:S(2)}, u32[]{:S(2)}) collective-permute-start(bf16[2,192,2,128]{3,2,1,0:T(2,128)(2,1)} %bitcast.119), channel_id=1, source_target_pairs={{0,14},{1,15},{2,12},{3,13},{4,10},{5,11},{6,8},{7,9},{8,6},{9,7},... | collective-permute-start | bytes 589832 | tf_op jit(solution)/shard_map/ppermute | solution.py:337
  257.4 6.5 %collective-permute-start.52 = (bf16[2,192,2,128]{3,2,1,0:T(2,128)(2,1)}, bf16[2,192,2,128]{3,2,1,0:T(2,128)(2,1)}, u32[]{:S(2)}, u32[]{:S(2)}) collective-permute-start(bf16[2,192,2,128]{3,2,1,0:T(2,128)(2,1)} %bitcast.118), channel_id=1, source_target_pairs={{0,3},{1,2},{2,1},{3,0},{4,7},{5,6},{6,5},{7,4},{8,11},{9,10},{10,... | collective-permute-start | bytes 589832 | tf_op jit(solution)/shard_map/ppermute | solution.py:337
  274.0 7.9 %collective-permute-done.51.refs_11_ = bf16[2,192,2,128]{3,2,1,0:T(2,128)(2,1)} collective-permute-done((bf16[2,192,2,128]{3,2,1,0:T(2,128)(2,1)}, bf16[2,192,2,128]{3,2,1,0:T(2,128)(2,1)}, u32[]{:S(2)}, u32[]{:S(2)}) %collective-permute-start.51) | collective-permute-done | bytes 196640 | tf_op jit(solution)/shard_map/ppermute | solution.py:337
  (124 shorter events, 116.3 us)
Async XLA Ops:
  9.4 27.3 %collective-permute-start.4 = (bf16[2,192,2,128]{3,2,1,0:T(2,128)(2,1)}, bf16[2,192,2,128]{3,2,1,0:T(2,128)(2,1)S(1)}, u32[]{:S(2)}, u32[]{:S(2)}) collective-permute-start(bf16[2,192,2,128]{3,2,1,0:T(2,128)(2,1)} %get-tuple-element.177), channel_id=1, source_target_pairs={{0,5},{1,4},{2,7},{3,6},{4,13},{5,12},{6,15},{7,14},{8,1},{9,0},{1... | collective-permute-start | bytes 589832 | tf_op jit(solution)/shard_map/ppermute | solution.py:337
  12.1 27.3 %collective-permute-start.5 = (bf16[2,192,2,128]{3,2,1,0:T(2,128)(2,1)}, bf16[2,192,2,128]{3,2,1,0:T(2,128)(2,1)}, u32[]{:S(2)}, u32[]{:S(2)}) collective-permute-start(bf16[2,192,2,128]{3,2,1,0:T(2,128)(2,1)} %get-tuple-element.178), channel_id=1, source_target_pairs={{0,9},{1,8},{2,11},{3,10},{4,1},{5,0},{6,3},{7,2},{8,13},{9,12},{1... | collective-permute-start | bytes 589832 | tf_op jit(solution)/shard_map/ppermute | solution.py:337
  16.4 26.5 %collective-permute-start.6 = (bf16[2,192,2,128]{3,2,1,0:T(2,128)(2,1)}, bf16[2,192,2,128]{3,2,1,0:T(2,128)(2,1)}, u32[]{:S(2)}, u32[]{:S(2)}) collective-permute-start(bf16[2,192,2,128]{3,2,1,0:T(2,128)(2,1)} %get-tuple-element.179), channel_id=1, source_target_pairs={{0,13},{1,12},{2,15},{3,14},{4,9},{5,8},{6,11},{7,10},{8,5},{9,4},... | collective-permute-start | bytes 589832 | tf_op jit(solution)/shard_map/ppermute | solution.py:337
  24.8 27.3 %collective-permute-start.7 = (bf16[2,192,2,128]{3,2,1,0:T(2,128)(2,1)}, bf16[2,192,2,128]{3,2,1,0:T(2,128)(2,1)}, u32[]{:S(2)}, u32[]{:S(2)}) collective-permute-start(bf16[2,192,2,128]{3,2,1,0:T(2,128)(2,1)} %get-tuple-element.180), channel_id=1, source_target_pairs={{0,2},{1,3},{2,0},{3,1},{4,6},{5,7},{6,4},{7,5},{8,10},{9,11},{10,... | collective-permute-start | bytes 589832 | tf_op jit(solution)/shard_map/ppermute | solution.py:337
  25.0 28.6 %collective-permute-start.8 = (bf16[2,192,2,128]{3,2,1,0:T(2,128)(2,1)}, bf16[2,192,2,128]{3,2,1,0:T(2,128)(2,1)}, u32[]{:S(2)}, u32[]{:S(2)}) collective-permute-start(bf16[2,192,2,128]{3,2,1,0:T(2,128)(2,1)} %get-tuple-element.181), channel_id=1, source_target_pairs={{0,6},{1,7},{2,4},{3,5},{4,14},{5,15},{6,12},{7,13},{8,2},{9,3},{1... | collective-permute-start | bytes 589832 | tf_op jit(solution)/shard_map/ppermute | solution.py:337
  39.4 30.1 %collective-permute-start.10 = (bf16[2,192,2,128]{3,2,1,0:T(2,128)(2,1)}, bf16[2,192,2,128]{3,2,1,0:T(2,128)(2,1)}, u32[]{:S(2)}, u32[]{:S(2)}) collective-permute-start(bf16[2,192,2,128]{3,2,1,0:T(2,128)(2,1)} %get-tuple-element.183), channel_id=1, source_target_pairs={{0,14},{1,15},{2,12},{3,13},{4,10},{5,11},{6,8},{7,9},{8,6},{9,7},... | collective-permute-start | bytes 589832 | tf_op jit(solution)/shard_map/ppermute | solution.py:337
  42.9 28.7 %collective-permute-start.11 = (bf16[2,192,2,128]{3,2,1,0:T(2,128)(2,1)}, bf16[2,192,2,128]{3,2,1,0:T(2,128)(2,1)}, u32[]{:S(2)}, u32[]{:S(2)}) collective-permute-start(bf16[2,192,2,128]{3,2,1,0:T(2,128)(2,1)} %get-tuple-element.196), channel_id=1, source_target_pairs={{0,3},{1,2},{2,1},{3,0},{4,7},{5,6},{6,5},{7,4},{8,11},{9,10},{10,... | collective-permute-start | bytes 589832 | tf_op jit(solution)/shard_map/ppermute | solution.py:337
  57.9 26.5 %collective-permute-start.14 = (bf16[2,192,2,128]{3,2,1,0:T(2,128)(2,1)}, bf16[2,192,2,128]{3,2,1,0:T(2,128)(2,1)}, u32[]{:S(2)}, u32[]{:S(2)}) collective-permute-start(bf16[2,192,2,128]{3,2,1,0:T(2,128)(2,1)} %get-tuple-element.199), channel_id=1, source_target_pairs={{0,15},{1,14},{2,13},{3,12},{4,11},{5,10},{6,9},{7,8},{8,7},{9,6},... | collective-permute-start | bytes 589832 | tf_op jit(solution)/shard_map/ppermute | solution.py:337
  73.9 29.5 %collective-permute-start.17 = (bf16[2,192,2,128]{3,2,1,0:T(2,128)(2,1)}, bf16[2,192,2,128]{3,2,1,0:T(2,128)(2,1)}, u32[]{:S(2)}, u32[]{:S(2)}) collective-permute-start(bf16[2,192,2,128]{3,2,1,0:T(2,128)(2,1)} %get-tuple-element.219), channel_id=1, source_target_pairs={{0,12},{1,13},{2,14},{3,15},{4,8},{5,9},{6,10},{7,11},{8,4},{9,5},... | collective-permute-start | bytes 589832 | tf_op jit(solution)/shard_map/ppermute | solution.py:337
  73.9 29.5 %collective-permute-start.18 = (bf16[2,192,2,128]{3,2,1,0:T(2,128)(2,1)}, bf16[2,192,2,128]{3,2,1,0:T(2,128)(2,1)}, u32[]{:S(2)}, u32[]{:S(2)}) collective-permute-start(bf16[2,192,2,128]{3,2,1,0:T(2,128)(2,1)} %get-tuple-element.220), channel_id=1, source_target_pairs={{0,1},{1,0},{2,3},{3,2},{4,5},{5,4},{6,7},{7,6},{8,9},{9,8},{10,11... | collective-permute-start | bytes 589832 | tf_op jit(solution)/shard_map/ppermute | solution.py:337
  107.6 32.6 %collective-permute-start.25 = (bf16[2,192,2,128]{3,2,1,0:T(2,128)(2,1)}, bf16[2,192,2,128]{3,2,1,0:T(2,128)(2,1)}, u32[]{:S(2)}, u32[]{:S(2)}) collective-permute-start(bf16[2,192,2,128]{3,2,1,0:T(2,128)(2,1)} %get-tuple-element.227), channel_id=1, source_target_pairs={{0,14},{1,15},{2,12},{3,13},{4,10},{5,11},{6,8},{7,9},{8,6},{9,7},... | collective-permute-start | bytes 589832 | tf_op jit(solution)/shard_map/ppermute | solution.py:337
  115.9 26.8 %collective-permute-start.26 = (bf16[2,192,2,128]{3,2,1,0:T(2,128)(2,1)}, bf16[2,192,2,128]{3,2,1,0:T(2,128)(2,1)}, u32[]{:S(2)}, u32[]{:S(2)}) collective-permute-start(bf16[2,192,2,128]{3,2,1,0:T(2,128)(2,1)} %get-tuple-element.240), channel_id=1, source_target_pairs={{0,3},{1,2},{2,1},{3,0},{4,7},{5,6},{6,5},{7,4},{8,11},{9,10},{10,... | collective-permute-start | bytes 589832 | tf_op jit(solution)/shard_map/ppermute | solution.py:337
  125.3 32.0 %collective-permute-start.29 = (bf16[2,192,2,128]{3,2,1,0:T(2,128)(2,1)}, bf16[2,192,2,128]{3,2,1,0:T(2,128)(2,1)}, u32[]{:S(2)}, u32[]{:S(2)}) collective-permute-start(bf16[2,192,2,128]{3,2,1,0:T(2,128)(2,1)} %get-tuple-element.243), channel_id=1, source_target_pairs={{0,15},{1,14},{2,13},{3,12},{4,11},{5,10},{6,9},{7,8},{8,7},{9,6},... | collective-permute-start | bytes 589832 | tf_op jit(solution)/shard_map/ppermute | solution.py:337
  144.6 29.5 %collective-permute-start.32 = (bf16[2,192,2,128]{3,2,1,0:T(2,128)(2,1)}, bf16[2,192,2,128]{3,2,1,0:T(2,128)(2,1)S(1)}, u32[]{:S(2)}, u32[]{:S(2)}) collective-permute-start(bf16[2,192,2,128]{3,2,1,0:T(2,128)(2,1)} %bitcast.135), channel_id=1, source_target_pairs={{0,12},{1,13},{2,14},{3,15},{4,8},{5,9},{6,10},{7,11},{8,4},{9,5},... | collective-permute-start | bytes 589832 | tf_op jit(solution)/shard_map/ppermute | solution.py:337
  144.6 29.5 %collective-permute-start.33 = (bf16[2,192,2,128]{3,2,1,0:T(2,128)(2,1)}, bf16[2,192,2,128]{3,2,1,0:T(2,128)(2,1)S(1)}, u32[]{:S(2)}, u32[]{:S(2)}) collective-permute-start(bf16[2,192,2,128]{3,2,1,0:T(2,128)(2,1)} %bitcast.133), channel_id=1, source_target_pairs={{0,1},{1,0},{2,3},{3,2},{4,5},{5,4},{6,7},{7,6},{8,9},{9,8},{10,11... | collective-permute-start | bytes 589832 | tf_op jit(solution)/shard_map/ppermute | solution.py:337
  178.3 32.7 %collective-permute-start.40 = (bf16[2,192,2,128]{3,2,1,0:T(2,128)(2,1)}, bf16[2,192,2,128]{3,2,1,0:T(2,128)(2,1)}, u32[]{:S(2)}, u32[]{:S(2)}) collective-permute-start(bf16[2,192,2,128]{3,2,1,0:T(2,128)(2,1)} %bitcast.114), channel_id=1, source_target_pairs={{0,14},{1,15},{2,12},{3,13},{4,10},{5,11},{6,8},{7,9},{8,6},{9,7},... | collective-permute-start | bytes 589832 | tf_op jit(solution)/shard_map/ppermute | solution.py:337
  186.5 27.3 %collective-permute-start.56 = (bf16[2,192,2,128]{3,2,1,0:T(2,128)(2,1)}, bf16[2,192,2,128]{3,2,1,0:T(2,128)(2,1)}, u32[]{:S(2)}, u32[]{:S(2)}) collective-permute-start(bf16[2,192,2,128]{3,2,1,0:T(2,128)(2,1)} %bitcast.113), channel_id=1, source_target_pairs={{0,3},{1,2},{2,1},{3,0},{4,7},{5,6},{6,5},{7,4},{8,11},{9,10},{10,... | collective-permute-start | bytes 589832 | tf_op jit(solution)/shard_map/ppermute | solution.py:337
  196.0 32.1 %collective-permute-start.59 = (bf16[2,192,2,128]{3,2,1,0:T(2,128)(2,1)}, bf16[2,192,2,128]{3,2,1,0:T(2,128)(2,1)}, u32[]{:S(2)}, u32[]{:S(2)}) collective-permute-start(bf16[2,192,2,128]{3,2,1,0:T(2,128)(2,1)} %bitcast.110), channel_id=1, source_target_pairs={{0,15},{1,14},{2,13},{3,12},{4,11},{5,10},{6,9},{7,8},{8,7},{9,6},... | collective-permute-start | bytes 589832 | tf_op jit(solution)/shard_map/ppermute | solution.py:337
  215.3 25.4 %collective-permute-start.43 = (bf16[2,192,2,128]{3,2,1,0:T(2,128)(2,1)}, bf16[2,192,2,128]{3,2,1,0:T(2,128)(2,1)}, u32[]{:S(2)}, u32[]{:S(2)}) collective-permute-start(bf16[2,192,2,128]{3,2,1,0:T(2,128)(2,1)} %bitcast.134), channel_id=1, source_target_pairs={{0,12},{1,13},{2,14},{3,15},{4,8},{5,9},{6,10},{7,11},{8,4},{9,5},... | collective-permute-start | bytes 589832 | tf_op jit(solution)/shard_map/ppermute | solution.py:337
  215.3 25.4 %collective-permute-start.44 = (bf16[2,192,2,128]{3,2,1,0:T(2,128)(2,1)}, bf16[2,192,2,128]{3,2,1,0:T(2,128)(2,1)}, u32[]{:S(2)}, u32[]{:S(2)}) collective-permute-start(bf16[2,192,2,128]{3,2,1,0:T(2,128)(2,1)} %bitcast.132), channel_id=1, source_target_pairs={{0,1},{1,0},{2,3},{3,2},{4,5},{5,4},{6,7},{7,6},{8,9},{9,8},{10,11... | collective-permute-start | bytes 589832 | tf_op jit(solution)/shard_map/ppermute | solution.py:337
  232.3 25.2 %collective-permute-start.47 = (bf16[2,192,2,128]{3,2,1,0:T(2,128)(2,1)}, bf16[2,192,2,128]{3,2,1,0:T(2,128)(2,1)}, u32[]{:S(2)}, u32[]{:S(2)}) collective-permute-start(bf16[2,192,2,128]{3,2,1,0:T(2,128)(2,1)} %bitcast.126), channel_id=1, source_target_pairs={{0,13},{1,12},{2,15},{3,14},{4,9},{5,8},{6,11},{7,10},{8,5},{9,4},... | collective-permute-start | bytes 589832 | tf_op jit(solution)/shard_map/ppermute | solution.py:337
  240.7 25.3 %collective-permute-start.49 = (bf16[2,192,2,128]{3,2,1,0:T(2,128)(2,1)}, bf16[2,192,2,128]{3,2,1,0:T(2,128)(2,1)}, u32[]{:S(2)}, u32[]{:S(2)}) collective-permute-start(bf16[2,192,2,128]{3,2,1,0:T(2,128)(2,1)} %bitcast.122), channel_id=1, source_target_pairs={{0,6},{1,7},{2,4},{3,5},{4,14},{5,15},{6,12},{7,13},{8,2},{9,3},{1... | collective-permute-start | bytes 589832 | tf_op jit(solution)/shard_map/ppermute | solution.py:337
  249.1 32.8 %collective-permute-start.51 = (bf16[2,192,2,128]{3,2,1,0:T(2,128)(2,1)}, bf16[2,192,2,128]{3,2,1,0:T(2,128)(2,1)}, u32[]{:S(2)}, u32[]{:S(2)}) collective-permute-start(bf16[2,192,2,128]{3,2,1,0:T(2,128)(2,1)} %bitcast.119), channel_id=1, source_target_pairs={{0,14},{1,15},{2,12},{3,13},{4,10},{5,11},{6,8},{7,9},{8,6},{9,7},... | collective-permute-start | bytes 589832 | tf_op jit(solution)/shard_map/ppermute | solution.py:337
  257.4 27.0 %collective-permute-start.52 = (bf16[2,192,2,128]{3,2,1,0:T(2,128)(2,1)}, bf16[2,192,2,128]{3,2,1,0:T(2,128)(2,1)}, u32[]{:S(2)}, u32[]{:S(2)}) collective-permute-start(bf16[2,192,2,128]{3,2,1,0:T(2,128)(2,1)} %bitcast.118), channel_id=1, source_target_pairs={{0,3},{1,2},{2,1},{3,0},{4,7},{5,6},{6,5},{7,4},{8,11},{9,10},{10,... | collective-permute-start | bytes 589832 | tf_op jit(solution)/shard_map/ppermute | solution.py:337
  (46 other events, 1748.1 us)

commit v13 on v5

v13 whole, which is shorter than its diff:
```python
import math

import jax
import jax.numpy as jnp
from jax import lax
from jax.experimental import pallas as pl
from jax.experimental.pallas import tpu as pltpu
from jax.sharding import PartitionSpec as P

HD = 128
SPAN = 64
NTOK = 128
CHUNKS = 2
F32 = jnp.float32
BF16 = jnp.bfloat16
ANY = pl.BlockSpec(memory_space=pl.ANY)
LIMIT = pltpu.CompilerParams(vmem_limit_bytes=56 * 2**20)


def dot(a, b, dims):
    return lax.dot_general(a, b, (dims, ((), ())), preferred_element_type=F32)


NT = ((1,), (1,))
NN = ((1,), (0,))
TN = ((0,), (0,))


def cost(microseconds):
    return pl.CostEstimate(
        flops=0, bytes_accessed=int(microseconds * 3.69e6), transcendentals=0
    )


def vmem(*shape):
    return pltpu.VMEM(shape, BF16)


def moves(devices):
    quarter = devices // 4
    return [(kind, offset) for offset in range(quarter) for kind in range(6)]


def reached(index, devices, move):
    kind, offset = move
    quarter = devices // 4
    plane, inner = index // quarter, index % quarter
    plane = (
        plane,
        (2 * plane + 1) % 5,
        (3 * plane + 2) % 5,
        (plane + 1) % 4,
        (plane + 3) % 4,
        plane ^ 1,
    )[kind]
    return plane * quarter + (inner ^ offset)


def part(index, devices, move):
    kind, _ = move
    half = devices // 2
    near = 1 - (index // half + reached(index, devices, move) // half) % 2
    return near * (0, 1, 1, 2, 2, 0)[kind]


def here():
    return lax.axis_index("fsdp")


def target(devices, move):
    return reached(here(), devices, move)


def source(devices, move):
    kind, offset = move
    return reached(here(), devices, ((0, 2, 1, 4, 3, 5)[kind], offset))


def whole(move):
    return move[0] == 0


def pack(queries, out_grad, neighbours, devices, chunk, chunks):
    half = devices // 2
    heads = neighbours.shape[2] // HD // half // chunks
    width = heads * HD
    order = moves(devices)

    def kernel(q_ref, g_ref, n_ref, *refs):
        outs, (plain, stage, come_t, come_r, go) = refs[: len(order)], refs[len(order) :]
        starts = [(i * chunks + chunk) * width for i in range(half)]
        token_loads = [
            pltpu.make_async_copy(
                ref.at[:, pl.ds(starts[i], width)], plain.at[i, pl.ds(n * SPAN, SPAN)], come_t.at[i, n]
            )
            for i in range(half)
            for n, ref in enumerate((q_ref, g_ref))
        ]
        row_loads = [
            pltpu.make_async_copy(
                n_ref.at[:, :, pl.ds(starts[i] + h * HD, HD)],
                stage.at[i, h, pl.ds(SPAN, NTOK)],
                come_r.at[i, h],
            )
            for i in range(half)
            for h in range(heads)
        ]
        for load in token_loads + row_loads:
            load.start()
        for load in token_loads:
            load.wait()
        for i in range(half):
            for h in range(heads):
                folded = stage.at[i, h].reshape(2 * (SPAN + NTOK), HD)
                folded[: 2 * SPAN] = plain[i, :, pl.ds(h * HD, HD)]
        for load in row_loads:
            load.wait()
        stores = []
        for i, move in enumerate(order):
            block = stage.at[lax.rem(target(devices, move), half)]
            if not whole(move):
                block = block.at[:, pl.ds(part(here(), devices, move) * SPAN, SPAN)]
            stores.append(pltpu.make_async_copy(block, outs[i], go.at[i]))
        for store in stores:
            store.start()
        for store in stores:
            store.wait()

    def shape(move):
        return jax.ShapeDtypeStruct((heads, SPAN + NTOK if whole(move) else SPAN, 2, HD), BF16)

    results = pl.pallas_call(
        kernel,
        in_specs=[ANY] * 3,
        out_specs=[ANY] * len(order),
        out_shape=[shape(move) for move in order],
        scratch_shapes=[
            vmem(half, 2 * SPAN, width),
            vmem(half, heads, SPAN + NTOK, 2, HD),
            pltpu.SemaphoreType.DMA((half, 2)),
            pltpu.SemaphoreType.DMA((half, heads)),
            pltpu.SemaphoreType.DMA((len(order),)),
        ],
        compiler_params=LIMIT,
        cost_estimate=cost(4),
        name="pack",
    )(queries, out_grad, neighbours)
    return list(results)


def unpack(blocks, before, devices, chunk, chunks):
    half = devices // 2
    heads = blocks[0].shape[0]
    width = heads * HD
    order = moves(devices)

    def kernel(*refs):
        ins = refs[: len(order)]
        o_ref, q_ref, n_ref, stage, outs, come, go_t, go_r = refs[-8:]
        starts = [(i * chunks + chunk) * width for i in range(half)]
        loads = []
        for i, move in enumerate(order):
            origin = source(devices, move)
            block = stage.at[origin]
            if not whole(move):
                block = block.at[:, pl.ds(part(origin, devices, move) * SPAN, SPAN)]
            loads.append(pltpu.make_async_copy(ins[i], block, come.at[i]))
        for load in loads:
            load.start()
        for load in loads:
            load.wait()
        base = here() // half * half
        stores = []
        for i in range(half):
            for h in range(heads):
                target_rows = n_ref.at[:, :, pl.ds(starts[i] + h * HD, HD)]
                piece = stage.at[base + i, h, pl.ds(SPAN, NTOK)]
                stores.append(pltpu.make_async_copy(piece, target_rows, go_r.at[i, h]))
                stores[-1].start()
        for i in range(half):
            for h in range(heads):
                two = [
                    stage.at[first + i, h].reshape(2 * (SPAN + NTOK), HD)[: 2 * SPAN].astype(F32)
                    for first in (base, half - base)
                ]
                outs[i, :, pl.ds(h * HD, HD)] = (two[0] + two[1]).astype(BF16)
            for n, ref in enumerate((o_ref, q_ref)):
                piece = outs.at[i, pl.ds(n * SPAN, SPAN)]
                stores.append(
                    pltpu.make_async_copy(piece, ref.at[:, pl.ds(starts[i], width)], go_t.at[i, n])
                )
                stores[-1].start()
        for store in stores:
            store.wait()

    total = half * width * chunks
    return pl.pallas_call(
        kernel,
        in_specs=[ANY] * (len(order) + len(before)),
        out_specs=[ANY] * 3,
        out_shape=[
            jax.ShapeDtypeStruct((SPAN, total), BF16),
            jax.ShapeDtypeStruct((SPAN, total), BF16),
            jax.ShapeDtypeStruct((NTOK, 2, total), BF16),
        ],
        input_output_aliases={len(order) + i: i for i in range(len(before))},
        scratch_shapes=[
            vmem(devices, heads, SPAN + NTOK, 2, HD),
            vmem(half, 2 * SPAN, width),
            pltpu.SemaphoreType.DMA((len(order),)),
            pltpu.SemaphoreType.DMA((half, 2)),
            pltpu.SemaphoreType.DMA((half, heads)),
        ],
        compiler_params=LIMIT,
        cost_estimate=cost(4),
        name="unpack",
    )(*blocks, *before)


def last_rows():
    rows = lax.broadcasted_iota(jnp.int32, (2 * SPAN, HD), 0)
    return lax.rem(rows, SPAN) == SPAN - 1


def collect(blocks, raw, spans_ref):
    devices = raw.shape[0]
    for block, move in zip(blocks, moves(devices)):
        origin = source(devices, move)
        if whole(move):
            for n in range(3):
                raw[origin, n] = block[0, n * 2 * SPAN : (n + 1) * 2 * SPAN]
        else:
            raw[origin, part(origin, devices, move)] = block[0]
    last = last_rows()
    for c in range(devices):
        own = raw[c, 0].astype(F32)
        after = raw[c + 1, 0].astype(F32) if c + 1 < devices else jnp.zeros_like(own)
        spans_ref[c] = jnp.where(last, own, after).astype(BF16)


def load_row(raw, row, words):
    words[:NTOK] = raw[row, 1].astype(F32)
    words[NTOK:] = raw[row, 2].astype(F32)
    keys = words[pl.ds(0, NTOK, stride=2), :].astype(BF16)
    values = words[pl.ds(1, NTOK, stride=2), :].astype(BF16)
    return keys, values


def pair(spans_ref, first, second, part):
    rows = pl.ds(part * SPAN, SPAN)
    return jnp.concatenate([spans_ref[first // 2, rows], spans_ref[second // 2, rows]], 0)


def products(keys, values, queries, grads):
    scores = dot(keys, queries, NT) * (1.0 / math.sqrt(HD))
    return scores, dot(values, grads, NT)


def stats_kernel(slots_ref, *refs):
    blocks, (out_ref, raw, spans_ref, words) = refs[:-4], refs[-4:]
    half = raw.shape[0] // 2
    collect(blocks, raw, spans_ref)
    base = here() // half * half
    for step in range(half):
        first, second = slots_ref[2 * (base + step)], slots_ref[2 * (base + step) + 1]
        keys, values = load_row(raw, base + step, words.at[step % 4])
        queries = pair(spans_ref, first, second, 0)
        grads = pair(spans_ref, first, second, 1)
        scores, prob_grad = products(keys, values, queries, grads)
        top = jnp.max(scores, 0, keepdims=True)
        power = jnp.exp(scores - top)
        out_ref[0, 0, pl.ds(step, 1)] = top
        out_ref[0, 1, pl.ds(step, 1)] = jnp.sum(power, 0, keepdims=True)
        out_ref[0, 2, pl.ds(step, 1)] = jnp.sum(power * prob_grad, 0, keepdims=True)


def block_specs(blocks):
    return [pl.BlockSpec((1,) + block.shape[1:], lambda h, slots: (h, 0, 0)) for block in blocks]


def row_stats(slots, blocks, devices):
    half = devices // 2
    heads = blocks[0].shape[0]
    return pl.pallas_call(
        stats_kernel,
        grid_spec=pltpu.PrefetchScalarGridSpec(
            num_scalar_prefetch=1,
            grid=(heads,),
            in_specs=block_specs(blocks),
            out_specs=pl.BlockSpec((1, 3, half, HD), lambda h, slots: (h, 0, 0, 0)),
            scratch_shapes=[
                vmem(devices, 3, 2 * SPAN, HD),
                vmem(devices, 2 * SPAN, HD),
                pltpu.VMEM((4, 2 * NTOK, HD), F32),
            ],
        ),
        out_shape=jax.ShapeDtypeStruct((heads, 3, half, HD), F32),
        compiler_params=LIMIT,
        cost_estimate=cost(6),
        name="row_stats",
    )(slots, *blocks)


def grads_kernel(slots_ref, *refs):
    count = (len(refs) - 8) // 2
    blocks, (own_ref, other_ref) = refs[:count], refs[count : count + 2]
    outs, (raw, done, spans_ref, words, by_slot, sums) = refs[count + 2 : -6], refs[-6:]
    devices = raw.shape[0]
    half = devices // 2
    scale = 1.0 / math.sqrt(HD)
    collect(blocks, raw, spans_ref)
    sums[...] = jnp.zeros_like(sums)
    base = here() // half * half
    left = lax.broadcasted_iota(jnp.int32, (1, HD), 1) < SPAN
    for ref, start in ((own_ref, base), (other_ref, half - base)):
        for i in range(3):
            block = ref[0, i]
            turned = pltpu.roll(block, SPAN, 1)
            firsts = jnp.where(left, block, turned)
            seconds = jnp.where(left, turned, block)
            for r in range(half):
                by_slot[i, pl.ds(slots_ref[2 * (start + r)], 1)] = firsts[r : r + 1]
                by_slot[i, pl.ds(slots_ref[2 * (start + r) + 1], 1)] = seconds[r : r + 1]

    def spread(first, second):
        def mate(slot):
            return slot + 1 - 2 * lax.rem(slot, 2)

        own = [jnp.where(left, by_slot[i, pl.ds(first, 1)], by_slot[i, pl.ds(second, 1)]) for i in range(3)]
        first, second = mate(first), mate(second)
        other = [jnp.where(left, by_slot[i, pl.ds(first, 1)], by_slot[i, pl.ds(second, 1)]) for i in range(3)]
        top = jnp.maximum(own[0], other[0])
        here, there = jnp.exp(own[0] - top), jnp.exp(other[0] - top)
        inverse = 1.0 / (own[1] * here + other[1] * there)
        return top, inverse, (own[2] * here + other[2] * there) * inverse

    for step in range(half):
        first, second = slots_ref[2 * (base + step)], slots_ref[2 * (base + step) + 1]
        keys, values = load_row(raw, base + step, words.at[step % 4])
        queries = pair(spans_ref, first, second, 0)
        grads = pair(spans_ref, first, second, 1)
        scores, prob_grad = products(keys, values, queries, grads)
        top, inverse, delta = spread(first, second)
        soft = jnp.exp(scores - top) * inverse
        weights = soft.astype(BF16)
        score_grad = (soft * (prob_grad - delta)).astype(BF16)
        joined = words.at[4 + step % 4]
        joined[pl.ds(0, NTOK, stride=2), :] = dot(score_grad, queries, NN) * scale
        joined[pl.ds(1, NTOK, stride=2), :] = dot(weights, grads, NN)
        done[base + step, 1] = joined[:NTOK].astype(BF16)
        done[base + step, 2] = joined[NTOK:].astype(BF16)
        attended = dot(weights, values, TN)
        query_grad = dot(score_grad, keys, TN) * scale
        for n, slot in enumerate((first, second)):
            piece = slice(n * SPAN, (n + 1) * SPAN)
            sums[slot // 2 + 1, :SPAN] += attended[piece]
            sums[slot // 2 + 1, SPAN:] += query_grad[piece]
    last = last_rows()
    for d in range(devices):
        done[d, 0] = jnp.where(last, sums[d + 1], sums[d]).astype(BF16)
    for out, move in zip(outs, moves(devices)):
        d = target(devices, move)
        if whole(move):
            for n in range(3):
                out[0, n * 2 * SPAN : (n + 1) * 2 * SPAN] = done[d, n]
        else:
            out[0] = done[d, part(here(), devices, move)]


def grads(slots, blocks, own, other, devices):
    half = devices // 2
    heads = blocks[0].shape[0]
    stats_block = pl.BlockSpec((1, 3, half, HD), lambda h, slots: (h, 0, 0, 0))
    results = pl.pallas_call(
        grads_kernel,
        grid_spec=pltpu.PrefetchScalarGridSpec(
            num_scalar_prefetch=1,
            grid=(heads,),
            in_specs=block_specs(blocks) + [stats_block, stats_block],
            out_specs=block_specs(blocks),
            scratch_shapes=[
                vmem(devices, 3, 2 * SPAN, HD),
                vmem(devices, 3, 2 * SPAN, HD),
                vmem(devices, 2 * SPAN, HD),
                pltpu.VMEM((8, 2 * NTOK, HD), F32),
                pltpu.VMEM((3, 2 * devices, HD), F32),
                pltpu.VMEM((devices + 1, 2 * SPAN, HD), F32),
            ],
        ),
        out_shape=[jax.ShapeDtypeStruct(block.shape, BF16) for block in blocks],
        compiler_params=LIMIT,
        cost_estimate=cost(12),
        name="grads",
    )(slots, *blocks, own, other)
    return list(results)


def after(later, earlier):
    some = len(earlier) * 3 // 4
    later, earlier[:some] = lax.optimization_barrier((later, earlier[:some]))
    return later


def swap(blocks, devices):
    return blocks[:1] + [
        lax.ppermute(block, "fsdp", [(i, reached(i, devices, move)) for i in range(devices)])
        for block, move in list(zip(blocks, moves(devices)))[1:]
    ]


def body(queries, out_grad, neighbours, neighbour_ids):
    devices = lax.axis_size("fsdp")
    half = devices // 2
    heads = queries.shape[1] // HD // half
    chunks = math.gcd(heads, CHUNKS)
    across = [(i, (i + half) % devices) for i in range(devices)]
    slots = jnp.argsort(neighbour_ids, stable=True).astype(jnp.int32)

    def compute(blocks):
        blocks = [block.reshape(block.shape[0], -1, HD) for block in blocks]
        own = row_stats(slots, blocks, devices)
        other = lax.ppermute(own, "fsdp", across)
        results = grads(slots, blocks, own, other, devices)
        return [block.reshape(block.shape[0], -1, 2, HD) for block in results]

    arrived, back = [], []
    for chunk in range(chunks):
        blocks = pack(queries, out_grad, neighbours, devices, chunk, chunks)
        if arrived:
            blocks = after(blocks, arrived[-1])
        arrived.append(swap(blocks, devices))
    for chunk in range(chunks):
        blocks = compute(arrived[chunk])
        if back:
            blocks = after(blocks, back[-1])
        elif chunks > 1:
            blocks = after(blocks, arrived[-1])
        back.append(swap(blocks, devices))
    outputs = ()
    for chunk in range(chunks):
        outputs = tuple(unpack(back[chunk], outputs, devices, chunk, chunks))
    return outputs


def solution(mesh):
    in_specs = (
        P(("groups", "fsdp"), None),
        P(("groups", "fsdp"), None),
        P(("groups", "fsdp"), None, None),
        P("groups"),
    )
    out_specs = (
        P(("groups", "fsdp"), None),
        P(("groups", "fsdp"), None),
        P(("groups", "fsdp"), None, None),
    )
    return jax.shard_map(body, mesh=mesh, in_specs=in_specs, out_specs=out_specs, check_vma=False)
```

time: 348 us -> 341 us (0.980)
  waiting for transfers between devices: 185 us -> 87.6 us
  starting transfers between devices: 104 us -> 181 us
  Pallas kernels: 54.4 us -> 63.3 us
    ppermute x60 -> x92, waiting for transfers between devices: 178 us -> 84.5 us  [swap(): lax.ppermute(block, 'fsdp', [(i, reached(i, devices, move)) for i in rang...]
    ppermute x60 -> x92, starting transfers between devices: 102 us -> 177 us  [swap(): lax.ppermute(block, 'fsdp', [(i, reached(i, devices, move)) for i in rang...]
    pallas_call x4, Pallas kernels: 16.8 us -> 20.8 us  [the longest x2 11.3 us: pack(): pl.pallas_call(kernel, in_specs=[ANY] * 3, out_specs=[ANY] * len(order),...]
  transfers between devices with their start and end apart: 62 -> 94, of which waited for: 40 -> 39; matrix products, arithmetic and copies ran while one was open for 0% -> 0% of each run, Pallas kernels for 13% -> 16%
where the time goes in v13:
time: 341 us; the launch traced here: 338 us
  starting transfers between devices  181 us (53%)
  waiting for transfers between devices  87.6 us (26%)
  Pallas kernels  63.3 us (19%)
    ppermute x92, starting transfers between devices, swap(): lax.ppermute(block, 'fsdp', [(i, reached(i, devices, move)) for i in rang...  177 us
    ppermute x92, waiting for transfers between devices, swap(): lax.ppermute(block, 'fsdp', [(i, reached(i, devices, move)) for i in rang...  84.5 us
    pallas_call x2, Pallas kernels, grads(): pl.pallas_call(grads_kernel, grid_spec=pltpu.PrefetchScalarGridSpec(num_s...  28.7 us
    pallas_call x2, Pallas kernels, row_stats(): pl.pallas_call(stats_kernel, grid_spec=pltpu.PrefetchScalarGridSpec(num_s...  13.9 us
    pallas_call x2, Pallas kernels, pack(): pl.pallas_call(kernel, in_specs=[ANY] * 3, out_specs=[ANY] * len(order),...  11.3 us
    pallas_call x2, Pallas kernels, unpack(): pl.pallas_call(kernel, in_specs=[ANY] * (len(order) + len(before)), out_s...  9.48 us
  transfers between devices with their start and end apart: 94, of which 39 were waited for; matrix products, arithmetic and copies ran while one was open for 0% of the time, Pallas kernels for 16%

profile of v13, /device:TPU:15, one launch (start us, length us, event | category | flops | bytes accessed | tf_op | source)
XLA Modules:
  0.0 338.1 jit_solution(11134232648957914196)
XLA Ops:
  0.6 5.7 %pack.3 = (bf16[4,192,2,128]{3,2,1,0:T(2,128)(2,1)}, bf16[4,64,2,128]{3,2,1,0:T(2,128)(2,1)}, bf16[4,64,2,128]{3,2,1,0:T(2,128)(2,1)}, bf16[4,64,2,128]{3,2,1,0:...) custom-call(bf16[64,8192]{1,0:T(8,128)(2,1)} %q_ref.3, ...), custom_call_target="tpu_custom_call" | custom-call | bytes 14760000 | tf_op jit(solution)/shard_map/pack/pallas_call | solution.py:132
  12.4 7.2 %collective-permute-start.6 = (bf16[4,64,2,128]{3,2,1,0:T(2,128)(2,1)}, bf16[4,64,2,128]{3,2,1,0:T(2,128)(2,1)S(1)}, u32[]{:S(2)}, u32[]{:S(2)}) collective-permute-start(bf16[4,64,2,128]{3,2,1,0:T(2,128)(2,1)} %get-tuple-element.261), channel_id=1, source_target_pairs={{0,5},{1,4},{2,7},{3,6},{4,13},{5,12},{6,15},{7,14},{8,1},{9,0},{1... | collective-permute-start | bytes 393224 | tf_op jit(solution)/shard_map/ppermute | solution.py:406
  42.2 5.3 %collective-permute-done.13 = bf16[4,64,2,128]{3,2,1,0:T(2,128)(2,1)S(1)} collective-permute-done((bf16[4,64,2,128]{3,2,1,0:T(2,128)(2,1)}, bf16[4,64,2,128]{3,2,1,0:T(2,128)(2,1)S(1)}, u32[]{:S(2)}, u32[]{:S(2)}) %collective-permute-start.13) | collective-permute-done | bytes 131104 | tf_op jit(solution)/shard_map/ppermute | solution.py:406
  65.6 5.6 %pack.2 = (bf16[4,192,2,128]{3,2,1,0:T(2,128)(2,1)}, bf16[4,64,2,128]{3,2,1,0:T(2,128)(2,1)}, bf16[4,64,2,128]{3,2,1,0:T(2,128)(2,1)}, bf16[4,64,2,128]{3,2,1,0:...) custom-call(bf16[64,8192]{1,0:T(8,128)(2,1)} %q_ref.3, ...), custom_call_target="tpu_custom_call" | custom-call | bytes 14760000 | tf_op jit(solution)/shard_map/pack/pallas_call | solution.py:132
  71.2 10.3 %collective-permute-start.24 = (bf16[4,64,2,128]{3,2,1,0:T(2,128)(2,1)}, bf16[4,64,2,128]{3,2,1,0:T(2,128)(2,1)S(1)}, u32[]{:S(2)}, u32[]{:S(2)}) collective-permute-start(bf16[4,64,2,128]{3,2,1,0:T(2,128)(2,1)} %get-tuple-element.321), channel_id=1, source_target_pairs={{0,4},{1,5},{2,6},{3,7},{4,12},{5,13},{6,14},{7,15},{8,0},{9,1},{1... | collective-permute-start | bytes 393224 | tf_op jit(solution)/shard_map/ppermute | solution.py:406
  85.6 6.9 %row_stats.2.refs_24_ = f32[4,3,8,128]{3,2,1,0:T(8,128)} custom-call(s32[32]{0:T(128)} %get-tuple-element.229.slots_ref, bf16[4,384,128]{2,1,0:T(8,128)(2,1)} %bitcast.98, bf16[4,128,128]{2,1,0:T(8,128)(2,1)} %bitcast.122, bf16[4,128,128]{2,1,0:T(8,128)(2,1)} %bitcast.126, bf16[4,128,128]{2,1,0:T(8,128)(2,1)} %bitcast.128, bf16[4,128,128]{2,1,0:T(8,128)(2,1)} %bitcast.132, ...), custom_call_target="tpu_custom_call" | custom-call | bytes 22140000 | tf_op jit(solution)/shard_map/row_stats/pallas_call | solution.py:284
  103.4 6.0 %collective-permute-start.34 = (bf16[4,64,2,128]{3,2,1,0:T(2,128)(2,1)S(1)}, bf16[4,64,2,128]{3,2,1,0:T(2,128)(2,1)S(1)}, u32[]{:S(2)}, u32[]{:S(2)}) collective-permute-start(bf16[4,64,2,128]{3,2,1,0:T(2,128)(2,1)S(1)} %copy-done.110), channel_id=1, source_target_pairs={{0,5},{1,4},{2,7},{3,6},{4,1},{5,0},{6,3},{7,2},{8,13},{9,12},{10,... | collective-permute-start | bytes 393224 | tf_op jit(solution)/shard_map/ppermute | solution.py:406
  114.7 7.1 %collective-permute-start.37 = (bf16[4,64,2,128]{3,2,1,0:T(2,128)(2,1)S(1)}, bf16[4,64,2,128]{3,2,1,0:T(2,128)(2,1)S(1)}, u32[]{:S(2)}, u32[]{:S(2)}) collective-permute-start(bf16[4,64,2,128]{3,2,1,0:T(2,128)(2,1)S(1)} %copy-done.107), channel_id=1, source_target_pairs={{0,10},{1,11},{2,8},{3,9},{4,2},{5,3},{6,0},{7,1},{8,14},{9,15},{1... | collective-permute-start | bytes 393224 | tf_op jit(solution)/shard_map/ppermute | solution.py:406
  134.9 5.8 %collective-permute-start.43 = (bf16[4,64,2,128]{3,2,1,0:T(2,128)(2,1)}, bf16[4,64,2,128]{3,2,1,0:T(2,128)(2,1)S(1)}, u32[]{:S(2)}, u32[]{:S(2)}) collective-permute-start(bf16[4,64,2,128]{3,2,1,0:T(2,128)(2,1)} %get-tuple-element.358), channel_id=1, source_target_pairs={{0,11},{1,10},{2,9},{3,8},{4,3},{5,2},{6,1},{7,0},{8,15},{9,14},{1... | collective-permute-start | bytes 393224 | tf_op jit(solution)/shard_map/ppermute | solution.py:406
  144.9 5.5 %collective-permute-start.46 = (bf16[4,64,2,128]{3,2,1,0:T(2,128)(2,1)}, bf16[4,64,2,128]{3,2,1,0:T(2,128)(2,1)S(1)}, u32[]{:S(2)}, u32[]{:S(2)}) collective-permute-start(bf16[4,64,2,128]{3,2,1,0:T(2,128)(2,1)} %get-tuple-element.361), channel_id=1, source_target_pairs={{0,7},{1,6},{2,5},{3,4},{4,3},{5,2},{6,1},{7,0},{8,15},{9,14},{10,... | collective-permute-start | bytes 393224 | tf_op jit(solution)/shard_map/ppermute | solution.py:406
  150.4 14.3 %grads.2 = (bf16[4,384,128]{2,1,0:T(8,128)(2,1)}, bf16[4,128,128]{2,1,0:T(8,128)(2,1)}, bf16[4,128,128]{2,1,0:T(8,128)(2,1)}, bf16[4,128,128]{2,1,0:T(8,128)(2,1...) custom-call(s32[32]{0:T(128)} %get-tuple-element.229.slots_ref, ...), custom_call_target="tpu_custom_call" | custom-call | bytes 44280000 | tf_op jit(solution)/shard_map/grads/pallas_call | solution.py:374
  164.9 5.7 %collective-permute-start.48 = (bf16[4,64,2,128]{3,2,1,0:T(2,128)(2,1)}, bf16[4,64,2,128]{3,2,1,0:T(2,128)(2,1)S(1)}, u32[]{:S(2)}, u32[]{:S(2)}) collective-permute-start(bf16[4,64,2,128]{3,2,1,0:T(2,128)(2,1)} %bitcast.226), channel_id=1, source_target_pairs={{0,4},{1,5},{2,6},{3,7},{4,12},{5,13},{6,14},{7,15},{8,0},{9,1},{1... | collective-permute-start | bytes 393224 | tf_op jit(solution)/shard_map/ppermute | solution.py:406
  171.8 6.9 %row_stats.3.refs_24_ = f32[4,3,8,128]{3,2,1,0:T(8,128)} custom-call(s32[32]{0:T(128)} %get-tuple-element.229.slots_ref, bf16[4,384,128]{2,1,0:T(8,128)(2,1)} %bitcast.96, bf16[4,128,128]{2,1,0:T(8,128)(2,1)} %bitcast.112, bf16[4,128,128]{2,1,0:T(8,128)(2,1)} %bitcast.114, bf16[4,128,128]{2,1,0:T(8,128)(2,1)} %bitcast.116, bf16[4,128,128]{2,1,0:T(8,128)(2,1)} %bitcast.118, ...), custom_call_target="tpu_custom_call" | custom-call | bytes 22140000 | tf_op jit(solution)/shard_map/row_stats/pallas_call | solution.py:284
  185.0 4.7 %collective-permute-start.54 = (bf16[4,64,2,128]{3,2,1,0:T(2,128)(2,1)S(1)}, bf16[4,64,2,128]{3,2,1,0:T(2,128)(2,1)S(1)}, u32[]{:S(2)}, u32[]{:S(2)}) collective-permute-start(bf16[4,64,2,128]{3,2,1,0:T(2,128)(2,1)S(1)} %bitcast.216), channel_id=1, source_target_pairs={{0,5},{1,4},{2,7},{3,6},{4,13},{5,12},{6,15},{7,14},{8,1},{9,0},{1... | collective-permute-start | bytes 393224 | tf_op jit(solution)/shard_map/ppermute | solution.py:406
  210.6 5.1 %collective-permute-done.61.refs_14_ = bf16[4,64,2,128]{3,2,1,0:T(2,128)(2,1)S(1)} collective-permute-done((bf16[4,64,2,128]{3,2,1,0:T(2,128)(2,1)S(1)}, bf16[4,64,2,128]{3,2,1,0:T(2,128)(2,1)S(1)}, u32[]{:S(2)}, u32[]{:S(2)}) %collective-permute-start.61) | collective-permute-done | bytes 131104 | tf_op jit(solution)/shard_map/ppermute | solution.py:406
  224.3 5.2 %collective-permute-done.89.refs_19_ = bf16[4,64,2,128]{3,2,1,0:T(2,128)(2,1)S(1)} collective-permute-done((bf16[4,64,2,128]{3,2,1,0:T(2,128)(2,1)S(1)}, bf16[4,64,2,128]{3,2,1,0:T(2,128)(2,1)S(1)}, u32[]{:S(2)}, u32[]{:S(2)}) %collective-permute-start.89) | collective-permute-done | bytes 131104 | tf_op jit(solution)/shard_map/ppermute | solution.py:406
  232.2 6.8 %collective-permute-start.93 = (bf16[4,64,2,128]{3,2,1,0:T(2,128)(2,1)S(1)}, bf16[4,64,2,128]{3,2,1,0:T(2,128)(2,1)}, u32[]{:S(2)}, u32[]{:S(2)}) collective-permute-start(bf16[4,64,2,128]{3,2,1,0:T(2,128)(2,1)S(1)} %bitcast.192), channel_id=1, source_target_pairs={{0,7},{1,6},{2,5},{3,4},{4,3},{5,2},{6,1},{7,0},{8,15},{9,14},{10,... | collective-permute-start | bytes 393224 | tf_op jit(solution)/shard_map/ppermute | solution.py:406
  239.0 14.3 %grads.3 = (bf16[4,384,128]{2,1,0:T(8,128)(2,1)}, bf16[4,128,128]{2,1,0:T(8,128)(2,1)}, bf16[4,128,128]{2,1,0:T(8,128)(2,1)}, bf16[4,128,128]{2,1,0:T(8,128)(2,1...) custom-call(s32[32]{0:T(128)} %get-tuple-element.229.slots_ref, ...), custom_call_target="tpu_custom_call" | custom-call | bytes 44280000 | tf_op jit(solution)/shard_map/grads/pallas_call | solution.py:374
  266.4 7.4 %collective-permute-start.73 = (bf16[4,64,2,128]{3,2,1,0:T(2,128)(2,1)}, bf16[4,64,2,128]{3,2,1,0:T(2,128)(2,1)S(1)}, u32[]{:S(2)}, u32[]{:S(2)}) collective-permute-start(bf16[4,64,2,128]{3,2,1,0:T(2,128)(2,1)} %bitcast.215), channel_id=1, source_target_pairs={{0,5},{1,4},{2,7},{3,6},{4,9},{5,8},{6,11},{7,10},{8,13},{9,12},{1... | collective-permute-start | bytes 393224 | tf_op jit(solution)/shard_map/ppermute | solution.py:406
  284.9 6.1 %collective-permute-start.81 = (bf16[4,64,2,128]{3,2,1,0:T(2,128)(2,1)}, bf16[4,64,2,128]{3,2,1,0:T(2,128)(2,1)S(1)}, u32[]{:S(2)}, u32[]{:S(2)}) collective-permute-start(bf16[4,64,2,128]{3,2,1,0:T(2,128)(2,1)} %bitcast.204), channel_id=1, source_target_pairs={{0,6},{1,7},{2,4},{3,5},{4,2},{5,3},{6,0},{7,1},{8,14},{9,15},{10,... | collective-permute-start | bytes 393224 | tf_op jit(solution)/shard_map/ppermute | solution.py:406
  297.5 4.7 %collective-permute-done.80.refs_16_ = bf16[4,64,2,128]{3,2,1,0:T(2,128)(2,1)S(1)} collective-permute-done((bf16[4,64,2,128]{3,2,1,0:T(2,128)(2,1)}, bf16[4,64,2,128]{3,2,1,0:T(2,128)(2,1)S(1)}, u32[]{:S(2)}, u32[]{:S(2)}) %collective-permute-start.80) | collective-permute-done | bytes 131104 | tf_op jit(solution)/shard_map/ppermute | solution.py:406
  314.9 4.8 %unpack.2 = (bf16[64,8192]{1,0:T(8,128)(2,1)}, bf16[64,8192]{1,0:T(8,128)(2,1)}, bf16[128,2,8192]{2,1,0:T(2,128)(2,1)}) custom-call(bf16[4,192,2,128]{3,2,1,0:T(2,128)(2,1)} %bitcast.185, bf16[4,64,2,128]{3,2,1,0:T(2,128)(2,1)} %copy-done.68, bf16[4,64,2,128]{3,2,1,0:T(2,128)(2,1)} %copy-done.69, bf16[4,64,2,128]{3,2,1,0:T(2,128)(2,1)} %copy-done.70, ...), custom_call_target="tpu_custom_call" | custom-call | bytes 14760000 | tf_op jit(solution)/shard_map/unpack/pallas_call | solution.py:197
  324.1 8.4 %collective-permute-done.82.refs_18_ = bf16[4,192,2,128]{3,2,1,0:T(2,128)(2,1)S(1)} collective-permute-done((bf16[4,192,2,128]{3,2,1,0:T(2,128)(2,1)}, bf16[4,192,2,128]{3,2,1,0:T(2,128)(2,1)S(1)}, u32[]{:S(2)}, u32[]{:S(2)}) %collective-permute-start.82) | collective-permute-done | bytes 393248 | tf_op jit(solution)/shard_map/ppermute | solution.py:406
  333.2 4.7 %unpack.3 = (bf16[64,8192]{1,0:T(8,128)(2,1)}, bf16[64,8192]{1,0:T(8,128)(2,1)}, bf16[128,2,8192]{2,1,0:T(2,128)(2,1)}) custom-call(bf16[4,192,2,128]{3,2,1,0:T(2,128)(2,1)} %bitcast.184, bf16[4,64,2,128]{3,2,1,0:T(2,128)(2,1)} %copy-done.48, bf16[4,64,2,128]{3,2,1,0:T(2,128)(2,1)} %copy-done.49, ...), custom_call_target="tpu_custom_call", output_to_operand_aliasing={{0}: (24, {}), {1}: (25, {}), {2}: (26, {})} | custom-call | bytes 14760000 | tf_op jit(solution)/shard_map/unpack/pallas_call | solution.py:197
  (414 shorter events, 171.4 us)
Async XLA Ops:
  30.7 31.1 %collective-permute-start.5 = (bf16[4,192,2,128]{3,2,1,0:T(2,128)(2,1)}, bf16[4,192,2,128]{3,2,1,0:T(2,128)(2,1)S(1)}, u32[]{:S(2)}, u32[]{:S(2)}) collective-permute-start(bf16[4,192,2,128]{3,2,1,0:T(2,128)(2,1)} %get-tuple-element.260), channel_id=1, source_target_pairs={{0,1},{1,0},{2,3},{3,2},{4,5},{5,4},{6,7},{7,6},{8,9},{9,8},{10,11... | collective-permute-start | bytes 1179656 | tf_op jit(solution)/shard_map/ppermute | solution.py:406
  32.9 30.2 %collective-permute-start.11 = (bf16[4,192,2,128]{3,2,1,0:T(2,128)(2,1)}, bf16[4,192,2,128]{3,2,1,0:T(2,128)(2,1)S(1)}, u32[]{:S(2)}, u32[]{:S(2)}) collective-permute-start(bf16[4,192,2,128]{3,2,1,0:T(2,128)(2,1)} %get-tuple-element.266), channel_id=1, source_target_pairs={{0,2},{1,3},{2,0},{3,1},{4,6},{5,7},{6,4},{7,5},{8,10},{9,11},{10,... | collective-permute-start | bytes 1179656 | tf_op jit(solution)/shard_map/ppermute | solution.py:406
  47.4 37.4 %collective-permute-start.17 = (bf16[4,192,2,128]{3,2,1,0:T(2,128)(2,1)}, bf16[4,192,2,128]{3,2,1,0:T(2,128)(2,1)S(1)}, u32[]{:S(2)}, u32[]{:S(2)}) collective-permute-start(bf16[4,192,2,128]{3,2,1,0:T(2,128)(2,1)} %get-tuple-element.290), channel_id=1, source_target_pairs={{0,3},{1,2},{2,1},{3,0},{4,7},{5,6},{6,5},{7,4},{8,11},{9,10},{10,... | collective-permute-start | bytes 1179656 | tf_op jit(solution)/shard_map/ppermute | solution.py:406
  60.5 21.1 %collective-permute-start.20 = (bf16[4,64,2,128]{3,2,1,0:T(2,128)(2,1)}, bf16[4,64,2,128]{3,2,1,0:T(2,128)(2,1)}, u32[]{:S(2)}, u32[]{:S(2)}) collective-permute-start(bf16[4,64,2,128]{3,2,1,0:T(2,128)(2,1)} %get-tuple-element.293), channel_id=1, source_target_pairs={{0,7},{1,6},{2,5},{3,4},{4,11},{5,10},{6,9},{7,8},{8,15},{9,14},{1... | collective-permute-start | bytes 393224 | tf_op jit(solution)/shard_map/ppermute | solution.py:406
  61.7 21.6 %collective-permute-start.21 = (bf16[4,64,2,128]{3,2,1,0:T(2,128)(2,1)}, bf16[4,64,2,128]{3,2,1,0:T(2,128)(2,1)}, u32[]{:S(2)}, u32[]{:S(2)}) collective-permute-start(bf16[4,64,2,128]{3,2,1,0:T(2,128)(2,1)} %get-tuple-element.294), channel_id=1, source_target_pairs={{0,15},{1,14},{2,13},{3,12},{4,3},{5,2},{6,1},{7,0},{8,7},{9,6},{1... | collective-permute-start | bytes 393224 | tf_op jit(solution)/shard_map/ppermute | solution.py:406
  63.1 20.6 %collective-permute-start.22 = (bf16[4,64,2,128]{3,2,1,0:T(2,128)(2,1)}, bf16[4,64,2,128]{3,2,1,0:T(2,128)(2,1)}, u32[]{:S(2)}, u32[]{:S(2)}) collective-permute-start(bf16[4,64,2,128]{3,2,1,0:T(2,128)(2,1)} %get-tuple-element.295), channel_id=1, source_target_pairs={{0,7},{1,6},{2,5},{3,4},{4,3},{5,2},{6,1},{7,0},{8,15},{9,14},{10,... | collective-permute-start | bytes 393224 | tf_op jit(solution)/shard_map/ppermute | solution.py:406
  71.2 27.7 %collective-permute-start.24 = (bf16[4,64,2,128]{3,2,1,0:T(2,128)(2,1)}, bf16[4,64,2,128]{3,2,1,0:T(2,128)(2,1)S(1)}, u32[]{:S(2)}, u32[]{:S(2)}) collective-permute-start(bf16[4,64,2,128]{3,2,1,0:T(2,128)(2,1)} %get-tuple-element.321), channel_id=1, source_target_pairs={{0,4},{1,5},{2,6},{3,7},{4,12},{5,13},{6,14},{7,15},{8,0},{9,1},{1... | collective-permute-start | bytes 393224 | tf_op jit(solution)/shard_map/ppermute | solution.py:406
  110.3 30.4 %collective-permute-start.29 = (bf16[4,192,2,128]{3,2,1,0:T(2,128)(2,1)}, bf16[4,192,2,128]{3,2,1,0:T(2,128)(2,1)S(1)}, u32[]{:S(2)}, u32[]{:S(2)}) collective-permute-start(bf16[4,192,2,128]{3,2,1,0:T(2,128)(2,1)} %get-tuple-element.326), channel_id=1, source_target_pairs={{0,1},{1,0},{2,3},{3,2},{4,5},{5,4},{6,7},{7,6},{8,9},{9,8},{10,11... | collective-permute-start | bytes 1179656 | tf_op jit(solution)/shard_map/ppermute | solution.py:406
  112.6 32.3 %collective-permute-start.35 = (bf16[4,192,2,128]{3,2,1,0:T(2,128)(2,1)S(1)}, bf16[4,192,2,128]{3,2,1,0:T(2,128)(2,1)S(1)}, u32[]{:S(2)}, u32[]{:S(2)}) collective-permute-start(bf16[4,192,2,128]{3,2,1,0:T(2,128)(2,1)S(1)} %copy-done.92), channel_id=1, source_target_pairs={{0,2},{1,3},{2,0},{3,1},{4,6},{5,7},{6,4},{7,5},{8,10},{9,11},{10,... | collective-permute-start | bytes 1179656 | tf_op jit(solution)/shard_map/ppermute | solution.py:406
  125.4 45.6 %collective-permute-start.41 = (bf16[4,192,2,128]{3,2,1,0:T(2,128)(2,1)S(1)}, bf16[4,192,2,128]{3,2,1,0:T(2,128)(2,1)S(1)}, u32[]{:S(2)}, u32[]{:S(2)}) collective-permute-start(bf16[4,192,2,128]{3,2,1,0:T(2,128)(2,1)S(1)} %copy-done.89), channel_id=1, source_target_pairs={{0,3},{1,2},{2,1},{3,0},{4,7},{5,6},{6,5},{7,4},{8,11},{9,10},{10,... | collective-permute-start | bytes 1179656 | tf_op jit(solution)/shard_map/ppermute | solution.py:406
  134.9 30.0 %collective-permute-start.43 = (bf16[4,64,2,128]{3,2,1,0:T(2,128)(2,1)}, bf16[4,64,2,128]{3,2,1,0:T(2,128)(2,1)S(1)}, u32[]{:S(2)}, u32[]{:S(2)}) collective-permute-start(bf16[4,64,2,128]{3,2,1,0:T(2,128)(2,1)} %get-tuple-element.358), channel_id=1, source_target_pairs={{0,11},{1,10},{2,9},{3,8},{4,3},{5,2},{6,1},{7,0},{8,15},{9,14},{1... | collective-permute-start | bytes 393224 | tf_op jit(solution)/shard_map/ppermute | solution.py:406
  140.7 29.9 %collective-permute-start.44 = (bf16[4,64,2,128]{3,2,1,0:T(2,128)(2,1)}, bf16[4,64,2,128]{3,2,1,0:T(2,128)(2,1)S(1)}, u32[]{:S(2)}, u32[]{:S(2)}) collective-permute-start(bf16[4,64,2,128]{3,2,1,0:T(2,128)(2,1)} %get-tuple-element.359), channel_id=1, source_target_pairs={{0,7},{1,6},{2,5},{3,4},{4,11},{5,10},{6,9},{7,8},{8,15},{9,14},{1... | collective-permute-start | bytes 393224 | tf_op jit(solution)/shard_map/ppermute | solution.py:406
  140.8 29.9 %collective-permute-start.45 = (bf16[4,64,2,128]{3,2,1,0:T(2,128)(2,1)}, bf16[4,64,2,128]{3,2,1,0:T(2,128)(2,1)S(1)}, u32[]{:S(2)}, u32[]{:S(2)}) collective-permute-start(bf16[4,64,2,128]{3,2,1,0:T(2,128)(2,1)} %get-tuple-element.360), channel_id=1, source_target_pairs={{0,15},{1,14},{2,13},{3,12},{4,3},{5,2},{6,1},{7,0},{8,7},{9,6},{1... | collective-permute-start | bytes 393224 | tf_op jit(solution)/shard_map/ppermute | solution.py:406
  144.9 26.1 %collective-permute-start.46 = (bf16[4,64,2,128]{3,2,1,0:T(2,128)(2,1)}, bf16[4,64,2,128]{3,2,1,0:T(2,128)(2,1)S(1)}, u32[]{:S(2)}, u32[]{:S(2)}) collective-permute-start(bf16[4,64,2,128]{3,2,1,0:T(2,128)(2,1)} %get-tuple-element.361), channel_id=1, source_target_pairs={{0,7},{1,6},{2,5},{3,4},{4,3},{5,2},{6,1},{7,0},{8,15},{9,14},{10,... | collective-permute-start | bytes 393224 | tf_op jit(solution)/shard_map/ppermute | solution.py:406
  198.0 31.5 %collective-permute-start.53 = (bf16[4,192,2,128]{3,2,1,0:T(2,128)(2,1)S(1)}, bf16[4,192,2,128]{3,2,1,0:T(2,128)(2,1)S(1)}, u32[]{:S(2)}, u32[]{:S(2)}) collective-permute-start(bf16[4,192,2,128]{3,2,1,0:T(2,128)(2,1)S(1)} %bitcast.191), channel_id=1, source_target_pairs={{0,1},{1,0},{2,3},{3,2},{4,5},{5,4},{6,7},{7,6},{8,9},{9,8},{10,11... | collective-permute-start | bytes 1179656 | tf_op jit(solution)/shard_map/ppermute | solution.py:406
  199.2 33.0 %collective-permute-start.59 = (bf16[4,192,2,128]{3,2,1,0:T(2,128)(2,1)S(1)}, bf16[4,192,2,128]{3,2,1,0:T(2,128)(2,1)S(1)}, u32[]{:S(2)}, u32[]{:S(2)}) collective-permute-start(bf16[4,192,2,128]{3,2,1,0:T(2,128)(2,1)S(1)} %bitcast.190), channel_id=1, source_target_pairs={{0,2},{1,3},{2,0},{3,1},{4,6},{5,7},{6,4},{7,5},{8,10},{9,11},{10,... | collective-permute-start | bytes 1179656 | tf_op jit(solution)/shard_map/ppermute | solution.py:406
  216.4 42.8 %collective-permute-start.88 = (bf16[4,192,2,128]{3,2,1,0:T(2,128)(2,1)S(1)}, bf16[4,192,2,128]{3,2,1,0:T(2,128)(2,1)S(1)}, u32[]{:S(2)}, u32[]{:S(2)}) collective-permute-start(bf16[4,192,2,128]{3,2,1,0:T(2,128)(2,1)S(1)} %bitcast.186), channel_id=1, source_target_pairs={{0,3},{1,2},{2,1},{3,0},{4,7},{5,6},{6,5},{7,4},{8,11},{9,10},{10,... | collective-permute-start | bytes 1179656 | tf_op jit(solution)/shard_map/ppermute | solution.py:406
  222.3 31.0 %collective-permute-start.90 = (bf16[4,64,2,128]{3,2,1,0:T(2,128)(2,1)S(1)}, bf16[4,64,2,128]{3,2,1,0:T(2,128)(2,1)S(1)}, u32[]{:S(2)}, u32[]{:S(2)}) collective-permute-start(bf16[4,64,2,128]{3,2,1,0:T(2,128)(2,1)S(1)} %bitcast.195), channel_id=1, source_target_pairs={{0,11},{1,10},{2,9},{3,8},{4,3},{5,2},{6,1},{7,0},{8,15},{9,14},{1... | collective-permute-start | bytes 393224 | tf_op jit(solution)/shard_map/ppermute | solution.py:406
  229.5 28.2 %collective-permute-start.91 = (bf16[4,64,2,128]{3,2,1,0:T(2,128)(2,1)S(1)}, bf16[4,64,2,128]{3,2,1,0:T(2,128)(2,1)S(1)}, u32[]{:S(2)}, u32[]{:S(2)}) collective-permute-start(bf16[4,64,2,128]{3,2,1,0:T(2,128)(2,1)S(1)} %bitcast.194), channel_id=1, source_target_pairs={{0,7},{1,6},{2,5},{3,4},{4,11},{5,10},{6,9},{7,8},{8,15},{9,14},{1... | collective-permute-start | bytes 393224 | tf_op jit(solution)/shard_map/ppermute | solution.py:406
  229.5 28.1 %collective-permute-start.92 = (bf16[4,64,2,128]{3,2,1,0:T(2,128)(2,1)S(1)}, bf16[4,64,2,128]{3,2,1,0:T(2,128)(2,1)}, u32[]{:S(2)}, u32[]{:S(2)}) collective-permute-start(bf16[4,64,2,128]{3,2,1,0:T(2,128)(2,1)S(1)} %bitcast.193), channel_id=1, source_target_pairs={{0,15},{1,14},{2,13},{3,12},{4,3},{5,2},{6,1},{7,0},{8,7},{9,6},{1... | collective-permute-start | bytes 393224 | tf_op jit(solution)/shard_map/ppermute | solution.py:406
  232.2 25.8 %collective-permute-start.93 = (bf16[4,64,2,128]{3,2,1,0:T(2,128)(2,1)S(1)}, bf16[4,64,2,128]{3,2,1,0:T(2,128)(2,1)}, u32[]{:S(2)}, u32[]{:S(2)}) collective-permute-start(bf16[4,64,2,128]{3,2,1,0:T(2,128)(2,1)S(1)} %bitcast.192), channel_id=1, source_target_pairs={{0,7},{1,6},{2,5},{3,4},{4,3},{5,2},{6,1},{7,0},{8,15},{9,14},{10,... | collective-permute-start | bytes 393224 | tf_op jit(solution)/shard_map/ppermute | solution.py:406
  295.8 25.2 %collective-permute-start.70 = (bf16[4,192,2,128]{3,2,1,0:T(2,128)(2,1)}, bf16[4,192,2,128]{3,2,1,0:T(2,128)(2,1)S(1)}, u32[]{:S(2)}, u32[]{:S(2)}) collective-permute-start(bf16[4,192,2,128]{3,2,1,0:T(2,128)(2,1)} %bitcast.189), channel_id=1, source_target_pairs={{0,1},{1,0},{2,3},{3,2},{4,5},{5,4},{6,7},{7,6},{8,9},{9,8},{10,11... | collective-permute-start | bytes 1179656 | tf_op jit(solution)/shard_map/ppermute | solution.py:406
  297.5 26.5 %collective-permute-start.76 = (bf16[4,192,2,128]{3,2,1,0:T(2,128)(2,1)}, bf16[4,192,2,128]{3,2,1,0:T(2,128)(2,1)S(1)}, u32[]{:S(2)}, u32[]{:S(2)}) collective-permute-start(bf16[4,192,2,128]{3,2,1,0:T(2,128)(2,1)} %bitcast.188), channel_id=1, source_target_pairs={{0,2},{1,3},{2,0},{3,1},{4,6},{5,7},{6,4},{7,5},{8,10},{9,11},{10,... | collective-permute-start | bytes 1179656 | tf_op jit(solution)/shard_map/ppermute | solution.py:406
  302.2 30.2 %collective-permute-start.82 = (bf16[4,192,2,128]{3,2,1,0:T(2,128)(2,1)}, bf16[4,192,2,128]{3,2,1,0:T(2,128)(2,1)S(1)}, u32[]{:S(2)}, u32[]{:S(2)}) collective-permute-start(bf16[4,192,2,128]{3,2,1,0:T(2,128)(2,1)} %bitcast.187), channel_id=1, source_target_pairs={{0,3},{1,2},{2,1},{3,0},{4,7},{5,6},{6,5},{7,4},{8,11},{9,10},{10,... | collective-permute-start | bytes 1179656 | tf_op jit(solution)/shard_map/ppermute | solution.py:406
  (190 other events, 6884.6 us)

commit v14 on v13

--- a/solution.py
+++ b/solution.py
@@ -10,7 +10,7 @@
 HD = 128
 SPAN = 64
 NTOK = 128
-CHUNKS = 2
+CHUNKS = 1
 F32 = jnp.float32
 BF16 = jnp.bfloat16
 ANY = pl.BlockSpec(memory_space=pl.ANY)

time: 341 us -> 367 us (1.076)
  waiting for transfers between devices: 87.6 us -> 162 us
  starting transfers between devices: 181 us -> 141 us
  Pallas kernels: 63.3 us -> 54.3 us
    ppermute x92 -> x46, waiting for transfers between devices: 84.5 us -> 159 us  [swap(): lax.ppermute(block, 'fsdp', [(i, reached(i, devices, move)) for i in rang...]
    ppermute x92 -> x46, starting transfers between devices: 177 us -> 139 us  [swap(): lax.ppermute(block, 'fsdp', [(i, reached(i, devices, move)) for i in rang...]
    pallas_call x2 -> x1, Pallas kernels: 28.7 us -> 25.9 us  [grads(): pl.pallas_call(grads_kernel, grid_spec=pltpu.PrefetchScalarGridSpec(num_s...]
    pallas_call x2 -> x1, Pallas kernels: 13.9 us -> 11.5 us  [row_stats(): pl.pallas_call(stats_kernel, grid_spec=pltpu.PrefetchScalarGridSpec(num_s...]
    pallas_call x2 -> x1, Pallas kernels: 9.48 us -> 7.49 us  [unpack(): pl.pallas_call(kernel, in_specs=[ANY] * (len(order) + len(before)), out_s...]
    pallas_call x2 -> x1, Pallas kernels: 11.3 us -> 9.34 us  [pack(): pl.pallas_call(kernel, in_specs=[ANY] * 3, out_specs=[ANY] * len(order),...]
  transfers between devices with their start and end apart: 94 -> 47, of which waited for: 39 -> 33; matrix products, arithmetic and copies ran while one was open for 0% -> 0% of each run, Pallas kernels for 16% -> 0%
where the time goes in v14:
time: 367 us; the launch traced here: 365 us
  waiting for transfers between devices  162 us (44%)
  starting transfers between devices  141 us (38%)
  Pallas kernels  54.3 us (15%)
  local copies, waits for them, and re-layouts  4.44 us (1%)
    ppermute x46, waiting for transfers between devices, swap(): lax.ppermute(block, 'fsdp', [(i, reached(i, devices, move)) for i in rang...  159 us
    ppermute x46, starting transfers between devices, swap(): lax.ppermute(block, 'fsdp', [(i, reached(i, devices, move)) for i in rang...  139 us
    pallas_call x1, Pallas kernels, grads(): pl.pallas_call(grads_kernel, grid_spec=pltpu.PrefetchScalarGridSpec(num_s...  25.9 us
    pallas_call x1, Pallas kernels, row_stats(): pl.pallas_call(stats_kernel, grid_spec=pltpu.PrefetchScalarGridSpec(num_s...  11.5 us
    pallas_call x1, Pallas kernels, pack(): pl.pallas_call(kernel, in_specs=[ANY] * 3, out_specs=[ANY] * len(order),...  9.34 us
    pallas_call x1, Pallas kernels, unpack(): pl.pallas_call(kernel, in_specs=[ANY] * (len(order) + len(before)), out_s...  7.49 us
  transfers between devices with their start and end apart: 47, of which 33 were waited for; matrix products, arithmetic and copies ran while one was open for 0% of the time, Pallas kernels for 0%

profile of v14, /device:TPU:15, one launch (start us, length us, event | category | flops | bytes accessed | tf_op | source)
XLA Modules:
  0.0 365.1 jit_solution(5781649500281616982)
XLA Ops:
  0.6 9.3 %pack.1 = (bf16[8,192,2,128]{3,2,1,0:T(2,128)(2,1)}, bf16[8,64,2,128]{3,2,1,0:T(2,128)(2,1)}, bf16[8,64,2,128]{3,2,1,0:T(2,128)(2,1)}, bf16[8,64,2,128]{3,2,1,0:...) custom-call(bf16[64,8192]{1,0:T(8,128)(2,1)} %q_ref.1, ...), custom_call_target="tpu_custom_call" | custom-call | bytes 14760000 | tf_op jit(solution)/shard_map/pack/pallas_call | solution.py:132
  18.4 10.4 %collective-permute-start.6 = (bf16[8,64,2,128]{3,2,1,0:T(2,128)(2,1)}, bf16[8,64,2,128]{3,2,1,0:T(2,128)(2,1)S(1)}, u32[]{:S(2)}, u32[]{:S(2)}) collective-permute-start(bf16[8,64,2,128]{3,2,1,0:T(2,128)(2,1)} %get-tuple-element.60), channel_id=1, source_target_pairs={{0,5},{1,4},{2,7},{3,6},{4,13},{5,12},{6,15},{7,14},{8,1},{9,0},{1... | collective-permute-start | bytes 786440 | tf_op jit(solution)/shard_map/ppermute | solution.py:406
  29.6 9.5 %collective-permute-start.8 = (bf16[8,64,2,128]{3,2,1,0:T(2,128)(2,1)}, bf16[8,64,2,128]{3,2,1,0:T(2,128)(2,1)S(1)}, u32[]{:S(2)}, u32[]{:S(2)}) collective-permute-start(bf16[8,64,2,128]{3,2,1,0:T(2,128)(2,1)} %get-tuple-element.62), channel_id=1, source_target_pairs={{0,5},{1,4},{2,7},{3,6},{4,9},{5,8},{6,11},{7,10},{8,13},{9,12},{1... | collective-permute-start | bytes 786440 | tf_op jit(solution)/shard_map/ppermute | solution.py:406
  39.2 6.4 %collective-permute-done.4 = bf16[8,64,2,128]{3,2,1,0:T(2,128)(2,1)S(1)} collective-permute-done((bf16[8,64,2,128]{3,2,1,0:T(2,128)(2,1)}, bf16[8,64,2,128]{3,2,1,0:T(2,128)(2,1)S(1)}, u32[]{:S(2)}, u32[]{:S(2)}) %collective-permute-start.4) | collective-permute-done | bytes 262176 | tf_op jit(solution)/shard_map/ppermute | solution.py:406
  59.2 9.7 %collective-permute-start.14 = (bf16[8,64,2,128]{3,2,1,0:T(2,128)(2,1)}, bf16[8,64,2,128]{3,2,1,0:T(2,128)(2,1)S(1)}, u32[]{:S(2)}, u32[]{:S(2)}) collective-permute-start(bf16[8,64,2,128]{3,2,1,0:T(2,128)(2,1)} %get-tuple-element.68), channel_id=1, source_target_pairs={{0,6},{1,7},{2,4},{3,5},{4,10},{5,11},{6,8},{7,9},{8,14},{9,15},{1... | collective-permute-start | bytes 786440 | tf_op jit(solution)/shard_map/ppermute | solution.py:406
  95.7 6.1 %collective-permute-done.16 = bf16[8,64,2,128]{3,2,1,0:T(2,128)(2,1)S(1)} collective-permute-done((bf16[8,64,2,128]{3,2,1,0:T(2,128)(2,1)}, bf16[8,64,2,128]{3,2,1,0:T(2,128)(2,1)S(1)}, u32[]{:S(2)}, u32[]{:S(2)}) %collective-permute-start.16) | collective-permute-done | bytes 262176 | tf_op jit(solution)/shard_map/ppermute | solution.py:406
  107.1 7.3 %collective-permute-done.19 = bf16[8,64,2,128]{3,2,1,0:T(2,128)(2,1)S(1)} collective-permute-done((bf16[8,64,2,128]{3,2,1,0:T(2,128)(2,1)}, bf16[8,64,2,128]{3,2,1,0:T(2,128)(2,1)S(1)}, u32[]{:S(2)}, u32[]{:S(2)}) %collective-permute-start.19) | collective-permute-done | bytes 262176 | tf_op jit(solution)/shard_map/ppermute | solution.py:406
  124.7 4.9 %collective-permute-done.22 = bf16[8,64,2,128]{3,2,1,0:T(2,128)(2,1)} collective-permute-done((bf16[8,64,2,128]{3,2,1,0:T(2,128)(2,1)}, bf16[8,64,2,128]{3,2,1,0:T(2,128)(2,1)}, u32[]{:S(2)}, u32[]{:S(2)}) %collective-permute-start.22) | collective-permute-done | bytes 262176 | tf_op jit(solution)/shard_map/ppermute | solution.py:406
  129.6 11.9 %collective-permute-done.11 = bf16[8,192,2,128]{3,2,1,0:T(2,128)(2,1)S(1)} collective-permute-done((bf16[8,192,2,128]{3,2,1,0:T(2,128)(2,1)}, bf16[8,192,2,128]{3,2,1,0:T(2,128)(2,1)S(1)}, u32[]{:S(2)}, u32[]{:S(2)}) %collective-permute-start.11) | collective-permute-done | bytes 786464 | tf_op jit(solution)/shard_map/ppermute | solution.py:406
  141.5 18.1 %collective-permute-done.17 = bf16[8,192,2,128]{3,2,1,0:T(2,128)(2,1)S(1)} collective-permute-done((bf16[8,192,2,128]{3,2,1,0:T(2,128)(2,1)}, bf16[8,192,2,128]{3,2,1,0:T(2,128)(2,1)S(1)}, u32[]{:S(2)}, u32[]{:S(2)}) %collective-permute-start.17) | collective-permute-done | bytes 786464 | tf_op jit(solution)/shard_map/ppermute | solution.py:406
  160.4 11.5 %row_stats.1.refs_24_ = f32[8,3,8,128]{3,2,1,0:T(8,128)} custom-call(s32[32]{0:T(128)} %get-tuple-element.52.slots_ref, bf16[8,384,128]{2,1,0:T(8,128)(2,1)} %bitcast.48, bf16[8,128,128]{2,1,0:T(8,128)(2,1)} %bitcast.56, bf16[8,128,128]{2,1,0:T(8,128)(2,1)} %bitcast.58, bf16[8,128,128]{2,1,0:T(8,128)(2,1)} %bitcast.60, bf16[8,128,128]{2,1,0:T(8,128)(2,1)} %bitcast.62, ...), custom_call_target="tpu_custom_call" | custom-call | bytes 22140000 | tf_op jit(solution)/shard_map/row_stats/pallas_call | solution.py:284
  178.0 25.9 %grads.1 = (bf16[8,384,128]{2,1,0:T(8,128)(2,1)}, bf16[8,128,128]{2,1,0:T(8,128)(2,1)}, bf16[8,128,128]{2,1,0:T(8,128)(2,1)}, bf16[8,128,128]{2,1,0:T(8,128)(2,1...) custom-call(s32[32]{0:T(128)} %get-tuple-element.52.slots_ref, ...), custom_call_target="tpu_custom_call" | custom-call | bytes 44280000 | tf_op jit(solution)/shard_map/grads/pallas_call | solution.py:374
  213.4 10.4 %collective-permute-start.30 = (bf16[8,64,2,128]{3,2,1,0:T(2,128)(2,1)}, bf16[8,64,2,128]{3,2,1,0:T(2,128)(2,1)S(1)}, u32[]{:S(2)}, u32[]{:S(2)}) collective-permute-start(bf16[8,64,2,128]{3,2,1,0:T(2,128)(2,1)} %bitcast.108), channel_id=1, source_target_pairs={{0,5},{1,4},{2,7},{3,6},{4,13},{5,12},{6,15},{7,14},{8,1},{9,0},{1... | collective-permute-start | bytes 786440 | tf_op jit(solution)/shard_map/ppermute | solution.py:406
  223.9 5.6 %collective-permute-start.31 = (bf16[8,64,2,128]{3,2,1,0:T(2,128)(2,1)}, bf16[8,64,2,128]{3,2,1,0:T(2,128)(2,1)S(1)}, u32[]{:S(2)}, u32[]{:S(2)}) collective-permute-start(bf16[8,64,2,128]{3,2,1,0:T(2,128)(2,1)} %bitcast.107), channel_id=1, source_target_pairs={{0,9},{1,8},{2,11},{3,10},{4,1},{5,0},{6,3},{7,2},{8,13},{9,12},{1... | collective-permute-start | bytes 786440 | tf_op jit(solution)/shard_map/ppermute | solution.py:406
  234.3 6.6 %collective-permute-done.28.refs_5_ = bf16[8,64,2,128]{3,2,1,0:T(2,128)(2,1)S(1)} collective-permute-done((bf16[8,64,2,128]{3,2,1,0:T(2,128)(2,1)}, bf16[8,64,2,128]{3,2,1,0:T(2,128)(2,1)S(1)}, u32[]{:S(2)}, u32[]{:S(2)}) %collective-permute-start.28) | collective-permute-done | bytes 262176 | tf_op jit(solution)/shard_map/ppermute | solution.py:406
  249.7 8.5 %collective-permute-start.37 = (bf16[8,64,2,128]{3,2,1,0:T(2,128)(2,1)}, bf16[8,64,2,128]{3,2,1,0:T(2,128)(2,1)S(1)}, u32[]{:S(2)}, u32[]{:S(2)}) collective-permute-start(bf16[8,64,2,128]{3,2,1,0:T(2,128)(2,1)} %bitcast.102), channel_id=1, source_target_pairs={{0,10},{1,11},{2,8},{3,9},{4,2},{5,3},{6,0},{7,1},{8,14},{9,15},{1... | collective-permute-start | bytes 786440 | tf_op jit(solution)/shard_map/ppermute | solution.py:406
  258.2 6.1 %collective-permute-start.38 = (bf16[8,64,2,128]{3,2,1,0:T(2,128)(2,1)}, bf16[8,64,2,128]{3,2,1,0:T(2,128)(2,1)S(1)}, u32[]{:S(2)}, u32[]{:S(2)}) collective-permute-start(bf16[8,64,2,128]{3,2,1,0:T(2,128)(2,1)} %bitcast.101), channel_id=1, source_target_pairs={{0,6},{1,7},{2,4},{3,5},{4,10},{5,11},{6,8},{7,9},{8,14},{9,15},{1... | collective-permute-start | bytes 786440 | tf_op jit(solution)/shard_map/ppermute | solution.py:406
  268.9 5.4 %collective-permute-start.40 = (bf16[8,64,2,128]{3,2,1,0:T(2,128)(2,1)}, bf16[8,64,2,128]{3,2,1,0:T(2,128)(2,1)S(1)}, u32[]{:S(2)}, u32[]{:S(2)}) collective-permute-start(bf16[8,64,2,128]{3,2,1,0:T(2,128)(2,1)} %bitcast.99), channel_id=1, source_target_pairs={{0,6},{1,7},{2,4},{3,5},{4,2},{5,3},{6,0},{7,1},{8,14},{9,15},{10,... | collective-permute-start | bytes 786440 | tf_op jit(solution)/shard_map/ppermute | solution.py:406
  286.9 8.4 %collective-permute-start.41 = (bf16[8,192,2,128]{3,2,1,0:T(2,128)(2,1)}, bf16[8,192,2,128]{3,2,1,0:T(2,128)(2,1)S(1)}, u32[]{:S(2)}, u32[]{:S(2)}) collective-permute-start(bf16[8,192,2,128]{3,2,1,0:T(2,128)(2,1)} %bitcast.91), channel_id=1, source_target_pairs={{0,3},{1,2},{2,1},{3,0},{4,7},{5,6},{6,5},{7,4},{8,11},{9,10},{10,... | collective-permute-start | bytes 2359304 | tf_op jit(solution)/shard_map/ppermute | solution.py:406
  310.4 4.9 %collective-permute-done.44.refs_21_ = bf16[8,64,2,128]{3,2,1,0:T(2,128)(2,1)S(1)} collective-permute-done((bf16[8,64,2,128]{3,2,1,0:T(2,128)(2,1)}, bf16[8,64,2,128]{3,2,1,0:T(2,128)(2,1)S(1)}, u32[]{:S(2)}, u32[]{:S(2)}) %collective-permute-start.44) | collective-permute-done | bytes 262176 | tf_op jit(solution)/shard_map/ppermute | solution.py:406
  320.6 5.4 %collective-permute-done.46.refs_23_ = bf16[8,64,2,128]{3,2,1,0:T(2,128)(2,1)S(1)} collective-permute-done((bf16[8,64,2,128]{3,2,1,0:T(2,128)(2,1)}, bf16[8,64,2,128]{3,2,1,0:T(2,128)(2,1)S(1)}, u32[]{:S(2)}, u32[]{:S(2)}) %collective-permute-start.46) | collective-permute-done | bytes 262176 | tf_op jit(solution)/shard_map/ppermute | solution.py:406
  326.0 12.1 %collective-permute-done.35.refs_12_ = bf16[8,192,2,128]{3,2,1,0:T(2,128)(2,1)S(1)} collective-permute-done((bf16[8,192,2,128]{3,2,1,0:T(2,128)(2,1)}, bf16[8,192,2,128]{3,2,1,0:T(2,128)(2,1)S(1)}, u32[]{:S(2)}, u32[]{:S(2)}) %collective-permute-start.35) | collective-permute-done | bytes 786464 | tf_op jit(solution)/shard_map/ppermute | solution.py:406
  338.2 18.4 %collective-permute-done.41.refs_18_ = bf16[8,192,2,128]{3,2,1,0:T(2,128)(2,1)S(1)} collective-permute-done((bf16[8,192,2,128]{3,2,1,0:T(2,128)(2,1)}, bf16[8,192,2,128]{3,2,1,0:T(2,128)(2,1)S(1)}, u32[]{:S(2)}, u32[]{:S(2)}) %collective-permute-start.41) | collective-permute-done | bytes 786464 | tf_op jit(solution)/shard_map/ppermute | solution.py:406
  357.4 7.5 %unpack.1 = (bf16[64,8192]{1,0:T(8,128)(2,1)}, bf16[64,8192]{1,0:T(8,128)(2,1)}, bf16[128,2,8192]{2,1,0:T(2,128)(2,1)}) custom-call(bf16[8,192,2,128]{3,2,1,0:T(2,128)(2,1)} %bitcast.90, bf16[8,64,2,128]{3,2,1,0:T(2,128)(2,1)} %copy-done.23, bf16[8,64,2,128]{3,2,1,0:T(2,128)(2,1)} %copy-done.24, bf16[8,64,2,128]{3,2,1,0:T(2,128)(2,1)} %copy-done.25, ...), custom_call_target="tpu_custom_call" | custom-call | bytes 14760000 | tf_op jit(solution)/shard_map/unpack/pallas_call | solution.py:197
  (166 shorter events, 133.7 us)
Async XLA Ops:
  13.8 31.7 %collective-permute-start.4 = (bf16[8,64,2,128]{3,2,1,0:T(2,128)(2,1)}, bf16[8,64,2,128]{3,2,1,0:T(2,128)(2,1)S(1)}, u32[]{:S(2)}, u32[]{:S(2)}) collective-permute-start(bf16[8,64,2,128]{3,2,1,0:T(2,128)(2,1)} %get-tuple-element.58), channel_id=1, source_target_pairs={{0,4},{1,5},{2,6},{3,7},{4,0},{5,1},{6,2},{7,3},{8,12},{9,13},{10,... | collective-permute-start | bytes 786440 | tf_op jit(solution)/shard_map/ppermute | solution.py:406
  18.4 29.7 %collective-permute-start.6 = (bf16[8,64,2,128]{3,2,1,0:T(2,128)(2,1)}, bf16[8,64,2,128]{3,2,1,0:T(2,128)(2,1)S(1)}, u32[]{:S(2)}, u32[]{:S(2)}) collective-permute-start(bf16[8,64,2,128]{3,2,1,0:T(2,128)(2,1)} %get-tuple-element.60), channel_id=1, source_target_pairs={{0,5},{1,4},{2,7},{3,6},{4,13},{5,12},{6,15},{7,14},{8,1},{9,0},{1... | collective-permute-start | bytes 786440 | tf_op jit(solution)/shard_map/ppermute | solution.py:406
  29.6 29.5 %collective-permute-start.8 = (bf16[8,64,2,128]{3,2,1,0:T(2,128)(2,1)}, bf16[8,64,2,128]{3,2,1,0:T(2,128)(2,1)S(1)}, u32[]{:S(2)}, u32[]{:S(2)}) collective-permute-start(bf16[8,64,2,128]{3,2,1,0:T(2,128)(2,1)} %get-tuple-element.62), channel_id=1, source_target_pairs={{0,5},{1,4},{2,7},{3,6},{4,9},{5,8},{6,11},{7,10},{8,13},{9,12},{1... | collective-permute-start | bytes 786440 | tf_op jit(solution)/shard_map/ppermute | solution.py:406
  39.2 29.7 %collective-permute-start.9 = (bf16[8,64,2,128]{3,2,1,0:T(2,128)(2,1)}, bf16[8,64,2,128]{3,2,1,0:T(2,128)(2,1)S(1)}, u32[]{:S(2)}, u32[]{:S(2)}) collective-permute-start(bf16[8,64,2,128]{3,2,1,0:T(2,128)(2,1)} %get-tuple-element.63), channel_id=1, source_target_pairs={{0,13},{1,12},{2,15},{3,14},{4,1},{5,0},{6,3},{7,2},{8,5},{9,4},{1... | collective-permute-start | bytes 786440 | tf_op jit(solution)/shard_map/ppermute | solution.py:406
  45.5 28.1 %collective-permute-start.10 = (bf16[8,64,2,128]{3,2,1,0:T(2,128)(2,1)}, bf16[8,64,2,128]{3,2,1,0:T(2,128)(2,1)S(1)}, u32[]{:S(2)}, u32[]{:S(2)}) collective-permute-start(bf16[8,64,2,128]{3,2,1,0:T(2,128)(2,1)} %get-tuple-element.64), channel_id=1, source_target_pairs={{0,5},{1,4},{2,7},{3,6},{4,1},{5,0},{6,3},{7,2},{8,13},{9,12},{10,... | collective-permute-start | bytes 786440 | tf_op jit(solution)/shard_map/ppermute | solution.py:406
  59.2 28.2 %collective-permute-start.14 = (bf16[8,64,2,128]{3,2,1,0:T(2,128)(2,1)}, bf16[8,64,2,128]{3,2,1,0:T(2,128)(2,1)S(1)}, u32[]{:S(2)}, u32[]{:S(2)}) collective-permute-start(bf16[8,64,2,128]{3,2,1,0:T(2,128)(2,1)} %get-tuple-element.68), channel_id=1, source_target_pairs={{0,6},{1,7},{2,4},{3,5},{4,10},{5,11},{6,8},{7,9},{8,14},{9,15},{1... | collective-permute-start | bytes 786440 | tf_op jit(solution)/shard_map/ppermute | solution.py:406
  73.6 28.1 %collective-permute-start.16 = (bf16[8,64,2,128]{3,2,1,0:T(2,128)(2,1)}, bf16[8,64,2,128]{3,2,1,0:T(2,128)(2,1)S(1)}, u32[]{:S(2)}, u32[]{:S(2)}) collective-permute-start(bf16[8,64,2,128]{3,2,1,0:T(2,128)(2,1)} %get-tuple-element.70), channel_id=1, source_target_pairs={{0,6},{1,7},{2,4},{3,5},{4,2},{5,3},{6,0},{7,1},{8,14},{9,15},{10,... | collective-permute-start | bytes 786440 | tf_op jit(solution)/shard_map/ppermute | solution.py:406
  75.7 29.6 %collective-permute-start.18 = (bf16[8,64,2,128]{3,2,1,0:T(2,128)(2,1)}, bf16[8,64,2,128]{3,2,1,0:T(2,128)(2,1)S(1)}, u32[]{:S(2)}, u32[]{:S(2)}) collective-permute-start(bf16[8,64,2,128]{3,2,1,0:T(2,128)(2,1)} %get-tuple-element.72), channel_id=1, source_target_pairs={{0,7},{1,6},{2,5},{3,4},{4,15},{5,14},{6,13},{7,12},{8,3},{9,2},{1... | collective-permute-start | bytes 786440 | tf_op jit(solution)/shard_map/ppermute | solution.py:406
  81.8 47.8 %collective-permute-start.5 = (bf16[8,192,2,128]{3,2,1,0:T(2,128)(2,1)}, bf16[8,192,2,128]{3,2,1,0:T(2,128)(2,1)S(1)}, u32[]{:S(2)}, u32[]{:S(2)}) collective-permute-start(bf16[8,192,2,128]{3,2,1,0:T(2,128)(2,1)} %get-tuple-element.59), channel_id=1, source_target_pairs={{0,1},{1,0},{2,3},{3,2},{4,5},{5,4},{6,7},{7,6},{8,9},{9,8},{10,11... | collective-permute-start | bytes 2359304 | tf_op jit(solution)/shard_map/ppermute | solution.py:406
  88.1 53.4 %collective-permute-start.11 = (bf16[8,192,2,128]{3,2,1,0:T(2,128)(2,1)}, bf16[8,192,2,128]{3,2,1,0:T(2,128)(2,1)S(1)}, u32[]{:S(2)}, u32[]{:S(2)}) collective-permute-start(bf16[8,192,2,128]{3,2,1,0:T(2,128)(2,1)} %get-tuple-element.65), channel_id=1, source_target_pairs={{0,2},{1,3},{2,0},{3,1},{4,6},{5,7},{6,4},{7,5},{8,10},{9,11},{10,... | collective-permute-start | bytes 2359304 | tf_op jit(solution)/shard_map/ppermute | solution.py:406
  92.7 66.8 %collective-permute-start.17 = (bf16[8,192,2,128]{3,2,1,0:T(2,128)(2,1)}, bf16[8,192,2,128]{3,2,1,0:T(2,128)(2,1)S(1)}, u32[]{:S(2)}, u32[]{:S(2)}) collective-permute-start(bf16[8,192,2,128]{3,2,1,0:T(2,128)(2,1)} %get-tuple-element.71), channel_id=1, source_target_pairs={{0,3},{1,2},{2,1},{3,0},{4,7},{5,6},{6,5},{7,4},{8,11},{9,10},{10,... | collective-permute-start | bytes 2359304 | tf_op jit(solution)/shard_map/ppermute | solution.py:406
  209.6 31.2 %collective-permute-start.28 = (bf16[8,64,2,128]{3,2,1,0:T(2,128)(2,1)}, bf16[8,64,2,128]{3,2,1,0:T(2,128)(2,1)S(1)}, u32[]{:S(2)}, u32[]{:S(2)}) collective-permute-start(bf16[8,64,2,128]{3,2,1,0:T(2,128)(2,1)} %bitcast.109), channel_id=1, source_target_pairs={{0,4},{1,5},{2,6},{3,7},{4,0},{5,1},{6,2},{7,3},{8,12},{9,13},{10,... | collective-permute-start | bytes 786440 | tf_op jit(solution)/shard_map/ppermute | solution.py:406
  213.4 31.8 %collective-permute-start.30 = (bf16[8,64,2,128]{3,2,1,0:T(2,128)(2,1)}, bf16[8,64,2,128]{3,2,1,0:T(2,128)(2,1)S(1)}, u32[]{:S(2)}, u32[]{:S(2)}) collective-permute-start(bf16[8,64,2,128]{3,2,1,0:T(2,128)(2,1)} %bitcast.108), channel_id=1, source_target_pairs={{0,5},{1,4},{2,7},{3,6},{4,13},{5,12},{6,15},{7,14},{8,1},{9,0},{1... | collective-permute-start | bytes 786440 | tf_op jit(solution)/shard_map/ppermute | solution.py:406
  229.5 28.7 %collective-permute-start.32 = (bf16[8,64,2,128]{3,2,1,0:T(2,128)(2,1)}, bf16[8,64,2,128]{3,2,1,0:T(2,128)(2,1)S(1)}, u32[]{:S(2)}, u32[]{:S(2)}) collective-permute-start(bf16[8,64,2,128]{3,2,1,0:T(2,128)(2,1)} %bitcast.106), channel_id=1, source_target_pairs={{0,5},{1,4},{2,7},{3,6},{4,9},{5,8},{6,11},{7,10},{8,13},{9,12},{1... | collective-permute-start | bytes 786440 | tf_op jit(solution)/shard_map/ppermute | solution.py:406
  231.3 33.1 %collective-permute-start.33 = (bf16[8,64,2,128]{3,2,1,0:T(2,128)(2,1)}, bf16[8,64,2,128]{3,2,1,0:T(2,128)(2,1)S(1)}, u32[]{:S(2)}, u32[]{:S(2)}) collective-permute-start(bf16[8,64,2,128]{3,2,1,0:T(2,128)(2,1)} %bitcast.105), channel_id=1, source_target_pairs={{0,13},{1,12},{2,15},{3,14},{4,1},{5,0},{6,3},{7,2},{8,5},{9,4},{1... | collective-permute-start | bytes 786440 | tf_op jit(solution)/shard_map/ppermute | solution.py:406
  240.8 28.1 %collective-permute-start.34 = (bf16[8,64,2,128]{3,2,1,0:T(2,128)(2,1)}, bf16[8,64,2,128]{3,2,1,0:T(2,128)(2,1)S(1)}, u32[]{:S(2)}, u32[]{:S(2)}) collective-permute-start(bf16[8,64,2,128]{3,2,1,0:T(2,128)(2,1)} %bitcast.104), channel_id=1, source_target_pairs={{0,5},{1,4},{2,7},{3,6},{4,1},{5,0},{6,3},{7,2},{8,13},{9,12},{10,... | collective-permute-start | bytes 786440 | tf_op jit(solution)/shard_map/ppermute | solution.py:406
  245.2 29.1 %collective-permute-start.36 = (bf16[8,64,2,128]{3,2,1,0:T(2,128)(2,1)}, bf16[8,64,2,128]{3,2,1,0:T(2,128)(2,1)S(1)}, u32[]{:S(2)}, u32[]{:S(2)}) collective-permute-start(bf16[8,64,2,128]{3,2,1,0:T(2,128)(2,1)} %bitcast.103), channel_id=1, source_target_pairs={{0,6},{1,7},{2,4},{3,5},{4,14},{5,15},{6,12},{7,13},{8,2},{9,3},{1... | collective-permute-start | bytes 786440 | tf_op jit(solution)/shard_map/ppermute | solution.py:406
  249.7 30.0 %collective-permute-start.37 = (bf16[8,64,2,128]{3,2,1,0:T(2,128)(2,1)}, bf16[8,64,2,128]{3,2,1,0:T(2,128)(2,1)S(1)}, u32[]{:S(2)}, u32[]{:S(2)}) collective-permute-start(bf16[8,64,2,128]{3,2,1,0:T(2,128)(2,1)} %bitcast.102), channel_id=1, source_target_pairs={{0,10},{1,11},{2,8},{3,9},{4,2},{5,3},{6,0},{7,1},{8,14},{9,15},{1... | collective-permute-start | bytes 786440 | tf_op jit(solution)/shard_map/ppermute | solution.py:406
  258.2 27.7 %collective-permute-start.38 = (bf16[8,64,2,128]{3,2,1,0:T(2,128)(2,1)}, bf16[8,64,2,128]{3,2,1,0:T(2,128)(2,1)S(1)}, u32[]{:S(2)}, u32[]{:S(2)}) collective-permute-start(bf16[8,64,2,128]{3,2,1,0:T(2,128)(2,1)} %bitcast.101), channel_id=1, source_target_pairs={{0,6},{1,7},{2,4},{3,5},{4,10},{5,11},{6,8},{7,9},{8,14},{9,15},{1... | collective-permute-start | bytes 786440 | tf_op jit(solution)/shard_map/ppermute | solution.py:406
  268.9 28.3 %collective-permute-start.40 = (bf16[8,64,2,128]{3,2,1,0:T(2,128)(2,1)}, bf16[8,64,2,128]{3,2,1,0:T(2,128)(2,1)S(1)}, u32[]{:S(2)}, u32[]{:S(2)}) collective-permute-start(bf16[8,64,2,128]{3,2,1,0:T(2,128)(2,1)} %bitcast.99), channel_id=1, source_target_pairs={{0,6},{1,7},{2,4},{3,5},{4,2},{5,3},{6,0},{7,1},{8,14},{9,15},{10,... | collective-permute-start | bytes 786440 | tf_op jit(solution)/shard_map/ppermute | solution.py:406
  274.3 29.7 %collective-permute-start.42 = (bf16[8,64,2,128]{3,2,1,0:T(2,128)(2,1)}, bf16[8,64,2,128]{3,2,1,0:T(2,128)(2,1)S(1)}, u32[]{:S(2)}, u32[]{:S(2)}) collective-permute-start(bf16[8,64,2,128]{3,2,1,0:T(2,128)(2,1)} %bitcast.98), channel_id=1, source_target_pairs={{0,7},{1,6},{2,5},{3,4},{4,15},{5,14},{6,13},{7,12},{8,3},{9,2},{1... | collective-permute-start | bytes 786440 | tf_op jit(solution)/shard_map/ppermute | solution.py:406
  279.7 46.3 %collective-permute-start.29 = (bf16[8,192,2,128]{3,2,1,0:T(2,128)(2,1)}, bf16[8,192,2,128]{3,2,1,0:T(2,128)(2,1)S(1)}, u32[]{:S(2)}, u32[]{:S(2)}) collective-permute-start(bf16[8,192,2,128]{3,2,1,0:T(2,128)(2,1)} %bitcast.93), channel_id=1, source_target_pairs={{0,1},{1,0},{2,3},{3,2},{4,5},{5,4},{6,7},{7,6},{8,9},{9,8},{10,11... | collective-permute-start | bytes 2359304 | tf_op jit(solution)/shard_map/ppermute | solution.py:406
  285.9 52.2 %collective-permute-start.35 = (bf16[8,192,2,128]{3,2,1,0:T(2,128)(2,1)}, bf16[8,192,2,128]{3,2,1,0:T(2,128)(2,1)S(1)}, u32[]{:S(2)}, u32[]{:S(2)}) collective-permute-start(bf16[8,192,2,128]{3,2,1,0:T(2,128)(2,1)} %bitcast.92), channel_id=1, source_target_pairs={{0,2},{1,3},{2,0},{3,1},{4,6},{5,7},{6,4},{7,5},{8,10},{9,11},{10,... | collective-permute-start | bytes 2359304 | tf_op jit(solution)/shard_map/ppermute | solution.py:406
  286.9 69.7 %collective-permute-start.41 = (bf16[8,192,2,128]{3,2,1,0:T(2,128)(2,1)}, bf16[8,192,2,128]{3,2,1,0:T(2,128)(2,1)S(1)}, u32[]{:S(2)}, u32[]{:S(2)}) collective-permute-start(bf16[8,192,2,128]{3,2,1,0:T(2,128)(2,1)} %bitcast.91), channel_id=1, source_target_pairs={{0,3},{1,2},{2,1},{3,0},{4,7},{5,6},{6,5},{7,4},{8,11},{9,10},{10,... | collective-permute-start | bytes 2359304 | tf_op jit(solution)/shard_map/ppermute | solution.py:406
  (68 other events, 3150.8 us)

commit v15 on v13

--- a/solution.py
+++ b/solution.py
@@ -38,7 +38,8 @@
 
 def moves(devices):
     quarter = devices // 4
-    return [(kind, offset) for offset in range(quarter) for kind in range(6)]
+    inner = [(0, 0)] + [(0, offset) for offset in range(quarter - 1, 0, -1)]
+    return inner + [(kind, offset) for offset in range(quarter) for kind in range(1, 6)]
 
 
 def reached(index, devices, move):

time: 341 us -> 346 us (1.015)
  waiting for transfers between devices: 87.6 us -> 97.8 us
    ppermute x92, waiting for transfers between devices: 84.5 us -> 92.1 us  [swap(): lax.ppermute(block, 'fsdp', [(i, reached(i, devices, move)) for i in rang...]
  transfers between devices with their start and end apart: 94 -> 94, of which waited for: 39 -> 38; matrix products, arithmetic and copies ran while one was open for 0% -> 0% of each run, Pallas kernels for 16% -> 15%
where the time goes in v15:
time: 346 us
  starting transfers between devices  179 us (52%)
  waiting for transfers between devices  97.8 us (28%)
  Pallas kernels  63.3 us (18%)
    ppermute x92, starting transfers between devices, swap(): lax.ppermute(block, 'fsdp', [(i, reached(i, devices, move)) for i in rang...  174 us
    ppermute x92, waiting for transfers between devices, swap(): lax.ppermute(block, 'fsdp', [(i, reached(i, devices, move)) for i in rang...  92.1 us
    pallas_call x2, Pallas kernels, grads(): pl.pallas_call(grads_kernel, grid_spec=pltpu.PrefetchScalarGridSpec(num_s...  28.8 us
    pallas_call x2, Pallas kernels, row_stats(): pl.pallas_call(stats_kernel, grid_spec=pltpu.PrefetchScalarGridSpec(num_s...  13.8 us
    pallas_call x2, Pallas kernels, pack(): pl.pallas_call(kernel, in_specs=[ANY] * 3, out_specs=[ANY] * len(order),...  11.3 us
    pallas_call x2, Pallas kernels, unpack(): pl.pallas_call(kernel, in_specs=[ANY] * (len(order) + len(before)), out_s...  9.43 us
  transfers between devices with their start and end apart: 94, of which 38 were waited for; matrix products, arithmetic and copies ran while one was open for 0% of the time, Pallas kernels for 15%

profile of v15, /device:TPU:15, one launch (start us, length us, event | category | flops | bytes accessed | tf_op | source)
XLA Modules:
  0.0 345.6 jit_solution(15780029769920795941)
XLA Ops:
  0.6 5.7 %pack.3 = (bf16[4,192,2,128]{3,2,1,0:T(2,128)(2,1)}, bf16[4,192,2,128]{3,2,1,0:T(2,128)(2,1)}, bf16[4,192,2,128]{3,2,1,0:T(2,128)(2,1)}, bf16[4,192,2,128]{3,2,1...) custom-call(bf16[64,8192]{1,0:T(8,128)(2,1)} %q_ref.3, ...), custom_call_target="tpu_custom_call" | custom-call | bytes 14760000 | tf_op jit(solution)/shard_map/pack/pallas_call | solution.py:133
  12.4 7.2 %collective-permute-start.8 = (bf16[4,64,2,128]{3,2,1,0:T(2,128)(2,1)}, bf16[4,64,2,128]{3,2,1,0:T(2,128)(2,1)S(1)}, u32[]{:S(2)}, u32[]{:S(2)}) collective-permute-start(bf16[4,64,2,128]{3,2,1,0:T(2,128)(2,1)} %get-tuple-element.263), channel_id=1, source_target_pairs={{0,5},{1,4},{2,7},{3,6},{4,13},{5,12},{6,15},{7,14},{8,1},{9,0},{1... | collective-permute-start | bytes 393224 | tf_op jit(solution)/shard_map/ppermute | solution.py:407
  51.9 7.3 %collective-permute-start.18 = (bf16[4,64,2,128]{3,2,1,0:T(2,128)(2,1)}, bf16[4,64,2,128]{3,2,1,0:T(2,128)(2,1)S(1)}, u32[]{:S(2)}, u32[]{:S(2)}) collective-permute-start(bf16[4,64,2,128]{3,2,1,0:T(2,128)(2,1)} %get-tuple-element.291), channel_id=1, source_target_pairs={{0,7},{1,6},{2,5},{3,4},{4,15},{5,14},{6,13},{7,12},{8,3},{9,2},{1... | collective-permute-start | bytes 393224 | tf_op jit(solution)/shard_map/ppermute | solution.py:407
  62.0 9.3 %collective-permute-done.1 = bf16[4,192,2,128]{3,2,1,0:T(2,128)(2,1)S(1)} collective-permute-done((bf16[4,192,2,128]{3,2,1,0:T(2,128)(2,1)}, bf16[4,192,2,128]{3,2,1,0:T(2,128)(2,1)S(1)}, u32[]{:S(2)}, u32[]{:S(2)}) %collective-permute-start.1) | collective-permute-done | bytes 393248 | tf_op jit(solution)/shard_map/ppermute | solution.py:407
  74.4 5.6 %pack.2 = (bf16[4,192,2,128]{3,2,1,0:T(2,128)(2,1)}, bf16[4,192,2,128]{3,2,1,0:T(2,128)(2,1)}, bf16[4,192,2,128]{3,2,1,0:T(2,128)(2,1)}, bf16[4,192,2,128]{3,2,1...) custom-call(bf16[64,8192]{1,0:T(8,128)(2,1)} %q_ref.3, ...), custom_call_target="tpu_custom_call" | custom-call | bytes 14760000 | tf_op jit(solution)/shard_map/pack/pallas_call | solution.py:133
  85.6 6.8 %row_stats.2.refs_24_ = f32[4,3,8,128]{3,2,1,0:T(8,128)} custom-call(s32[32]{0:T(128)} %get-tuple-element.229.slots_ref, bf16[4,384,128]{2,1,0:T(8,128)(2,1)} %bitcast.98, bf16[4,384,128]{2,1,0:T(8,128)(2,1)} %bitcast.104, bf16[4,384,128]{2,1,0:T(8,128)(2,1)} %bitcast.108, bf16[4,384,128]{2,1,0:T(8,128)(2,1)} %bitcast.110, bf16[4,128,128]{2,1,0:T(8,128)(2,1)} %bitcast.120, ...), custom_call_target="tpu_custom_call" | custom-call | bytes 22140000 | tf_op jit(solution)/shard_map/row_stats/pallas_call | solution.py:285
  105.0 6.2 %collective-permute-start.36 = (bf16[4,64,2,128]{3,2,1,0:T(2,128)(2,1)S(1)}, bf16[4,64,2,128]{3,2,1,0:T(2,128)(2,1)S(1)}, u32[]{:S(2)}, u32[]{:S(2)}) collective-permute-start(bf16[4,64,2,128]{3,2,1,0:T(2,128)(2,1)S(1)} %copy-done.112), channel_id=1, source_target_pairs={{0,5},{1,4},{2,7},{3,6},{4,1},{5,0},{6,3},{7,2},{8,13},{9,12},{10,... | collective-permute-start | bytes 393224 | tf_op jit(solution)/shard_map/ppermute | solution.py:407
  132.7 6.9 %collective-permute-start.42 = (bf16[4,64,2,128]{3,2,1,0:T(2,128)(2,1)}, bf16[4,64,2,128]{3,2,1,0:T(2,128)(2,1)S(1)}, u32[]{:S(2)}, u32[]{:S(2)}) collective-permute-start(bf16[4,64,2,128]{3,2,1,0:T(2,128)(2,1)} %get-tuple-element.357), channel_id=1, source_target_pairs={{0,7},{1,6},{2,5},{3,4},{4,15},{5,14},{6,13},{7,12},{8,3},{9,2},{1... | collective-permute-start | bytes 393224 | tf_op jit(solution)/shard_map/ppermute | solution.py:407
  142.4 13.1 %collective-permute-done.25 = bf16[4,192,2,128]{3,2,1,0:T(2,128)(2,1)S(1)} collective-permute-done((bf16[4,192,2,128]{3,2,1,0:T(2,128)(2,1)S(1)}, bf16[4,192,2,128]{3,2,1,0:T(2,128)(2,1)S(1)}, u32[]{:S(2)}, u32[]{:S(2)}) %collective-permute-start.25) | collective-permute-done | bytes 393248 | tf_op jit(solution)/shard_map/ppermute | solution.py:407
  157.3 14.3 %grads.2 = (bf16[4,384,128]{2,1,0:T(8,128)(2,1)}, bf16[4,384,128]{2,1,0:T(8,128)(2,1)}, bf16[4,384,128]{2,1,0:T(8,128)(2,1)}, bf16[4,384,128]{2,1,0:T(8,128)(2,1...) custom-call(s32[32]{0:T(128)} %get-tuple-element.229.slots_ref, ...), custom_call_target="tpu_custom_call" | custom-call | bytes 44280000 | tf_op jit(solution)/shard_map/grads/pallas_call | solution.py:375
  175.2 7.0 %row_stats.3.refs_24_ = f32[4,3,8,128]{3,2,1,0:T(8,128)} custom-call(s32[32]{0:T(128)} %get-tuple-element.229.slots_ref, bf16[4,384,128]{2,1,0:T(8,128)(2,1)} %bitcast.96, bf16[4,384,128]{2,1,0:T(8,128)(2,1)} %bitcast.100, bf16[4,384,128]{2,1,0:T(8,128)(2,1)} %bitcast.102, bf16[4,384,128]{2,1,0:T(8,128)(2,1)} %bitcast.106, bf16[4,128,128]{2,1,0:T(8,128)(2,1)} %bitcast.112, ...), custom_call_target="tpu_custom_call" | custom-call | bytes 22140000 | tf_op jit(solution)/shard_map/row_stats/pallas_call | solution.py:285
  189.1 5.2 %collective-permute-start.56 = (bf16[4,64,2,128]{3,2,1,0:T(2,128)(2,1)S(1)}, bf16[4,64,2,128]{3,2,1,0:T(2,128)(2,1)S(1)}, u32[]{:S(2)}, u32[]{:S(2)}) collective-permute-start(bf16[4,64,2,128]{3,2,1,0:T(2,128)(2,1)S(1)} %bitcast.221), channel_id=1, source_target_pairs={{0,5},{1,4},{2,7},{3,6},{4,13},{5,12},{6,15},{7,14},{8,1},{9,0},{1... | collective-permute-start | bytes 393224 | tf_op jit(solution)/shard_map/ppermute | solution.py:407
  207.3 5.3 %collective-permute-start.61 = (bf16[4,64,2,128]{3,2,1,0:T(2,128)(2,1)S(1)}, bf16[4,64,2,128]{3,2,1,0:T(2,128)(2,1)S(1)}, u32[]{:S(2)}, u32[]{:S(2)}) collective-permute-start(bf16[4,64,2,128]{3,2,1,0:T(2,128)(2,1)S(1)} %bitcast.211), channel_id=1, source_target_pairs={{0,6},{1,7},{2,4},{3,5},{4,14},{5,15},{6,12},{7,13},{8,2},{9,3},{1... | collective-permute-start | bytes 393224 | tf_op jit(solution)/shard_map/ppermute | solution.py:407
  212.7 5.0 %collective-permute-done.61.refs_14_ = bf16[4,64,2,128]{3,2,1,0:T(2,128)(2,1)S(1)} collective-permute-done((bf16[4,64,2,128]{3,2,1,0:T(2,128)(2,1)S(1)}, bf16[4,64,2,128]{3,2,1,0:T(2,128)(2,1)S(1)}, u32[]{:S(2)}, u32[]{:S(2)}) %collective-permute-start.61) | collective-permute-done | bytes 131104 | tf_op jit(solution)/shard_map/ppermute | solution.py:407
  227.8 4.7 %collective-permute-start.89 = (bf16[4,64,2,128]{3,2,1,0:T(2,128)(2,1)S(1)}, bf16[4,64,2,128]{3,2,1,0:T(2,128)(2,1)S(1)}, u32[]{:S(2)}, u32[]{:S(2)}) collective-permute-start(bf16[4,64,2,128]{3,2,1,0:T(2,128)(2,1)S(1)} %bitcast.196), channel_id=1, source_target_pairs={{0,7},{1,6},{2,5},{3,4},{4,15},{5,14},{6,13},{7,12},{8,3},{9,2},{1... | collective-permute-start | bytes 393224 | tf_op jit(solution)/shard_map/ppermute | solution.py:407
  236.4 6.5 %collective-permute-start.91 = (bf16[4,64,2,128]{3,2,1,0:T(2,128)(2,1)S(1)}, bf16[4,64,2,128]{3,2,1,0:T(2,128)(2,1)S(1)}, u32[]{:S(2)}, u32[]{:S(2)}) collective-permute-start(bf16[4,64,2,128]{3,2,1,0:T(2,128)(2,1)S(1)} %bitcast.194), channel_id=1, source_target_pairs={{0,7},{1,6},{2,5},{3,4},{4,11},{5,10},{6,9},{7,8},{8,15},{9,14},{1... | collective-permute-start | bytes 393224 | tf_op jit(solution)/shard_map/ppermute | solution.py:407
  243.0 14.4 %grads.3 = (bf16[4,384,128]{2,1,0:T(8,128)(2,1)}, bf16[4,384,128]{2,1,0:T(8,128)(2,1)}, bf16[4,384,128]{2,1,0:T(8,128)(2,1)}, bf16[4,384,128]{2,1,0:T(8,128)(2,1...) custom-call(s32[32]{0:T(128)} %get-tuple-element.229.slots_ref, ...), custom_call_target="tpu_custom_call" | custom-call | bytes 44280000 | tf_op jit(solution)/shard_map/grads/pallas_call | solution.py:375
  263.9 5.0 %collective-permute-start.72 = (bf16[4,64,2,128]{3,2,1,0:T(2,128)(2,1)}, bf16[4,64,2,128]{3,2,1,0:T(2,128)(2,1)S(1)}, u32[]{:S(2)}, u32[]{:S(2)}) collective-permute-start(bf16[4,64,2,128]{3,2,1,0:T(2,128)(2,1)} %bitcast.222), channel_id=1, source_target_pairs={{0,4},{1,5},{2,6},{3,7},{4,0},{5,1},{6,2},{7,3},{8,12},{9,13},{10,... | collective-permute-start | bytes 393224 | tf_op jit(solution)/shard_map/ppermute | solution.py:407
  271.6 7.5 %collective-permute-start.75 = (bf16[4,64,2,128]{3,2,1,0:T(2,128)(2,1)}, bf16[4,64,2,128]{3,2,1,0:T(2,128)(2,1)S(1)}, u32[]{:S(2)}, u32[]{:S(2)}) collective-permute-start(bf16[4,64,2,128]{3,2,1,0:T(2,128)(2,1)} %bitcast.216), channel_id=1, source_target_pairs={{0,5},{1,4},{2,7},{3,6},{4,9},{5,8},{6,11},{7,10},{8,13},{9,12},{1... | collective-permute-start | bytes 393224 | tf_op jit(solution)/shard_map/ppermute | solution.py:407
  287.0 5.6 %collective-permute-start.80 = (bf16[4,64,2,128]{3,2,1,0:T(2,128)(2,1)}, bf16[4,64,2,128]{3,2,1,0:T(2,128)(2,1)S(1)}, u32[]{:S(2)}, u32[]{:S(2)}) collective-permute-start(bf16[4,64,2,128]{3,2,1,0:T(2,128)(2,1)} %bitcast.206), channel_id=1, source_target_pairs={{0,6},{1,7},{2,4},{3,5},{4,10},{5,11},{6,8},{7,9},{8,14},{9,15},{1... | collective-permute-start | bytes 393224 | tf_op jit(solution)/shard_map/ppermute | solution.py:407
  312.9 4.6 %collective-permute-done.84.refs_20_ = bf16[4,64,2,128]{3,2,1,0:T(2,128)(2,1)S(1)} collective-permute-done((bf16[4,64,2,128]{3,2,1,0:T(2,128)(2,1)}, bf16[4,64,2,128]{3,2,1,0:T(2,128)(2,1)S(1)}, u32[]{:S(2)}, u32[]{:S(2)}) %collective-permute-start.84) | collective-permute-done | bytes 131104 | tf_op jit(solution)/shard_map/ppermute | solution.py:407
  322.0 4.8 %unpack.2 = (bf16[64,8192]{1,0:T(8,128)(2,1)}, bf16[64,8192]{1,0:T(8,128)(2,1)}, bf16[128,2,8192]{2,1,0:T(2,128)(2,1)}) custom-call(bf16[4,192,2,128]{3,2,1,0:T(2,128)(2,1)} %bitcast.185, bf16[4,192,2,128]{3,2,1,0:T(2,128)(2,1)} %copy-done.45, bf16[4,192,2,128]{3,2,1,0:T(2,128)(2,1)} %copy-done.46, bf16[4,192,2,128]{3,2,1,0:T(2,128)(2,1)} %copy-done.47, ...), custom_call_target="tpu_custom_call" | custom-call | bytes 14760000 | tf_op jit(solution)/shard_map/unpack/pallas_call | solution.py:198
  331.4 8.4 %collective-permute-done.66.refs_2_ = bf16[4,192,2,128]{3,2,1,0:T(2,128)(2,1)S(1)} collective-permute-done((bf16[4,192,2,128]{3,2,1,0:T(2,128)(2,1)}, bf16[4,192,2,128]{3,2,1,0:T(2,128)(2,1)S(1)}, u32[]{:S(2)}, u32[]{:S(2)}) %collective-permute-start.66) | collective-permute-done | bytes 393248 | tf_op jit(solution)/shard_map/ppermute | solution.py:407
  340.7 4.7 %unpack.3 = (bf16[64,8192]{1,0:T(8,128)(2,1)}, bf16[64,8192]{1,0:T(8,128)(2,1)}, bf16[128,2,8192]{2,1,0:T(2,128)(2,1)}) custom-call(bf16[4,192,2,128]{3,2,1,0:T(2,128)(2,1)} %bitcast.184, bf16[4,192,2,128]{3,2,1,0:T(2,128)(2,1)} %copy-done.42, bf16[4,192,2,128]{3,2,1,0:T(2,128)(2,1)} %copy-done.43, ...), custom_call_target="tpu_custom_call", output_to_operand_aliasing={{0}: (24, {}), {1}: (25, {}), {2}: (26, {})} | custom-call | bytes 14760000 | tf_op jit(solution)/shard_map/unpack/pallas_call | solution.py:198
  (420 shorter events, 172.2 us)
Async XLA Ops:
  30.7 28.5 %collective-permute-start = (bf16[4,192,2,128]{3,2,1,0:T(2,128)(2,1)}, bf16[4,192,2,128]{3,2,1,0:T(2,128)(2,1)S(1)}, u32[]{:S(2)}, u32[]{:S(2)}) collective-permute-start(bf16[4,192,2,128]{3,2,1,0:T(2,128)(2,1)} %get-tuple-element.255), channel_id=1, source_target_pairs={{0,3},{1,2},{2,1},{3,0},{4,7},{5,6},{6,5},{7,4},{8,11},{9,10},{10,... | collective-permute-start | bytes 1179656 | tf_op jit(solution)/shard_map/ppermute | solution.py:407
  32.9 38.4 %collective-permute-start.1 = (bf16[4,192,2,128]{3,2,1,0:T(2,128)(2,1)}, bf16[4,192,2,128]{3,2,1,0:T(2,128)(2,1)S(1)}, u32[]{:S(2)}, u32[]{:S(2)}) collective-permute-start(bf16[4,192,2,128]{3,2,1,0:T(2,128)(2,1)} %get-tuple-element.256), channel_id=1, source_target_pairs={{0,2},{1,3},{2,0},{3,1},{4,6},{5,7},{6,4},{7,5},{8,10},{9,11},{10,... | collective-permute-start | bytes 1179656 | tf_op jit(solution)/shard_map/ppermute | solution.py:407
  34.1 38.6 %collective-permute-start.2 = (bf16[4,192,2,128]{3,2,1,0:T(2,128)(2,1)}, bf16[4,192,2,128]{3,2,1,0:T(2,128)(2,1)S(1)}, u32[]{:S(2)}, u32[]{:S(2)}) collective-permute-start(bf16[4,192,2,128]{3,2,1,0:T(2,128)(2,1)} %get-tuple-element.257), channel_id=1, source_target_pairs={{0,1},{1,0},{2,3},{3,2},{4,5},{5,4},{6,7},{7,6},{8,9},{9,8},{10,11... | collective-permute-start | bytes 1179656 | tf_op jit(solution)/shard_map/ppermute | solution.py:407
  51.9 28.2 %collective-permute-start.18 = (bf16[4,64,2,128]{3,2,1,0:T(2,128)(2,1)}, bf16[4,64,2,128]{3,2,1,0:T(2,128)(2,1)S(1)}, u32[]{:S(2)}, u32[]{:S(2)}) collective-permute-start(bf16[4,64,2,128]{3,2,1,0:T(2,128)(2,1)} %get-tuple-element.291), channel_id=1, source_target_pairs={{0,7},{1,6},{2,5},{3,4},{4,15},{5,14},{6,13},{7,12},{8,3},{9,2},{1... | collective-permute-start | bytes 393224 | tf_op jit(solution)/shard_map/ppermute | solution.py:407
  59.1 21.7 %collective-permute-start.19 = (bf16[4,64,2,128]{3,2,1,0:T(2,128)(2,1)}, bf16[4,64,2,128]{3,2,1,0:T(2,128)(2,1)}, u32[]{:S(2)}, u32[]{:S(2)}) collective-permute-start(bf16[4,64,2,128]{3,2,1,0:T(2,128)(2,1)} %get-tuple-element.292), channel_id=1, source_target_pairs={{0,11},{1,10},{2,9},{3,8},{4,3},{5,2},{6,1},{7,0},{8,15},{9,14},{1... | collective-permute-start | bytes 393224 | tf_op jit(solution)/shard_map/ppermute | solution.py:407
  59.2 24.2 %collective-permute-start.20 = (bf16[4,64,2,128]{3,2,1,0:T(2,128)(2,1)}, bf16[4,64,2,128]{3,2,1,0:T(2,128)(2,1)}, u32[]{:S(2)}, u32[]{:S(2)}) collective-permute-start(bf16[4,64,2,128]{3,2,1,0:T(2,128)(2,1)} %get-tuple-element.293), channel_id=1, source_target_pairs={{0,7},{1,6},{2,5},{3,4},{4,11},{5,10},{6,9},{7,8},{8,15},{9,14},{1... | collective-permute-start | bytes 393224 | tf_op jit(solution)/shard_map/ppermute | solution.py:407
  80.9 21.3 %collective-permute-start.28 = (bf16[4,64,2,128]{3,2,1,0:T(2,128)(2,1)}, bf16[4,64,2,128]{3,2,1,0:T(2,128)(2,1)S(1)}, u32[]{:S(2)}, u32[]{:S(2)}) collective-permute-start(bf16[4,64,2,128]{3,2,1,0:T(2,128)(2,1)} %get-tuple-element.325), channel_id=1, source_target_pairs={{0,8},{1,9},{2,10},{3,11},{4,0},{5,1},{6,2},{7,3},{8,12},{9,13},{1... | collective-permute-start | bytes 393224 | tf_op jit(solution)/shard_map/ppermute | solution.py:407
  111.3 28.3 %collective-permute-start.24 = (bf16[4,192,2,128]{3,2,1,0:T(2,128)(2,1)S(1)}, bf16[4,192,2,128]{3,2,1,0:T(2,128)(2,1)S(1)}, u32[]{:S(2)}, u32[]{:S(2)}) collective-permute-start(bf16[4,192,2,128]{3,2,1,0:T(2,128)(2,1)S(1)} %copy-done.93), channel_id=1, source_target_pairs={{0,3},{1,2},{2,1},{3,0},{4,7},{5,6},{6,5},{7,4},{8,11},{9,10},{10,... | collective-permute-start | bytes 1179656 | tf_op jit(solution)/shard_map/ppermute | solution.py:407
  114.9 40.6 %collective-permute-start.25 = (bf16[4,192,2,128]{3,2,1,0:T(2,128)(2,1)S(1)}, bf16[4,192,2,128]{3,2,1,0:T(2,128)(2,1)S(1)}, u32[]{:S(2)}, u32[]{:S(2)}) collective-permute-start(bf16[4,192,2,128]{3,2,1,0:T(2,128)(2,1)S(1)} %copy-done.92), channel_id=1, source_target_pairs={{0,2},{1,3},{2,0},{3,1},{4,6},{5,7},{6,4},{7,5},{8,10},{9,11},{10,... | collective-permute-start | bytes 1179656 | tf_op jit(solution)/shard_map/ppermute | solution.py:407
  116.2 41.1 %collective-permute-start.26 = (bf16[4,192,2,128]{3,2,1,0:T(2,128)(2,1)S(1)}, bf16[4,192,2,128]{3,2,1,0:T(2,128)(2,1)S(1)}, u32[]{:S(2)}, u32[]{:S(2)}) collective-permute-start(bf16[4,192,2,128]{3,2,1,0:T(2,128)(2,1)S(1)} %copy-done.90), channel_id=1, source_target_pairs={{0,1},{1,0},{2,3},{3,2},{4,5},{5,4},{6,7},{7,6},{8,9},{9,8},{10,11... | collective-permute-start | bytes 1179656 | tf_op jit(solution)/shard_map/ppermute | solution.py:407
  132.7 39.2 %collective-permute-start.42 = (bf16[4,64,2,128]{3,2,1,0:T(2,128)(2,1)}, bf16[4,64,2,128]{3,2,1,0:T(2,128)(2,1)S(1)}, u32[]{:S(2)}, u32[]{:S(2)}) collective-permute-start(bf16[4,64,2,128]{3,2,1,0:T(2,128)(2,1)} %get-tuple-element.357), channel_id=1, source_target_pairs={{0,7},{1,6},{2,5},{3,4},{4,15},{5,14},{6,13},{7,12},{8,3},{9,2},{1... | collective-permute-start | bytes 393224 | tf_op jit(solution)/shard_map/ppermute | solution.py:407
  139.6 34.3 %collective-permute-start.43 = (bf16[4,64,2,128]{3,2,1,0:T(2,128)(2,1)}, bf16[4,64,2,128]{3,2,1,0:T(2,128)(2,1)S(1)}, u32[]{:S(2)}, u32[]{:S(2)}) collective-permute-start(bf16[4,64,2,128]{3,2,1,0:T(2,128)(2,1)} %get-tuple-element.358), channel_id=1, source_target_pairs={{0,11},{1,10},{2,9},{3,8},{4,3},{5,2},{6,1},{7,0},{8,15},{9,14},{1... | collective-permute-start | bytes 393224 | tf_op jit(solution)/shard_map/ppermute | solution.py:407
  139.6 34.3 %collective-permute-start.44 = (bf16[4,64,2,128]{3,2,1,0:T(2,128)(2,1)}, bf16[4,64,2,128]{3,2,1,0:T(2,128)(2,1)S(1)}, u32[]{:S(2)}, u32[]{:S(2)}) collective-permute-start(bf16[4,64,2,128]{3,2,1,0:T(2,128)(2,1)} %get-tuple-element.359), channel_id=1, source_target_pairs={{0,7},{1,6},{2,5},{3,4},{4,11},{5,10},{6,9},{7,8},{8,15},{9,14},{1... | collective-permute-start | bytes 393224 | tf_op jit(solution)/shard_map/ppermute | solution.py:407
  173.9 20.5 %collective-permute-start.53 = (bf16[4,64,2,128]{3,2,1,0:T(2,128)(2,1)}, bf16[4,64,2,128]{3,2,1,0:T(2,128)(2,1)S(1)}, u32[]{:S(2)}, u32[]{:S(2)}) collective-permute-start(bf16[4,64,2,128]{3,2,1,0:T(2,128)(2,1)} %bitcast.227), channel_id=1, source_target_pairs={{0,4},{1,5},{2,6},{3,7},{4,8},{5,9},{6,10},{7,11},{8,12},{9,13},{1... | collective-permute-start | bytes 393224 | tf_op jit(solution)/shard_map/ppermute | solution.py:407
  199.5 33.1 %collective-permute-start.48 = (bf16[4,192,2,128]{3,2,1,0:T(2,128)(2,1)S(1)}, bf16[4,192,2,128]{3,2,1,0:T(2,128)(2,1)S(1)}, u32[]{:S(2)}, u32[]{:S(2)}) collective-permute-start(bf16[4,192,2,128]{3,2,1,0:T(2,128)(2,1)S(1)} %bitcast.191), channel_id=1, source_target_pairs={{0,3},{1,2},{2,1},{3,0},{4,7},{5,6},{6,5},{7,4},{8,11},{9,10},{10,... | collective-permute-start | bytes 1179656 | tf_op jit(solution)/shard_map/ppermute | solution.py:407
  203.5 32.9 %collective-permute-start.49 = (bf16[4,192,2,128]{3,2,1,0:T(2,128)(2,1)S(1)}, bf16[4,192,2,128]{3,2,1,0:T(2,128)(2,1)S(1)}, u32[]{:S(2)}, u32[]{:S(2)}) collective-permute-start(bf16[4,192,2,128]{3,2,1,0:T(2,128)(2,1)S(1)} %bitcast.190), channel_id=1, source_target_pairs={{0,2},{1,3},{2,0},{3,1},{4,6},{5,7},{6,4},{7,5},{8,10},{9,11},{10,... | collective-permute-start | bytes 1179656 | tf_op jit(solution)/shard_map/ppermute | solution.py:407
  204.7 38.2 %collective-permute-start.50 = (bf16[4,192,2,128]{3,2,1,0:T(2,128)(2,1)S(1)}, bf16[4,192,2,128]{3,2,1,0:T(2,128)(2,1)S(1)}, u32[]{:S(2)}, u32[]{:S(2)}) collective-permute-start(bf16[4,192,2,128]{3,2,1,0:T(2,128)(2,1)S(1)} %bitcast.189), channel_id=1, source_target_pairs={{0,1},{1,0},{2,3},{3,2},{4,5},{5,4},{6,7},{7,6},{8,9},{9,8},{10,11... | collective-permute-start | bytes 1179656 | tf_op jit(solution)/shard_map/ppermute | solution.py:407
  222.5 34.9 %collective-permute-start.88 = (bf16[4,64,2,128]{3,2,1,0:T(2,128)(2,1)S(1)}, bf16[4,64,2,128]{3,2,1,0:T(2,128)(2,1)S(1)}, u32[]{:S(2)}, u32[]{:S(2)}) collective-permute-start(bf16[4,64,2,128]{3,2,1,0:T(2,128)(2,1)S(1)} %bitcast.197), channel_id=1, source_target_pairs={{0,6},{1,7},{2,4},{3,5},{4,2},{5,3},{6,0},{7,1},{8,14},{9,15},{10,... | collective-permute-start | bytes 393224 | tf_op jit(solution)/shard_map/ppermute | solution.py:407
  227.8 31.5 %collective-permute-start.89 = (bf16[4,64,2,128]{3,2,1,0:T(2,128)(2,1)S(1)}, bf16[4,64,2,128]{3,2,1,0:T(2,128)(2,1)S(1)}, u32[]{:S(2)}, u32[]{:S(2)}) collective-permute-start(bf16[4,64,2,128]{3,2,1,0:T(2,128)(2,1)S(1)} %bitcast.196), channel_id=1, source_target_pairs={{0,7},{1,6},{2,5},{3,4},{4,15},{5,14},{6,13},{7,12},{8,3},{9,2},{1... | collective-permute-start | bytes 393224 | tf_op jit(solution)/shard_map/ppermute | solution.py:407
  232.6 28.7 %collective-permute-start.90 = (bf16[4,64,2,128]{3,2,1,0:T(2,128)(2,1)S(1)}, bf16[4,64,2,128]{3,2,1,0:T(2,128)(2,1)S(1)}, u32[]{:S(2)}, u32[]{:S(2)}) collective-permute-start(bf16[4,64,2,128]{3,2,1,0:T(2,128)(2,1)S(1)} %bitcast.195), channel_id=1, source_target_pairs={{0,11},{1,10},{2,9},{3,8},{4,3},{5,2},{6,1},{7,0},{8,15},{9,14},{1... | collective-permute-start | bytes 393224 | tf_op jit(solution)/shard_map/ppermute | solution.py:407
  236.4 24.9 %collective-permute-start.91 = (bf16[4,64,2,128]{3,2,1,0:T(2,128)(2,1)S(1)}, bf16[4,64,2,128]{3,2,1,0:T(2,128)(2,1)S(1)}, u32[]{:S(2)}, u32[]{:S(2)}) collective-permute-start(bf16[4,64,2,128]{3,2,1,0:T(2,128)(2,1)S(1)} %bitcast.194), channel_id=1, source_target_pairs={{0,7},{1,6},{2,5},{3,4},{4,11},{5,10},{6,9},{7,8},{8,15},{9,14},{1... | collective-permute-start | bytes 393224 | tf_op jit(solution)/shard_map/ppermute | solution.py:407
  301.7 29.7 %collective-permute-start.65 = (bf16[4,192,2,128]{3,2,1,0:T(2,128)(2,1)}, bf16[4,192,2,128]{3,2,1,0:T(2,128)(2,1)S(1)}, u32[]{:S(2)}, u32[]{:S(2)}) collective-permute-start(bf16[4,192,2,128]{3,2,1,0:T(2,128)(2,1)} %bitcast.188), channel_id=1, source_target_pairs={{0,3},{1,2},{2,1},{3,0},{4,7},{5,6},{6,5},{7,4},{8,11},{9,10},{10,... | collective-permute-start | bytes 1179656 | tf_op jit(solution)/shard_map/ppermute | solution.py:407
  302.3 37.5 %collective-permute-start.66 = (bf16[4,192,2,128]{3,2,1,0:T(2,128)(2,1)}, bf16[4,192,2,128]{3,2,1,0:T(2,128)(2,1)S(1)}, u32[]{:S(2)}, u32[]{:S(2)}) collective-permute-start(bf16[4,192,2,128]{3,2,1,0:T(2,128)(2,1)} %bitcast.187), channel_id=1, source_target_pairs={{0,2},{1,3},{2,0},{3,1},{4,6},{5,7},{6,4},{7,5},{8,10},{9,11},{10,... | collective-permute-start | bytes 1179656 | tf_op jit(solution)/shard_map/ppermute | solution.py:407
  306.3 33.6 %collective-permute-start.67 = (bf16[4,192,2,128]{3,2,1,0:T(2,128)(2,1)}, bf16[4,192,2,128]{3,2,1,0:T(2,128)(2,1)S(1)}, u32[]{:S(2)}, u32[]{:S(2)}) collective-permute-start(bf16[4,192,2,128]{3,2,1,0:T(2,128)(2,1)} %bitcast.186), channel_id=1, source_target_pairs={{0,1},{1,0},{2,3},{3,2},{4,5},{5,4},{6,7},{7,6},{8,9},{9,8},{10,11... | collective-permute-start | bytes 1179656 | tf_op jit(solution)/shard_map/ppermute | solution.py:407
  (193 other events, 6999.7 us)

commit v16 on v12

--- a/solution.py
+++ b/solution.py
@@ -58,16 +58,17 @@
     return reached(lax.axis_index("fsdp"), devices, ((0, 2, 1, 3)[kind], offset))
 
 
-def pack(queries, out_grad, neighbours, devices, chunk, chunks):
+def pack(queries, out_grad, neighbours, devices, picked, chunk, chunks):
     heads = neighbours.shape[2] // HD // devices // chunks
     width = heads * HD
+    count = len(moves(devices)[picked])
 
     def kernel(q_ref, g_ref, n_ref, *refs):
-        outs, (plain, tokens, rows, come_t, come_r, go_t, go_r) = refs[:devices], refs[devices:]
-        every = range(devices)
+        outs, (plain, tokens, rows, come_t, come_r, go_t, go_r) = refs[:count], refs[count:]
+        every = range(count)
         columns = [
             pl.ds(pl.multiple_of((target(devices, move) * chunks + chunk) * width, width), width)
-            for move in moves(devices)
+            for move in moves(devices)[picked]
         ]
         token_loads = [
             [
@@ -110,16 +111,16 @@
     results = pl.pallas_call(
         kernel,
         in_specs=[ANY] * 3,
-        out_specs=[ANY] * devices,
-        out_shape=[shape] * devices,
+        out_specs=[ANY] * count,
+        out_shape=[shape] * count,
         scratch_shapes=[
-            vmem(devices, 2 * SPAN, width),
-            vmem(devices, heads, SPAN, 2, HD),
-            vmem(devices, NTOK, 2, width),
-            pltpu.SemaphoreType.DMA((devices, 2)),
-            pltpu.SemaphoreType.DMA((devices,)),
-            pltpu.SemaphoreType.DMA((devices,)),
-            pltpu.SemaphoreType.DMA((devices, heads)),
+            vmem(count, 2 * SPAN, width),
+            vmem(count, heads, SPAN, 2, HD),
+            vmem(count, NTOK, 2, width),
+            pltpu.SemaphoreType.DMA((count, 2)),
+            pltpu.SemaphoreType.DMA((count,)),
+            pltpu.SemaphoreType.DMA((count,)),
+            pltpu.SemaphoreType.DMA((count, heads)),
         ],
         compiler_params=LIMIT,
         cost_estimate=cost(4),
@@ -128,17 +129,18 @@
     return list(results)
 
 
-def unpack(blocks, before, chunk, chunks):
-    devices, heads = len(blocks), blocks[0].shape[0]
+def unpack(blocks, before, devices, picked, chunk, chunks):
+    blocks = blocks[picked]
+    count, heads = len(blocks), blocks[0].shape[0]
     width = heads * HD
 
     def kernel(*refs):
-        ins, flat = refs[:devices], refs[devices : 2 * devices]
+        ins, flat = refs[:count], refs[count : 2 * count]
         o_ref, q_ref, n_ref, rows, tokens, come_r, come_t, go_r, go_t = refs[-9:]
-        every = range(devices)
+        every = range(count)
         columns = [
             pl.ds(pl.multiple_of((source(devices, move) * chunks + chunk) * width, width), width)
-            for move in moves(devices)
+            for move in moves(devices)[picked]
         ]
         row_loads = [
             [
@@ -183,21 +185,21 @@
     total = devices * width * chunks
     return pl.pallas_call(
         kernel,
-        in_specs=[ANY] * (2 * devices + len(before)),
+        in_specs=[ANY] * (2 * count + len(before)),
         out_specs=[ANY] * 3,
         out_shape=[
             jax.ShapeDtypeStruct((SPAN, total), BF16),
             jax.ShapeDtypeStruct((SPAN, total), BF16),
             jax.ShapeDtypeStruct((NTOK, 2, total), BF16),
         ],
-        input_output_aliases={2 * devices + i: i for i in range(len(before))},
+        input_output_aliases={2 * count + i: i for i in range(len(before))},
         scratch_shapes=[
-            vmem(devices, NTOK, 2, width),
-            vmem(devices, 2 * SPAN, width),
-            pltpu.SemaphoreType.DMA((devices, heads)),
-            pltpu.SemaphoreType.DMA((devices, heads)),
-            pltpu.SemaphoreType.DMA((devices,)),
-            pltpu.SemaphoreType.DMA((devices, 2)),
+            vmem(count, NTOK, 2, width),
+            vmem(count, 2 * SPAN, width),
+            pltpu.SemaphoreType.DMA((count, heads)),
+            pltpu.SemaphoreType.DMA((count, heads)),
+            pltpu.SemaphoreType.DMA((count,)),
+            pltpu.SemaphoreType.DMA((count, 2)),
         ],
         compiler_params=LIMIT,
         cost_estimate=cost(4),
@@ -331,6 +333,10 @@
     return later
 
 
+def pieces(devices, first):
+    return [slice(0, first)] + ([slice(first, devices)] if first < devices else [])
+
+
 def swap(blocks):
     devices = len(blocks)
     return blocks[:1] + [
@@ -346,7 +352,9 @@
     slots = jnp.argsort(neighbour_ids, stable=True).astype(jnp.int32)
     arrived, back = [], []
     for chunk in range(chunks):
-        blocks = pack(queries, out_grad, neighbours, devices, chunk, chunks)
+        blocks = []
+        for picked in pieces(devices, devices * 3 // 8 if chunk == 0 else devices):
+            blocks += pack(queries, out_grad, neighbours, devices, picked, chunk, chunks)
         if arrived:
             blocks = after(blocks, arrived[-1])
         arrived.append(swap(blocks))
@@ -360,7 +368,8 @@
         back.append(swap(blocks))
     outputs = ()
     for chunk in range(chunks):
-        outputs = tuple(unpack(back[chunk], outputs, chunk, chunks))
+        for picked in pieces(devices, devices * 3 // 4 if chunk == chunks - 1 else devices):
+            outputs = tuple(unpack(back[chunk], outputs, devices, picked, chunk, chunks))
     return outputs
 
 

time: 297 us -> 294 us (0.990)
  waiting for transfers between devices: 143 us -> 139 us
  starting transfers between devices: 115 us -> 112 us
    ppermute x60, waiting for transfers between devices: 143 us -> 139 us  [swap(): lax.ppermute(block, 'fsdp', [(i, reached(i, devices, move)) for i in rang...]
    pallas_call x4 -> x6, Pallas kernels: 16.5 us -> 19.4 us  [the longest x3 10.4 us: pack(): pl.pallas_call(kernel, in_specs=[ANY] * 3, out_specs=[ANY] * count, out_s...]
  transfers between devices with their start and end apart: 60 -> 60, of which waited for: 34 -> 32; matrix products, arithmetic and copies ran while one was open for 1% -> 1% of each run, Pallas kernels for 9% -> 11%
where the time goes in v16:
time: 294 us; the launch traced here: 291 us
  waiting for transfers between devices  139 us (47%)
  starting transfers between devices  112 us (38%)
  Pallas kernels  36.4 us (12%)
    ppermute x60, waiting for transfers between devices, swap(): lax.ppermute(block, 'fsdp', [(i, reached(i, devices, move)) for i in rang...  139 us
    ppermute x60, starting transfers between devices, swap(): lax.ppermute(block, 'fsdp', [(i, reached(i, devices, move)) for i in rang...  112 us
    pallas_call x2, Pallas kernels, attention(): pl.pallas_call(attention_kernel, grid_spec=pltpu.PrefetchScalarGridSpec(n...  17 us
    pallas_call x3, Pallas kernels, pack(): pl.pallas_call(kernel, in_specs=[ANY] * 3, out_specs=[ANY] * count, out_s...  10.4 us
    pallas_call x3, Pallas kernels, unpack(): pl.pallas_call(kernel, in_specs=[ANY] * (2 * count + len(before)), out_sp...  9 us
  transfers between devices with their start and end apart: 60, of which 32 were waited for; matrix products, arithmetic and copies ran while one was open for 1% of the time, Pallas kernels for 11%

profile of v16, /device:TPU:15, one launch (start us, length us, event | category | flops | bytes accessed | tf_op | source)
XLA Modules:
  0.0 290.7 jit_solution(4366841869980665347)
XLA Ops:
  17.4 5.5 %collective-permute-done.2 = bf16[2,192,2,128]{3,2,1,0:T(2,128)(2,1)S(1)} collective-permute-done((bf16[2,192,2,128]{3,2,1,0:T(2,128)(2,1)}, bf16[2,192,2,128]{3,2,1,0:T(2,128)(2,1)S(1)}, u32[]{:S(2)}, u32[]{:S(2)}) %collective-permute-start.2) | collective-permute-done | bytes 196640 | tf_op jit(solution)/shard_map/ppermute | solution.py:343
  24.2 10.7 %collective-permute-done.4 = bf16[2,192,2,128]{3,2,1,0:T(2,128)(2,1)S(1)} collective-permute-done((bf16[2,192,2,128]{3,2,1,0:T(2,128)(2,1)}, bf16[2,192,2,128]{3,2,1,0:T(2,128)(2,1)S(1)}, u32[]{:S(2)}, u32[]{:S(2)}) %collective-permute-start.4) | collective-permute-done | bytes 196640 | tf_op jit(solution)/shard_map/ppermute | solution.py:343
  41.1 9.1 %collective-permute-start.11 = (bf16[2,192,2,128]{3,2,1,0:T(2,128)(2,1)}, bf16[2,192,2,128]{3,2,1,0:T(2,128)(2,1)}, u32[]{:S(2)}, u32[]{:S(2)}) collective-permute-start(bf16[2,192,2,128]{3,2,1,0:T(2,128)(2,1)} %get-tuple-element.199), channel_id=1, source_target_pairs={{0,3},{1,2},{2,1},{3,0},{4,7},{5,6},{6,5},{7,4},{8,11},{9,10},{10,... | collective-permute-start | bytes 589832 | tf_op jit(solution)/shard_map/ppermute | solution.py:343
  56.3 4.4 %pack.3 = (bf16[2,192,2,128]{3,2,1,0:T(2,128)(2,1)}, bf16[2,192,2,128]{3,2,1,0:T(2,128)(2,1)}, bf16[2,192,2,128]{3,2,1,0:T(2,128)(2,1)}, bf16[2,192,2,128]{3,2,1...) custom-call(bf16[64,8192]{1,0:T(8,128)(2,1)} %q_ref.5, ...), custom_call_target="tpu_custom_call" | custom-call | bytes 14760000 | tf_op jit(solution)/shard_map/pack/pallas_call | solution.py:111
  60.7 7.0 %collective-permute-done.10 = bf16[2,192,2,128]{3,2,1,0:T(2,128)(2,1)} collective-permute-done((bf16[2,192,2,128]{3,2,1,0:T(2,128)(2,1)}, bf16[2,192,2,128]{3,2,1,0:T(2,128)(2,1)}, u32[]{:S(2)}, u32[]{:S(2)}) %collective-permute-start.10) | collective-permute-done | bytes 196640 | tf_op jit(solution)/shard_map/ppermute | solution.py:343
  72.1 4.6 %collective-permute-start.18 = (bf16[2,192,2,128]{3,2,1,0:T(2,128)(2,1)}, bf16[2,192,2,128]{3,2,1,0:T(2,128)(2,1)}, u32[]{:S(2)}, u32[]{:S(2)}) collective-permute-start(bf16[2,192,2,128]{3,2,1,0:T(2,128)(2,1)} %get-tuple-element.223), channel_id=1, source_target_pairs={{0,1},{1,0},{2,3},{3,2},{4,5},{5,4},{6,7},{7,6},{8,9},{9,8},{10,11... | collective-permute-start | bytes 589832 | tf_op jit(solution)/shard_map/ppermute | solution.py:343
  76.8 5.8 %collective-permute-done.14 = bf16[2,192,2,128]{3,2,1,0:T(2,128)(2,1)} collective-permute-done((bf16[2,192,2,128]{3,2,1,0:T(2,128)(2,1)}, bf16[2,192,2,128]{3,2,1,0:T(2,128)(2,1)}, u32[]{:S(2)}, u32[]{:S(2)}) %collective-permute-start.14) | collective-permute-done | bytes 196640 | tf_op jit(solution)/shard_map/ppermute | solution.py:343
  82.6 6.3 %collective-permute-done.15 = bf16[2,192,2,128]{3,2,1,0:T(2,128)(2,1)} collective-permute-done((bf16[2,192,2,128]{3,2,1,0:T(2,128)(2,1)}, bf16[2,192,2,128]{3,2,1,0:T(2,128)(2,1)}, u32[]{:S(2)}, u32[]{:S(2)}) %collective-permute-start.15) | collective-permute-done | bytes 196640 | tf_op jit(solution)/shard_map/ppermute | solution.py:343
  92.6 9.0 %collective-permute-done.17 = bf16[2,192,2,128]{3,2,1,0:T(2,128)(2,1)} collective-permute-done((bf16[2,192,2,128]{3,2,1,0:T(2,128)(2,1)}, bf16[2,192,2,128]{3,2,1,0:T(2,128)(2,1)}, u32[]{:S(2)}, u32[]{:S(2)}) %collective-permute-start.17) | collective-permute-done | bytes 196640 | tf_op jit(solution)/shard_map/ppermute | solution.py:343
  105.8 8.3 %collective-permute-start.25 = (bf16[2,192,2,128]{3,2,1,0:T(2,128)(2,1)}, bf16[2,192,2,128]{3,2,1,0:T(2,128)(2,1)}, u32[]{:S(2)}, u32[]{:S(2)}) collective-permute-start(bf16[2,192,2,128]{3,2,1,0:T(2,128)(2,1)} %get-tuple-element.230), channel_id=1, source_target_pairs={{0,14},{1,15},{2,12},{3,13},{4,10},{5,11},{6,8},{7,9},{8,6},{9,7},... | collective-permute-start | bytes 589832 | tf_op jit(solution)/shard_map/ppermute | solution.py:343
  114.1 6.7 %collective-permute-start.26 = (bf16[2,192,2,128]{3,2,1,0:T(2,128)(2,1)}, bf16[2,192,2,128]{3,2,1,0:T(2,128)(2,1)}, u32[]{:S(2)}, u32[]{:S(2)}) collective-permute-start(bf16[2,192,2,128]{3,2,1,0:T(2,128)(2,1)} %get-tuple-element.243), channel_id=1, source_target_pairs={{0,3},{1,2},{2,1},{3,0},{4,7},{5,6},{6,5},{7,4},{8,11},{9,10},{10,... | collective-permute-start | bytes 589832 | tf_op jit(solution)/shard_map/ppermute | solution.py:343
  129.2 8.5 %attention.2 = (bf16[2,384,128]{2,1,0:T(8,128)(2,1)}, bf16[2,384,128]{2,1,0:T(8,128)(2,1)}, bf16[2,384,128]{2,1,0:T(8,128)(2,1)}, bf16[2,384,128]{2,1,0:T(8,128)...) custom-call(s32[32]{0:T(128)} %get-tuple-element.158.slots_ref, ...), custom_call_target="tpu_custom_call" | custom-call | bytes 29520000 | tf_op jit(solution)/shard_map/attention/pallas_call | solution.py:304
  145.7 9.7 %collective-permute-done.29 = bf16[2,192,2,128]{3,2,1,0:T(2,128)(2,1)} collective-permute-done((bf16[2,192,2,128]{3,2,1,0:T(2,128)(2,1)}, bf16[2,192,2,128]{3,2,1,0:T(2,128)(2,1)}, u32[]{:S(2)}, u32[]{:S(2)}) %collective-permute-start.29) | collective-permute-done | bytes 196640 | tf_op jit(solution)/shard_map/ppermute | solution.py:343
  163.2 9.1 %collective-permute-done.32.refs_3_ = bf16[2,192,2,128]{3,2,1,0:T(2,128)(2,1)S(1)} collective-permute-done((bf16[2,192,2,128]{3,2,1,0:T(2,128)(2,1)}, bf16[2,192,2,128]{3,2,1,0:T(2,128)(2,1)S(1)}, u32[]{:S(2)}, u32[]{:S(2)}) %collective-permute-start.32) | collective-permute-done | bytes 196640 | tf_op jit(solution)/shard_map/ppermute | solution.py:343
  176.5 8.2 %collective-permute-start.40 = (bf16[2,192,2,128]{3,2,1,0:T(2,128)(2,1)}, bf16[2,192,2,128]{3,2,1,0:T(2,128)(2,1)}, u32[]{:S(2)}, u32[]{:S(2)}) collective-permute-start(bf16[2,192,2,128]{3,2,1,0:T(2,128)(2,1)} %bitcast.118), channel_id=1, source_target_pairs={{0,14},{1,15},{2,12},{3,13},{4,10},{5,11},{6,8},{7,9},{8,6},{9,7},... | collective-permute-start | bytes 589832 | tf_op jit(solution)/shard_map/ppermute | solution.py:343
  184.7 6.8 %collective-permute-start.56 = (bf16[2,192,2,128]{3,2,1,0:T(2,128)(2,1)}, bf16[2,192,2,128]{3,2,1,0:T(2,128)(2,1)}, u32[]{:S(2)}, u32[]{:S(2)}) collective-permute-start(bf16[2,192,2,128]{3,2,1,0:T(2,128)(2,1)} %bitcast.117), channel_id=1, source_target_pairs={{0,3},{1,2},{2,1},{3,0},{4,7},{5,6},{6,5},{7,4},{8,11},{9,10},{10,... | collective-permute-start | bytes 589832 | tf_op jit(solution)/shard_map/ppermute | solution.py:343
  197.5 8.5 %attention.3 = (bf16[2,384,128]{2,1,0:T(8,128)(2,1)}, bf16[2,384,128]{2,1,0:T(8,128)(2,1)}, bf16[2,384,128]{2,1,0:T(8,128)(2,1)}, bf16[2,384,128]{2,1,0:T(8,128)...) custom-call(s32[32]{0:T(128)} %get-tuple-element.158.slots_ref, ...), custom_call_target="tpu_custom_call" | custom-call | bytes 29520000 | tf_op jit(solution)/shard_map/attention/pallas_call | solution.py:304
  213.5 4.7 %collective-permute-start.48 = (bf16[2,192,2,128]{3,2,1,0:T(2,128)(2,1)}, bf16[2,192,2,128]{3,2,1,0:T(2,128)(2,1)}, u32[]{:S(2)}, u32[]{:S(2)}) collective-permute-start(bf16[2,192,2,128]{3,2,1,0:T(2,128)(2,1)} %bitcast.132), channel_id=1, source_target_pairs={{0,1},{1,0},{2,3},{3,2},{4,5},{5,4},{6,7},{7,6},{8,9},{9,8},{10,11... | collective-permute-start | bytes 589832 | tf_op jit(solution)/shard_map/ppermute | solution.py:343
  218.1 8.1 %collective-permute-done.59.refs_15_ = bf16[2,192,2,128]{3,2,1,0:T(2,128)(2,1)} collective-permute-done((bf16[2,192,2,128]{3,2,1,0:T(2,128)(2,1)}, bf16[2,192,2,128]{3,2,1,0:T(2,128)(2,1)}, u32[]{:S(2)}, u32[]{:S(2)}) %collective-permute-start.59) | collective-permute-done | bytes 196640 | tf_op jit(solution)/shard_map/ppermute | solution.py:343
  234.1 4.8 %collective-permute-done.47.refs_3_ = bf16[2,192,2,128]{3,2,1,0:T(2,128)(2,1)} collective-permute-done((bf16[2,192,2,128]{3,2,1,0:T(2,128)(2,1)}, bf16[2,192,2,128]{3,2,1,0:T(2,128)(2,1)}, u32[]{:S(2)}, u32[]{:S(2)}) %collective-permute-start.47) | collective-permute-done | bytes 196640 | tf_op jit(solution)/shard_map/ppermute | solution.py:343
  238.9 8.4 %collective-permute-done.49.refs_5_ = bf16[2,192,2,128]{3,2,1,0:T(2,128)(2,1)} collective-permute-done((bf16[2,192,2,128]{3,2,1,0:T(2,128)(2,1)}, bf16[2,192,2,128]{3,2,1,0:T(2,128)(2,1)}, u32[]{:S(2)}, u32[]{:S(2)}) %collective-permute-start.49) | collective-permute-done | bytes 196640 | tf_op jit(solution)/shard_map/ppermute | solution.py:343
  247.3 8.3 %collective-permute-start.55 = (bf16[2,192,2,128]{3,2,1,0:T(2,128)(2,1)}, bf16[2,192,2,128]{3,2,1,0:T(2,128)(2,1)}, u32[]{:S(2)}, u32[]{:S(2)}) collective-permute-start(bf16[2,192,2,128]{3,2,1,0:T(2,128)(2,1)} %bitcast.119), channel_id=1, source_target_pairs={{0,14},{1,15},{2,12},{3,13},{4,10},{5,11},{6,8},{7,9},{8,6},{9,7},... | collective-permute-start | bytes 589832 | tf_op jit(solution)/shard_map/ppermute | solution.py:343
  255.6 6.5 %collective-permute-start.41 = (bf16[2,192,2,128]{3,2,1,0:T(2,128)(2,1)}, bf16[2,192,2,128]{3,2,1,0:T(2,128)(2,1)}, u32[]{:S(2)}, u32[]{:S(2)}) collective-permute-start(bf16[2,192,2,128]{3,2,1,0:T(2,128)(2,1)} %bitcast.116), channel_id=1, source_target_pairs={{0,3},{1,2},{2,1},{3,0},{4,7},{5,6},{6,5},{7,4},{8,11},{9,10},{10,... | collective-permute-start | bytes 589832 | tf_op jit(solution)/shard_map/ppermute | solution.py:343
  272.1 7.9 %collective-permute-done.55.refs_11_ = bf16[2,192,2,128]{3,2,1,0:T(2,128)(2,1)} collective-permute-done((bf16[2,192,2,128]{3,2,1,0:T(2,128)(2,1)}, bf16[2,192,2,128]{3,2,1,0:T(2,128)(2,1)}, u32[]{:S(2)}, u32[]{:S(2)}) %collective-permute-start.55) | collective-permute-done | bytes 196640 | tf_op jit(solution)/shard_map/ppermute | solution.py:343
  (126 shorter events, 112.8 us)
Async XLA Ops:
  7.6 27.3 %collective-permute-start.4 = (bf16[2,192,2,128]{3,2,1,0:T(2,128)(2,1)}, bf16[2,192,2,128]{3,2,1,0:T(2,128)(2,1)S(1)}, u32[]{:S(2)}, u32[]{:S(2)}) collective-permute-start(bf16[2,192,2,128]{3,2,1,0:T(2,128)(2,1)} %get-tuple-element.180), channel_id=1, source_target_pairs={{0,5},{1,4},{2,7},{3,6},{4,13},{5,12},{6,15},{7,14},{8,1},{9,0},{1... | collective-permute-start | bytes 589832 | tf_op jit(solution)/shard_map/ppermute | solution.py:343
  14.6 26.5 %collective-permute-start.6 = (bf16[2,192,2,128]{3,2,1,0:T(2,128)(2,1)}, bf16[2,192,2,128]{3,2,1,0:T(2,128)(2,1)}, u32[]{:S(2)}, u32[]{:S(2)}) collective-permute-start(bf16[2,192,2,128]{3,2,1,0:T(2,128)(2,1)} %get-tuple-element.182), channel_id=1, source_target_pairs={{0,13},{1,12},{2,15},{3,14},{4,9},{5,8},{6,11},{7,10},{8,5},{9,4},... | collective-permute-start | bytes 589832 | tf_op jit(solution)/shard_map/ppermute | solution.py:343
  22.9 27.3 %collective-permute-start.7 = (bf16[2,192,2,128]{3,2,1,0:T(2,128)(2,1)}, bf16[2,192,2,128]{3,2,1,0:T(2,128)(2,1)}, u32[]{:S(2)}, u32[]{:S(2)}) collective-permute-start(bf16[2,192,2,128]{3,2,1,0:T(2,128)(2,1)} %get-tuple-element.183), channel_id=1, source_target_pairs={{0,2},{1,3},{2,0},{3,1},{4,6},{5,7},{6,4},{7,5},{8,10},{9,11},{10,... | collective-permute-start | bytes 589832 | tf_op jit(solution)/shard_map/ppermute | solution.py:343
  23.2 28.6 %collective-permute-start.8 = (bf16[2,192,2,128]{3,2,1,0:T(2,128)(2,1)}, bf16[2,192,2,128]{3,2,1,0:T(2,128)(2,1)}, u32[]{:S(2)}, u32[]{:S(2)}) collective-permute-start(bf16[2,192,2,128]{3,2,1,0:T(2,128)(2,1)} %get-tuple-element.184), channel_id=1, source_target_pairs={{0,6},{1,7},{2,4},{3,5},{4,14},{5,15},{6,12},{7,13},{8,2},{9,3},{1... | collective-permute-start | bytes 589832 | tf_op jit(solution)/shard_map/ppermute | solution.py:343
  37.7 30.0 %collective-permute-start.10 = (bf16[2,192,2,128]{3,2,1,0:T(2,128)(2,1)}, bf16[2,192,2,128]{3,2,1,0:T(2,128)(2,1)}, u32[]{:S(2)}, u32[]{:S(2)}) collective-permute-start(bf16[2,192,2,128]{3,2,1,0:T(2,128)(2,1)} %get-tuple-element.186), channel_id=1, source_target_pairs={{0,14},{1,15},{2,12},{3,13},{4,10},{5,11},{6,8},{7,9},{8,6},{9,7},... | collective-permute-start | bytes 589832 | tf_op jit(solution)/shard_map/ppermute | solution.py:343
  41.1 28.5 %collective-permute-start.11 = (bf16[2,192,2,128]{3,2,1,0:T(2,128)(2,1)}, bf16[2,192,2,128]{3,2,1,0:T(2,128)(2,1)}, u32[]{:S(2)}, u32[]{:S(2)}) collective-permute-start(bf16[2,192,2,128]{3,2,1,0:T(2,128)(2,1)} %get-tuple-element.199), channel_id=1, source_target_pairs={{0,3},{1,2},{2,1},{3,0},{4,7},{5,6},{6,5},{7,4},{8,11},{9,10},{10,... | collective-permute-start | bytes 589832 | tf_op jit(solution)/shard_map/ppermute | solution.py:343
  56.1 26.5 %collective-permute-start.14 = (bf16[2,192,2,128]{3,2,1,0:T(2,128)(2,1)}, bf16[2,192,2,128]{3,2,1,0:T(2,128)(2,1)}, u32[]{:S(2)}, u32[]{:S(2)}) collective-permute-start(bf16[2,192,2,128]{3,2,1,0:T(2,128)(2,1)} %get-tuple-element.202), channel_id=1, source_target_pairs={{0,15},{1,14},{2,13},{3,12},{4,11},{5,10},{6,9},{7,8},{8,7},{9,6},... | collective-permute-start | bytes 589832 | tf_op jit(solution)/shard_map/ppermute | solution.py:343
  72.1 29.4 %collective-permute-start.17 = (bf16[2,192,2,128]{3,2,1,0:T(2,128)(2,1)}, bf16[2,192,2,128]{3,2,1,0:T(2,128)(2,1)}, u32[]{:S(2)}, u32[]{:S(2)}) collective-permute-start(bf16[2,192,2,128]{3,2,1,0:T(2,128)(2,1)} %get-tuple-element.222), channel_id=1, source_target_pairs={{0,12},{1,13},{2,14},{3,15},{4,8},{5,9},{6,10},{7,11},{8,4},{9,5},... | collective-permute-start | bytes 589832 | tf_op jit(solution)/shard_map/ppermute | solution.py:343
  72.1 29.4 %collective-permute-start.18 = (bf16[2,192,2,128]{3,2,1,0:T(2,128)(2,1)}, bf16[2,192,2,128]{3,2,1,0:T(2,128)(2,1)}, u32[]{:S(2)}, u32[]{:S(2)}) collective-permute-start(bf16[2,192,2,128]{3,2,1,0:T(2,128)(2,1)} %get-tuple-element.223), channel_id=1, source_target_pairs={{0,1},{1,0},{2,3},{3,2},{4,5},{5,4},{6,7},{7,6},{8,9},{9,8},{10,11... | collective-permute-start | bytes 589832 | tf_op jit(solution)/shard_map/ppermute | solution.py:343
  105.8 32.6 %collective-permute-start.25 = (bf16[2,192,2,128]{3,2,1,0:T(2,128)(2,1)}, bf16[2,192,2,128]{3,2,1,0:T(2,128)(2,1)}, u32[]{:S(2)}, u32[]{:S(2)}) collective-permute-start(bf16[2,192,2,128]{3,2,1,0:T(2,128)(2,1)} %get-tuple-element.230), channel_id=1, source_target_pairs={{0,14},{1,15},{2,12},{3,13},{4,10},{5,11},{6,8},{7,9},{8,6},{9,7},... | collective-permute-start | bytes 589832 | tf_op jit(solution)/shard_map/ppermute | solution.py:343
  114.1 26.8 %collective-permute-start.26 = (bf16[2,192,2,128]{3,2,1,0:T(2,128)(2,1)}, bf16[2,192,2,128]{3,2,1,0:T(2,128)(2,1)}, u32[]{:S(2)}, u32[]{:S(2)}) collective-permute-start(bf16[2,192,2,128]{3,2,1,0:T(2,128)(2,1)} %get-tuple-element.243), channel_id=1, source_target_pairs={{0,3},{1,2},{2,1},{3,0},{4,7},{5,6},{6,5},{7,4},{8,11},{9,10},{10,... | collective-permute-start | bytes 589832 | tf_op jit(solution)/shard_map/ppermute | solution.py:343
  123.4 32.0 %collective-permute-start.29 = (bf16[2,192,2,128]{3,2,1,0:T(2,128)(2,1)}, bf16[2,192,2,128]{3,2,1,0:T(2,128)(2,1)}, u32[]{:S(2)}, u32[]{:S(2)}) collective-permute-start(bf16[2,192,2,128]{3,2,1,0:T(2,128)(2,1)} %get-tuple-element.246), channel_id=1, source_target_pairs={{0,15},{1,14},{2,13},{3,12},{4,11},{5,10},{6,9},{7,8},{8,7},{9,6},... | collective-permute-start | bytes 589832 | tf_op jit(solution)/shard_map/ppermute | solution.py:343
  142.8 29.5 %collective-permute-start.32 = (bf16[2,192,2,128]{3,2,1,0:T(2,128)(2,1)}, bf16[2,192,2,128]{3,2,1,0:T(2,128)(2,1)S(1)}, u32[]{:S(2)}, u32[]{:S(2)}) collective-permute-start(bf16[2,192,2,128]{3,2,1,0:T(2,128)(2,1)} %bitcast.135), channel_id=1, source_target_pairs={{0,12},{1,13},{2,14},{3,15},{4,8},{5,9},{6,10},{7,11},{8,4},{9,5},... | collective-permute-start | bytes 589832 | tf_op jit(solution)/shard_map/ppermute | solution.py:343
  142.8 29.5 %collective-permute-start.33 = (bf16[2,192,2,128]{3,2,1,0:T(2,128)(2,1)}, bf16[2,192,2,128]{3,2,1,0:T(2,128)(2,1)S(1)}, u32[]{:S(2)}, u32[]{:S(2)}) collective-permute-start(bf16[2,192,2,128]{3,2,1,0:T(2,128)(2,1)} %bitcast.133), channel_id=1, source_target_pairs={{0,1},{1,0},{2,3},{3,2},{4,5},{5,4},{6,7},{7,6},{8,9},{9,8},{10,11... | collective-permute-start | bytes 589832 | tf_op jit(solution)/shard_map/ppermute | solution.py:343
  159.6 25.1 %collective-permute-start.36 = (bf16[2,192,2,128]{3,2,1,0:T(2,128)(2,1)}, bf16[2,192,2,128]{3,2,1,0:T(2,128)(2,1)}, u32[]{:S(2)}, u32[]{:S(2)}) collective-permute-start(bf16[2,192,2,128]{3,2,1,0:T(2,128)(2,1)} %bitcast.127), channel_id=1, source_target_pairs={{0,13},{1,12},{2,15},{3,14},{4,9},{5,8},{6,11},{7,10},{8,5},{9,4},... | collective-permute-start | bytes 589832 | tf_op jit(solution)/shard_map/ppermute | solution.py:343
  176.5 32.7 %collective-permute-start.40 = (bf16[2,192,2,128]{3,2,1,0:T(2,128)(2,1)}, bf16[2,192,2,128]{3,2,1,0:T(2,128)(2,1)}, u32[]{:S(2)}, u32[]{:S(2)}) collective-permute-start(bf16[2,192,2,128]{3,2,1,0:T(2,128)(2,1)} %bitcast.118), channel_id=1, source_target_pairs={{0,14},{1,15},{2,12},{3,13},{4,10},{5,11},{6,8},{7,9},{8,6},{9,7},... | collective-permute-start | bytes 589832 | tf_op jit(solution)/shard_map/ppermute | solution.py:343
  184.7 27.3 %collective-permute-start.56 = (bf16[2,192,2,128]{3,2,1,0:T(2,128)(2,1)}, bf16[2,192,2,128]{3,2,1,0:T(2,128)(2,1)}, u32[]{:S(2)}, u32[]{:S(2)}) collective-permute-start(bf16[2,192,2,128]{3,2,1,0:T(2,128)(2,1)} %bitcast.117), channel_id=1, source_target_pairs={{0,3},{1,2},{2,1},{3,0},{4,7},{5,6},{6,5},{7,4},{8,11},{9,10},{10,... | collective-permute-start | bytes 589832 | tf_op jit(solution)/shard_map/ppermute | solution.py:343
  194.1 32.1 %collective-permute-start.59 = (bf16[2,192,2,128]{3,2,1,0:T(2,128)(2,1)}, bf16[2,192,2,128]{3,2,1,0:T(2,128)(2,1)}, u32[]{:S(2)}, u32[]{:S(2)}) collective-permute-start(bf16[2,192,2,128]{3,2,1,0:T(2,128)(2,1)} %bitcast.110), channel_id=1, source_target_pairs={{0,15},{1,14},{2,13},{3,12},{4,11},{5,10},{6,9},{7,8},{8,7},{9,6},... | collective-permute-start | bytes 589832 | tf_op jit(solution)/shard_map/ppermute | solution.py:343
  213.5 25.4 %collective-permute-start.47 = (bf16[2,192,2,128]{3,2,1,0:T(2,128)(2,1)}, bf16[2,192,2,128]{3,2,1,0:T(2,128)(2,1)}, u32[]{:S(2)}, u32[]{:S(2)}) collective-permute-start(bf16[2,192,2,128]{3,2,1,0:T(2,128)(2,1)} %bitcast.134), channel_id=1, source_target_pairs={{0,12},{1,13},{2,14},{3,15},{4,8},{5,9},{6,10},{7,11},{8,4},{9,5},... | collective-permute-start | bytes 589832 | tf_op jit(solution)/shard_map/ppermute | solution.py:343
  213.5 25.4 %collective-permute-start.48 = (bf16[2,192,2,128]{3,2,1,0:T(2,128)(2,1)}, bf16[2,192,2,128]{3,2,1,0:T(2,128)(2,1)}, u32[]{:S(2)}, u32[]{:S(2)}) collective-permute-start(bf16[2,192,2,128]{3,2,1,0:T(2,128)(2,1)} %bitcast.132), channel_id=1, source_target_pairs={{0,1},{1,0},{2,3},{3,2},{4,5},{5,4},{6,7},{7,6},{8,9},{9,8},{10,11... | collective-permute-start | bytes 589832 | tf_op jit(solution)/shard_map/ppermute | solution.py:343
  230.4 25.2 %collective-permute-start.51 = (bf16[2,192,2,128]{3,2,1,0:T(2,128)(2,1)}, bf16[2,192,2,128]{3,2,1,0:T(2,128)(2,1)}, u32[]{:S(2)}, u32[]{:S(2)}) collective-permute-start(bf16[2,192,2,128]{3,2,1,0:T(2,128)(2,1)} %bitcast.126), channel_id=1, source_target_pairs={{0,13},{1,12},{2,15},{3,14},{4,9},{5,8},{6,11},{7,10},{8,5},{9,4},... | collective-permute-start | bytes 589832 | tf_op jit(solution)/shard_map/ppermute | solution.py:343
  238.9 25.3 %collective-permute-start.53 = (bf16[2,192,2,128]{3,2,1,0:T(2,128)(2,1)}, bf16[2,192,2,128]{3,2,1,0:T(2,128)(2,1)}, u32[]{:S(2)}, u32[]{:S(2)}) collective-permute-start(bf16[2,192,2,128]{3,2,1,0:T(2,128)(2,1)} %bitcast.122), channel_id=1, source_target_pairs={{0,6},{1,7},{2,4},{3,5},{4,14},{5,15},{6,12},{7,13},{8,2},{9,3},{1... | collective-permute-start | bytes 589832 | tf_op jit(solution)/shard_map/ppermute | solution.py:343
  247.3 32.8 %collective-permute-start.55 = (bf16[2,192,2,128]{3,2,1,0:T(2,128)(2,1)}, bf16[2,192,2,128]{3,2,1,0:T(2,128)(2,1)}, u32[]{:S(2)}, u32[]{:S(2)}) collective-permute-start(bf16[2,192,2,128]{3,2,1,0:T(2,128)(2,1)} %bitcast.119), channel_id=1, source_target_pairs={{0,14},{1,15},{2,12},{3,13},{4,10},{5,11},{6,8},{7,9},{8,6},{9,7},... | collective-permute-start | bytes 589832 | tf_op jit(solution)/shard_map/ppermute | solution.py:343
  255.6 27.5 %collective-permute-start.41 = (bf16[2,192,2,128]{3,2,1,0:T(2,128)(2,1)}, bf16[2,192,2,128]{3,2,1,0:T(2,128)(2,1)}, u32[]{:S(2)}, u32[]{:S(2)}) collective-permute-start(bf16[2,192,2,128]{3,2,1,0:T(2,128)(2,1)} %bitcast.116), channel_id=1, source_target_pairs={{0,3},{1,2},{2,1},{3,0},{4,7},{5,6},{6,5},{7,4},{8,11},{9,10},{10,... | collective-permute-start | bytes 589832 | tf_op jit(solution)/shard_map/ppermute | solution.py:343
  (46 other events, 1747.8 us)

commit v17 on v16

--- a/solution.py
+++ b/solution.py
@@ -328,7 +328,7 @@
 
 
 def after(later, earlier):
-    some = len(earlier) * 3 // 4
+    some = len(earlier) // 2
     later, earlier[:some] = lax.optimization_barrier((later, earlier[:some]))
     return later
 
@@ -353,7 +353,7 @@
     arrived, back = [], []
     for chunk in range(chunks):
         blocks = []
-        for picked in pieces(devices, devices * 3 // 8 if chunk == 0 else devices):
+        for picked in pieces(devices, devices // 4 if chunk == 0 else devices):
             blocks += pack(queries, out_grad, neighbours, devices, picked, chunk, chunks)
         if arrived:
             blocks = after(blocks, arrived[-1])
@@ -368,7 +368,7 @@
         back.append(swap(blocks))
     outputs = ()
     for chunk in range(chunks):
-        for picked in pieces(devices, devices * 3 // 4 if chunk == chunks - 1 else devices):
+        for picked in pieces(devices, devices * 7 // 8 if chunk == chunks - 1 else devices):
             outputs = tuple(unpack(back[chunk], outputs, devices, picked, chunk, chunks))
     return outputs
 

time: 294 us -> 294 us (level)
  transfers between devices with their start and end apart: 60 -> 60, of which waited for: 32 -> 33; matrix products, arithmetic and copies ran while one was open for 1% -> 1% of each run, Pallas kernels for 11% -> 11%
where the time goes in v17:
time: 294 us; the launch traced here: 291 us
  waiting for transfers between devices  138 us (47%)
  starting transfers between devices  112 us (38%)
  Pallas kernels  36.4 us (12%)
    ppermute x60, waiting for transfers between devices, swap(): lax.ppermute(block, 'fsdp', [(i, reached(i, devices, move)) for i in rang...  138 us
    ppermute x60, starting transfers between devices, swap(): lax.ppermute(block, 'fsdp', [(i, reached(i, devices, move)) for i in rang...  112 us
    pallas_call x2, Pallas kernels, attention(): pl.pallas_call(attention_kernel, grid_spec=pltpu.PrefetchScalarGridSpec(n...  17 us
    pallas_call x3, Pallas kernels, pack(): pl.pallas_call(kernel, in_specs=[ANY] * 3, out_specs=[ANY] * count, out_s...  10.4 us
    pallas_call x3, Pallas kernels, unpack(): pl.pallas_call(kernel, in_specs=[ANY] * (2 * count + len(before)), out_sp...  8.95 us
  transfers between devices with their start and end apart: 60, of which 33 were waited for; matrix products, arithmetic and copies ran while one was open for 1% of the time, Pallas kernels for 11%

profile of v17, /device:TPU:15, one launch (start us, length us, event | category | flops | bytes accessed | tf_op | source)
XLA Modules:
  0.0 290.7 jit_solution(11000430527057389191)
XLA Ops:
  17.1 5.5 %collective-permute-done.2 = bf16[2,192,2,128]{3,2,1,0:T(2,128)(2,1)S(1)} collective-permute-done((bf16[2,192,2,128]{3,2,1,0:T(2,128)(2,1)}, bf16[2,192,2,128]{3,2,1,0:T(2,128)(2,1)S(1)}, u32[]{:S(2)}, u32[]{:S(2)}) %collective-permute-start.2) | collective-permute-done | bytes 196640 | tf_op jit(solution)/shard_map/ppermute | solution.py:343
  23.9 10.7 %collective-permute-done.4 = bf16[2,192,2,128]{3,2,1,0:T(2,128)(2,1)S(1)} collective-permute-done((bf16[2,192,2,128]{3,2,1,0:T(2,128)(2,1)}, bf16[2,192,2,128]{3,2,1,0:T(2,128)(2,1)S(1)}, u32[]{:S(2)}, u32[]{:S(2)}) %collective-permute-start.4) | collective-permute-done | bytes 196640 | tf_op jit(solution)/shard_map/ppermute | solution.py:343
  40.8 9.1 %collective-permute-start.11 = (bf16[2,192,2,128]{3,2,1,0:T(2,128)(2,1)}, bf16[2,192,2,128]{3,2,1,0:T(2,128)(2,1)}, u32[]{:S(2)}, u32[]{:S(2)}) collective-permute-start(bf16[2,192,2,128]{3,2,1,0:T(2,128)(2,1)} %get-tuple-element.183), channel_id=1, source_target_pairs={{0,3},{1,2},{2,1},{3,0},{4,7},{5,6},{6,5},{7,4},{8,11},{9,10},{10,... | collective-permute-start | bytes 589832 | tf_op jit(solution)/shard_map/ppermute | solution.py:343
  55.9 4.4 %pack.3 = (bf16[2,192,2,128]{3,2,1,0:T(2,128)(2,1)}, bf16[2,192,2,128]{3,2,1,0:T(2,128)(2,1)}, bf16[2,192,2,128]{3,2,1,0:T(2,128)(2,1)}, bf16[2,192,2,128]{3,2,1...) custom-call(bf16[64,8192]{1,0:T(8,128)(2,1)} %q_ref.5, ...), custom_call_target="tpu_custom_call" | custom-call | bytes 14760000 | tf_op jit(solution)/shard_map/pack/pallas_call | solution.py:111
  60.3 7.0 %collective-permute-done.10 = bf16[2,192,2,128]{3,2,1,0:T(2,128)(2,1)} collective-permute-done((bf16[2,192,2,128]{3,2,1,0:T(2,128)(2,1)}, bf16[2,192,2,128]{3,2,1,0:T(2,128)(2,1)}, u32[]{:S(2)}, u32[]{:S(2)}) %collective-permute-start.10) | collective-permute-done | bytes 196640 | tf_op jit(solution)/shard_map/ppermute | solution.py:343
  71.8 4.6 %collective-permute-start.18 = (bf16[2,192,2,128]{3,2,1,0:T(2,128)(2,1)}, bf16[2,192,2,128]{3,2,1,0:T(2,128)(2,1)}, u32[]{:S(2)}, u32[]{:S(2)}) collective-permute-start(bf16[2,192,2,128]{3,2,1,0:T(2,128)(2,1)} %get-tuple-element.207), channel_id=1, source_target_pairs={{0,1},{1,0},{2,3},{3,2},{4,5},{5,4},{6,7},{7,6},{8,9},{9,8},{10,11... | collective-permute-start | bytes 589832 | tf_op jit(solution)/shard_map/ppermute | solution.py:343
  76.4 5.8 %collective-permute-done.14 = bf16[2,192,2,128]{3,2,1,0:T(2,128)(2,1)} collective-permute-done((bf16[2,192,2,128]{3,2,1,0:T(2,128)(2,1)}, bf16[2,192,2,128]{3,2,1,0:T(2,128)(2,1)}, u32[]{:S(2)}, u32[]{:S(2)}) %collective-permute-start.14) | collective-permute-done | bytes 196640 | tf_op jit(solution)/shard_map/ppermute | solution.py:343
  82.3 6.3 %collective-permute-done.15 = bf16[2,192,2,128]{3,2,1,0:T(2,128)(2,1)} collective-permute-done((bf16[2,192,2,128]{3,2,1,0:T(2,128)(2,1)}, bf16[2,192,2,128]{3,2,1,0:T(2,128)(2,1)}, u32[]{:S(2)}, u32[]{:S(2)}) %collective-permute-start.15) | collective-permute-done | bytes 196640 | tf_op jit(solution)/shard_map/ppermute | solution.py:343
  92.3 9.0 %collective-permute-done.17 = bf16[2,192,2,128]{3,2,1,0:T(2,128)(2,1)} collective-permute-done((bf16[2,192,2,128]{3,2,1,0:T(2,128)(2,1)}, bf16[2,192,2,128]{3,2,1,0:T(2,128)(2,1)}, u32[]{:S(2)}, u32[]{:S(2)}) %collective-permute-start.17) | collective-permute-done | bytes 196640 | tf_op jit(solution)/shard_map/ppermute | solution.py:343
  105.4 8.3 %collective-permute-start.25 = (bf16[2,192,2,128]{3,2,1,0:T(2,128)(2,1)}, bf16[2,192,2,128]{3,2,1,0:T(2,128)(2,1)}, u32[]{:S(2)}, u32[]{:S(2)}) collective-permute-start(bf16[2,192,2,128]{3,2,1,0:T(2,128)(2,1)} %get-tuple-element.222), channel_id=1, source_target_pairs={{0,14},{1,15},{2,12},{3,13},{4,10},{5,11},{6,8},{7,9},{8,6},{9,7},... | collective-permute-start | bytes 589832 | tf_op jit(solution)/shard_map/ppermute | solution.py:343
  113.8 6.7 %collective-permute-start.26 = (bf16[2,192,2,128]{3,2,1,0:T(2,128)(2,1)}, bf16[2,192,2,128]{3,2,1,0:T(2,128)(2,1)}, u32[]{:S(2)}, u32[]{:S(2)}) collective-permute-start(bf16[2,192,2,128]{3,2,1,0:T(2,128)(2,1)} %get-tuple-element.223), channel_id=1, source_target_pairs={{0,3},{1,2},{2,1},{3,0},{4,7},{5,6},{6,5},{7,4},{8,11},{9,10},{10,... | collective-permute-start | bytes 589832 | tf_op jit(solution)/shard_map/ppermute | solution.py:343
  128.9 8.5 %attention.2 = (bf16[2,384,128]{2,1,0:T(8,128)(2,1)}, bf16[2,384,128]{2,1,0:T(8,128)(2,1)}, bf16[2,384,128]{2,1,0:T(8,128)(2,1)}, bf16[2,384,128]{2,1,0:T(8,128)...) custom-call(s32[32]{0:T(128)} %get-tuple-element.146.slots_ref, ...), custom_call_target="tpu_custom_call" | custom-call | bytes 29520000 | tf_op jit(solution)/shard_map/attention/pallas_call | solution.py:304
  145.4 9.7 %collective-permute-done.29 = bf16[2,192,2,128]{3,2,1,0:T(2,128)(2,1)} collective-permute-done((bf16[2,192,2,128]{3,2,1,0:T(2,128)(2,1)}, bf16[2,192,2,128]{3,2,1,0:T(2,128)(2,1)}, u32[]{:S(2)}, u32[]{:S(2)}) %collective-permute-start.29) | collective-permute-done | bytes 196640 | tf_op jit(solution)/shard_map/ppermute | solution.py:343
  162.9 9.1 %collective-permute-done.32.refs_3_ = bf16[2,192,2,128]{3,2,1,0:T(2,128)(2,1)S(1)} collective-permute-done((bf16[2,192,2,128]{3,2,1,0:T(2,128)(2,1)}, bf16[2,192,2,128]{3,2,1,0:T(2,128)(2,1)S(1)}, u32[]{:S(2)}, u32[]{:S(2)}) %collective-permute-start.32) | collective-permute-done | bytes 196640 | tf_op jit(solution)/shard_map/ppermute | solution.py:343
  176.1 8.3 %collective-permute-start.55 = (bf16[2,192,2,128]{3,2,1,0:T(2,128)(2,1)}, bf16[2,192,2,128]{3,2,1,0:T(2,128)(2,1)S(1)}, u32[]{:S(2)}, u32[]{:S(2)}) collective-permute-start(bf16[2,192,2,128]{3,2,1,0:T(2,128)(2,1)} %bitcast.128), channel_id=1, source_target_pairs={{0,14},{1,15},{2,12},{3,13},{4,10},{5,11},{6,8},{7,9},{8,6},{9,7},... | collective-permute-start | bytes 589832 | tf_op jit(solution)/shard_map/ppermute | solution.py:343
  184.5 6.7 %collective-permute-start.56 = (bf16[2,192,2,128]{3,2,1,0:T(2,128)(2,1)}, bf16[2,192,2,128]{3,2,1,0:T(2,128)(2,1)S(1)}, u32[]{:S(2)}, u32[]{:S(2)}) collective-permute-start(bf16[2,192,2,128]{3,2,1,0:T(2,128)(2,1)} %bitcast.127), channel_id=1, source_target_pairs={{0,3},{1,2},{2,1},{3,0},{4,7},{5,6},{6,5},{7,4},{8,11},{9,10},{10,... | collective-permute-start | bytes 589832 | tf_op jit(solution)/shard_map/ppermute | solution.py:343
  197.2 8.5 %attention.3 = (bf16[2,384,128]{2,1,0:T(8,128)(2,1)}, bf16[2,384,128]{2,1,0:T(8,128)(2,1)}, bf16[2,384,128]{2,1,0:T(8,128)(2,1)}, bf16[2,384,128]{2,1,0:T(8,128)...) custom-call(s32[32]{0:T(128)} %get-tuple-element.146.slots_ref, ...), custom_call_target="tpu_custom_call" | custom-call | bytes 29520000 | tf_op jit(solution)/shard_map/attention/pallas_call | solution.py:304
  213.2 4.7 %collective-permute-start.42 = (bf16[2,192,2,128]{3,2,1,0:T(2,128)(2,1)}, bf16[2,192,2,128]{3,2,1,0:T(2,128)(2,1)S(1)}, u32[]{:S(2)}, u32[]{:S(2)}) collective-permute-start(bf16[2,192,2,128]{3,2,1,0:T(2,128)(2,1)} %bitcast.144), channel_id=1, source_target_pairs={{0,1},{1,0},{2,3},{3,2},{4,5},{5,4},{6,7},{7,6},{8,9},{9,8},{10,11... | collective-permute-start | bytes 589832 | tf_op jit(solution)/shard_map/ppermute | solution.py:343
  217.8 8.1 %collective-permute-done.59.refs_15_ = bf16[2,192,2,128]{3,2,1,0:T(2,128)(2,1)} collective-permute-done((bf16[2,192,2,128]{3,2,1,0:T(2,128)(2,1)}, bf16[2,192,2,128]{3,2,1,0:T(2,128)(2,1)}, u32[]{:S(2)}, u32[]{:S(2)}) %collective-permute-start.59) | collective-permute-done | bytes 196640 | tf_op jit(solution)/shard_map/ppermute | solution.py:343
  233.6 4.9 %collective-permute-done.41.refs_3_ = bf16[2,192,2,128]{3,2,1,0:T(2,128)(2,1)S(1)} collective-permute-done((bf16[2,192,2,128]{3,2,1,0:T(2,128)(2,1)}, bf16[2,192,2,128]{3,2,1,0:T(2,128)(2,1)S(1)}, u32[]{:S(2)}, u32[]{:S(2)}) %collective-permute-start.41) | collective-permute-done | bytes 196640 | tf_op jit(solution)/shard_map/ppermute | solution.py:343
  238.6 8.3 %collective-permute-done.43.refs_5_ = bf16[2,192,2,128]{3,2,1,0:T(2,128)(2,1)S(1)} collective-permute-done((bf16[2,192,2,128]{3,2,1,0:T(2,128)(2,1)}, bf16[2,192,2,128]{3,2,1,0:T(2,128)(2,1)S(1)}, u32[]{:S(2)}, u32[]{:S(2)}) %collective-permute-start.43) | collective-permute-done | bytes 196640 | tf_op jit(solution)/shard_map/ppermute | solution.py:343
  246.9 8.2 %collective-permute-start.49 = (bf16[2,192,2,128]{3,2,1,0:T(2,128)(2,1)}, bf16[2,192,2,128]{3,2,1,0:T(2,128)(2,1)}, u32[]{:S(2)}, u32[]{:S(2)}) collective-permute-start(bf16[2,192,2,128]{3,2,1,0:T(2,128)(2,1)} %bitcast.131), channel_id=1, source_target_pairs={{0,14},{1,15},{2,12},{3,13},{4,10},{5,11},{6,8},{7,9},{8,6},{9,7},... | collective-permute-start | bytes 589832 | tf_op jit(solution)/shard_map/ppermute | solution.py:343
  255.1 6.6 %collective-permute-start.50 = (bf16[2,192,2,128]{3,2,1,0:T(2,128)(2,1)}, bf16[2,192,2,128]{3,2,1,0:T(2,128)(2,1)}, u32[]{:S(2)}, u32[]{:S(2)}) collective-permute-start(bf16[2,192,2,128]{3,2,1,0:T(2,128)(2,1)} %bitcast.130), channel_id=1, source_target_pairs={{0,3},{1,2},{2,1},{3,0},{4,7},{5,6},{6,5},{7,4},{8,11},{9,10},{10,... | collective-permute-start | bytes 589832 | tf_op jit(solution)/shard_map/ppermute | solution.py:343
  271.8 7.8 %collective-permute-done.49.refs_11_ = bf16[2,192,2,128]{3,2,1,0:T(2,128)(2,1)} collective-permute-done((bf16[2,192,2,128]{3,2,1,0:T(2,128)(2,1)}, bf16[2,192,2,128]{3,2,1,0:T(2,128)(2,1)}, u32[]{:S(2)}, u32[]{:S(2)}) %collective-permute-start.49) | collective-permute-done | bytes 196640 | tf_op jit(solution)/shard_map/ppermute | solution.py:343
  (150 shorter events, 112.8 us)
Async XLA Ops:
  12.9 24.5 %collective-permute-start.5 = (bf16[2,192,2,128]{3,2,1,0:T(2,128)(2,1)}, bf16[2,192,2,128]{3,2,1,0:T(2,128)(2,1)}, u32[]{:S(2)}, u32[]{:S(2)}) collective-permute-start(bf16[2,192,2,128]{3,2,1,0:T(2,128)(2,1)} %get-tuple-element.169), channel_id=1, source_target_pairs={{0,9},{1,8},{2,11},{3,10},{4,1},{5,0},{6,3},{7,2},{8,13},{9,12},{1... | collective-permute-start | bytes 589832 | tf_op jit(solution)/shard_map/ppermute | solution.py:343
  14.3 26.5 %collective-permute-start.6 = (bf16[2,192,2,128]{3,2,1,0:T(2,128)(2,1)}, bf16[2,192,2,128]{3,2,1,0:T(2,128)(2,1)}, u32[]{:S(2)}, u32[]{:S(2)}) collective-permute-start(bf16[2,192,2,128]{3,2,1,0:T(2,128)(2,1)} %get-tuple-element.170), channel_id=1, source_target_pairs={{0,13},{1,12},{2,15},{3,14},{4,9},{5,8},{6,11},{7,10},{8,5},{9,4},... | collective-permute-start | bytes 589832 | tf_op jit(solution)/shard_map/ppermute | solution.py:343
  22.6 27.3 %collective-permute-start.7 = (bf16[2,192,2,128]{3,2,1,0:T(2,128)(2,1)}, bf16[2,192,2,128]{3,2,1,0:T(2,128)(2,1)}, u32[]{:S(2)}, u32[]{:S(2)}) collective-permute-start(bf16[2,192,2,128]{3,2,1,0:T(2,128)(2,1)} %get-tuple-element.179), channel_id=1, source_target_pairs={{0,2},{1,3},{2,0},{3,1},{4,6},{5,7},{6,4},{7,5},{8,10},{9,11},{10,... | collective-permute-start | bytes 589832 | tf_op jit(solution)/shard_map/ppermute | solution.py:343
  22.8 28.6 %collective-permute-start.8 = (bf16[2,192,2,128]{3,2,1,0:T(2,128)(2,1)}, bf16[2,192,2,128]{3,2,1,0:T(2,128)(2,1)}, u32[]{:S(2)}, u32[]{:S(2)}) collective-permute-start(bf16[2,192,2,128]{3,2,1,0:T(2,128)(2,1)} %get-tuple-element.180), channel_id=1, source_target_pairs={{0,6},{1,7},{2,4},{3,5},{4,14},{5,15},{6,12},{7,13},{8,2},{9,3},{1... | collective-permute-start | bytes 589832 | tf_op jit(solution)/shard_map/ppermute | solution.py:343
  37.3 30.0 %collective-permute-start.10 = (bf16[2,192,2,128]{3,2,1,0:T(2,128)(2,1)}, bf16[2,192,2,128]{3,2,1,0:T(2,128)(2,1)}, u32[]{:S(2)}, u32[]{:S(2)}) collective-permute-start(bf16[2,192,2,128]{3,2,1,0:T(2,128)(2,1)} %get-tuple-element.182), channel_id=1, source_target_pairs={{0,14},{1,15},{2,12},{3,13},{4,10},{5,11},{6,8},{7,9},{8,6},{9,7},... | collective-permute-start | bytes 589832 | tf_op jit(solution)/shard_map/ppermute | solution.py:343
  40.8 28.5 %collective-permute-start.11 = (bf16[2,192,2,128]{3,2,1,0:T(2,128)(2,1)}, bf16[2,192,2,128]{3,2,1,0:T(2,128)(2,1)}, u32[]{:S(2)}, u32[]{:S(2)}) collective-permute-start(bf16[2,192,2,128]{3,2,1,0:T(2,128)(2,1)} %get-tuple-element.183), channel_id=1, source_target_pairs={{0,3},{1,2},{2,1},{3,0},{4,7},{5,6},{6,5},{7,4},{8,11},{9,10},{10,... | collective-permute-start | bytes 589832 | tf_op jit(solution)/shard_map/ppermute | solution.py:343
  55.8 26.5 %collective-permute-start.14 = (bf16[2,192,2,128]{3,2,1,0:T(2,128)(2,1)}, bf16[2,192,2,128]{3,2,1,0:T(2,128)(2,1)}, u32[]{:S(2)}, u32[]{:S(2)}) collective-permute-start(bf16[2,192,2,128]{3,2,1,0:T(2,128)(2,1)} %get-tuple-element.186), channel_id=1, source_target_pairs={{0,15},{1,14},{2,13},{3,12},{4,11},{5,10},{6,9},{7,8},{8,7},{9,6},... | collective-permute-start | bytes 589832 | tf_op jit(solution)/shard_map/ppermute | solution.py:343
  71.8 29.4 %collective-permute-start.17 = (bf16[2,192,2,128]{3,2,1,0:T(2,128)(2,1)}, bf16[2,192,2,128]{3,2,1,0:T(2,128)(2,1)}, u32[]{:S(2)}, u32[]{:S(2)}) collective-permute-start(bf16[2,192,2,128]{3,2,1,0:T(2,128)(2,1)} %get-tuple-element.206), channel_id=1, source_target_pairs={{0,12},{1,13},{2,14},{3,15},{4,8},{5,9},{6,10},{7,11},{8,4},{9,5},... | collective-permute-start | bytes 589832 | tf_op jit(solution)/shard_map/ppermute | solution.py:343
  71.8 29.4 %collective-permute-start.18 = (bf16[2,192,2,128]{3,2,1,0:T(2,128)(2,1)}, bf16[2,192,2,128]{3,2,1,0:T(2,128)(2,1)}, u32[]{:S(2)}, u32[]{:S(2)}) collective-permute-start(bf16[2,192,2,128]{3,2,1,0:T(2,128)(2,1)} %get-tuple-element.207), channel_id=1, source_target_pairs={{0,1},{1,0},{2,3},{3,2},{4,5},{5,4},{6,7},{7,6},{8,9},{9,8},{10,11... | collective-permute-start | bytes 589832 | tf_op jit(solution)/shard_map/ppermute | solution.py:343
  105.4 32.6 %collective-permute-start.25 = (bf16[2,192,2,128]{3,2,1,0:T(2,128)(2,1)}, bf16[2,192,2,128]{3,2,1,0:T(2,128)(2,1)}, u32[]{:S(2)}, u32[]{:S(2)}) collective-permute-start(bf16[2,192,2,128]{3,2,1,0:T(2,128)(2,1)} %get-tuple-element.222), channel_id=1, source_target_pairs={{0,14},{1,15},{2,12},{3,13},{4,10},{5,11},{6,8},{7,9},{8,6},{9,7},... | collective-permute-start | bytes 589832 | tf_op jit(solution)/shard_map/ppermute | solution.py:343
  113.8 26.8 %collective-permute-start.26 = (bf16[2,192,2,128]{3,2,1,0:T(2,128)(2,1)}, bf16[2,192,2,128]{3,2,1,0:T(2,128)(2,1)}, u32[]{:S(2)}, u32[]{:S(2)}) collective-permute-start(bf16[2,192,2,128]{3,2,1,0:T(2,128)(2,1)} %get-tuple-element.223), channel_id=1, source_target_pairs={{0,3},{1,2},{2,1},{3,0},{4,7},{5,6},{6,5},{7,4},{8,11},{9,10},{10,... | collective-permute-start | bytes 589832 | tf_op jit(solution)/shard_map/ppermute | solution.py:343
  123.1 32.0 %collective-permute-start.29 = (bf16[2,192,2,128]{3,2,1,0:T(2,128)(2,1)}, bf16[2,192,2,128]{3,2,1,0:T(2,128)(2,1)}, u32[]{:S(2)}, u32[]{:S(2)}) collective-permute-start(bf16[2,192,2,128]{3,2,1,0:T(2,128)(2,1)} %get-tuple-element.226), channel_id=1, source_target_pairs={{0,15},{1,14},{2,13},{3,12},{4,11},{5,10},{6,9},{7,8},{8,7},{9,6},... | collective-permute-start | bytes 589832 | tf_op jit(solution)/shard_map/ppermute | solution.py:343
  142.4 29.5 %collective-permute-start.32 = (bf16[2,192,2,128]{3,2,1,0:T(2,128)(2,1)}, bf16[2,192,2,128]{3,2,1,0:T(2,128)(2,1)S(1)}, u32[]{:S(2)}, u32[]{:S(2)}) collective-permute-start(bf16[2,192,2,128]{3,2,1,0:T(2,128)(2,1)} %bitcast.147), channel_id=1, source_target_pairs={{0,12},{1,13},{2,14},{3,15},{4,8},{5,9},{6,10},{7,11},{8,4},{9,5},... | collective-permute-start | bytes 589832 | tf_op jit(solution)/shard_map/ppermute | solution.py:343
  142.4 29.5 %collective-permute-start.33 = (bf16[2,192,2,128]{3,2,1,0:T(2,128)(2,1)}, bf16[2,192,2,128]{3,2,1,0:T(2,128)(2,1)}, u32[]{:S(2)}, u32[]{:S(2)}) collective-permute-start(bf16[2,192,2,128]{3,2,1,0:T(2,128)(2,1)} %bitcast.145), channel_id=1, source_target_pairs={{0,1},{1,0},{2,3},{3,2},{4,5},{5,4},{6,7},{7,6},{8,9},{9,8},{10,11... | collective-permute-start | bytes 589832 | tf_op jit(solution)/shard_map/ppermute | solution.py:343
  159.3 25.2 %collective-permute-start.36 = (bf16[2,192,2,128]{3,2,1,0:T(2,128)(2,1)}, bf16[2,192,2,128]{3,2,1,0:T(2,128)(2,1)}, u32[]{:S(2)}, u32[]{:S(2)}) collective-permute-start(bf16[2,192,2,128]{3,2,1,0:T(2,128)(2,1)} %bitcast.139), channel_id=1, source_target_pairs={{0,13},{1,12},{2,15},{3,14},{4,9},{5,8},{6,11},{7,10},{8,5},{9,4},... | collective-permute-start | bytes 589832 | tf_op jit(solution)/shard_map/ppermute | solution.py:343
  176.1 32.7 %collective-permute-start.55 = (bf16[2,192,2,128]{3,2,1,0:T(2,128)(2,1)}, bf16[2,192,2,128]{3,2,1,0:T(2,128)(2,1)S(1)}, u32[]{:S(2)}, u32[]{:S(2)}) collective-permute-start(bf16[2,192,2,128]{3,2,1,0:T(2,128)(2,1)} %bitcast.128), channel_id=1, source_target_pairs={{0,14},{1,15},{2,12},{3,13},{4,10},{5,11},{6,8},{7,9},{8,6},{9,7},... | collective-permute-start | bytes 589832 | tf_op jit(solution)/shard_map/ppermute | solution.py:343
  184.5 27.2 %collective-permute-start.56 = (bf16[2,192,2,128]{3,2,1,0:T(2,128)(2,1)}, bf16[2,192,2,128]{3,2,1,0:T(2,128)(2,1)S(1)}, u32[]{:S(2)}, u32[]{:S(2)}) collective-permute-start(bf16[2,192,2,128]{3,2,1,0:T(2,128)(2,1)} %bitcast.127), channel_id=1, source_target_pairs={{0,3},{1,2},{2,1},{3,0},{4,7},{5,6},{6,5},{7,4},{8,11},{9,10},{10,... | collective-permute-start | bytes 589832 | tf_op jit(solution)/shard_map/ppermute | solution.py:343
  193.8 32.1 %collective-permute-start.59 = (bf16[2,192,2,128]{3,2,1,0:T(2,128)(2,1)}, bf16[2,192,2,128]{3,2,1,0:T(2,128)(2,1)}, u32[]{:S(2)}, u32[]{:S(2)}) collective-permute-start(bf16[2,192,2,128]{3,2,1,0:T(2,128)(2,1)} %bitcast.122), channel_id=1, source_target_pairs={{0,15},{1,14},{2,13},{3,12},{4,11},{5,10},{6,9},{7,8},{8,7},{9,6},... | collective-permute-start | bytes 589832 | tf_op jit(solution)/shard_map/ppermute | solution.py:343
  213.1 25.4 %collective-permute-start.41 = (bf16[2,192,2,128]{3,2,1,0:T(2,128)(2,1)}, bf16[2,192,2,128]{3,2,1,0:T(2,128)(2,1)S(1)}, u32[]{:S(2)}, u32[]{:S(2)}) collective-permute-start(bf16[2,192,2,128]{3,2,1,0:T(2,128)(2,1)} %bitcast.146), channel_id=1, source_target_pairs={{0,12},{1,13},{2,14},{3,15},{4,8},{5,9},{6,10},{7,11},{8,4},{9,5},... | collective-permute-start | bytes 589832 | tf_op jit(solution)/shard_map/ppermute | solution.py:343
  213.2 25.4 %collective-permute-start.42 = (bf16[2,192,2,128]{3,2,1,0:T(2,128)(2,1)}, bf16[2,192,2,128]{3,2,1,0:T(2,128)(2,1)S(1)}, u32[]{:S(2)}, u32[]{:S(2)}) collective-permute-start(bf16[2,192,2,128]{3,2,1,0:T(2,128)(2,1)} %bitcast.144), channel_id=1, source_target_pairs={{0,1},{1,0},{2,3},{3,2},{4,5},{5,4},{6,7},{7,6},{8,9},{9,8},{10,11... | collective-permute-start | bytes 589832 | tf_op jit(solution)/shard_map/ppermute | solution.py:343
  230.1 25.1 %collective-permute-start.45 = (bf16[2,192,2,128]{3,2,1,0:T(2,128)(2,1)}, bf16[2,192,2,128]{3,2,1,0:T(2,128)(2,1)S(1)}, u32[]{:S(2)}, u32[]{:S(2)}) collective-permute-start(bf16[2,192,2,128]{3,2,1,0:T(2,128)(2,1)} %bitcast.138), channel_id=1, source_target_pairs={{0,13},{1,12},{2,15},{3,14},{4,9},{5,8},{6,11},{7,10},{8,5},{9,4},... | collective-permute-start | bytes 589832 | tf_op jit(solution)/shard_map/ppermute | solution.py:343
  238.6 25.2 %collective-permute-start.47 = (bf16[2,192,2,128]{3,2,1,0:T(2,128)(2,1)}, bf16[2,192,2,128]{3,2,1,0:T(2,128)(2,1)S(1)}, u32[]{:S(2)}, u32[]{:S(2)}) collective-permute-start(bf16[2,192,2,128]{3,2,1,0:T(2,128)(2,1)} %bitcast.134), channel_id=1, source_target_pairs={{0,6},{1,7},{2,4},{3,5},{4,14},{5,15},{6,12},{7,13},{8,2},{9,3},{1... | collective-permute-start | bytes 589832 | tf_op jit(solution)/shard_map/ppermute | solution.py:343
  246.9 32.7 %collective-permute-start.49 = (bf16[2,192,2,128]{3,2,1,0:T(2,128)(2,1)}, bf16[2,192,2,128]{3,2,1,0:T(2,128)(2,1)}, u32[]{:S(2)}, u32[]{:S(2)}) collective-permute-start(bf16[2,192,2,128]{3,2,1,0:T(2,128)(2,1)} %bitcast.131), channel_id=1, source_target_pairs={{0,14},{1,15},{2,12},{3,13},{4,10},{5,11},{6,8},{7,9},{8,6},{9,7},... | collective-permute-start | bytes 589832 | tf_op jit(solution)/shard_map/ppermute | solution.py:343
  255.1 27.0 %collective-permute-start.50 = (bf16[2,192,2,128]{3,2,1,0:T(2,128)(2,1)}, bf16[2,192,2,128]{3,2,1,0:T(2,128)(2,1)}, u32[]{:S(2)}, u32[]{:S(2)}) collective-permute-start(bf16[2,192,2,128]{3,2,1,0:T(2,128)(2,1)} %bitcast.130), channel_id=1, source_target_pairs={{0,3},{1,2},{2,1},{3,0},{4,7},{5,6},{6,5},{7,4},{8,11},{9,10},{10,... | collective-permute-start | bytes 589832 | tf_op jit(solution)/shard_map/ppermute | solution.py:343
  (58 other events, 1864.9 us)
